TPU v7x, 32 devices: a whole 2x2x4 slice. The times are simulated.
32 devices in a mesh: prefill: 4 (over z), prefix: 4 (over y, x), tensor: 2 (over core).
Axes of the slice: x: 2, y: 2, z: 4, core: 2. Of those that a mesh axis runs over, the one named last changes fastest.
Arguments:
- hidden_in: bfloat16 [128, 4, 4608], P('prefill', None, 'prefix'), may hold values from -12 to 12
- pre_gain: float32 [4608], P('prefix'), may hold values from 0.1 to 1.9
- w_query: bfloat16 [4608, 4096], P('prefix', 'tensor'), may hold values from -0.1875 to 0.1875
- key_projection: bfloat16 [4608, 2048], P('prefix', 'tensor'), may hold values from -0.25 to 0.25
- value_projection: bfloat16 [4608, 2048], P('prefix', 'tensor'), may hold values from -0.09375 to 0.09375
- w_out: bfloat16 [4096, 4608], P('tensor', 'prefix'), may hold values from -0.125 to 0.125
- post_gain: float32 [4608], P('prefix'), may hold values from 0.1 to 1.9
- prompt_keys: bfloat16 [8192, 2048], P(('prefill', 'prefix'), 'tensor'), may hold values from -6 to 6
- prompt_values: bfloat16 [8192, 2048], P(('prefill', 'prefix'), 'tensor'), may hold values from -6 to 6
- suffix_key_cache: bfloat16 [128, 256, 2048], P(('prefill', 'prefix'), None, 'tensor'), may hold values from -12 to 12
- suffix_value_cache: bfloat16 [128, 256, 2048], P(('prefill', 'prefix'), None, 'tensor'), may hold values from -6 to 6
- suffix_len: int32 [128], P('prefill'), may hold values from 1 to 256, as said below
Outputs:
- hidden_out: bfloat16 [128, 4, 4608], P('prefill', None, 'prefix')
Inputs may be any that keep to these rules, and one draw needn't show every extreme that they name: `suffix_len`: some row has exactly 256 valid entries.
All inputs are finite; a program needn't handle non-finite values.
Results may differ from a plain program's by a relative error of at most 0.0092.
Values may be sent and summed in bfloat16 or wider, within the bound.
No kernel may reach another device: no remote copies, remote signals or barrier semaphores. Data moves between devices by JAX's collectives and lax.ppermute only.
A program may use at most 128 MiB of HBM per device.

v0:
```python
import jax
import jax.numpy as jnp
from jax import lax
from jax.sharding import PartitionSpec as P

MODEL_WIDTH = 4608
QUERY_HEADS = 32
HEAD_SIZE = 128


SOFTCAP = 50.0
EPSILON = 1e-06


def apply_rotation(values, token_positions, heads):
    width = values.shape[1] // heads
    half = width // 2
    freq = 10000.0 ** (-2.0 * jnp.arange(half, dtype=jnp.float32) / width)
    angle = token_positions[:, None] * freq[None, :]
    cosine = jnp.cos(angle)[:, None, :]
    sine = jnp.sin(angle)[:, None, :]
    parts = values.reshape(values.shape[0], heads, width)
    first = parts[:, :, :half]
    second = parts[:, :, half:]
    turned = jnp.concatenate(
        [first * cosine - second * sine, second * cosine + first * sine], axis=2
    )
    return turned.reshape(values.shape[0], heads * width)


def soft_weight(scores):
    return jnp.exp(SOFTCAP * jnp.tanh(scores / SOFTCAP))


def shared_attention(queries, keys, values):
    count = queries.shape[0]
    kv_heads = keys.shape[1] // HEAD_SIZE
    heads_per_group = queries.shape[1] // keys.shape[1]
    grouped = queries.reshape(count, kv_heads, heads_per_group, HEAD_SIZE)
    key_head_rows = keys.reshape(keys.shape[0], kv_heads, HEAD_SIZE)
    value_head_rows = values.reshape(values.shape[0], kv_heads, HEAD_SIZE)
    scores = jnp.einsum(
        "nkgd,mkd->nkgm", grouped, key_head_rows, preferred_element_type=jnp.float32
    )
    weights = soft_weight(scores)
    totals = jnp.sum(weights, axis=3).reshape(count, kv_heads * heads_per_group)
    summed = jnp.einsum(
        "nkgm,mkd->nkgd",
        weights.astype(jnp.bfloat16),
        value_head_rows,
        preferred_element_type=jnp.float32,
    )
    return (summed.reshape(count, kv_heads * heads_per_group * HEAD_SIZE), totals)


def own_attention(
    queries, cached_key_rows, cached_value_rows, latest_keys, latest_values, lengths, steps
):
    members = lengths.shape[0]
    slots = cached_key_rows.shape[1]
    kv_heads = cached_key_rows.shape[2] // HEAD_SIZE
    heads_per_group = queries.shape[1] // cached_key_rows.shape[2]
    grouped = queries.reshape(members, steps, kv_heads, heads_per_group, HEAD_SIZE)
    cache_k = cached_key_rows.reshape(members, slots, kv_heads, HEAD_SIZE)
    cache_v = cached_value_rows.reshape(members, slots, kv_heads, HEAD_SIZE)
    valid = jnp.arange(slots, dtype=jnp.int32)[None, :] < lengths[:, None]
    cache_scores = jnp.einsum(
        "rjkgd,rmkd->rjkgm", grouped, cache_k, preferred_element_type=jnp.float32
    )
    cache_weights = jnp.where(valid[:, None, None, None, :], soft_weight(cache_scores), 0.0)
    new_k = latest_keys.reshape(members, steps, kv_heads, HEAD_SIZE)
    new_v = latest_values.reshape(members, steps, kv_heads, HEAD_SIZE)
    step_ids = jnp.arange(steps, dtype=jnp.int32)
    causal = step_ids[None, :] <= step_ids[:, None]
    new_scores = jnp.einsum("rjkgd,rikd->rjkgi", grouped, new_k, preferred_element_type=jnp.float32)
    new_weights = jnp.where(causal[None, :, None, None, :], soft_weight(new_scores), 0.0)
    totals = jnp.sum(cache_weights, axis=4) + jnp.sum(new_weights, axis=4)
    summed = jnp.einsum(
        "rjkgm,rmkd->rjkgd",
        cache_weights.astype(jnp.bfloat16),
        cache_v,
        preferred_element_type=jnp.float32,
    )
    summed = summed + jnp.einsum(
        "rjkgi,rikd->rjkgd",
        new_weights.astype(jnp.bfloat16),
        new_v,
        preferred_element_type=jnp.float32,
    )
    flat_rows = members * steps
    return (
        summed.reshape(flat_rows, kv_heads * heads_per_group * HEAD_SIZE),
        totals.reshape(flat_rows, kv_heads * heads_per_group),
    )


def per_device(
    hidden_in,
    pre_gain,
    w_query,
    key_projection,
    value_projection,
    w_out,
    post_gain,
    prompt_keys,
    prompt_values,
    suffix_key_cache,
    suffix_value_cache,
    suffix_len,
):
    group_rows, steps, local_width = hidden_in.shape
    members = suffix_key_cache.shape[0]
    query_cols = w_query.shape[1]
    kv_cols = key_projection.shape[1]
    heads = query_cols // HEAD_SIZE
    kv_heads = kv_cols // HEAD_SIZE
    own_count = members * steps
    prompt_total = prompt_keys.shape[0] * lax.axis_size("prefill") * lax.axis_size("prefix")
    signal = hidden_in.astype(jnp.float32).reshape(group_rows * steps, local_width)
    squares = lax.psum(jnp.sum(signal * signal, axis=1), "prefix")
    normed = (signal * lax.rsqrt(squares[:, None] / MODEL_WIDTH + EPSILON) * pre_gain).astype(
        jnp.bfloat16
    )
    weights_all = jnp.concatenate([w_query, key_projection, value_projection], axis=1)
    step_ids = jnp.arange(steps, dtype=jnp.int32)
    group_positions = (
        (prompt_total + suffix_len[:, None] + step_ids[None, :]).reshape(-1).astype(jnp.float32)
    )
    first_row = lax.axis_index("prefix") * members
    own_lengths = lax.dynamic_slice_in_dim(suffix_len, first_row, members)
    own_positions = lax.dynamic_slice_in_dim(group_positions, first_row * steps, own_count)
    scale = (MODEL_WIDTH // QUERY_HEADS) ** (-0.5)
    own_proj = lax.psum_scatter(
        jnp.dot(normed, weights_all, preferred_element_type=jnp.float32),
        "prefix",
        scatter_dimension=0,
        tiled=True,
    )
    own_queries = (apply_rotation(own_proj[:, :query_cols], own_positions, heads) * scale).astype(
        jnp.bfloat16
    )
    group_queries = lax.all_gather(own_queries, "prefix", axis=0, tiled=True)
    latest_keys = apply_rotation(
        own_proj[:, query_cols : query_cols + kv_cols], own_positions, kv_heads
    ).astype(jnp.bfloat16)
    latest_values = own_proj[:, query_cols + kv_cols :].astype(jnp.bfloat16)
    summed, totals = shared_attention(
        group_queries,
        lax.all_gather(prompt_keys, "prefill", axis=0, tiled=True),
        lax.all_gather(prompt_values, "prefill", axis=0, tiled=True),
    )
    prompt_totals = totals
    far_sums, far_totals = (
        lax.psum_scatter(summed, "prefix", scatter_dimension=0, tiled=True),
        lax.psum_scatter(prompt_totals, "prefix", scatter_dimension=0, tiled=True),
    )
    near_sums, near_totals = own_attention(
        own_queries,
        suffix_key_cache,
        suffix_value_cache,
        latest_keys,
        latest_values,
        own_lengths,
        steps,
    )
    totals = far_totals + near_totals
    sums = (far_sums + near_sums).reshape(own_count, heads, HEAD_SIZE)
    mixed = (sums / totals[:, :, None]).reshape(own_count, query_cols).astype(jnp.bfloat16)
    head_terms = jnp.dot(
        lax.all_gather(mixed, "prefix", axis=0, tiled=True),
        w_out,
        preferred_element_type=jnp.float32,
    )
    attended = lax.psum(head_terms, "tensor")
    out_squares = lax.psum(jnp.sum(attended * attended, axis=1), "prefix")
    branch = attended * lax.rsqrt(out_squares[:, None] / MODEL_WIDTH + EPSILON) * post_gain
    return (signal + branch).astype(jnp.bfloat16).reshape(group_rows, steps, local_width)


def solution(mesh):
    return jax.shard_map(
        per_device,
        mesh=mesh,
        in_specs=(
            P("prefill", None, "prefix"),
            P("prefix"),
            P("prefix", "tensor"),
            P("prefix", "tensor"),
            P("prefix", "tensor"),
            P("tensor", "prefix"),
            P("prefix"),
            P(("prefill", "prefix"), "tensor"),
            P(("prefill", "prefix"), "tensor"),
            P(("prefill", "prefix"), None, "tensor"),
            P(("prefill", "prefix"), None, "tensor"),
            P("prefill"),
        ),
        out_specs=P("prefill", None, "prefix"),
        check_vma=False,
    )
```

profile of v0, /device:TPU:0, one launch (start us, length us, event | category | flops | bytes accessed | tf_op | source)
XLA Modules:
  0.0 290.1 jit_solution(18274686848331685987)
XLA Ops:
  7.4 1.0 reshape.157
  8.4 1.2 multiply_reduce_fusion.1
  9.7 11.4 %psum.21 = f32[128]{0:T(128)S(1)} all-reduce(f32[128]{0:T(128)S(1)} %reduce_sum.48), channel_id=1, replica_groups=mesh['prefill'=4,'prefix'=4,'tensor'=2] {'prefix'}, use_global_device_ids=true, to_apply=%region_1.0 | all-reduce | flops 128 | bytes 1024 | tf_op jit(solution)/shard_map/psum | solution.py:120
  21.0 6.8 %fusion = f32[128,4096]{1,0:T(8,128)} fusion(bf16[1152,1024]{1,0:T(8,128)(2,1)} %param.16, bf16[1152,1024]{1,0:T(8,128)(2,1)} %param.15, bf16[1152,2048]{1,0:T(8,128)(2,1)} %param.14, f32[128,1152]{1,0:T(8,128)S(1)} %reshape.157, f32[1152]{0:T(1024)} %param.13, f32[128]{0:T(128)S(1)} %add_rsqrt_fusion.1), kind=kOutput, calls=%fused_computation.3 | convolution fusion | flops 1236713472 | bytes 12129280 | tf_op jit(solution)/shard_map/dot_general | solution.py:134
  27.9 1.4 copy.50
  29.3 0.5 all-gather.5.cloned.1.call-update
  30.2 5.4 %copy.93 = bf16[256,8,8,128]{3,2,1,0:T(8,128)(2,1)} copy(bf16[256,8,8,128]{3,1,2,0:T(8,128)(2,1)} %bitcast.88) | data formatting | bytes 8388608
  35.7 3.0 %copy.94 = bf16[256,8,8,128]{3,2,1,0:T(8,128)(2,1)} copy(bf16[256,8,8,128]{3,1,2,0:T(8,128)(2,1)S(1)} %bitcast.89) | data formatting | bytes 8388608
  38.8 0.1 multiply_cosine_fusion
  39.0 4.9 %bitcast_bitcast_fusion.1 = bf16[8,256,8,128,1]{3,2,1,0,4:T(8,128)(2,1)} fusion(bf16[8,256,8,128]{3,2,1,0:T(8,128)(2,1)} %bitcast.87), kind=kLoop, calls=%fused_computation.11 | loop fusion | bytes 8388608 | tf_op jit(solution)/shard_map/reshape | solution.py:64
  43.9 2.3 bitcast_bitcast_fusion
  46.2 16.4 %reduce-scatter.6.cloned.1.call-done = f32[32,4096]{1,0:T(8,128)} async-done(((f32[128,4096]{1,0:T(8,128)}), f32[32,4096]{1,0:T(8,128)}) %reduce-scatter.6.cloned.1.call-update) | async-done | bytes 524304 | tf_op jit(solution)/shard_map/reduce_scatter | solution.py:133
  62.6 1.0 slice_bitcast_fusion
  63.6 0.2 multiply_subtract_fusion
  63.8 0.1 fusion.38
  64.0 9.9 %all_gather.12 = bf16[128,2048]{1,0:T(8,128)(2,1)S(1)} all-gather(bf16[32,2048]{1,0:T(8,128)(2,1)S(1)} %bitcast.98), channel_id=1, replica_groups=mesh['prefill'=4,'prefix'=4,'tensor'=2] {'prefix'}, dimensions={0}, use_global_device_ids=true | all-gather | bytes 655360 | tf_op jit(solution)/shard_map/all_gather | solution.py:142
  73.9 0.3 copy.49
  74.2 35.8 %all-gather.3.cloned.1.call-done = bf16[2048,1024]{0,1:T(8,128)(2,1)} async-done(((bf16[512,1024]{0,1:T(8,128)(2,1)}), bf16[2048,1024]{0,1:T(8,128)(2,1)}) %all-gather.3.cloned.1.call-update) | async-done | bytes 4194320 | tf_op jit(solution)/shard_map/all_gather | solution.py:149
  110.0 11.5 %bitcast_reduce_fusion = (f32[128,8,2]{0,2,1:T(2,128)S(1)}, f32[8,128,2,2048]{3,1,2,0:T(8,128)}) fusion(bf16[128,8,2,128]{0,3,2,1:T(8,128)(2,1)S(1)} %bitcast.99, bf16[2048,8,128,1]{0,2,3,1:T(8,128)(2,1)} %bitcast.103), kind=kOutput, calls=%fused_computation | convolution fusion | flops 1086322688 | bytes 21504000 | tf_op jit(solution)/shard_map/nkgd,mkd->nkgm/dot_general | solution.py:42
  121.5 0.7 copy.88
  122.3 68.3 %all-gather.5.cloned.1.call-done = bf16[2048,1024]{1,0:T(8,128)(2,1)} async-done(((bf16[512,1024]{1,0:T(8,128)(2,1)}), bf16[2048,1024]{1,0:T(8,128)(2,1)}) %all-gather.5.cloned.1.call-update) | async-done | bytes 4194320 | tf_op jit(solution)/shard_map/all_gather | solution.py:150
  190.6 6.5 %copy.53 = bf16[2048,1024]{0,1:T(8,128)(2,1)} copy(bf16[2048,1024]{1,0:T(8,128)(2,1)} %all-gather.5.cloned.1.call-done) | data formatting | bytes 8388608 | tf_op jit(solution)/shard_map/all_gather | solution.py:150
  197.1 10.5 %fusion.6 = f32[8,128,2,128]{1,3,2,0:T(8,128)S(1)} fusion(bf16[2048,8,128,1]{0,2,3,1:T(8,128)(2,1)} %bitcast.90, f32[8,128,2,2048]{3,1,2,0:T(8,128)} %get-tuple-element.14), kind=kOutput, calls=%fused_computation.9 | convolution fusion | flops 1086324736 | bytes 22020096 | tf_op jit(solution)/shard_map/nkgm,mkd->nkgd/dot_general | solution.py:47
  207.6 1.3 copy.54
  209.0 0.2 all-reduce.2.cloned.1.call-start
  209.2 0.9 slice_bitcast_fusion.1
  210.2 0.1 subtract_convert_fusion
  210.4 0.3 fusion.41
  210.7 0.5 copy.60
  211.3 0.5 copy.62
  211.7 1.1 fusion.45
  212.8 0.2 convolution_bitcast_fusion
  213.0 3.7 %fusion.51 = (f32[8,4,8,2]{1,3,2,0:T(2,128)S(1)}, bf16[8,4,8,2,256]{4,1,3,2,0:T(4,128)(2,1)S(1)}) fusion(bf16[8,256,8,128,1]{3,2,1,0,4:T(8,128)(2,1)} %bitcast_bitcast_fusion.1, bf16[8,4,8,2,128]{4,3,2,1,0:T(2,128)(2,1)S(1)} %bitcast.97, pred[8,256]{1,0:T(8,128)(4,1)S(1)} %iota_compare_fusion), kind=kOutput, calls=%fused_computation.66 | convolution fusion | flops 34209280 | bytes 4591616 | tf_op jit(solution)/shard_map/rjkgd,rmkd->rjkgm/dot_general | solution.py:67
  216.8 0.7 fusion.26
  217.4 0.1 copy.63
  217.6 0.2 reshape.167
  217.8 0.2 copy.90
  218.1 0.8 copy.89
  219.0 16.4 %reduce-scatter.8.cloned.1.call-done = f32[32,2048]{1,0:T(8,128)} async-done(((f32[128,2048]{1,0:T(8,128)}), f32[32,2048]{1,0:T(8,128)}) %reduce-scatter.8.cloned.1.call-update) | async-done | bytes 262160 | tf_op jit(solution)/shard_map/reduce_scatter | solution.py:154
  235.4 0.1 div.38
  235.6 1.1 fusion.37
  236.6 10.0 %all_gather.15 = bf16[128,2048]{1,0:T(8,128)(2,1)S(1)} all-gather(bf16[32,2048]{1,0:T(8,128)(2,1)S(1)} %fusion.37), channel_id=1, replica_groups=mesh['prefill'=4,'prefix'=4,'tensor'=2] {'prefix'}, dimensions={0}, use_global_device_ids=true | all-gather | bytes 655360 | tf_op jit(solution)/shard_map/all_gather | solution.py:170
  246.6 4.0 %fusion.52 = f32[128,1152]{1,0:T(8,128)} fusion(bf16[128,2048]{1,0:T(8,128)(2,1)S(1)} %all_gather.15, bf16[2048,1152]{1,0:T(8,128)(2,1)} %param.17), kind=kOutput, calls=%fused_computation.67 | convolution fusion | flops 603979776 | bytes 5832704 | tf_op jit(solution)/shard_map/dot_general | solution.py:169
  250.7 19.0 %all-reduce.2.cloned.1.call-done = f32[128,1152]{1,0:T(8,128)} async-done(((f32[128,1152]{1,0:T(8,128)}), f32[128,1152]{1,0:T(8,128)}) %all-reduce.2.cloned.1.call-update) | async-done | bytes 589840 | tf_op jit(solution)/shard_map/psum | solution.py:174
  269.7 1.2 multiply_reduce_fusion
  270.8 10.1 %psum.23 = f32[128]{0:T(128)S(1)} all-reduce(f32[128]{0:T(128)S(1)} %multiply_reduce_fusion), channel_id=1, replica_groups=mesh['prefill'=4,'prefix'=4,'tensor'=2] {'prefix'}, use_global_device_ids=true, to_apply=%region_10.11 | all-reduce | flops 128 | bytes 1024 | tf_op jit(solution)/shard_map/psum | solution.py:175
  281.0 1.2 add_convert_fusion
  282.2 0.8 reshape.169
  (45 shorter events, 1.4 us)
Async XLA Ops:
  7.4 55.2 %reduce-scatter.6.cloned.1.call-start = ((), (), s32[]{:S(2)}) async-start(), calls=%async_computation.3 | async-start | bytes 2621440 | tf_op jit(solution)/shard_map/reduce_scatter | solution.py:133
  21.0 6.9 %copy-start.3 = (bf16[512,1024]{1,0:T(8,128)(2,1)S(1)}, bf16[512,1024]{1,0:T(8,128)(2,1)}, u32[]{:S(2)}) copy-start(bf16[512,1024]{1,0:T(8,128)(2,1)} %param.19) | copy-start | bytes 3145732
  27.8 2.1 copy-start.5
  27.9 82.1 %all-gather.3.cloned.1.call-start = ((), (), s32[]{:S(2)}) async-start(), calls=%async_computation.4 | async-start | bytes 5242880 | tf_op jit(solution)/shard_map/all_gather | solution.py:149
  29.3 161.3 %all-gather.5.cloned.1.call-start = ((), (), s32[]{:S(2)}) async-start(), calls=%async_computation.5 | async-start | bytes 5242880 | tf_op jit(solution)/shard_map/all_gather | solution.py:150
  29.9 188.3 %reduce-scatter.10.cloned.1.call-start = ((), (), s32[]{:S(2)}) async-start(), calls=%async_computation.8 | async-start | bytes 81920
  30.1 5.5 %copy-start.2 = (bf16[8,256,1024]{2,1,0:T(8,128)(2,1)S(1)}, bf16[8,256,1024]{2,1,0:T(8,128)(2,1)}, u32[]{:S(2)}) copy-start(bf16[8,256,1024]{2,1,0:T(8,128)(2,1)} %param.22) | copy-start | bytes 12582916
  38.7 5.2 %copy-start.1 = (bf16[256,8,8,128]{3,2,1,0:T(8,128)(2,1)S(1)}, bf16[256,8,8,128]{3,2,1,0:T(8,128)(2,1)}, u32[]{:S(2)}) copy-start(bf16[256,8,8,128]{3,2,1,0:T(8,128)(2,1)} %copy.94) | copy-start | bytes 12582916
  122.3 113.2 %reduce-scatter.8.cloned.1.call-start = ((), (), s32[]{:S(2)}) async-start(), calls=%async_computation.6 | async-start | bytes 1310720 | tf_op jit(solution)/shard_map/reduce_scatter | solution.py:154
  209.0 60.7 %all-reduce.2.cloned.1.call-start = ((), (), s32[]{:S(2)}) async-start(), calls=%async_computation.7 | async-start | bytes 1179648 | tf_op jit(solution)/shard_map/psum | solution.py:174
  211.7 5.0 %copy-start = (bf16[8,256,8,128,1]{3,2,1,0,4:T(8,128)(2,1)S(1)}, bf16[8,256,8,128,1]{3,2,1,0,4:T(8,128)(2,1)}, u32[]{:S(2)}) copy-start(bf16[8,256,8,128,1]{3,2,1,0,4:T(8,128)(2,1)} %bitcast_bitcast_fusion) | copy-start | bytes 12582916
  217.8 63.2 %copy-start.4 = (f32[1152]{0:T(1024)S(1)}, f32[1152]{0:T(1024)}, u32[]{:S(2)}) copy-start(f32[1152]{0:T(1024)} %param.18) | copy-start | bytes 13828
Sparse Core Ops, SparseCore 0:
  28.0 34.5 reduce-scatter.5
  122.4 22.1 reduce-scatter.9
  209.1 26.2 reduce-scatter.7
  250.8 18.8 all-reduce.1
Sparse Core Ops, SparseCore 1:
  30.0 80.0 all-gather.2
  111.4 79.1 all-gather.4
where the time goes:
time: 291 us; the launch traced here: 290 us
  waiting for transfers between devices  157 us (54%)
  blocking collectives  41.4 us (14%)
  matrix products  37.7 us (13%)
  local copies, waits for them, and re-layouts  33.6 us (12%)
  between operations  14.8 us (5%)
  other arithmetic  5.66 us (2%)
    all_gather x1, waiting for transfers between devices, per_device(): lax.all_gather(prompt_values, 'prefill', axis=0, tiled=True)  68.3 us
    all_gather x1, waiting for transfers between devices, per_device(): lax.all_gather(prompt_keys, 'prefill', axis=0, tiled=True)  35.8 us
    psum x1, waiting for transfers between devices, per_device(): attended = lax.psum(head_terms, 'tensor')  19 us
    reduce_scatter x1, waiting for transfers between devices, per_device(): lax.psum_scatter(jnp.dot(normed, weights_all, preferred_element_type=jnp....  16.4 us
    reduce_scatter x1, waiting for transfers between devices, per_device(): lax.psum_scatter(summed, 'prefix', scatter_dimension=0, tiled=True)  16.4 us
    unnamed x25, local copies, waits for them, and re-layouts  14.6 us
    dot_general x1, matrix products, shared_attention(): jnp.einsum('nkgd,mkd->nkgm', grouped, key_head_rows, preferred_element_ty...  11.5 us
    psum x1, blocking collectives, per_device(): squares = lax.psum(jnp.sum(signal * signal, axis=1), 'prefix')  11.4 us
  transfers between devices with their start and end apart: 6, of which 5 were waited for; matrix products, arithmetic and copies ran while one was open for 20% of the time, Pallas kernels for 0%

commit v1 on v0

--- a/solution.py
+++ b/solution.py
@@ -1,6 +1,10 @@
+import functools
+
 import jax
 import jax.numpy as jnp
 from jax import lax
+from jax.experimental import pallas as pl
+from jax.experimental.pallas import tpu as pltpu
 from jax.sharding import PartitionSpec as P
 
 MODEL_WIDTH = 4608
@@ -10,6 +14,9 @@
 
 SOFTCAP = 50.0
 EPSILON = 1e-06
+LOG2_E = 1.4426950408889634
+LANES = 128
+VMEM_LIMIT = 32 * 1024 * 1024
 
 
 def apply_rotation(values, token_positions, heads):
@@ -177,9 +184,663 @@
     return (signal + branch).astype(jnp.bfloat16).reshape(group_rows, steps, local_width)
 
 
+def paired(values, axis, mask):
+    size = lax.axis_size(axis)
+    return lax.ppermute(values, axis, [(i, i ^ mask) for i in range(size)])
+
+
+def call(kernel, prefetch, operands, out_shape, in_specs, out_specs, grid, scratch, flops, moved):
+    return pl.pallas_call(
+        kernel,
+        out_shape=out_shape,
+        grid_spec=pltpu.PrefetchScalarGridSpec(
+            num_scalar_prefetch=len(prefetch),
+            grid=grid,
+            in_specs=in_specs,
+            out_specs=out_specs,
+            scratch_shapes=scratch,
+        ),
+        compiler_params=pltpu.CompilerParams(vmem_limit_bytes=VMEM_LIMIT),
+        cost_estimate=pl.CostEstimate(flops=flops, bytes_accessed=moved, transcendentals=0),
+    )(*prefetch, *operands)
+
+
+def whole(array):
+    rank = len(array.shape)
+    return pl.BlockSpec(array.shape, lambda *_: (0,) * rank)
+
+
+def shape(dims, dtype):
+    return jax.ShapeDtypeStruct(dims, dtype)
+
+
+def dot_last(left, right):
+    return lax.dot_general(left, right, (((1,), (1,)), ((), ())), preferred_element_type=jnp.float32)
+
+
+def dot_first(left, right):
+    return lax.dot_general(left, right, (((0,), (0,)), ((), ())), preferred_element_type=jnp.float32)
+
+
+def capped_weight(scores):
+    return jnp.exp2(jnp.tanh(scores * (1.0 / SOFTCAP)) * (SOFTCAP * LOG2_E))
+
+
+def split_rows(rows):
+    high = rows.astype(jnp.bfloat16).astype(jnp.float32)
+    return jnp.concatenate([high, rows - high], axis=0).astype(jnp.bfloat16)
+
+
+def joined_row(block, index):
+    pair = block.astype(jnp.float32)
+    return pair[index : index + 1] + pair[8 + index : 9 + index]
+
+
+def down_rows(row):
+    return jnp.broadcast_to(row, (LANES, row.shape[1])).T
+
+
+def lower_half(tiles):
+    return lax.broadcasted_iota(jnp.int32, tiles.shape, 1) < tiles.shape[1] // 2
+
+
+def interleave(first, second):
+    low = lower_half(first)
+    half = first.shape[1] // 2
+    return (
+        jnp.where(low, first, pltpu.roll(second, half, 1)),
+        jnp.where(low, pltpu.roll(first, half, 1), second),
+    )
+
+
+def rotated(values, cosine, sine):
+    return values * cosine + pltpu.roll(values, HEAD_SIZE // 2, 1) * sine
+
+
+def query_projection_kernel(place, x_ref, gain_ref, w_ref, *refs):
+    *sent, own_ref, squares_ref, scaled = refs
+    step = pl.program_id(0)
+    rows = x_ref.shape[0]
+
+    @pl.when(step == 0)
+    def _():
+        x = x_ref[...].astype(jnp.float32)
+        scaled[...] = (x * gain_ref[...]).astype(jnp.bfloat16)
+        total = jnp.sum(x * x, axis=1, keepdims=True)
+        across = jnp.broadcast_to(total, (rows, LANES)).T[:8]
+        squares_ref[...] = across
+        tail = split_rows(across)
+        for ref in sent:
+            ref[rows:, :] = jnp.zeros((16, ref.shape[1]), jnp.bfloat16)
+            ref[rows:, :rows] = tail
+
+    product = jnp.dot(scaled[...], w_ref[...], preferred_element_type=jnp.float32)
+    for index, ref in enumerate(sent):
+
+        @pl.when(step == index)
+        def _():
+            ref[:rows, :] = product.astype(jnp.bfloat16)
+
+    @pl.when(step == len(sent))
+    def _():
+        own_ref[...] = product
+
+
+def query_projection(place, x, gain, weights, parts):
+    rows, width = x.shape
+    columns = weights.shape[1] // parts
+    return call(
+        query_projection_kernel,
+        (place,),
+        (x, gain, weights),
+        [shape((rows + 16, columns), jnp.bfloat16)] * (parts - 1)
+        + [shape((rows, columns), jnp.float32), shape((8, rows), jnp.float32)],
+        [
+            pl.BlockSpec((rows, width), lambda i, p: (0, 0)),
+            pl.BlockSpec((1, width), lambda i, p: (0, 0)),
+            pl.BlockSpec((width, columns), lambda i, p: (0, p[0] ^ ((i + 1) % parts))),
+        ],
+        [pl.BlockSpec((rows + 16, columns), lambda i, p: (0, 0))] * (parts - 1)
+        + [
+            pl.BlockSpec((rows, columns), lambda i, p: (0, 0)),
+            pl.BlockSpec((8, rows), lambda i, p: (0, 0)),
+        ],
+        (parts,),
+        [pltpu.VMEM((rows, width), jnp.bfloat16)],
+        2 * rows * width * weights.shape[1],
+        2 * width * weights.shape[1],
+    )
+
+
+def pair_projection_kernel(place, x_ref, gain_ref, k_ref, v_ref, *refs):
+    *outs, scaled, product = refs
+    rows = x_ref.shape[0]
+    share = rows // len(outs)
+    step = pl.program_id(0)
+
+    @pl.when(step == 0)
+    def _():
+        scaled[...] = (x_ref[...].astype(jnp.float32) * gain_ref[...]).astype(jnp.bfloat16)
+
+    for half, w_ref in enumerate((k_ref, v_ref)):
+        product[...] = jnp.dot(scaled[...], w_ref[...], preferred_element_type=jnp.float32)
+        for mask, ref in enumerate(outs):
+            first = pl.multiple_of((place[0] ^ mask) * share, share)
+            ref[half] = product[pl.ds(first, share), :].astype(ref.dtype)
+
+
+def pair_projection(place, x, gain, key_weights, value_weights, parts):
+    rows, width = x.shape
+    columns = key_weights.shape[1]
+    block = columns // 2
+    share = rows // parts
+    return call(
+        pair_projection_kernel,
+        (place,),
+        (x, gain, key_weights, value_weights),
+        [shape((2, share, columns), jnp.float32)]
+        + [shape((2, share, columns), jnp.bfloat16)] * (parts - 1),
+        [
+            pl.BlockSpec((rows, width), lambda i, p: (0, 0)),
+            pl.BlockSpec((1, width), lambda i, p: (0, 0)),
+            pl.BlockSpec((width, block), lambda i, p: (0, i)),
+            pl.BlockSpec((width, block), lambda i, p: (0, i)),
+        ],
+        [pl.BlockSpec((2, share, block), lambda i, p: (0, 0, i))] * parts,
+        (2,),
+        [pltpu.VMEM((rows, width), jnp.bfloat16), pltpu.VMEM((rows, block), jnp.float32)],
+        4 * rows * width * columns,
+        4 * width * columns,
+    )
+
+
+def query_rope_kernel(parts, place, own_ref, *refs):
+    received, (squares_ref, cos_ref, sin_ref, query_ref, *rest) = refs[: parts - 1], refs[parts - 1 :]
+    *suffix_refs, inverse_ref, held = rest
+    rows, columns = own_ref.shape
+    squares = squares_ref[0:1, :]
+    total = own_ref[...]
+    for ref in received:
+        squares = squares + joined_row(ref[rows:, :rows], 0)
+        total = total + ref[:rows, :].astype(jnp.float32)
+    inverse = lax.rsqrt(down_rows(squares) / MODEL_WIDTH + EPSILON)
+    inverse_ref[...] = inverse
+    scale = (MODEL_WIDTH // QUERY_HEADS) ** (-0.5)
+    cosine = cos_ref[...] * inverse * scale
+    sine = sin_ref[...] * inverse * scale
+    pair = 2 * HEAD_SIZE
+    for head in range(columns // pair):
+        tiles = []
+        for member in range(2):
+            at = head * pair + member * HEAD_SIZE
+            turned = rotated(total[:, at : at + HEAD_SIZE], cosine, sine)
+            tiles.append(turned.reshape(rows // 8, 8, HEAD_SIZE))
+        even, odd = interleave(*tiles)
+        held[head * 2 * rows : (head + 1) * 2 * rows, :] = jnp.stack([even, odd], axis=1).reshape(
+            2 * rows, HEAD_SIZE
+        )
+    query_ref[...] = held[...].astype(jnp.bfloat16)
+    share = 2 * rows // parts
+    for mask, ref in enumerate(suffix_refs):
+        for head in range(columns // pair):
+            first = pl.multiple_of(head * 2 * rows + (place[0] ^ mask) * share, share)
+            ref[head * share : (head + 1) * share, :] = held[pl.ds(first, share), :].astype(
+                jnp.bfloat16
+            )
+
+
+def query_rope(place, own, received, squares, cosine, sine, parts):
+    rows, columns = own.shape
+    count = rows * columns // HEAD_SIZE
+    operands = (own, *received, squares, cosine, sine)
+    outs = (
+        [shape((count, HEAD_SIZE), jnp.bfloat16)]
+        + [shape((count // parts, HEAD_SIZE), jnp.bfloat16)] * parts
+        + [shape((rows, LANES), jnp.float32)]
+    )
+    return call(
+        functools.partial(query_rope_kernel, parts),
+        (place,),
+        operands,
+        outs,
+        [whole(a) for a in operands],
+        [whole(a) for a in outs],
+        (1,),
+        [pltpu.VMEM((count, HEAD_SIZE), jnp.float32)],
+        10 * rows * columns,
+        12 * rows * columns,
+    )
+
+
+def prompt_kernel(parts, packed, place, q_ref, *refs):
+    keys, values, outs = refs[:parts], refs[parts : 2 * parts], refs[2 * parts :]
+    tokens, columns = keys[0].shape
+    heads = columns // HEAD_SIZE
+    count = q_ref.shape[0] // heads
+    ones = jnp.ones((tokens, LANES), jnp.bfloat16)
+    for head in range(heads):
+        at = slice(head * HEAD_SIZE, (head + 1) * HEAD_SIZE)
+        rows = slice(head * count, (head + 1) * count)
+        query = q_ref[rows, :]
+        total = None
+        for k_ref, v_ref in zip(keys, values):
+            weight = capped_weight(dot_last(query, k_ref[:, at])).astype(jnp.bfloat16)
+            term = jnp.dot(
+                weight,
+                jnp.concatenate([v_ref[:, at], ones], axis=1),
+                preferred_element_type=jnp.float32,
+            )
+            total = term if total is None else total + term
+        outs[0][rows, :] = total[:, :HEAD_SIZE].astype(outs[0].dtype)
+        weight_sum = total[:, HEAD_SIZE:]
+        if packed:
+            held = outs[1]
+            for block in range(count // LANES):
+                held[head * (count // LANES) + block, :] = weight_sum[
+                    block * LANES : (block + 1) * LANES
+                ].T[0]
+        else:
+            outs[1][rows, :] = weight_sum
+    if packed:
+        outs[0][heads * count :, :] = split_rows(outs[1][...])
+
+
+def prompt_attention(place, queries, prompt_keys, keys, prompt_values, values, packed):
+    parts = len(keys) + 1
+    tokens, columns = keys[0].shape
+    count = queries.shape[0]
+    chosen = pl.BlockSpec((tokens, columns), lambda i, p: (0, p[0]))
+    if packed:
+        outs = shape((count + 16, HEAD_SIZE), jnp.bfloat16)
+        out_specs = whole(outs)
+        scratch = [pltpu.VMEM((8, LANES), jnp.float32)]
+    else:
+        outs = [shape((count, HEAD_SIZE), jnp.float32)] * 2
+        out_specs = [whole(a) for a in outs]
+        scratch = []
+    return call(
+        functools.partial(prompt_kernel, parts, packed),
+        (place,),
+        (queries, prompt_keys, *keys, prompt_values, *values),
+        outs,
+        [whole(queries), chosen]
+        + [whole(a) for a in keys]
+        + [chosen]
+        + [whole(a) for a in values],
+        out_specs,
+        (1,),
+        scratch,
+        4 * count * parts * tokens * HEAD_SIZE,
+        4 * parts * tokens * columns,
+    )
+
+
+def suffix_kernel(parts, place, lengths, *refs):
+    queries, refs = refs[:parts], refs[parts:]
+    latest, refs = refs[:parts], refs[parts:]
+    (k_ref, v_ref, inverse_ref, cos_ref, sin_ref), refs = refs[:5], refs[5:]
+    outs, refs = refs[: parts + 1], refs[parts + 1 :]
+    query_held, spread, new_keys, new_values, result, sums, totals, packed = refs
+    member = pl.program_id(0)
+    members = pl.num_programs(0)
+    slots, columns = k_ref.shape[1:]
+    heads = columns // HEAD_SIZE
+    near = heads // parts
+    share = latest[0].shape[1]
+    here = place[0]
+
+    @pl.when(member == 0)
+    def _():
+        spread[...] = jnp.zeros(spread.shape, jnp.float32)
+        packed[...] = jnp.zeros(packed.shape, jnp.float32)
+        for mask in range(parts):
+            query_held[mask] = queries[mask][...].astype(jnp.float32)
+        rows = pl.ds(pl.multiple_of(here * share, share), share)
+        inverse = inverse_ref[rows, :]
+        cosine = cos_ref[rows, :] * inverse
+        sine = sin_ref[rows, :] * inverse
+        for head in range(heads):
+            at = slice(head * HEAD_SIZE, (head + 1) * HEAD_SIZE)
+            key = latest[0][0, :, at]
+            value = latest[0][1, :, at]
+            for ref in latest[1:]:
+                key = key + ref[0, :, at].astype(jnp.float32)
+                value = value + ref[1, :, at].astype(jnp.float32)
+            new_keys[:, at] = rotated(key, cosine, sine)
+            new_values[:, at] = value * inverse
+
+    def places(mask, head):
+        owner = here ^ mask
+        row = pl.ds(pl.multiple_of((owner * near + head) * 8, 8), 8)
+        column = pl.ds(pl.multiple_of((owner * near + head) * HEAD_SIZE, HEAD_SIZE), HEAD_SIZE)
+        local = pl.ds(pl.multiple_of(head * members * 8 + member * 8, 8), 8)
+        return row, column, local
+
+    for mask in range(parts):
+        for head in range(near):
+            row, column, local = places(mask, head)
+            spread[row, column] = query_held[mask, local, :]
+    query = spread[...].astype(jnp.bfloat16)
+    weight = capped_weight(dot_last(k_ref[0], query))
+    valid = lax.broadcasted_iota(jnp.int32, weight.shape, 0) < lengths[here * members + member]
+    weight = jnp.where(valid, weight, 0.0).astype(jnp.bfloat16)
+    tile = pl.ds(pl.multiple_of((member // 2) * 8, 8), 8)
+    new_weight = capped_weight(dot_last(new_keys[tile, :].astype(jnp.bfloat16), query))
+    slot = lax.broadcasted_iota(jnp.int32, new_weight.shape, 0)
+    decode_step = lax.broadcasted_iota(jnp.int32, new_weight.shape, 1) % 4
+    valid = (slot // 4 == member % 2) & (slot % 4 <= decode_step)
+    new_weight = jnp.where(valid, new_weight, 0.0).astype(jnp.bfloat16)
+    result[:, :columns] = dot_first(weight, v_ref[0]) + dot_first(
+        new_weight, new_values[tile, :].astype(jnp.bfloat16)
+    )
+    result[:, columns:] = dot_first(weight, jnp.ones((slots, LANES), jnp.bfloat16)) + dot_first(
+        new_weight, jnp.ones((8, LANES), jnp.bfloat16)
+    )
+    for mask in range(parts):
+        for head in range(near):
+            row, column, local = places(mask, head)
+            sums[mask, local, :] = result[row, column]
+            totals[mask, local, :] = result[row, columns:]
+
+    @pl.when(member == members - 1)
+    def _():
+        count = sums.shape[1]
+        outs[0][...] = sums[0]
+        outs[1][...] = totals[0]
+        for mask in range(1, parts):
+            ref = outs[mask + 1]
+            ref[:count, :] = sums[mask].astype(jnp.bfloat16)
+            packed[0, :] = totals[mask].T[0]
+            ref[count:, :] = split_rows(packed[...])
+
+
+def suffix_attention(
+    place, lengths, queries, latest, cache_keys, cache_values, inverse, cosine, sine
+):
+    parts = len(queries)
+    members, slots, columns = cache_keys.shape
+    count = queries[0].shape[0]
+    share = latest[0].shape[1]
+    spread_rows = 8 * columns // HEAD_SIZE
+    operands = (*queries, *latest, cache_keys, cache_values, inverse, cosine, sine)
+    outs = [shape((count, HEAD_SIZE), jnp.float32)] * 2 + [
+        shape((count + 16, HEAD_SIZE), jnp.bfloat16)
+    ] * (parts - 1)
+    cache = pl.BlockSpec((1, slots, columns), lambda i, p, n: (i, 0, 0))
+    return call(
+        functools.partial(suffix_kernel, parts),
+        (place, lengths),
+        operands,
+        outs,
+        [whole(a) for a in queries]
+        + [whole(a) for a in latest]
+        + [cache, cache, whole(inverse), whole(cosine), whole(sine)],
+        [whole(a) for a in outs],
+        (members,),
+        [
+            pltpu.VMEM((parts, count, HEAD_SIZE), jnp.float32),
+            pltpu.VMEM((spread_rows, columns), jnp.float32),
+            pltpu.VMEM((share, columns), jnp.float32),
+            pltpu.VMEM((share, columns), jnp.float32),
+            pltpu.VMEM((spread_rows, columns + LANES), jnp.float32),
+            pltpu.VMEM((parts, count, HEAD_SIZE), jnp.float32),
+            pltpu.VMEM((parts, count, HEAD_SIZE), jnp.float32),
+            pltpu.VMEM((8, LANES), jnp.float32),
+        ],
+        4 * members * spread_rows * slots * columns,
+        4 * members * slots * columns,
+    )
+
+
+def mix_kernel(parts, far, place, sum_ref, total_ref, *refs):
+    prompt, refs = refs[:far], refs[far:]
+    near_sum, near_total, *suffix = refs[: parts + 1]
+    out_ref, sums, totals = refs[parts + 1 :]
+    count = sum_ref.shape[0]
+    rows = out_ref.shape[0]
+    heads = count // (2 * rows)
+    total = sum_ref[...]
+    for ref in prompt:
+        total = total + ref[:count, :].astype(jnp.float32)
+    sums[...] = total
+    for block in range(count // LANES):
+        at = slice(block * LANES, (block + 1) * LANES)
+        total = total_ref[at, :]
+        for ref in prompt:
+            total = total + down_rows(joined_row(ref[count:, :], block))
+        totals[at, :] = total
+    share = 2 * rows // parts
+    for mask in range(parts):
+        if mask == 0:
+            near, near_weight = near_sum[...], near_total[...]
+        else:
+            ref = suffix[mask - 1]
+            near = ref[: count // parts, :].astype(jnp.float32)
+            near_weight = down_rows(joined_row(ref[count // parts :, :], 0))
+        for head in range(heads):
+            first = pl.multiple_of(head * 2 * rows + (place[0] ^ mask) * share, share)
+            at = pl.ds(first, share)
+            local = slice(head * share, (head + 1) * share)
+            sums[at, :] = sums[at, :] + near[local]
+            totals[at, :] = totals[at, :] + near_weight[local]
+    mixed = sums[...] / totals[...]
+    for head in range(heads):
+        tiles = mixed[head * 2 * rows : (head + 1) * 2 * rows].reshape(rows // 8, 2, 8, HEAD_SIZE)
+        for member, part in enumerate(interleave(tiles[:, 0], tiles[:, 1])):
+            at = (2 * head + member) * HEAD_SIZE
+            out_ref[:, at : at + HEAD_SIZE] = part.reshape(rows, HEAD_SIZE).astype(jnp.bfloat16)
+
+
+def mix(place, sums, totals, prompt, suffix, rows):
+    count = sums.shape[0]
+    operands = (sums, totals, *prompt, *suffix)
+    out = shape((rows, count // rows * HEAD_SIZE), jnp.bfloat16)
+    return call(
+        functools.partial(mix_kernel, len(suffix) - 1, len(prompt)),
+        (place,),
+        operands,
+        out,
+        [whole(a) for a in operands],
+        whole(out),
+        (1,),
+        [pltpu.VMEM((count, HEAD_SIZE), jnp.float32)] * 2,
+        10 * count * HEAD_SIZE,
+        8 * count * HEAD_SIZE,
+    )
+
+
+def output_kernel(masks, started, place, *refs):
+    inputs, refs = refs[: len(masks)], refs[len(masks) :]
+    w_ref, out_ref = refs[0], refs[-1]
+    step = pl.program_id(0)
+    for index, ref in enumerate(inputs):
+
+        @pl.when(step == index)
+        def _():
+            term = jnp.dot(ref[...], w_ref[...], preferred_element_type=jnp.float32)
+            if index > 0:
+                out_ref[...] += term
+            elif started:
+                out_ref[...] = refs[1][...] + term
+            else:
+                out_ref[...] = term
+
+
+def output_projection(place, masks, mixed, weights, started=None):
+    rows, depth = mixed[0].shape
+    width = weights.shape[1]
+    chosen = pl.BlockSpec(
+        (depth, width), lambda i, p: (p[0] ^ (i + masks[0]), 0)
+    )
+    out = shape((rows, width), jnp.float32)
+    more = () if started is None else (started,)
+    return call(
+        functools.partial(output_kernel, masks, started is not None),
+        (place,),
+        (*mixed, weights, *more),
+        out,
+        [whole(a) for a in mixed] + [chosen] + [whole(a) for a in more],
+        whole(out),
+        (len(masks),),
+        [],
+        2 * len(masks) * rows * depth * width,
+        2 * len(masks) * depth * width,
+    )
+
+
+def attended_kernel(place, here_ref, there_ref, out_ref, squares_ref):
+    attended = here_ref[...] + there_ref[...]
+    out_ref[...] = attended
+    total = jnp.sum(attended * attended, axis=1, keepdims=True)
+    squares_ref[...] = jnp.broadcast_to(total, (total.shape[0], LANES)).T[:8]
+
+
+def attended_squares(place, here, there):
+    outs = [shape(here.shape, jnp.float32), shape((8, here.shape[0]), jnp.float32)]
+    return call(
+        attended_kernel,
+        (place,),
+        (here, there),
+        outs,
+        [whole(here), whole(there)],
+        [whole(a) for a in outs],
+        (1,),
+        [],
+        4 * here.size,
+        12 * here.size,
+    )
+
+
+def finish_kernel(place, x_ref, attended_ref, gain_ref, *refs):
+    *squares, out_ref = refs
+    total = squares[0][0:1, :]
+    for ref in squares[1:]:
+        total = total + ref[0:1, :]
+    inverse = lax.rsqrt(down_rows(total) / MODEL_WIDTH + EPSILON)
+    for at in range(0, x_ref.shape[1], LANES):
+        lanes = slice(at, at + LANES)
+        branch = attended_ref[:, lanes] * inverse * gain_ref[:, lanes]
+        out_ref[:, lanes] = (x_ref[:, lanes].astype(jnp.float32) + branch).astype(jnp.bfloat16)
+
+
+def finish(place, x, attended, gain, squares):
+    operands = (x, attended, gain, *squares)
+    out = shape(x.shape, jnp.bfloat16)
+    return call(
+        finish_kernel,
+        (place,),
+        operands,
+        out,
+        [whole(a) for a in operands],
+        whole(out),
+        (1,),
+        [],
+        4 * x.size,
+        8 * x.size,
+    )
+
+
+def by_heads(
+    hidden_in,
+    pre_gain,
+    w_query,
+    key_projection,
+    value_projection,
+    w_out,
+    post_gain,
+    prompt_keys,
+    prompt_values,
+    suffix_key_cache,
+    suffix_value_cache,
+    suffix_len,
+):
+    group_rows, steps, local_width = hidden_in.shape
+    rows = group_rows * steps
+    parts = lax.axis_size("prefix")
+    groups = lax.axis_size("prefill")
+    prompt_total = prompt_keys.shape[0] * groups * parts
+    here = lax.axis_index("prefix")
+    place = here.astype(jnp.int32).reshape(1)
+    x = hidden_in.reshape(rows, local_width)
+    gain = pre_gain.reshape(1, local_width)
+    near = range(1, parts)
+    far = range(1, groups)
+
+    *sent, own, squares = query_projection(place, x, gain, w_query, parts)
+    received = [paired(a, "prefix", m) for m, a in zip(near, sent)]
+
+    columns = prompt_keys.shape[1] // parts
+
+    def spread(cache):
+        return [
+            paired(
+                lax.dynamic_slice_in_dim(cache, (here ^ m) * columns, columns, axis=1), "prefix", m
+            )
+            for m in near
+        ]
+
+    keys = spread(prompt_keys)
+    values = spread(prompt_values)
+
+    positions = (
+        (prompt_total + suffix_len[:, None] + jnp.arange(steps, dtype=jnp.int32)[None, :])
+        .reshape(-1)
+        .astype(jnp.float32)
+    )
+    half = HEAD_SIZE // 2
+    freq = 10000.0 ** (-2.0 * jnp.arange(half, dtype=jnp.float32) / HEAD_SIZE)
+    angle = positions[:, None] * freq[None, :]
+    cosine, sine = jnp.cos(angle), jnp.sin(angle)
+    cosine = jnp.concatenate([cosine, cosine], axis=1)
+    sine = jnp.concatenate([-sine, sine], axis=1)
+
+    own_pair, *sent = pair_projection(place, x, gain, key_projection, value_projection, parts)
+    latest = [own_pair] + [paired(a, "prefix", m) for m, a in zip(near, sent)]
+
+    queries, *split_queries, inverse = query_rope(
+        place, own, received, squares, cosine, sine, parts
+    )
+    far_queries = [paired(queries, "prefill", m) for m in far]
+    suffix_queries = [split_queries[0]] + [
+        paired(a, "prefix", m) for m, a in zip(near, split_queries[1:])
+    ]
+
+    def prompt(chunk, packed):
+        return prompt_attention(place, chunk, prompt_keys, keys, prompt_values, values, packed)
+
+    sums, totals = prompt(queries, False)
+    prompt_results = [paired(prompt(q, True), "prefill", m) for m, q in zip(far, far_queries)]
+    near_sums, near_totals, *sent = suffix_attention(
+        place,
+        suffix_len,
+        suffix_queries,
+        latest,
+        suffix_key_cache,
+        suffix_value_cache,
+        inverse,
+        cosine,
+        sine,
+    )
+    suffix = [near_sums, near_totals] + [paired(a, "prefix", m) for m, a in zip(near, sent)]
+    mixed = mix(place, sums, totals, prompt_results, suffix, rows)
+    others = [paired(mixed, "prefix", m) for m in near]
+    head_terms = output_projection(place, (0,), [mixed], w_out)
+    head_terms = output_projection(place, tuple(near), others, w_out, head_terms)
+    attended, squares = attended_squares(place, head_terms, paired(head_terms, "tensor", 1))
+    squares = [squares] + [paired(squares, "prefix", m) for m in near]
+    out = finish(place, x, attended, post_gain.reshape(1, local_width), squares)
+    return out.reshape(group_rows, steps, local_width)
+
+
+def heads_divide(mesh):
+    sizes = [mesh.shape[name] for name in ("prefill", "prefix", "tensor")]
+    key_heads = QUERY_HEADS // 2 // sizes[2]
+    return key_heads % sizes[1] == 0 and sizes[1] == 4 and sizes[2] == 2 and sizes[0] in (2, 4)
+
+
 def solution(mesh):
     return jax.shard_map(
-        per_device,
+        by_heads if heads_divide(mesh) else per_device,
         mesh=mesh,
         in_specs=(
             P("prefill", None, "prefix"),

time: 291 us -> 93.9 us (0.32)
  waiting for transfers between devices: 157 us -> 20.5 us
  starting transfers between devices: 0.4 us -> 43.4 us
  blocking collectives: 41.4 us -> 0 us
  matrix products: 37.7 us -> 0 us
  local copies, waits for them, and re-layouts: 33.6 us -> 7.84 us
  Pallas kernels: 0 us -> 21.2 us
  between operations: 14.8 us -> 0.23 us
  other arithmetic: 5.66 us -> 0.5 us
    all_gather x2 -> x0, waiting for transfers between devices: 104 us -> none  [the longest x1 68.3 us: per_device(): lax.all_gather(prompt_values, 'prefill', axis=0, tiled=True)]
    ppermute x0 -> x31, starting transfers between devices: none -> 43.4 us  [paired(): return lax.ppermute(values, axis, [(i, i ^ mask) for i in range(size)])]
    dot_general x8 -> x0, matrix products: 37.7 us -> none  [the longest x1 11.5 us: shared_attention(): jnp.einsum('nkgd,mkd->nkgm', grouped, key_head_rows, preferred_element_ty...]
    reduce_scatter x2 -> x0, waiting for transfers between devices: 32.8 us -> none  [the longest x1 16.4 us: per_device(): lax.psum_scatter(jnp.dot(normed, weights_all, preferred_element_type=jnp....]
    psum x2 -> x0, blocking collectives: 21.5 us -> none  [the longest x1 11.4 us: per_device(): squares = lax.psum(jnp.sum(signal * signal, axis=1), 'prefix')]
    pallas_call x0 -> x13, Pallas kernels: none -> 21.2 us  [call(): pl.pallas_call(kernel, out_shape=out_shape, grid_spec=pltpu.PrefetchScala...]
    ppermute x0 -> x31, waiting for transfers between devices: none -> 20.5 us  [paired(): return lax.ppermute(values, axis, [(i, i ^ mask) for i in range(size)])]
    all_gather x2 -> x0, blocking collectives: 19.9 us -> none  [the longest x1 9.98 us: per_device(): lax.all_gather(mixed, 'prefix', axis=0, tiled=True)]
  transfers between devices with their start and end apart: 6 -> 31, of which waited for: 5 -> 15; matrix products, arithmetic and copies ran while one was open for 20% -> 2% of each run, Pallas kernels for 0% -> 18%
where the time goes in v1:
time: 93.9 us; the launch traced here: 93.7 us
  starting transfers between devices  43.4 us (46%)
  Pallas kernels  21.2 us (23%)
  waiting for transfers between devices  20.5 us (22%)
  local copies, waits for them, and re-layouts  7.84 us (8%)
    ppermute x31, starting transfers between devices, paired(): return lax.ppermute(values, axis, [(i, i ^ mask) for i in range(size)])  43.4 us
    pallas_call x13, Pallas kernels, call(): pl.pallas_call(kernel, out_shape=out_shape, grid_spec=pltpu.PrefetchScala...  21.2 us
    ppermute x31, waiting for transfers between devices, paired(): return lax.ppermute(values, axis, [(i, i ^ mask) for i in range(size)])  20.5 us
    unnamed x22, local copies, waits for them, and re-layouts  4.04 us
  transfers between devices with their start and end apart: 31, of which 15 were waited for; matrix products, arithmetic and copies ran while one was open for 2% of the time, Pallas kernels for 18%

profile of v1, /device:TPU:0, one launch (start us, length us, event | category | flops | bytes accessed | tf_op | source)
XLA Modules:
  0.0 93.7 jit_solution(1425641727852286757)
XLA Ops:
  0.0 1.2 %reshape.38.x_ref = bf16[128,1152]{1,0:T(8,128)(2,1)S(1)} reshape(bf16[32,4,1152]{2,1,0:T(4,128)(2,1)} %param.12) | data formatting | bytes 589824 | tf_op jit(solution)/shard_map/reshape | solution.py:764
  1.9 2.3 %copy-done.2 = bf16[1152,2048]{1,0:T(8,128)(2,1)S(1)} copy-done((bf16[1152,2048]{1,0:T(8,128)(2,1)S(1)}, bf16[1152,2048]{1,0:T(8,128)(2,1)}, u32[]{:S(2)}) %copy-start.2) | copy-done | bytes 4718616
  4.2 2.9 %shard_map.118 = (bf16[144,512]{1,0:T(8,128)(2,1)}, bf16[144,512]{1,0:T(8,128)(2,1)}, bf16[144,512]{1,0:T(8,128)(2,1)}, f32[128,512]{1,0:T(8,128)S(1)}, f32[8,128]{1,0:T(8,128)S(1)}) custom-call(s32[1]{0:T(128)} %bitcast.place, bf16[128,1152]{1,0:T(8,128)(2,1)S(1)} %reshape.38.x_ref, f32[1,1152]{1,0:T(1,128)S(1)} %reshape.39.gain_ref, ...), custom_call_target="tpu_custom_call" | custom-call | flops 603979776 | bytes 4718592 | tf_op jit(solution)/shard_map/pallas_call | solution.py:193
  7.1 2.9 %collective-permute-start = (bf16[144,512]{1,0:T(8,128)(2,1)}, bf16[144,512]{1,0:T(8,128)(2,1)S(1)}, u32[]{:S(2)}, u32[]{:S(2)}) collective-permute-start(bf16[144,512]{1,0:T(8,128)(2,1)} %get-tuple-element.30), channel_id=1, source_target_pairs={{0,2},{2,0},{4,6},{6,4},{1,3},{3,1},{5,7},{7,5},{8,10},{10,8},{12,... | collective-permute-start | bytes 442376 | tf_op jit(solution)/shard_map/ppermute | solution.py:189
  10.1 1.5 %collective-permute-start.1 = (bf16[144,512]{1,0:T(8,128)(2,1)}, bf16[144,512]{1,0:T(8,128)(2,1)S(1)}, u32[]{:S(2)}, u32[]{:S(2)}) collective-permute-start(bf16[144,512]{1,0:T(8,128)(2,1)} %get-tuple-element.31), channel_id=1, source_target_pairs={{0,4},{2,6},{4,0},{6,2},{1,5},{3,7},{5,1},{7,3},{8,12},{10,14},{12... | collective-permute-start | bytes 442376 | tf_op jit(solution)/shard_map/ppermute | solution.py:189
  11.6 0.9 constant_dynamic-slice_fusion.3
  12.5 2.0 %collective-permute-start.3 = (bf16[512,256]{1,0:T(8,128)(2,1)}, bf16[512,256]{1,0:T(8,128)(2,1)S(1)}, u32[]{:S(2)}, u32[]{:S(2)}) collective-permute-start(bf16[512,256]{1,0:T(8,128)(2,1)} %get-tuple-element.58), channel_id=1, source_target_pairs={{0,2},{2,0},{4,6},{6,4},{1,3},{3,1},{5,7},{7,5},{8,10},{10,8},{12,... | collective-permute-start | bytes 786440 | tf_op jit(solution)/shard_map/ppermute | solution.py:189
  14.5 1.5 %collective-permute-start.4 = (bf16[512,256]{1,0:T(8,128)(2,1)}, bf16[512,256]{1,0:T(8,128)(2,1)S(1)}, u32[]{:S(2)}, u32[]{:S(2)}) collective-permute-start(bf16[512,256]{1,0:T(8,128)(2,1)} %get-tuple-element.57), channel_id=1, source_target_pairs={{0,4},{2,6},{4,0},{6,2},{1,5},{3,7},{5,1},{7,3},{8,12},{10,14},{12... | collective-permute-start | bytes 786440 | tf_op jit(solution)/shard_map/ppermute | solution.py:189
  16.3 1.6 %collective-permute-start.5 = (bf16[512,256]{1,0:T(8,128)(2,1)}, bf16[512,256]{1,0:T(8,128)(2,1)S(1)}, u32[]{:S(2)}, u32[]{:S(2)}) collective-permute-start(bf16[512,256]{1,0:T(8,128)(2,1)} %get-tuple-element.56), channel_id=1, source_target_pairs={{0,6},{2,4},{4,2},{6,0},{1,7},{3,5},{5,3},{7,1},{8,14},{10,12},{12... | collective-permute-start | bytes 786440 | tf_op jit(solution)/shard_map/ppermute | solution.py:189
  18.0 1.3 %collective-permute-done.1.refs_1_ = bf16[144,512]{1,0:T(8,128)(2,1)S(1)} collective-permute-done((bf16[144,512]{1,0:T(8,128)(2,1)}, bf16[144,512]{1,0:T(8,128)(2,1)S(1)}, u32[]{:S(2)}, u32[]{:S(2)}) %collective-permute-start.1) | collective-permute-done | bytes 147488 | tf_op jit(solution)/shard_map/ppermute | solution.py:189
  19.6 2.0 %collective-permute-start.7 = (bf16[512,256]{1,0:T(8,128)(2,1)S(1)}, bf16[512,256]{1,0:T(8,128)(2,1)S(1)}, u32[]{:S(2)}, u32[]{:S(2)}) collective-permute-start(bf16[512,256]{1,0:T(8,128)(2,1)S(1)} %get-tuple-element.54), channel_id=1, source_target_pairs={{0,4},{2,6},{4,0},{6,2},{1,5},{3,7},{5,1},{7,3},{8,12},{10,14},{12... | collective-permute-start | bytes 786440 | tf_op jit(solution)/shard_map/ppermute | solution.py:189
  21.6 2.6 %collective-permute-done.3.refs_1_ = bf16[512,256]{1,0:T(8,128)(2,1)S(1)} collective-permute-done((bf16[512,256]{1,0:T(8,128)(2,1)}, bf16[512,256]{1,0:T(8,128)(2,1)S(1)}, u32[]{:S(2)}, u32[]{:S(2)}) %collective-permute-start.3) | collective-permute-done | bytes 262176 | tf_op jit(solution)/shard_map/ppermute | solution.py:189
  24.2 2.6 %collective-permute-start.8 = (bf16[512,256]{1,0:T(8,128)(2,1)S(1)}, bf16[512,256]{1,0:T(8,128)(2,1)S(1)}, u32[]{:S(2)}, u32[]{:S(2)}) collective-permute-start(bf16[512,256]{1,0:T(8,128)(2,1)S(1)} %get-tuple-element.53), channel_id=1, source_target_pairs={{0,6},{2,4},{4,2},{6,0},{1,7},{3,5},{5,3},{7,1},{8,14},{10,12},{12... | collective-permute-start | bytes 786440 | tf_op jit(solution)/shard_map/ppermute | solution.py:189
  27.2 1.1 %shard_map.119 = (bf16[512,128]{1,0:T(8,128)(2,1)S(1)}, bf16[128,128]{1,0:T(8,128)(2,1)S(1)}, bf16[128,128]{1,0:T(8,128)(2,1)S(1)}, bf16[128,128]{1,0:T(8,128)(2...) custom-call(s32[1]{0:T(128)} %bitcast.place, f32[128,512]{1,0:T(8,128)S(1)} %get-tuple-element.29.own_ref, ...), custom_call_target="tpu_custom_call" | custom-call | flops 655360 | bytes 786432 | tf_op jit(solution)/shard_map/pallas_call | solution.py:193
  28.3 2.2 %collective-permute-done.4.refs_2_ = bf16[512,256]{1,0:T(8,128)(2,1)S(1)} collective-permute-done((bf16[512,256]{1,0:T(8,128)(2,1)}, bf16[512,256]{1,0:T(8,128)(2,1)S(1)}, u32[]{:S(2)}, u32[]{:S(2)}) %collective-permute-start.4) | collective-permute-done | bytes 262176 | tf_op jit(solution)/shard_map/ppermute | solution.py:189
  30.5 3.3 %collective-permute-start.13 = (bf16[512,128]{1,0:T(8,128)(2,1)S(1)}, bf16[512,128]{1,0:T(8,128)(2,1)S(1)}, u32[]{:S(2)}, u32[]{:S(2)}) collective-permute-start(bf16[512,128]{1,0:T(8,128)(2,1)S(1)} %get-tuple-element.34.q_ref), channel_id=1, source_target_pairs={{0,24},{8,16},{16,8},{24,0},{1,25},{9,17},{17,9},{25,1},{2,26},{10... | collective-permute-start | bytes 393224 | tf_op jit(solution)/shard_map/ppermute | solution.py:189
  33.8 1.7 %copy-done.6 = bf16[1152,1024]{1,0:T(8,128)(2,1)S(1)} copy-done((bf16[1152,1024]{1,0:T(8,128)(2,1)S(1)}, bf16[1152,1024]{1,0:T(8,128)(2,1)}, u32[]{:S(2)}) %copy-start.6) | copy-done | bytes 2359320
  35.5 1.5 %shard_map.124 = (f32[2,32,1024]{2,1,0:T(8,128)S(1)}, bf16[2,32,1024]{2,1,0:T(8,128)(2,1)S(1)}, bf16[2,32,1024]{2,1,0:T(8,128)(2,1)S(1)}, bf16[2,32,1024]{2,1,0:T(8,128)(2,1)S(1)}) custom-call(s32[1]{0:T(128)} %bitcast.place, bf16[128,1152]{1,0:T(8,128)(2,1)S(1)} %reshape.38.x_ref, f32[1,1152]{1,0:T(1,128)S(1)} %reshape.39.gain_ref, ...), custom_call_target="tpu_custom_call" | custom-call | flops 603979776 | bytes 4718592 | tf_op jit(solution)/shard_map/pallas_call | solution.py:193
  37.0 1.3 %collective-permute-start.18 = (bf16[2,32,1024]{2,1,0:T(8,128)(2,1)S(1)}, bf16[2,32,1024]{2,1,0:T(8,128)(2,1)S(1)}, u32[]{:S(2)}, u32[]{:S(2)}) collective-permute-start(bf16[2,32,1024]{2,1,0:T(8,128)(2,1)S(1)} %get-tuple-element.42), channel_id=1, source_target_pairs={{0,2},{2,0},{4,6},{6,4},{1,3},{3,1},{5,7},{7,5},{8,10},{10,8},{12,... | collective-permute-start | bytes 393224 | tf_op jit(solution)/shard_map/ppermute | solution.py:189
  38.3 2.1 %collective-permute-done.7.refs_6_ = bf16[512,256]{1,0:T(8,128)(2,1)S(1)} collective-permute-done((bf16[512,256]{1,0:T(8,128)(2,1)S(1)}, bf16[512,256]{1,0:T(8,128)(2,1)S(1)}, u32[]{:S(2)}, u32[]{:S(2)}) %collective-permute-start.7) | collective-permute-done | bytes 262176 | tf_op jit(solution)/shard_map/ppermute | solution.py:189
  40.3 1.6 %collective-permute-start.9 = (bf16[512,128]{1,0:T(8,128)(2,1)S(1)}, bf16[512,128]{1,0:T(8,128)(2,1)S(1)}, u32[]{:S(2)}, u32[]{:S(2)}) collective-permute-start(bf16[512,128]{1,0:T(8,128)(2,1)S(1)} %get-tuple-element.34.q_ref), channel_id=1, source_target_pairs={{0,8},{8,0},{16,24},{24,16},{1,9},{9,1},{17,25},{25,17},{2,10},{10... | collective-permute-start | bytes 393224 | tf_op jit(solution)/shard_map/ppermute | solution.py:189
  42.1 2.2 %collective-permute-start.19 = (bf16[2,32,1024]{2,1,0:T(8,128)(2,1)S(1)}, bf16[2,32,1024]{2,1,0:T(8,128)(2,1)S(1)}, u32[]{:S(2)}, u32[]{:S(2)}) collective-permute-start(bf16[2,32,1024]{2,1,0:T(8,128)(2,1)S(1)} %get-tuple-element.43), channel_id=1, source_target_pairs={{0,4},{2,6},{4,0},{6,2},{1,5},{3,7},{5,1},{7,3},{8,12},{10,14},{12... | collective-permute-start | bytes 393224 | tf_op jit(solution)/shard_map/ppermute | solution.py:189
  45.1 1.6 %shard_map.123 = bf16[528,128]{1,0:T(8,128)(2,1)S(1)} custom-call(s32[1]{0:T(128)} %bitcast.place, bf16[512,128]{1,0:T(8,128)(2,1)S(1)} %collective-permute-done.13.q_ref, bf16[512,1024]{1,0:T(8,128)(2,1)S(1)} %copy-done, bf16[512,256]{1,0:T(8,128)(2,1)S(1)} %collective-permute-done.3.refs_1_, bf16[512,256]{1,0:T(8,128)(2,1)S(1)} %collective-permute-done.4.refs_2_, ...), custom_call_target="tpu_custom_call" | custom-call | flops 536870912 | bytes 2097152 | tf_op jit(solution)/shard_map/pallas_call | solution.py:193
  46.7 0.8 collective-permute-start.15
  47.5 1.6 %shard_map.122 = bf16[528,128]{1,0:T(8,128)(2,1)S(1)} custom-call(s32[1]{0:T(128)} %bitcast.place, bf16[512,128]{1,0:T(8,128)(2,1)S(1)} %collective-permute-done.11.q_ref, bf16[512,1024]{1,0:T(8,128)(2,1)S(1)} %copy-done, bf16[512,256]{1,0:T(8,128)(2,1)S(1)} %collective-permute-done.3.refs_1_, bf16[512,256]{1,0:T(8,128)(2,1)S(1)} %collective-permute-done.4.refs_2_, ...), custom_call_target="tpu_custom_call" | custom-call | flops 536870912 | bytes 2097152 | tf_op jit(solution)/shard_map/pallas_call | solution.py:193
  49.1 2.0 %collective-permute-start.16 = (bf16[128,128]{1,0:T(8,128)(2,1)S(1)}, bf16[128,128]{1,0:T(8,128)(2,1)S(1)}, u32[]{:S(2)}, u32[]{:S(2)}) collective-permute-start(bf16[128,128]{1,0:T(8,128)(2,1)S(1)} %get-tuple-element.39), channel_id=1, source_target_pairs={{0,4},{2,6},{4,0},{6,2},{1,5},{3,7},{5,1},{7,3},{8,12},{10,14},{12... | collective-permute-start | bytes 98312 | tf_op jit(solution)/shard_map/ppermute | solution.py:189
  51.9 1.6 %shard_map.121 = bf16[528,128]{1,0:T(8,128)(2,1)S(1)} custom-call(s32[1]{0:T(128)} %bitcast.place, bf16[512,128]{1,0:T(8,128)(2,1)S(1)} %collective-permute-done.9.q_ref, bf16[512,1024]{1,0:T(8,128)(2,1)S(1)} %copy-done, bf16[512,256]{1,0:T(8,128)(2,1)S(1)} %collective-permute-done.3.refs_1_, bf16[512,256]{1,0:T(8,128)(2,1)S(1)} %collective-permute-done.4.refs_2_, ...), custom_call_target="tpu_custom_call" | custom-call | flops 536870912 | bytes 2097152 | tf_op jit(solution)/shard_map/pallas_call | solution.py:193
  53.5 3.6 %collective-permute-start.14 = (bf16[528,128]{1,0:T(8,128)(2,1)S(1)}, bf16[528,128]{1,0:T(8,128)(2,1)S(1)}, u32[]{:S(2)}, u32[]{:S(2)}) collective-permute-start(bf16[528,128]{1,0:T(8,128)(2,1)S(1)} %shard_map.123), channel_id=1, source_target_pairs={{0,24},{8,16},{16,8},{24,0},{1,25},{9,17},{17,9},{25,1},{2,26},{10... | collective-permute-start | bytes 405512 | tf_op jit(solution)/shard_map/ppermute | solution.py:189
  57.2 0.8 collective-permute-start.10
  58.0 7.1 %shard_map.125 = (f32[128,128]{1,0:T(8,128)S(1)}, f32[128,128]{1,0:T(8,128)S(1)}, bf16[144,128]{1,0:T(8,128)(2,1)S(1)}, bf16[144,128]{1,0:T(8,128)(2,1)S(1)}, bf16[144,128]{1,0:T(8,128)(2,1)S(1)}) custom-call(s32[1]{0:T(128)} %bitcast.place, s32[32]{0:T(128)S(1)} %copy-done.7, bf16[128,128]{1,0:T(8,128)(2,1)S(1)} %get-tuple-element.37.refs_0_, ...), custom_call_target="tpu_custom_call" | custom-call | flops 536870912 | bytes 8388608 | tf_op jit(solution)/shard_map/pallas_call | solution.py:193
  65.1 0.8 collective-permute-start.21
  65.9 2.0 %collective-permute-start.22 = (bf16[144,128]{1,0:T(8,128)(2,1)S(1)}, bf16[144,128]{1,0:T(8,128)(2,1)S(1)}, u32[]{:S(2)}, u32[]{:S(2)}) collective-permute-start(bf16[144,128]{1,0:T(8,128)(2,1)S(1)} %get-tuple-element.49), channel_id=1, source_target_pairs={{0,4},{2,6},{4,0},{6,2},{1,5},{3,7},{5,1},{7,3},{8,12},{10,14},{12... | collective-permute-start | bytes 110600 | tf_op jit(solution)/shard_map/ppermute | solution.py:189
  67.9 1.2 %collective-permute-done.21.refs_5_ = bf16[144,128]{1,0:T(8,128)(2,1)S(1)} collective-permute-done((bf16[144,128]{1,0:T(8,128)(2,1)S(1)}, bf16[144,128]{1,0:T(8,128)(2,1)S(1)}, u32[]{:S(2)}, u32[]{:S(2)}) %collective-permute-start.21) | collective-permute-done | bytes 36896 | tf_op jit(solution)/shard_map/ppermute | solution.py:189
  69.1 2.2 %collective-permute-start.23 = (bf16[144,128]{1,0:T(8,128)(2,1)S(1)}, bf16[144,128]{1,0:T(8,128)(2,1)S(1)}, u32[]{:S(2)}, u32[]{:S(2)}) collective-permute-start(bf16[144,128]{1,0:T(8,128)(2,1)S(1)} %get-tuple-element.50), channel_id=1, source_target_pairs={{0,6},{2,4},{4,2},{6,0},{1,7},{3,5},{5,3},{7,1},{8,14},{10,12},{12... | collective-permute-start | bytes 110600 | tf_op jit(solution)/shard_map/ppermute | solution.py:189
  71.3 1.5 %shard_map.120 = (f32[512,128]{1,0:T(8,128)S(1)}, f32[512,128]{1,0:T(8,128)S(1)}) custom-call(s32[1]{0:T(128)} %bitcast.place, bf16[512,128]{1,0:T(8,128)(2,1)S(1)} %get-tuple-element.34.q_ref, bf16[512,1024]{1,0:T(8,128)(2,1)S(1)} %copy-done, bf16[512,256]{1,0:T(8,128)(2,1)S(1)} %collective-permute-done.3.refs_1_, ...), custom_call_target="tpu_custom_call" | custom-call | flops 536870912 | bytes 2097152 | tf_op jit(solution)/shard_map/pallas_call | solution.py:193
  72.8 1.5 %collective-permute-done.23.refs_7_ = bf16[144,128]{1,0:T(8,128)(2,1)S(1)} collective-permute-done((bf16[144,128]{1,0:T(8,128)(2,1)S(1)}, bf16[144,128]{1,0:T(8,128)(2,1)S(1)}, u32[]{:S(2)}, u32[]{:S(2)}) %collective-permute-start.23) | collective-permute-done | bytes 36896 | tf_op jit(solution)/shard_map/ppermute | solution.py:189
  74.9 0.9 collective-permute-start.24
  75.7 1.8 %collective-permute-start.25 = (bf16[128,512]{1,0:T(8,128)(2,1)S(1)}, bf16[128,512]{1,0:T(8,128)(2,1)S(1)}, u32[]{:S(2)}, u32[]{:S(2)}) collective-permute-start(bf16[128,512]{1,0:T(8,128)(2,1)S(1)} %shard_map.126.refs_0_), channel_id=1, source_target_pairs={{0,4},{2,6},{4,0},{6,2},{1,5},{3,7},{5,1},{7,3},{8,12},{10,14},{12... | collective-permute-start | bytes 393224 | tf_op jit(solution)/shard_map/ppermute | solution.py:189
  77.5 0.9 collective-permute-start.26
  78.8 1.1 %collective-permute-done.24.refs_0_ = bf16[128,512]{1,0:T(8,128)(2,1)S(1)} collective-permute-done((bf16[128,512]{1,0:T(8,128)(2,1)S(1)}, bf16[128,512]{1,0:T(8,128)(2,1)S(1)}, u32[]{:S(2)}, u32[]{:S(2)}) %collective-permute-start.24) | collective-permute-done | bytes 131104 | tf_op jit(solution)/shard_map/ppermute | solution.py:189
  79.9 1.6 %collective-permute-done.25.refs_1_ = bf16[128,512]{1,0:T(8,128)(2,1)S(1)} collective-permute-done((bf16[128,512]{1,0:T(8,128)(2,1)S(1)}, bf16[128,512]{1,0:T(8,128)(2,1)S(1)}, u32[]{:S(2)}, u32[]{:S(2)}) %collective-permute-start.25) | collective-permute-done | bytes 131104 | tf_op jit(solution)/shard_map/ppermute | solution.py:189
  81.4 1.9 %collective-permute-done.26.refs_2_ = bf16[128,512]{1,0:T(8,128)(2,1)S(1)} collective-permute-done((bf16[128,512]{1,0:T(8,128)(2,1)S(1)}, bf16[128,512]{1,0:T(8,128)(2,1)S(1)}, u32[]{:S(2)}, u32[]{:S(2)}) %collective-permute-start.26) | collective-permute-done | bytes 131104 | tf_op jit(solution)/shard_map/ppermute | solution.py:189
  83.4 1.1 %shard_map.128.here_ref = f32[128,1152]{1,0:T(8,128)S(1)} custom-call(s32[1]{0:T(128)} %bitcast.place, bf16[128,512]{1,0:T(8,128)(2,1)S(1)} %collective-permute-done.24.refs_0_, bf16[128,512]{1,0:T(8,128)(2,1)S(1)} %collective-permute-done.25.refs_1_, bf16[128,512]{1,0:T(8,128)(2,1)S(1)} %collective-permute-done.26.refs_2_, bf16[2048,1152]{1,0:T(8,128)(2,1)S(1)} %bitcast.2, ...), custom_call_target="tpu_custom_call" | custom-call | flops 452984832 | bytes 3538944 | tf_op jit(solution)/shard_map/pallas_call | solution.py:193
  84.6 2.0 %collective-permute-done.27.there_ref = f32[128,1152]{1,0:T(8,128)S(1)} collective-permute-done((f32[128,1152]{1,0:T(8,128)S(1)}, f32[128,1152]{1,0:T(8,128)S(1)}, u32[]{:S(2)}, u32[]{:S(2)}) %collective-permute-start.27) | collective-permute-done | bytes 589856 | tf_op jit(solution)/shard_map/ppermute | solution.py:189
  86.9 1.3 %collective-permute-start.29 = (f32[8,128]{1,0:T(8,128)S(1)}, f32[8,128]{1,0:T(8,128)S(1)}, u32[]{:S(2)}, u32[]{:S(2)}) collective-permute-start(f32[8,128]{1,0:T(8,128)S(1)} %get-tuple-element.52.refs_0_), channel_id=1, source_target_pairs={{0,4},{2,6},{4,0},{6,2},{1,5},{3,7},{5,1},{7,3},{8,12},{10,14},{12... | collective-permute-start | bytes 12296 | tf_op jit(solution)/shard_map/ppermute | solution.py:189
  88.2 2.0 %collective-permute-start.30 = (f32[8,128]{1,0:T(8,128)S(1)}, f32[8,128]{1,0:T(8,128)S(1)}, u32[]{:S(2)}, u32[]{:S(2)}) collective-permute-start(f32[8,128]{1,0:T(8,128)S(1)} %get-tuple-element.52.refs_0_), channel_id=1, source_target_pairs={{0,6},{2,4},{4,2},{6,0},{1,7},{3,5},{5,3},{7,1},{8,14},{10,12},{12... | collective-permute-start | bytes 12296 | tf_op jit(solution)/shard_map/ppermute | solution.py:189
  90.5 2.2 %collective-permute-done.30.refs_3_ = f32[8,128]{1,0:T(8,128)S(1)} collective-permute-done((f32[8,128]{1,0:T(8,128)S(1)}, f32[8,128]{1,0:T(8,128)S(1)}, u32[]{:S(2)}, u32[]{:S(2)}) %collective-permute-start.30) | collective-permute-done | bytes 4128 | tf_op jit(solution)/shard_map/ppermute | solution.py:189
  92.9 0.8 reshape.41
  (62 shorter events, 5.2 us)
Async XLA Ops:
  0.0 11.6 %copy-start = (bf16[512,1024]{1,0:T(8,128)(2,1)S(1)}, bf16[512,1024]{1,0:T(8,128)(2,1)}, u32[]{:S(2)}) copy-start(bf16[512,1024]{1,0:T(8,128)(2,1)} %refs_0_.7) | copy-start | bytes 3145732
  0.0 16.2 %copy-start.1 = (bf16[512,1024]{1,0:T(8,128)(2,1)S(1)}, bf16[512,1024]{1,0:T(8,128)(2,1)}, u32[]{:S(2)}) copy-start(bf16[512,1024]{1,0:T(8,128)(2,1)} %refs_4_.7) | copy-start | bytes 3145732
  1.9 2.3 %copy-start.2 = (bf16[1152,2048]{1,0:T(8,128)(2,1)S(1)}, bf16[1152,2048]{1,0:T(8,128)(2,1)}, u32[]{:S(2)}) copy-start(bf16[1152,2048]{1,0:T(8,128)(2,1)} %w_ref.1) | copy-start | bytes 14155780
  4.2 11.7 %copy-start.7 = (s32[32]{0:T(128)S(1)}, s32[32]{0:T(128)}, u32[]{:S(2)}) copy-start(s32[32]{0:T(128)} %lengths.1) | copy-start | bytes 388
  7.1 9.2 %collective-permute-start = (bf16[144,512]{1,0:T(8,128)(2,1)}, bf16[144,512]{1,0:T(8,128)(2,1)S(1)}, u32[]{:S(2)}, u32[]{:S(2)}) collective-permute-start(bf16[144,512]{1,0:T(8,128)(2,1)} %get-tuple-element.30), channel_id=1, source_target_pairs={{0,2},{2,0},{4,6},{6,4},{1,3},{3,1},{5,7},{7,5},{8,10},{10,8},{12,... | collective-permute-start | bytes 442376 | tf_op jit(solution)/shard_map/ppermute | solution.py:189
  10.1 9.2 %collective-permute-start.1 = (bf16[144,512]{1,0:T(8,128)(2,1)}, bf16[144,512]{1,0:T(8,128)(2,1)S(1)}, u32[]{:S(2)}, u32[]{:S(2)}) collective-permute-start(bf16[144,512]{1,0:T(8,128)(2,1)} %get-tuple-element.31), channel_id=1, source_target_pairs={{0,4},{2,6},{4,0},{6,2},{1,5},{3,7},{5,1},{7,3},{8,12},{10,14},{12... | collective-permute-start | bytes 442376 | tf_op jit(solution)/shard_map/ppermute | solution.py:189
  11.6 8.1 %collective-permute-start.2 = (bf16[144,512]{1,0:T(8,128)(2,1)}, bf16[144,512]{1,0:T(8,128)(2,1)}, u32[]{:S(2)}, u32[]{:S(2)}) collective-permute-start(bf16[144,512]{1,0:T(8,128)(2,1)} %get-tuple-element.32), channel_id=1, source_target_pairs={{0,6},{2,4},{4,2},{6,0},{1,7},{3,5},{5,3},{7,1},{8,14},{10,12},{12... | collective-permute-start | bytes 442376 | tf_op jit(solution)/shard_map/ppermute | solution.py:189
  12.5 11.7 %collective-permute-start.3 = (bf16[512,256]{1,0:T(8,128)(2,1)}, bf16[512,256]{1,0:T(8,128)(2,1)S(1)}, u32[]{:S(2)}, u32[]{:S(2)}) collective-permute-start(bf16[512,256]{1,0:T(8,128)(2,1)} %get-tuple-element.58), channel_id=1, source_target_pairs={{0,2},{2,0},{4,6},{6,4},{1,3},{3,1},{5,7},{7,5},{8,10},{10,8},{12,... | collective-permute-start | bytes 786440 | tf_op jit(solution)/shard_map/ppermute | solution.py:189
  14.5 16.0 %collective-permute-start.4 = (bf16[512,256]{1,0:T(8,128)(2,1)}, bf16[512,256]{1,0:T(8,128)(2,1)S(1)}, u32[]{:S(2)}, u32[]{:S(2)}) collective-permute-start(bf16[512,256]{1,0:T(8,128)(2,1)} %get-tuple-element.57), channel_id=1, source_target_pairs={{0,4},{2,6},{4,0},{6,2},{1,5},{3,7},{5,1},{7,3},{8,12},{10,14},{12... | collective-permute-start | bytes 786440 | tf_op jit(solution)/shard_map/ppermute | solution.py:189
  16.2 17.6 %copy-start.5 = (bf16[1152,1024]{1,0:T(8,128)(2,1)S(1)}, bf16[1152,1024]{1,0:T(8,128)(2,1)}, u32[]{:S(2)}) copy-start(bf16[1152,1024]{1,0:T(8,128)(2,1)} %k_ref.1) | copy-start | bytes 7077892
  16.3 17.5 %collective-permute-start.5 = (bf16[512,256]{1,0:T(8,128)(2,1)}, bf16[512,256]{1,0:T(8,128)(2,1)S(1)}, u32[]{:S(2)}, u32[]{:S(2)}) collective-permute-start(bf16[512,256]{1,0:T(8,128)(2,1)} %get-tuple-element.56), channel_id=1, source_target_pairs={{0,6},{2,4},{4,2},{6,0},{1,7},{3,5},{5,3},{7,1},{8,14},{10,12},{12... | collective-permute-start | bytes 786440 | tf_op jit(solution)/shard_map/ppermute | solution.py:189
  19.2 17.8 %collective-permute-start.6 = (bf16[512,256]{1,0:T(8,128)(2,1)S(1)}, bf16[512,256]{1,0:T(8,128)(2,1)S(1)}, u32[]{:S(2)}, u32[]{:S(2)}) collective-permute-start(bf16[512,256]{1,0:T(8,128)(2,1)S(1)} %get-tuple-element.55), channel_id=1, source_target_pairs={{0,2},{2,0},{4,6},{6,4},{1,3},{3,1},{5,7},{7,5},{8,10},{10,8},{12,... | collective-permute-start | bytes 786440 | tf_op jit(solution)/shard_map/ppermute | solution.py:189
  19.6 20.7 %collective-permute-start.7 = (bf16[512,256]{1,0:T(8,128)(2,1)S(1)}, bf16[512,256]{1,0:T(8,128)(2,1)S(1)}, u32[]{:S(2)}, u32[]{:S(2)}) collective-permute-start(bf16[512,256]{1,0:T(8,128)(2,1)S(1)} %get-tuple-element.54), channel_id=1, source_target_pairs={{0,4},{2,6},{4,0},{6,2},{1,5},{3,7},{5,1},{7,3},{8,12},{10,14},{12... | collective-permute-start | bytes 786440 | tf_op jit(solution)/shard_map/ppermute | solution.py:189
  24.2 17.9 %collective-permute-start.8 = (bf16[512,256]{1,0:T(8,128)(2,1)S(1)}, bf16[512,256]{1,0:T(8,128)(2,1)S(1)}, u32[]{:S(2)}, u32[]{:S(2)}) collective-permute-start(bf16[512,256]{1,0:T(8,128)(2,1)S(1)} %get-tuple-element.53), channel_id=1, source_target_pairs={{0,6},{2,4},{4,2},{6,0},{1,7},{3,5},{5,3},{7,1},{8,14},{10,12},{12... | collective-permute-start | bytes 786440 | tf_op jit(solution)/shard_map/ppermute | solution.py:189
  30.5 13.8 %collective-permute-start.13 = (bf16[512,128]{1,0:T(8,128)(2,1)S(1)}, bf16[512,128]{1,0:T(8,128)(2,1)S(1)}, u32[]{:S(2)}, u32[]{:S(2)}) collective-permute-start(bf16[512,128]{1,0:T(8,128)(2,1)S(1)} %get-tuple-element.34.q_ref), channel_id=1, source_target_pairs={{0,24},{8,16},{16,8},{24,0},{1,25},{9,17},{17,9},{25,1},{2,26},{10... | collective-permute-start | bytes 393224 | tf_op jit(solution)/shard_map/ppermute | solution.py:189
  33.8 12.9 %collective-permute-start.11 = (bf16[512,128]{1,0:T(8,128)(2,1)S(1)}, bf16[512,128]{1,0:T(8,128)(2,1)S(1)}, u32[]{:S(2)}, u32[]{:S(2)}) collective-permute-start(bf16[512,128]{1,0:T(8,128)(2,1)S(1)} %get-tuple-element.34.q_ref), channel_id=1, source_target_pairs={{0,16},{8,24},{16,0},{24,8},{1,17},{9,25},{17,1},{25,9},{2,18},{10... | collective-permute-start | bytes 393224 | tf_op jit(solution)/shard_map/ppermute | solution.py:189
  33.8 1.7 %copy-start.6 = (bf16[1152,1024]{1,0:T(8,128)(2,1)S(1)}, bf16[1152,1024]{1,0:T(8,128)(2,1)}, u32[]{:S(2)}) copy-start(bf16[1152,1024]{1,0:T(8,128)(2,1)} %v_ref.1) | copy-start | bytes 7077892
  37.0 12.1 %collective-permute-start.18 = (bf16[2,32,1024]{2,1,0:T(8,128)(2,1)S(1)}, bf16[2,32,1024]{2,1,0:T(8,128)(2,1)S(1)}, u32[]{:S(2)}, u32[]{:S(2)}) collective-permute-start(bf16[2,32,1024]{2,1,0:T(8,128)(2,1)S(1)} %get-tuple-element.42), channel_id=1, source_target_pairs={{0,2},{2,0},{4,6},{6,4},{1,3},{3,1},{5,7},{7,5},{8,10},{10,8},{12,... | collective-permute-start | bytes 393224 | tf_op jit(solution)/shard_map/ppermute | solution.py:189
  40.3 10.8 %collective-permute-start.9 = (bf16[512,128]{1,0:T(8,128)(2,1)S(1)}, bf16[512,128]{1,0:T(8,128)(2,1)S(1)}, u32[]{:S(2)}, u32[]{:S(2)}) collective-permute-start(bf16[512,128]{1,0:T(8,128)(2,1)S(1)} %get-tuple-element.34.q_ref), channel_id=1, source_target_pairs={{0,8},{8,0},{16,24},{24,16},{1,9},{9,1},{17,25},{25,17},{2,10},{10... | collective-permute-start | bytes 393224 | tf_op jit(solution)/shard_map/ppermute | solution.py:189
  42.1 11.4 %collective-permute-start.19 = (bf16[2,32,1024]{2,1,0:T(8,128)(2,1)S(1)}, bf16[2,32,1024]{2,1,0:T(8,128)(2,1)S(1)}, u32[]{:S(2)}, u32[]{:S(2)}) collective-permute-start(bf16[2,32,1024]{2,1,0:T(8,128)(2,1)S(1)} %get-tuple-element.43), channel_id=1, source_target_pairs={{0,4},{2,6},{4,0},{6,2},{1,5},{3,7},{5,1},{7,3},{8,12},{10,14},{12... | collective-permute-start | bytes 393224 | tf_op jit(solution)/shard_map/ppermute | solution.py:189
  44.3 12.8 %collective-permute-start.20 = (bf16[2,32,1024]{2,1,0:T(8,128)(2,1)S(1)}, bf16[2,32,1024]{2,1,0:T(8,128)(2,1)S(1)}, u32[]{:S(2)}, u32[]{:S(2)}) collective-permute-start(bf16[2,32,1024]{2,1,0:T(8,128)(2,1)S(1)} %get-tuple-element.44), channel_id=1, source_target_pairs={{0,6},{2,4},{4,2},{6,0},{1,7},{3,5},{5,3},{7,1},{8,14},{10,12},{12... | collective-permute-start | bytes 393224 | tf_op jit(solution)/shard_map/ppermute | solution.py:189
  45.1 12.8 %copy-start.4 = (bf16[8,256,1024]{2,1,0:T(8,128)(2,1)S(1)}, bf16[8,256,1024]{2,1,0:T(8,128)(2,1)}, u32[]{:S(2)}) copy-start(bf16[8,256,1024]{2,1,0:T(8,128)(2,1)} %refs_9_.1) | copy-start | bytes 12582916
  46.7 11.3 %copy-start.3 = (bf16[8,256,1024]{2,1,0:T(8,128)(2,1)S(1)}, bf16[8,256,1024]{2,1,0:T(8,128)(2,1)}, u32[]{:S(2)}) copy-start(bf16[8,256,1024]{2,1,0:T(8,128)(2,1)} %refs_8_.1) | copy-start | bytes 12582916
  46.7 10.4 %collective-permute-start.15 = (bf16[128,128]{1,0:T(8,128)(2,1)S(1)}, bf16[128,128]{1,0:T(8,128)(2,1)S(1)}, u32[]{:S(2)}, u32[]{:S(2)}) collective-permute-start(bf16[128,128]{1,0:T(8,128)(2,1)S(1)} %get-tuple-element.38), channel_id=1, source_target_pairs={{0,2},{2,0},{4,6},{6,4},{1,3},{3,1},{5,7},{7,5},{8,10},{10,8},{12,... | collective-permute-start | bytes 98312 | tf_op jit(solution)/shard_map/ppermute | solution.py:189
  49.1 8.8 %collective-permute-start.16 = (bf16[128,128]{1,0:T(8,128)(2,1)S(1)}, bf16[128,128]{1,0:T(8,128)(2,1)S(1)}, u32[]{:S(2)}, u32[]{:S(2)}) collective-permute-start(bf16[128,128]{1,0:T(8,128)(2,1)S(1)} %get-tuple-element.39), channel_id=1, source_target_pairs={{0,4},{2,6},{4,0},{6,2},{1,5},{3,7},{5,1},{7,3},{8,12},{10,14},{12... | collective-permute-start | bytes 98312 | tf_op jit(solution)/shard_map/ppermute | solution.py:189
  51.1 6.8 %collective-permute-start.17 = (bf16[128,128]{1,0:T(8,128)(2,1)S(1)}, bf16[128,128]{1,0:T(8,128)(2,1)S(1)}, u32[]{:S(2)}, u32[]{:S(2)}) collective-permute-start(bf16[128,128]{1,0:T(8,128)(2,1)S(1)} %get-tuple-element.40), channel_id=1, source_target_pairs={{0,6},{2,4},{4,2},{6,0},{1,7},{3,5},{5,3},{7,1},{8,14},{10,12},{12... | collective-permute-start | bytes 98312 | tf_op jit(solution)/shard_map/ppermute | solution.py:189
  53.5 20.9 %collective-permute-start.14 = (bf16[528,128]{1,0:T(8,128)(2,1)S(1)}, bf16[528,128]{1,0:T(8,128)(2,1)S(1)}, u32[]{:S(2)}, u32[]{:S(2)}) collective-permute-start(bf16[528,128]{1,0:T(8,128)(2,1)S(1)} %shard_map.123), channel_id=1, source_target_pairs={{0,24},{8,16},{16,8},{24,0},{1,25},{9,17},{17,9},{25,1},{2,26},{10... | collective-permute-start | bytes 405512 | tf_op jit(solution)/shard_map/ppermute | solution.py:189
  57.1 17.3 %collective-permute-start.12 = (bf16[528,128]{1,0:T(8,128)(2,1)S(1)}, bf16[528,128]{1,0:T(8,128)(2,1)S(1)}, u32[]{:S(2)}, u32[]{:S(2)}) collective-permute-start(bf16[528,128]{1,0:T(8,128)(2,1)S(1)} %shard_map.122), channel_id=1, source_target_pairs={{0,16},{8,24},{16,0},{24,8},{1,17},{9,25},{17,1},{25,9},{2,18},{10... | collective-permute-start | bytes 405512 | tf_op jit(solution)/shard_map/ppermute | solution.py:189
  57.2 17.2 %collective-permute-start.10 = (bf16[528,128]{1,0:T(8,128)(2,1)S(1)}, bf16[528,128]{1,0:T(8,128)(2,1)S(1)}, u32[]{:S(2)}, u32[]{:S(2)}) collective-permute-start(bf16[528,128]{1,0:T(8,128)(2,1)S(1)} %shard_map.121), channel_id=1, source_target_pairs={{0,8},{8,0},{16,24},{24,16},{1,9},{9,1},{17,25},{25,17},{2,10},{10... | collective-permute-start | bytes 405512 | tf_op jit(solution)/shard_map/ppermute | solution.py:189
  57.9 20.5 %slice-start = ((s8[4718592]{0:T(1024)(128)(4,1)}), s8[4194304]{0:T(1024)(128)(4,1)S(1)}, s32[]{:S(2)}) async-start(s8[4718592]{0:T(1024)(128)(4,1)} %bitcast.1), calls=%async_computation | async-start | bytes 8388608
  58.0 20.4 %slice-start.1 = ((s8[4718592]{0:T(1024)(128)(4,1)}), s8[524288]{0:T(1024)(128)(4,1)S(1)}, s32[]{:S(2)}) async-start(s8[4718592]{0:T(1024)(128)(4,1)} %bitcast.1), calls=%async_computation.1 | async-start | bytes 1048576
  65.1 4.0 %collective-permute-start.21 = (bf16[144,128]{1,0:T(8,128)(2,1)S(1)}, bf16[144,128]{1,0:T(8,128)(2,1)S(1)}, u32[]{:S(2)}, u32[]{:S(2)}) collective-permute-start(bf16[144,128]{1,0:T(8,128)(2,1)S(1)} %get-tuple-element.48), channel_id=1, source_target_pairs={{0,2},{2,0},{4,6},{6,4},{1,3},{3,1},{5,7},{7,5},{8,10},{10,8},{12,... | collective-permute-start | bytes 110600 | tf_op jit(solution)/shard_map/ppermute | solution.py:189
  65.9 6.9 %collective-permute-start.22 = (bf16[144,128]{1,0:T(8,128)(2,1)S(1)}, bf16[144,128]{1,0:T(8,128)(2,1)S(1)}, u32[]{:S(2)}, u32[]{:S(2)}) collective-permute-start(bf16[144,128]{1,0:T(8,128)(2,1)S(1)} %get-tuple-element.49), channel_id=1, source_target_pairs={{0,4},{2,6},{4,0},{6,2},{1,5},{3,7},{5,1},{7,3},{8,12},{10,14},{12... | collective-permute-start | bytes 110600 | tf_op jit(solution)/shard_map/ppermute | solution.py:189
  69.1 5.3 %collective-permute-start.23 = (bf16[144,128]{1,0:T(8,128)(2,1)S(1)}, bf16[144,128]{1,0:T(8,128)(2,1)S(1)}, u32[]{:S(2)}, u32[]{:S(2)}) collective-permute-start(bf16[144,128]{1,0:T(8,128)(2,1)S(1)} %get-tuple-element.50), channel_id=1, source_target_pairs={{0,6},{2,4},{4,2},{6,0},{1,7},{3,5},{5,3},{7,1},{8,14},{10,12},{12... | collective-permute-start | bytes 110600 | tf_op jit(solution)/shard_map/ppermute | solution.py:189
  74.9 5.0 %collective-permute-start.24 = (bf16[128,512]{1,0:T(8,128)(2,1)S(1)}, bf16[128,512]{1,0:T(8,128)(2,1)S(1)}, u32[]{:S(2)}, u32[]{:S(2)}) collective-permute-start(bf16[128,512]{1,0:T(8,128)(2,1)S(1)} %shard_map.126.refs_0_), channel_id=1, source_target_pairs={{0,2},{2,0},{4,6},{6,4},{1,3},{3,1},{5,7},{7,5},{8,10},{10,8},{12,... | collective-permute-start | bytes 393224 | tf_op jit(solution)/shard_map/ppermute | solution.py:189
  75.7 5.7 %collective-permute-start.25 = (bf16[128,512]{1,0:T(8,128)(2,1)S(1)}, bf16[128,512]{1,0:T(8,128)(2,1)S(1)}, u32[]{:S(2)}, u32[]{:S(2)}) collective-permute-start(bf16[128,512]{1,0:T(8,128)(2,1)S(1)} %shard_map.126.refs_0_), channel_id=1, source_target_pairs={{0,4},{2,6},{4,0},{6,2},{1,5},{3,7},{5,1},{7,3},{8,12},{10,14},{12... | collective-permute-start | bytes 393224 | tf_op jit(solution)/shard_map/ppermute | solution.py:189
  77.5 5.9 %collective-permute-start.26 = (bf16[128,512]{1,0:T(8,128)(2,1)S(1)}, bf16[128,512]{1,0:T(8,128)(2,1)S(1)}, u32[]{:S(2)}, u32[]{:S(2)}) collective-permute-start(bf16[128,512]{1,0:T(8,128)(2,1)S(1)} %shard_map.126.refs_0_), channel_id=1, source_target_pairs={{0,6},{2,4},{4,2},{6,0},{1,7},{3,5},{5,3},{7,1},{8,14},{10,12},{12... | collective-permute-start | bytes 393224 | tf_op jit(solution)/shard_map/ppermute | solution.py:189
  78.8 11.5 %copy-start.8 = (f32[1152]{0:T(1024)S(1)}, f32[1152]{0:T(1024)}, u32[]{:S(2)}) copy-start(f32[1152]{0:T(1024)} %param.18) | copy-start | bytes 13828
  84.5 2.1 %collective-permute-start.27 = (f32[128,1152]{1,0:T(8,128)S(1)}, f32[128,1152]{1,0:T(8,128)S(1)}, u32[]{:S(2)}, u32[]{:S(2)}) collective-permute-start(f32[128,1152]{1,0:T(8,128)S(1)} %shard_map.128.here_ref), channel_id=1, source_target_pairs={{0,1},{1,0},{2,3},{3,2},{4,5},{5,4},{6,7},{7,6},{8,9},{9,8},{10,11... | collective-permute-start | bytes 1769480 | tf_op jit(solution)/shard_map/ppermute | solution.py:189
  86.7 3.6 %collective-permute-start.28 = (f32[8,128]{1,0:T(8,128)S(1)}, f32[8,128]{1,0:T(8,128)S(1)}, u32[]{:S(2)}, u32[]{:S(2)}) collective-permute-start(f32[8,128]{1,0:T(8,128)S(1)} %get-tuple-element.52.refs_0_), channel_id=1, source_target_pairs={{0,2},{2,0},{4,6},{6,4},{1,3},{3,1},{5,7},{7,5},{8,10},{10,8},{12,... | collective-permute-start | bytes 12296 | tf_op jit(solution)/shard_map/ppermute | solution.py:189
  86.9 3.6 %collective-permute-start.29 = (f32[8,128]{1,0:T(8,128)S(1)}, f32[8,128]{1,0:T(8,128)S(1)}, u32[]{:S(2)}, u32[]{:S(2)}) collective-permute-start(f32[8,128]{1,0:T(8,128)S(1)} %get-tuple-element.52.refs_0_), channel_id=1, source_target_pairs={{0,4},{2,6},{4,0},{6,2},{1,5},{3,7},{5,1},{7,3},{8,12},{10,14},{12... | collective-permute-start | bytes 12296 | tf_op jit(solution)/shard_map/ppermute | solution.py:189
  88.2 4.5 %collective-permute-start.30 = (f32[8,128]{1,0:T(8,128)S(1)}, f32[8,128]{1,0:T(8,128)S(1)}, u32[]{:S(2)}, u32[]{:S(2)}) collective-permute-start(f32[8,128]{1,0:T(8,128)S(1)} %get-tuple-element.52.refs_0_), channel_id=1, source_target_pairs={{0,6},{2,4},{4,2},{6,0},{1,7},{3,5},{5,3},{7,1},{8,14},{10,12},{12... | collective-permute-start | bytes 12296 | tf_op jit(solution)/shard_map/ppermute | solution.py:189

commit v2 on v1

--- a/solution.py
+++ b/solution.py
@@ -17,6 +17,7 @@
 LOG2_E = 1.4426950408889634
 LANES = 128
 VMEM_LIMIT = 32 * 1024 * 1024
+LARGE_VMEM_LIMIT = 60 * 1024 * 1024
 
 
 def apply_rotation(values, token_positions, heads):
@@ -189,7 +190,19 @@
     return lax.ppermute(values, axis, [(i, i ^ mask) for i in range(size)])
 
 
-def call(kernel, prefetch, operands, out_shape, in_specs, out_specs, grid, scratch, flops, moved):
+def call(
+    kernel,
+    prefetch,
+    operands,
+    out_shape,
+    in_specs,
+    out_specs,
+    grid,
+    scratch,
+    flops,
+    moved,
+    limit=VMEM_LIMIT,
+):
     return pl.pallas_call(
         kernel,
         out_shape=out_shape,
@@ -200,7 +213,7 @@
             out_specs=out_specs,
             scratch_shapes=scratch,
         ),
-        compiler_params=pltpu.CompilerParams(vmem_limit_bytes=VMEM_LIMIT),
+        compiler_params=pltpu.CompilerParams(vmem_limit_bytes=limit),
         cost_estimate=pl.CostEstimate(flops=flops, bytes_accessed=moved, transcendentals=0),
     )(*prefetch, *operands)
 
@@ -208,6 +221,13 @@
 def whole(array):
     rank = len(array.shape)
     return pl.BlockSpec(array.shape, lambda *_: (0,) * rank)
+
+
+def corner(array):
+    rank = len(array.shape)
+    return pl.BlockSpec(
+        (1,) * (rank - 2) + (32 // array.dtype.itemsize, LANES), lambda *_: (0,) * rank
+    )
 
 
 def shape(dims, dtype):
@@ -257,15 +277,24 @@
     return values * cosine + pltpu.roll(values, HEAD_SIZE // 2, 1) * sine
 
 
+def flat_rows(ref):
+    members, steps, width = ref.shape
+    return ref[...].astype(jnp.float32).reshape(members * steps, width)
+
+
+def gain_row(ref):
+    return ref[...].reshape(1, ref.shape[0])
+
+
 def query_projection_kernel(place, x_ref, gain_ref, w_ref, *refs):
-    *sent, own_ref, squares_ref, scaled = refs
+    *sent, own_ref, squares_ref, scaled_ref = refs
     step = pl.program_id(0)
-    rows = x_ref.shape[0]
+    rows = scaled_ref.shape[0]
 
     @pl.when(step == 0)
     def _():
-        x = x_ref[...].astype(jnp.float32)
-        scaled[...] = (x * gain_ref[...]).astype(jnp.bfloat16)
+        x = flat_rows(x_ref)
+        scaled_ref[...] = (x * gain_row(gain_ref)).astype(jnp.bfloat16)
         total = jnp.sum(x * x, axis=1, keepdims=True)
         across = jnp.broadcast_to(total, (rows, LANES)).T[:8]
         squares_ref[...] = across
@@ -274,7 +303,7 @@
             ref[rows:, :] = jnp.zeros((16, ref.shape[1]), jnp.bfloat16)
             ref[rows:, :rows] = tail
 
-    product = jnp.dot(scaled[...], w_ref[...], preferred_element_type=jnp.float32)
+    product = jnp.dot(scaled_ref[...], w_ref[...], preferred_element_type=jnp.float32)
     for index, ref in enumerate(sent):
 
         @pl.when(step == index)
@@ -287,70 +316,114 @@
 
 
 def query_projection(place, x, gain, weights, parts):
-    rows, width = x.shape
+    members, steps, width = x.shape
+    rows = members * steps
     columns = weights.shape[1] // parts
+    outs = [shape((rows + 16, columns), jnp.bfloat16)] * (parts - 1) + [
+        shape((rows, columns), jnp.float32),
+        shape((8, rows), jnp.float32),
+        shape((rows, width), jnp.bfloat16),
+    ]
     return call(
         query_projection_kernel,
         (place,),
         (x, gain, weights),
-        [shape((rows + 16, columns), jnp.bfloat16)] * (parts - 1)
-        + [shape((rows, columns), jnp.float32), shape((8, rows), jnp.float32)],
+        outs,
         [
-            pl.BlockSpec((rows, width), lambda i, p: (0, 0)),
-            pl.BlockSpec((1, width), lambda i, p: (0, 0)),
+            whole(x),
+            whole(gain),
             pl.BlockSpec((width, columns), lambda i, p: (0, p[0] ^ ((i + 1) % parts))),
         ],
-        [pl.BlockSpec((rows + 16, columns), lambda i, p: (0, 0))] * (parts - 1)
-        + [
-            pl.BlockSpec((rows, columns), lambda i, p: (0, 0)),
-            pl.BlockSpec((8, rows), lambda i, p: (0, 0)),
-        ],
+        [whole(a) for a in outs],
         (parts,),
-        [pltpu.VMEM((rows, width), jnp.bfloat16)],
+        [],
         2 * rows * width * weights.shape[1],
         2 * width * weights.shape[1],
-    )
-
-
-def pair_projection_kernel(place, x_ref, gain_ref, k_ref, v_ref, *refs):
-    *outs, scaled, product = refs
-    rows = x_ref.shape[0]
-    share = rows // len(outs)
+        LARGE_VMEM_LIMIT,
+    )
+
+
+def cache_columns_kernel(place, k_ref, v_ref, token_ref, *outs):
     step = pl.program_id(0)
-
-    @pl.when(step == 0)
+    width = k_ref.shape[1]
+    for index, ref in enumerate(outs):
+
+        @pl.when(step == index)
+        def _():
+            ref[:, :width] = k_ref[...]
+            ref[:, width:] = v_ref[...]
+
+
+def cache_columns(place, keys, values, head, heads, parts, token):
+    tokens = keys.shape[0]
+    chosen = pl.BlockSpec(
+        (tokens, HEAD_SIZE), lambda i, p: (0, (p[0] ^ (i + 1)) * heads + head)
+    )
+    outs = [shape((tokens, 2 * HEAD_SIZE), jnp.bfloat16)] * (parts - 1)
+    return call(
+        cache_columns_kernel,
+        (place,),
+        (keys, values, token),
+        outs,
+        [chosen, chosen, corner(token)],
+        [whole(a) for a in outs],
+        (parts - 1,),
+        [],
+        0,
+        8 * (parts - 1) * tokens * HEAD_SIZE,
+    )
+
+
+def pair_projection_kernel(place, scaled_ref, k_ref, v_ref, *refs):
+    parts = len(refs) // 2 + 1
+    queries, (own_ref, *outs) = refs[: parts - 1], refs[parts - 1 :]
+    rows = scaled_ref.shape[0]
+    columns = k_ref.shape[1]
+    step = pl.program_id(0)
+    terms = [
+        jnp.dot(scaled_ref[...], w_ref[...], preferred_element_type=jnp.float32)
+        for w_ref in (k_ref, v_ref)
+    ]
+
+    def store(ref):
+        for index, term in enumerate(terms):
+            ref[:rows, index * columns : (index + 1) * columns] = term.astype(ref.dtype)
+
+    for index, (query_ref, ref) in enumerate(zip(queries, outs)):
+
+        @pl.when(step == index)
+        def _():
+            store(ref)
+            tall = ref.shape[0] - rows
+            for piece in range(query_ref.shape[0] // tall):
+                at = slice(piece * HEAD_SIZE, (piece + 1) * HEAD_SIZE)
+                ref[rows:, at] = query_ref[piece * tall : (piece + 1) * tall, :]
+
+    @pl.when(step == parts - 1)
     def _():
-        scaled[...] = (x_ref[...].astype(jnp.float32) * gain_ref[...]).astype(jnp.bfloat16)
-
-    for half, w_ref in enumerate((k_ref, v_ref)):
-        product[...] = jnp.dot(scaled[...], w_ref[...], preferred_element_type=jnp.float32)
-        for mask, ref in enumerate(outs):
-            first = pl.multiple_of((place[0] ^ mask) * share, share)
-            ref[half] = product[pl.ds(first, share), :].astype(ref.dtype)
-
-
-def pair_projection(place, x, gain, key_weights, value_weights, parts):
-    rows, width = x.shape
-    columns = key_weights.shape[1]
-    block = columns // 2
-    share = rows // parts
+        store(own_ref)
+
+
+def pair_projection(place, scaled, key_weights, value_weights, queries):
+    parts = len(queries) + 1
+    rows, width = scaled.shape
+    columns = key_weights.shape[1] // parts
+    tall = queries[0].shape[0] * HEAD_SIZE // (2 * columns)
+    chosen = pl.BlockSpec((width, columns), lambda i, p: (0, p[0] ^ ((i + 1) % parts)))
+    outs = [shape((rows, 2 * columns), jnp.float32)] + [
+        shape((rows + tall, 2 * columns), jnp.bfloat16)
+    ] * (parts - 1)
     return call(
         pair_projection_kernel,
         (place,),
-        (x, gain, key_weights, value_weights),
-        [shape((2, share, columns), jnp.float32)]
-        + [shape((2, share, columns), jnp.bfloat16)] * (parts - 1),
-        [
-            pl.BlockSpec((rows, width), lambda i, p: (0, 0)),
-            pl.BlockSpec((1, width), lambda i, p: (0, 0)),
-            pl.BlockSpec((width, block), lambda i, p: (0, i)),
-            pl.BlockSpec((width, block), lambda i, p: (0, i)),
-        ],
-        [pl.BlockSpec((2, share, block), lambda i, p: (0, 0, i))] * parts,
-        (2,),
-        [pltpu.VMEM((rows, width), jnp.bfloat16), pltpu.VMEM((rows, block), jnp.float32)],
-        4 * rows * width * columns,
-        4 * width * columns,
+        (scaled, key_weights, value_weights, *queries),
+        outs,
+        [whole(scaled), chosen, chosen] + [whole(a) for a in queries],
+        [whole(a) for a in outs],
+        (parts,),
+        [],
+        4 * rows * width * key_weights.shape[1],
+        4 * width * key_weights.shape[1],
     )
 
 
@@ -412,102 +485,197 @@
     )
 
 
-def prompt_kernel(parts, packed, place, q_ref, *refs):
-    keys, values, outs = refs[:parts], refs[parts : 2 * parts], refs[2 * parts :]
-    tokens, columns = keys[0].shape
-    heads = columns // HEAD_SIZE
-    count = q_ref.shape[0] // heads
-    ones = jnp.ones((tokens, LANES), jnp.bfloat16)
+def attend(query, pairs):
+    result = None
+    for key, value in pairs:
+        weight = capped_weight(dot_last(query, key)).astype(jnp.bfloat16)
+        ones = jnp.ones((value.shape[0], LANES), jnp.bfloat16)
+        term = jnp.dot(
+            weight, jnp.concatenate([value, ones], axis=1), preferred_element_type=jnp.float32
+        )
+        result = term if result is None else result + term
+    return result
+
+
+def cached_pairs(k_ref, v_ref, received):
+    return [(k_ref[...], v_ref[...])] + [
+        (ref[:, :HEAD_SIZE], ref[:, HEAD_SIZE:]) for ref in received
+    ]
+
+
+def total_rows(totals):
+    return [
+        totals[at : at + LANES].T[0:1] for at in range(0, totals.shape[0], LANES)
+    ]
+
+
+def prompt_first_kernel(chunks, place, *refs):
+    queries, refs = refs[:chunks], refs[chunks:]
+    k_ref, v_ref, *received = refs[: -2 * chunks]
+    outs = refs[-2 * chunks :]
+    for index, query_ref in enumerate(queries):
+        sum_ref, total_ref = outs[2 * index : 2 * index + 2]
+        result = attend(query_ref[...], cached_pairs(k_ref, v_ref, received))
+        sum_ref[...] = result[:, :HEAD_SIZE].astype(sum_ref.dtype)
+        if index == 0:
+            total_ref[...] = result[:, HEAD_SIZE:]
+        else:
+            total_ref[...] = jnp.zeros(total_ref.shape, jnp.float32)
+            for row, values in enumerate(total_rows(result[:, HEAD_SIZE:])):
+                total_ref[row : row + 1, :] = values
+
+
+def prompt_first(place, queries, prompt_keys, prompt_values, received, heads):
+    count = queries[0].shape[0] // heads
+    tokens = prompt_keys.shape[0]
+    chosen = pl.BlockSpec((tokens, HEAD_SIZE), lambda i, p: (0, p[0] * heads))
+    outs = [shape((count, HEAD_SIZE), jnp.float32)] * 2 + [
+        shape((count, HEAD_SIZE), jnp.bfloat16),
+        shape((8, LANES), jnp.float32),
+    ] * (len(queries) - 1)
+    parts = len(received) + 1
+    return call(
+        functools.partial(prompt_first_kernel, len(queries)),
+        (place,),
+        (*queries, prompt_keys, prompt_values, *received),
+        outs,
+        [pl.BlockSpec((count, HEAD_SIZE), lambda *_: (0, 0))] * len(queries)
+        + [chosen, chosen]
+        + [whole(a) for a in received],
+        [whole(a) for a in outs],
+        (1,),
+        [],
+        6 * len(queries) * count * parts * tokens * HEAD_SIZE,
+        4 * parts * tokens * HEAD_SIZE,
+    )
+
+
+def prompt_second_kernel(place, q_ref, k_ref, v_ref, *refs):
+    *received, sum_ref, total_ref, token_ref, out_ref, held = refs
+    count = q_ref.shape[0]
+    result = attend(q_ref[...], cached_pairs(k_ref, v_ref, received))
+    out_ref[:count, :] = sum_ref[...]
+    out_ref[count : 2 * count, :] = result[:, :HEAD_SIZE].astype(jnp.bfloat16)
+    held[...] = total_ref[...]
+    for row, values in enumerate(total_rows(result[:, HEAD_SIZE:])):
+        at = count // LANES + row
+        held[at : at + 1, :] = values
+    out_ref[2 * count :, :] = split_rows(held[...])
+
+
+def prompt_second(place, queries, prompt_keys, prompt_values, received, first, heads, token):
+    count = queries.shape[0] // heads
+    tokens = prompt_keys.shape[0]
+    chosen = pl.BlockSpec((tokens, HEAD_SIZE), lambda i, p: (0, p[0] * heads + 1))
+    out = shape((heads * count + 16, HEAD_SIZE), jnp.bfloat16)
+    parts = len(received) + 1
+    return call(
+        prompt_second_kernel,
+        (place,),
+        (queries, prompt_keys, prompt_values, *received, *first, token),
+        out,
+        [pl.BlockSpec((count, HEAD_SIZE), lambda *_: (1, 0)), chosen, chosen]
+        + [whole(a) for a in (*received, *first)]
+        + [corner(token)],
+        whole(out),
+        (1,),
+        [pltpu.VMEM((8, LANES), jnp.float32)],
+        6 * count * parts * tokens * HEAD_SIZE,
+        4 * parts * tokens * HEAD_SIZE,
+    )
+
+
+def own_kernel(parts, place, q_ref, k_ref, v_ref, *refs):
+    received, refs = refs[: parts - 1], refs[parts - 1 :]
+    first_sum, first_total, pair_ref, *refs = refs
+    terms, refs = refs[: parts - 1], refs[parts - 1 :]
+    inverse_ref, cos_ref, sin_ref, *_, sum_ref, total_ref = refs
+    count = first_sum.shape[0]
+    rows = inverse_ref.shape[0]
+    inverse = inverse_ref[...]
+    cosine = cos_ref[...] * inverse
+    sine = sin_ref[...] * inverse
+    pair = pair_ref[...]
+    for ref in terms:
+        pair = pair + ref[:rows, :].astype(jnp.float32)
+    heads = pair.shape[1] // (2 * HEAD_SIZE)
+    query_row = lax.broadcasted_iota(jnp.int32, (count, rows), 0)
+    key_row = lax.broadcasted_iota(jnp.int32, (count, rows), 1)
+    same = query_row // 8 == key_row // 4
+    valid = same & (key_row % 4 <= query_row % 4)
+    ones = jnp.ones((rows, LANES), jnp.bfloat16)
     for head in range(heads):
-        at = slice(head * HEAD_SIZE, (head + 1) * HEAD_SIZE)
-        rows = slice(head * count, (head + 1) * count)
-        query = q_ref[rows, :]
-        total = None
-        for k_ref, v_ref in zip(keys, values):
-            weight = capped_weight(dot_last(query, k_ref[:, at])).astype(jnp.bfloat16)
-            term = jnp.dot(
-                weight,
-                jnp.concatenate([v_ref[:, at], ones], axis=1),
-                preferred_element_type=jnp.float32,
-            )
-            total = term if total is None else total + term
-        outs[0][rows, :] = total[:, :HEAD_SIZE].astype(outs[0].dtype)
-        weight_sum = total[:, HEAD_SIZE:]
-        if packed:
-            held = outs[1]
-            for block in range(count // LANES):
-                held[head * (count // LANES) + block, :] = weight_sum[
-                    block * LANES : (block + 1) * LANES
-                ].T[0]
+        at = slice(head * count, (head + 1) * count)
+        query = q_ref[at, :]
+        key = rotated(pair[:, head * HEAD_SIZE : (head + 1) * HEAD_SIZE], cosine, sine)
+        value_at = (heads + head) * HEAD_SIZE
+        value = pair[:, value_at : value_at + HEAD_SIZE] * inverse
+        weight = capped_weight(dot_last(query, key.astype(jnp.bfloat16)))
+        weight = jnp.where(valid, weight, 0.0).astype(jnp.bfloat16)
+        result = jnp.dot(
+            weight,
+            jnp.concatenate([value.astype(jnp.bfloat16), ones], axis=1),
+            preferred_element_type=jnp.float32,
+        )
+        if head == 0:
+            sum_ref[at, :] = first_sum[...] + result[:, :HEAD_SIZE]
+            total_ref[at, :] = first_total[...] + result[:, HEAD_SIZE:]
         else:
-            outs[1][rows, :] = weight_sum
-    if packed:
-        outs[0][heads * count :, :] = split_rows(outs[1][...])
-
-
-def prompt_attention(place, queries, prompt_keys, keys, prompt_values, values, packed):
-    parts = len(keys) + 1
-    tokens, columns = keys[0].shape
-    count = queries.shape[0]
-    chosen = pl.BlockSpec((tokens, columns), lambda i, p: (0, p[0]))
-    if packed:
-        outs = shape((count + 16, HEAD_SIZE), jnp.bfloat16)
-        out_specs = whole(outs)
-        scratch = [pltpu.VMEM((8, LANES), jnp.float32)]
-    else:
-        outs = [shape((count, HEAD_SIZE), jnp.float32)] * 2
-        out_specs = [whole(a) for a in outs]
-        scratch = []
-    return call(
-        functools.partial(prompt_kernel, parts, packed),
+            result = result + attend(query, cached_pairs(k_ref, v_ref, received))
+            sum_ref[at, :] = result[:, :HEAD_SIZE]
+            total_ref[at, :] = result[:, HEAD_SIZE:]
+
+
+def own_attention_sums(
+    place, queries, prompt_keys, prompt_values, received, first, pair, terms, tables, tokens_after
+):
+    count = first[0].shape[0]
+    heads = queries.shape[0] // count
+    tokens = prompt_keys.shape[0]
+    parts = len(received) + 1
+    chosen = pl.BlockSpec((tokens, HEAD_SIZE), lambda i, p: (0, p[0] * heads + 1))
+    operands = (*received, *first, pair, *terms, *tables)
+    outs = [shape(queries.shape, jnp.float32)] * 2
+    return call(
+        functools.partial(own_kernel, parts),
         (place,),
-        (queries, prompt_keys, *keys, prompt_values, *values),
+        (queries, prompt_keys, prompt_values, *operands, *tokens_after),
         outs,
-        [whole(queries), chosen]
-        + [whole(a) for a in keys]
-        + [chosen]
-        + [whole(a) for a in values],
-        out_specs,
+        [whole(queries), chosen, chosen]
+        + [whole(a) for a in operands]
+        + [corner(a) for a in tokens_after],
+        [whole(a) for a in outs],
         (1,),
-        scratch,
-        4 * count * parts * tokens * HEAD_SIZE,
-        4 * parts * tokens * columns,
-    )
-
-
-def suffix_kernel(parts, place, lengths, *refs):
-    queries, refs = refs[:parts], refs[parts:]
-    latest, refs = refs[:parts], refs[parts:]
-    (k_ref, v_ref, inverse_ref, cos_ref, sin_ref), refs = refs[:5], refs[5:]
-    outs, refs = refs[: parts + 1], refs[parts + 1 :]
-    query_held, spread, new_keys, new_values, result, sums, totals, packed = refs
+        [],
+        6 * count * parts * tokens * HEAD_SIZE,
+        4 * parts * tokens * HEAD_SIZE,
+    )
+
+
+def suffix_kernel(parts, place, lengths, own_ref, *refs):
+    received, (k_ref, v_ref, _), refs = refs[: parts - 1], refs[parts - 1 : parts + 2], refs[parts + 2 :]
+    outs, (query_held, spread, result, sums, totals, packed) = refs[: parts + 1], refs[parts + 1 :]
     member = pl.program_id(0)
     members = pl.num_programs(0)
     slots, columns = k_ref.shape[1:]
     heads = columns // HEAD_SIZE
     near = heads // parts
-    share = latest[0].shape[1]
     here = place[0]
 
     @pl.when(member == 0)
     def _():
         spread[...] = jnp.zeros(spread.shape, jnp.float32)
         packed[...] = jnp.zeros(packed.shape, jnp.float32)
-        for mask in range(parts):
-            query_held[mask] = queries[mask][...].astype(jnp.float32)
-        rows = pl.ds(pl.multiple_of(here * share, share), share)
-        inverse = inverse_ref[rows, :]
-        cosine = cos_ref[rows, :] * inverse
-        sine = sin_ref[rows, :] * inverse
-        for head in range(heads):
-            at = slice(head * HEAD_SIZE, (head + 1) * HEAD_SIZE)
-            key = latest[0][0, :, at]
-            value = latest[0][1, :, at]
-            for ref in latest[1:]:
-                key = key + ref[0, :, at].astype(jnp.float32)
-                value = value + ref[1, :, at].astype(jnp.float32)
-            new_keys[:, at] = rotated(key, cosine, sine)
-            new_values[:, at] = value * inverse
+        query_held[0] = own_ref[...].astype(jnp.float32)
+        count = own_ref.shape[0]
+        for mask, ref in enumerate(received, start=1):
+            pieces = ref.shape[1] // HEAD_SIZE
+            tall = count // pieces
+            for piece in range(pieces):
+                at = slice(piece * HEAD_SIZE, (piece + 1) * HEAD_SIZE)
+                query_held[mask, piece * tall : (piece + 1) * tall, :] = ref[
+                    ref.shape[0] - tall :, at
+                ].astype(jnp.float32)
 
     def places(mask, head):
         owner = here ^ mask
@@ -520,22 +688,11 @@
         for head in range(near):
             row, column, local = places(mask, head)
             spread[row, column] = query_held[mask, local, :]
-    query = spread[...].astype(jnp.bfloat16)
-    weight = capped_weight(dot_last(k_ref[0], query))
+    weight = capped_weight(dot_last(k_ref[0], spread[...].astype(jnp.bfloat16)))
     valid = lax.broadcasted_iota(jnp.int32, weight.shape, 0) < lengths[here * members + member]
     weight = jnp.where(valid, weight, 0.0).astype(jnp.bfloat16)
-    tile = pl.ds(pl.multiple_of((member // 2) * 8, 8), 8)
-    new_weight = capped_weight(dot_last(new_keys[tile, :].astype(jnp.bfloat16), query))
-    slot = lax.broadcasted_iota(jnp.int32, new_weight.shape, 0)
-    decode_step = lax.broadcasted_iota(jnp.int32, new_weight.shape, 1) % 4
-    valid = (slot // 4 == member % 2) & (slot % 4 <= decode_step)
-    new_weight = jnp.where(valid, new_weight, 0.0).astype(jnp.bfloat16)
-    result[:, :columns] = dot_first(weight, v_ref[0]) + dot_first(
-        new_weight, new_values[tile, :].astype(jnp.bfloat16)
-    )
-    result[:, columns:] = dot_first(weight, jnp.ones((slots, LANES), jnp.bfloat16)) + dot_first(
-        new_weight, jnp.ones((8, LANES), jnp.bfloat16)
-    )
+    result[:, :columns] = dot_first(weight, v_ref[0])
+    result[:, columns:] = dot_first(weight, jnp.ones((slots, LANES), jnp.bfloat16))
     for mask in range(parts):
         for head in range(near):
             row, column, local = places(mask, head)
@@ -550,19 +707,16 @@
         for mask in range(1, parts):
             ref = outs[mask + 1]
             ref[:count, :] = sums[mask].astype(jnp.bfloat16)
-            packed[0, :] = totals[mask].T[0]
+            packed[0:1, :] = totals[mask].T[0:1]
             ref[count:, :] = split_rows(packed[...])
 
 
-def suffix_attention(
-    place, lengths, queries, latest, cache_keys, cache_values, inverse, cosine, sine
-):
-    parts = len(queries)
+def suffix_attention(place, lengths, own, received, cache_keys, cache_values, token):
+    parts = len(received) + 1
     members, slots, columns = cache_keys.shape
-    count = queries[0].shape[0]
-    share = latest[0].shape[1]
+    count = own.shape[0]
     spread_rows = 8 * columns // HEAD_SIZE
-    operands = (*queries, *latest, cache_keys, cache_values, inverse, cosine, sine)
+    operands = (own, *received, cache_keys, cache_values, token)
     outs = [shape((count, HEAD_SIZE), jnp.float32)] * 2 + [
         shape((count + 16, HEAD_SIZE), jnp.bfloat16)
     ] * (parts - 1)
@@ -572,16 +726,12 @@
         (place, lengths),
         operands,
         outs,
-        [whole(a) for a in queries]
-        + [whole(a) for a in latest]
-        + [cache, cache, whole(inverse), whole(cosine), whole(sine)],
+        [whole(own)] + [whole(a) for a in received] + [cache, cache, corner(token)],
         [whole(a) for a in outs],
         (members,),
         [
             pltpu.VMEM((parts, count, HEAD_SIZE), jnp.float32),
             pltpu.VMEM((spread_rows, columns), jnp.float32),
-            pltpu.VMEM((share, columns), jnp.float32),
-            pltpu.VMEM((share, columns), jnp.float32),
             pltpu.VMEM((spread_rows, columns + LANES), jnp.float32),
             pltpu.VMEM((parts, count, HEAD_SIZE), jnp.float32),
             pltpu.VMEM((parts, count, HEAD_SIZE), jnp.float32),
@@ -717,10 +867,11 @@
     for ref in squares[1:]:
         total = total + ref[0:1, :]
     inverse = lax.rsqrt(down_rows(total) / MODEL_WIDTH + EPSILON)
-    for at in range(0, x_ref.shape[1], LANES):
+    for at in range(0, x_ref.shape[2], LANES):
         lanes = slice(at, at + LANES)
-        branch = attended_ref[:, lanes] * inverse * gain_ref[:, lanes]
-        out_ref[:, lanes] = (x_ref[:, lanes].astype(jnp.float32) + branch).astype(jnp.bfloat16)
+        branch = attended_ref[:, lanes] * inverse * gain_ref[lanes].reshape(1, LANES)
+        x = x_ref[:, :, lanes].astype(jnp.float32)
+        out_ref[:, :, lanes] = (x + branch.reshape(x.shape)).astype(jnp.bfloat16)
 
 
 def finish(place, x, attended, gain, squares):
@@ -754,33 +905,24 @@
     suffix_value_cache,
     suffix_len,
 ):
-    group_rows, steps, local_width = hidden_in.shape
+    group_rows, steps, _ = hidden_in.shape
     rows = group_rows * steps
     parts = lax.axis_size("prefix")
     groups = lax.axis_size("prefill")
+    heads = prompt_keys.shape[1] // HEAD_SIZE // parts
     prompt_total = prompt_keys.shape[0] * groups * parts
-    here = lax.axis_index("prefix")
-    place = here.astype(jnp.int32).reshape(1)
-    x = hidden_in.reshape(rows, local_width)
-    gain = pre_gain.reshape(1, local_width)
+    place = lax.axis_index("prefix").astype(jnp.int32).reshape(1)
     near = range(1, parts)
     far = range(1, groups)
 
-    *sent, own, squares = query_projection(place, x, gain, w_query, parts)
-    received = [paired(a, "prefix", m) for m, a in zip(near, sent)]
-
-    columns = prompt_keys.shape[1] // parts
-
-    def spread(cache):
-        return [
-            paired(
-                lax.dynamic_slice_in_dim(cache, (here ^ m) * columns, columns, axis=1), "prefix", m
-            )
-            for m in near
-        ]
-
-    keys = spread(prompt_keys)
-    values = spread(prompt_values)
+    def swapped(arrays, axis):
+        return [paired(a, axis, m) for m, a in enumerate(arrays, start=1)]
+
+    *sent, own, squares, scaled = query_projection(place, hidden_in, pre_gain, w_query, parts)
+    received = swapped(sent, "prefix")
+    first_head = swapped(
+        cache_columns(place, prompt_keys, prompt_values, 0, heads, parts, squares), "prefix"
+    )
 
     positions = (
         (prompt_total + suffix_len[:, None] + jnp.arange(steps, dtype=jnp.int32)[None, :])
@@ -794,48 +936,64 @@
     cosine = jnp.concatenate([cosine, cosine], axis=1)
     sine = jnp.concatenate([-sine, sine], axis=1)
 
-    own_pair, *sent = pair_projection(place, x, gain, key_projection, value_projection, parts)
-    latest = [own_pair] + [paired(a, "prefix", m) for m, a in zip(near, sent)]
-
     queries, *split_queries, inverse = query_rope(
         place, own, received, squares, cosine, sine, parts
     )
     far_queries = [paired(queries, "prefill", m) for m in far]
-    suffix_queries = [split_queries[0]] + [
-        paired(a, "prefix", m) for m, a in zip(near, split_queries[1:])
+    pair, *sent = pair_projection(
+        place, scaled, key_projection, value_projection, split_queries[1:]
+    )
+    terms = swapped(sent, "prefix")
+    second_head = swapped(
+        cache_columns(place, prompt_keys, prompt_values, 1, heads, parts, pair), "prefix"
+    )
+
+    first = prompt_first(
+        place, [queries, *far_queries], prompt_keys, prompt_values, first_head, heads
+    )
+    near_sums, near_totals, *sent = suffix_attention(
+        place, suffix_len, split_queries[0], terms, suffix_key_cache, suffix_value_cache, first[1]
+    )
+    suffix = [near_sums, near_totals, *swapped(sent, "prefix")]
+    packed = [
+        prompt_second(
+            place,
+            far_queries[m - 1],
+            prompt_keys,
+            prompt_values,
+            second_head,
+            first[2 * m : 2 * m + 2],
+            heads,
+            near_totals,
+        )
+        for m in far
     ]
-
-    def prompt(chunk, packed):
-        return prompt_attention(place, chunk, prompt_keys, keys, prompt_values, values, packed)
-
-    sums, totals = prompt(queries, False)
-    prompt_results = [paired(prompt(q, True), "prefill", m) for m, q in zip(far, far_queries)]
-    near_sums, near_totals, *sent = suffix_attention(
+    prompt_results = swapped(packed, "prefill")
+    sums, totals = own_attention_sums(
         place,
-        suffix_len,
-        suffix_queries,
-        latest,
-        suffix_key_cache,
-        suffix_value_cache,
-        inverse,
-        cosine,
-        sine,
-    )
-    suffix = [near_sums, near_totals] + [paired(a, "prefix", m) for m, a in zip(near, sent)]
+        queries,
+        prompt_keys,
+        prompt_values,
+        second_head,
+        first[:2],
+        pair,
+        terms,
+        (inverse, cosine, sine),
+        packed,
+    )
     mixed = mix(place, sums, totals, prompt_results, suffix, rows)
     others = [paired(mixed, "prefix", m) for m in near]
     head_terms = output_projection(place, (0,), [mixed], w_out)
     head_terms = output_projection(place, tuple(near), others, w_out, head_terms)
     attended, squares = attended_squares(place, head_terms, paired(head_terms, "tensor", 1))
     squares = [squares] + [paired(squares, "prefix", m) for m in near]
-    out = finish(place, x, attended, post_gain.reshape(1, local_width), squares)
-    return out.reshape(group_rows, steps, local_width)
+    return finish(place, hidden_in, attended, post_gain, squares)
 
 
 def heads_divide(mesh):
     sizes = [mesh.shape[name] for name in ("prefill", "prefix", "tensor")]
     key_heads = QUERY_HEADS // 2 // sizes[2]
-    return key_heads % sizes[1] == 0 and sizes[1] == 4 and sizes[2] == 2 and sizes[0] in (2, 4)
+    return key_heads == 2 * sizes[1] and sizes[1] == 4 and sizes[2] == 2 and sizes[0] in (2, 4)
 
 
 def solution(mesh):

time: 93.9 us -> 93.8 us (level)
  starting transfers between devices: 43.4 us -> 34.9 us
  waiting for transfers between devices: 20.5 us -> 25.5 us
  Pallas kernels: 21.2 us -> 25.7 us
  local copies, waits for them, and re-layouts: 7.84 us -> 6.73 us
    ppermute x31 -> x28, starting transfers between devices: 43.4 us -> 34.9 us  [paired(): return lax.ppermute(values, axis, [(i, i ^ mask) for i in range(size)])]
    ppermute x31 -> x28, waiting for transfers between devices: 20.5 us -> 25.5 us  [paired(): return lax.ppermute(values, axis, [(i, i ^ mask) for i in range(size)])]
    pallas_call x13 -> x16, Pallas kernels: 21.2 us -> 25.7 us  [call(): pl.pallas_call(kernel, out_shape=out_shape, grid_spec=pltpu.PrefetchScala...]
    reshape x4 -> x0, local copies, waits for them, and re-layouts: 2.68 us -> none  [the longest x1 1.18 us: by_heads(): x = hidden_in.reshape(rows, local_width)]
    unnamed x22 -> x30, local copies, waits for them, and re-layouts: 4.04 us -> 6.62 us
    dynamic_slice x2 -> x0, local copies, waits for them, and re-layouts: 1.01 us -> none  [spread(): lax.dynamic_slice_in_dim(cache, (here ^ m) * columns, columns, axis=1)]
  transfers between devices with their start and end apart: 31 -> 28, of which waited for: 15 -> 13; matrix products, arithmetic and copies ran while one was open for 2% -> 1% of each run, Pallas kernels for 18% -> 18%
where the time goes in v2:
time: 93.8 us; the launch traced here: 93.5 us
  starting transfers between devices  34.9 us (37%)
  Pallas kernels  25.7 us (27%)
  waiting for transfers between devices  25.5 us (27%)
  local copies, waits for them, and re-layouts  6.73 us (7%)
    ppermute x28, starting transfers between devices, paired(): return lax.ppermute(values, axis, [(i, i ^ mask) for i in range(size)])  34.9 us
    pallas_call x16, Pallas kernels, call(): pl.pallas_call(kernel, out_shape=out_shape, grid_spec=pltpu.PrefetchScala...  25.7 us
    ppermute x28, waiting for transfers between devices, paired(): return lax.ppermute(values, axis, [(i, i ^ mask) for i in range(size)])  25.5 us
    unnamed x30, local copies, waits for them, and re-layouts  6.62 us
  transfers between devices with their start and end apart: 28, of which 13 were waited for; matrix products, arithmetic and copies ran while one was open for 1% of the time, Pallas kernels for 18%

profile of v2, /device:TPU:0, one launch (start us, length us, event | category | flops | bytes accessed | tf_op | source)
XLA Modules:
  0.0 93.5 jit_solution(17534013137095512475)
XLA Ops:
  0.0 5.2 %shard_map.118 = (bf16[144,512]{1,0:T(8,128)(2,1)}, bf16[144,512]{1,0:T(8,128)(2,1)}, bf16[144,512]{1,0:T(8,128)(2,1)}, f32[128,512]{1,0:T(8,128)}, f32[8,128]{1,0:T(8,128)}, /*index=5*/bf16[128,1152]{1,0:T(8,128)(2,1)}) custom-call(s32[1]{0:T(128)} %bitcast.place, bf16[32,4,1152]{2,1,0:T(4,128)(2,1)} %x_ref.3, f32[1152]{0:T(1024)} %gain_ref.2, ...), custom_call_target="tpu_custom_call" | custom-call | flops 603979776 | bytes 4718592 | tf_op jit(solution)/shard_map/pallas_call | solution.py:206
  5.2 3.0 %collective-permute-start = (bf16[144,512]{1,0:T(8,128)(2,1)}, bf16[144,512]{1,0:T(8,128)(2,1)S(1)}, u32[]{:S(2)}, u32[]{:S(2)}) collective-permute-start(bf16[144,512]{1,0:T(8,128)(2,1)} %get-tuple-element.45), channel_id=1, source_target_pairs={{0,2},{2,0},{4,6},{6,4},{1,3},{3,1},{5,7},{7,5},{8,10},{10,8},{12,... | collective-permute-start | bytes 442376 | tf_op jit(solution)/shard_map/ppermute | solution.py:190
  8.2 1.5 %collective-permute-start.1 = (bf16[144,512]{1,0:T(8,128)(2,1)}, bf16[144,512]{1,0:T(8,128)(2,1)S(1)}, u32[]{:S(2)}, u32[]{:S(2)}) collective-permute-start(bf16[144,512]{1,0:T(8,128)(2,1)} %get-tuple-element.46), channel_id=1, source_target_pairs={{0,4},{2,6},{4,0},{6,2},{1,5},{3,7},{5,1},{7,3},{8,12},{10,14},{12... | collective-permute-start | bytes 442376 | tf_op jit(solution)/shard_map/ppermute | solution.py:190
  9.7 0.7 copy-done.9
  10.4 1.3 %shard_map.122 = (bf16[512,256]{1,0:T(8,128)(2,1)}, bf16[512,256]{1,0:T(8,128)(2,1)}, bf16[512,256]{1,0:T(8,128)(2,1)S(1)}) custom-call(s32[1]{0:T(128)} %bitcast.place, bf16[512,1024]{1,0:T(8,128)(2,1)S(1)} %copy-done, bf16[512,1024]{1,0:T(8,128)(2,1)S(1)} %copy-done.1, f32[8,128]{1,0:T(8,128)S(1)} %copy-done.9), custom_call_target="tpu_custom_call" | custom-call | bytes 1572864 | tf_op jit(solution)/shard_map/pallas_call | solution.py:206
  11.7 2.0 %collective-permute-start.9 = (bf16[512,256]{1,0:T(8,128)(2,1)}, bf16[512,256]{1,0:T(8,128)(2,1)S(1)}, u32[]{:S(2)}, u32[]{:S(2)}) collective-permute-start(bf16[512,256]{1,0:T(8,128)(2,1)} %get-tuple-element.58), channel_id=1, source_target_pairs={{0,2},{2,0},{4,6},{6,4},{1,3},{3,1},{5,7},{7,5},{8,10},{10,8},{12,... | collective-permute-start | bytes 786440 | tf_op jit(solution)/shard_map/ppermute | solution.py:190
  13.6 1.5 %collective-permute-start.10 = (bf16[512,256]{1,0:T(8,128)(2,1)}, bf16[512,256]{1,0:T(8,128)(2,1)S(1)}, u32[]{:S(2)}, u32[]{:S(2)}) collective-permute-start(bf16[512,256]{1,0:T(8,128)(2,1)} %get-tuple-element.59), channel_id=1, source_target_pairs={{0,4},{2,6},{4,0},{6,2},{1,5},{3,7},{5,1},{7,3},{8,12},{10,14},{12... | collective-permute-start | bytes 786440 | tf_op jit(solution)/shard_map/ppermute | solution.py:190
  16.2 0.7 collective-permute-done.1.refs_1_
  16.9 0.7 collective-permute-done.2.refs_2_
  17.6 0.9 %copy-done.8 = f32[128,512]{1,0:T(8,128)S(1)} copy-done((f32[128,512]{1,0:T(8,128)S(1)}, f32[128,512]{1,0:T(8,128)}, u32[]{:S(2)}) %copy-start.8) | copy-done | bytes 262168
  18.6 0.7 copy-done.10
  19.5 3.7 %collective-permute-start.8 = (bf16[512,128]{1,0:T(8,128)(2,1)S(1)}, bf16[512,128]{1,0:T(8,128)(2,1)S(1)}, u32[]{:S(2)}, u32[]{:S(2)}) collective-permute-start(bf16[512,128]{1,0:T(8,128)(2,1)S(1)} %get-tuple-element.49.refs_0_.q_ref), channel_id=1, source_target_pairs={{0,24},{8,16},{16,8},{24,0},{1,25},{9,17},{17,9},{25,1},{2,26},{10... | collective-permute-start | bytes 393224 | tf_op jit(solution)/shard_map/ppermute | solution.py:190
  23.2 1.7 %copy-done.4 = bf16[1152,1024]{1,0:T(8,128)(2,1)S(1)} copy-done((bf16[1152,1024]{1,0:T(8,128)(2,1)S(1)}, bf16[1152,1024]{1,0:T(8,128)(2,1)}, u32[]{:S(2)}) %copy-start.4) | copy-done | bytes 2359320
  24.8 1.7 %copy-done.5 = bf16[1152,1024]{1,0:T(8,128)(2,1)S(1)} copy-done((bf16[1152,1024]{1,0:T(8,128)(2,1)S(1)}, bf16[1152,1024]{1,0:T(8,128)(2,1)}, u32[]{:S(2)}) %copy-start.5) | copy-done | bytes 2359320
  26.5 1.0 %copy-done.7 = bf16[128,1152]{1,0:T(8,128)(2,1)S(1)} copy-done((bf16[128,1152]{1,0:T(8,128)(2,1)S(1)}, bf16[128,1152]{1,0:T(8,128)(2,1)}, u32[]{:S(2)}) %copy-start.7) | copy-done | bytes 294936
  27.4 2.2 %shard_map.120 = (f32[128,512]{1,0:T(8,128)S(1)}, bf16[160,512]{1,0:T(8,128)(2,1)S(1)}, bf16[160,512]{1,0:T(8,128)(2,1)S(1)}, bf16[160,512]{1,0:T(8,128)(2,1)S(1)}) custom-call(s32[1]{0:T(128)} %bitcast.place, bf16[128,1152]{1,0:T(8,128)(2,1)S(1)} %copy-done.7, bf16[1152,1024]{1,0:T(8,128)(2,1)S(1)} %copy-done.4, bf16[1152,1024]{1,0:T(8,128)(2,1)S(1)} %copy-done.5, ...), custom_call_target="tpu_custom_call" | custom-call | flops 603979776 | bytes 4718592 | tf_op jit(solution)/shard_map/pallas_call | solution.py:206
  29.7 1.7 %collective-permute-start.12 = (bf16[160,512]{1,0:T(8,128)(2,1)S(1)}, bf16[160,512]{1,0:T(8,128)(2,1)S(1)}, u32[]{:S(2)}, u32[]{:S(2)}) collective-permute-start(bf16[160,512]{1,0:T(8,128)(2,1)S(1)} %get-tuple-element.63), channel_id=1, source_target_pairs={{0,2},{2,0},{4,6},{6,4},{1,3},{3,1},{5,7},{7,5},{8,10},{10,8},{12,... | collective-permute-start | bytes 491528 | tf_op jit(solution)/shard_map/ppermute | solution.py:190
  31.4 0.8 collective-permute-start.6
  33.2 1.6 %collective-permute-start.4 = (bf16[512,256]{1,0:T(8,128)(2,1)S(1)}, bf16[512,256]{1,0:T(8,128)(2,1)S(1)}, u32[]{:S(2)}, u32[]{:S(2)}) collective-permute-start(bf16[512,256]{1,0:T(8,128)(2,1)S(1)} %get-tuple-element.56), channel_id=1, source_target_pairs={{0,4},{2,6},{4,0},{6,2},{1,5},{3,7},{5,1},{7,3},{8,12},{10,14},{12... | collective-permute-start | bytes 786440 | tf_op jit(solution)/shard_map/ppermute | solution.py:190
  34.8 1.4 %collective-permute-start.5 = (bf16[512,256]{1,0:T(8,128)(2,1)S(1)}, bf16[512,256]{1,0:T(8,128)(2,1)S(1)}, u32[]{:S(2)}, u32[]{:S(2)}) collective-permute-start(bf16[512,256]{1,0:T(8,128)(2,1)S(1)} %get-tuple-element.57), channel_id=1, source_target_pairs={{0,6},{2,4},{4,2},{6,0},{1,7},{3,5},{5,3},{7,1},{8,14},{10,12},{12... | collective-permute-start | bytes 786440 | tf_op jit(solution)/shard_map/ppermute | solution.py:190
  36.9 1.6 %collective-permute-start.14 = (bf16[160,512]{1,0:T(8,128)(2,1)S(1)}, bf16[160,512]{1,0:T(8,128)(2,1)S(1)}, u32[]{:S(2)}, u32[]{:S(2)}) collective-permute-start(bf16[160,512]{1,0:T(8,128)(2,1)S(1)} %get-tuple-element.65), channel_id=1, source_target_pairs={{0,6},{2,4},{4,2},{6,0},{1,7},{3,5},{5,3},{7,1},{8,14},{10,12},{12... | collective-permute-start | bytes 491528 | tf_op jit(solution)/shard_map/ppermute | solution.py:190
  38.5 2.7 %shard_map.123 = (f32[256,128]{1,0:T(8,128)S(1)}, f32[256,128]{1,0:T(8,128)S(1)}, bf16[256,128]{1,0:T(8,128)(2,1)S(1)}, f32[8,128]{1,0:T(8,128)S(1)}, bf16[256,1...) custom-call(s32[1]{0:T(128)} %bitcast.place, ...), custom_call_target="tpu_custom_call" | custom-call | flops 1610612736 | bytes 1048576 | tf_op jit(solution)/shard_map/pallas_call | solution.py:206
  41.2 10.9 %collective-permute-done.13.refs_1_.refs_7_ = bf16[160,512]{1,0:T(8,128)(2,1)S(1)} collective-permute-done((bf16[160,512]{1,0:T(8,128)(2,1)S(1)}, bf16[160,512]{1,0:T(8,128)(2,1)S(1)}, u32[]{:S(2)}, u32[]{:S(2)}) %collective-permute-start.13) | collective-permute-done | bytes 163872 | tf_op jit(solution)/shard_map/ppermute | solution.py:190
  52.0 6.3 %shard_map.124 = (f32[128,128]{1,0:T(8,128)S(1)}, f32[128,128]{1,0:T(8,128)S(1)}, bf16[144,128]{1,0:T(8,128)(2,1)S(1)}, bf16[144,128]{1,0:T(8,128)(2,1)S(1)}, bf16[144,128]{1,0:T(8,128)(2,1)S(1)}) custom-call(s32[1]{0:T(128)} %bitcast.place, s32[32]{0:T(128)S(1)} %copy-done.12, bf16[128,128]{1,0:T(8,128)(2,1)S(1)} %get-tuple-element.69.own_ref, ...), custom_call_target="tpu_custom_call" | custom-call | flops 536870912 | bytes 8388608 | tf_op jit(solution)/shard_map/pallas_call | solution.py:206
  58.4 1.0 %shard_map.125.refs_12_ = bf16[528,128]{1,0:T(8,128)(2,1)S(1)} custom-call(s32[1]{0:T(128)} %bitcast.place, bf16[512,128]{1,0:T(8,128)(2,1)S(1)} %collective-permute-done.6.refs_1_.q_ref, bf16[512,1024]{1,0:T(8,128)(2,1)S(1)} %copy-done, bf16[512,1024]{1,0:T(8,128)(2,1)S(1)} %copy-done.1, bf16[512,256]{1,0:T(8,128)(2,1)S(1)} %collective-permute-done.3.refs_0_, ...), custom_call_target="tpu_custom_call" | custom-call | flops 402653184 | bytes 1048576 | tf_op jit(solution)/shard_map/pallas_call | solution.py:206
  59.7 1.0 %shard_map.126.refs_13_ = bf16[528,128]{1,0:T(8,128)(2,1)S(1)} custom-call(s32[1]{0:T(128)} %bitcast.place, bf16[512,128]{1,0:T(8,128)(2,1)S(1)} %collective-permute-done.7.refs_2_.q_ref, bf16[512,1024]{1,0:T(8,128)(2,1)S(1)} %copy-done, bf16[512,1024]{1,0:T(8,128)(2,1)S(1)} %copy-done.1, bf16[512,256]{1,0:T(8,128)(2,1)S(1)} %collective-permute-done.3.refs_0_, ...), custom_call_target="tpu_custom_call" | custom-call | flops 402653184 | bytes 1048576 | tf_op jit(solution)/shard_map/pallas_call | solution.py:206
  60.7 2.9 %collective-permute-start.16 = (bf16[528,128]{1,0:T(8,128)(2,1)S(1)}, bf16[528,128]{1,0:T(8,128)(2,1)S(1)}, u32[]{:S(2)}, u32[]{:S(2)}) collective-permute-start(bf16[528,128]{1,0:T(8,128)(2,1)S(1)} %shard_map.126.refs_13_), channel_id=1, source_target_pairs={{0,16},{8,24},{16,0},{24,8},{1,17},{9,25},{17,1},{25,9},{2,18},{10... | collective-permute-start | bytes 405512 | tf_op jit(solution)/shard_map/ppermute | solution.py:190
  63.6 1.0 %shard_map.127.refs_14_ = bf16[528,128]{1,0:T(8,128)(2,1)S(1)} custom-call(s32[1]{0:T(128)} %bitcast.place, bf16[512,128]{1,0:T(8,128)(2,1)S(1)} %collective-permute-done.8.refs_3_.q_ref, bf16[512,1024]{1,0:T(8,128)(2,1)S(1)} %copy-done, bf16[512,1024]{1,0:T(8,128)(2,1)S(1)} %copy-done.1, bf16[512,256]{1,0:T(8,128)(2,1)S(1)} %collective-permute-done.3.refs_0_, ...), custom_call_target="tpu_custom_call" | custom-call | flops 402653184 | bytes 1048576 | tf_op jit(solution)/shard_map/pallas_call | solution.py:206
  64.6 1.4 %collective-permute-start.17 = (bf16[528,128]{1,0:T(8,128)(2,1)S(1)}, bf16[528,128]{1,0:T(8,128)(2,1)S(1)}, u32[]{:S(2)}, u32[]{:S(2)}) collective-permute-start(bf16[528,128]{1,0:T(8,128)(2,1)S(1)} %shard_map.127.refs_14_), channel_id=1, source_target_pairs={{0,24},{8,16},{16,8},{24,0},{1,25},{9,17},{17,9},{25,1},{2,26},{10... | collective-permute-start | bytes 405512 | tf_op jit(solution)/shard_map/ppermute | solution.py:190
  66.0 0.9 collective-permute-start.18
  66.9 0.9 collective-permute-start.19
  67.8 2.1 %collective-permute-done.18.refs_5_ = bf16[144,128]{1,0:T(8,128)(2,1)S(1)} collective-permute-done((bf16[144,128]{1,0:T(8,128)(2,1)S(1)}, bf16[144,128]{1,0:T(8,128)(2,1)S(1)}, u32[]{:S(2)}, u32[]{:S(2)}) %collective-permute-start.18) | collective-permute-done | bytes 36896 | tf_op jit(solution)/shard_map/ppermute | solution.py:190
  69.9 1.3 %collective-permute-start.20 = (bf16[144,128]{1,0:T(8,128)(2,1)S(1)}, bf16[144,128]{1,0:T(8,128)(2,1)S(1)}, u32[]{:S(2)}, u32[]{:S(2)}) collective-permute-start(bf16[144,128]{1,0:T(8,128)(2,1)S(1)} %get-tuple-element.80), channel_id=1, source_target_pairs={{0,6},{2,4},{4,2},{6,0},{1,7},{3,5},{5,3},{7,1},{8,14},{10,12},{12... | collective-permute-start | bytes 110600 | tf_op jit(solution)/shard_map/ppermute | solution.py:190
  71.2 1.2 %shard_map.128 = (f32[512,128]{1,0:T(8,128)S(1)}, f32[512,128]{1,0:T(8,128)S(1)}) custom-call(s32[1]{0:T(128)} %bitcast.place, bf16[512,128]{1,0:T(8,128)(2,1)S(1)} %get-tuple-element.49.refs_0_.q_ref, bf16[512,1024]{1,0:T(8,128)(2,1)S(1)} %copy-done, bf16[512,1024]{1,0:T(8,128)(2,1)S(1)} %copy-done.1, bf16[512,256]{1,0:T(8,128)(2,1)S(1)} %collective-permute-done.3.refs_0_, ...), custom_call_target="tpu_custom_call" | custom-call | flops 402653184 | bytes 1048576 | tf_op jit(solution)/shard_map/pallas_call | solution.py:206
  72.4 2.7 %collective-permute-done.20.refs_7_ = bf16[144,128]{1,0:T(8,128)(2,1)S(1)} collective-permute-done((bf16[144,128]{1,0:T(8,128)(2,1)S(1)}, bf16[144,128]{1,0:T(8,128)(2,1)S(1)}, u32[]{:S(2)}, u32[]{:S(2)}) %collective-permute-start.20) | collective-permute-done | bytes 36896 | tf_op jit(solution)/shard_map/ppermute | solution.py:190
  75.5 1.4 %collective-permute-start.23 = (bf16[128,512]{1,0:T(8,128)(2,1)S(1)}, bf16[128,512]{1,0:T(8,128)(2,1)S(1)}, u32[]{:S(2)}, u32[]{:S(2)}) collective-permute-start(bf16[128,512]{1,0:T(8,128)(2,1)S(1)} %shard_map.129.refs_0_), channel_id=1, source_target_pairs={{0,6},{2,4},{4,2},{6,0},{1,7},{3,5},{5,3},{7,1},{8,14},{10,12},{12... | collective-permute-start | bytes 393224 | tf_op jit(solution)/shard_map/ppermute | solution.py:190
  77.0 1.2 %collective-permute-start.22 = (bf16[128,512]{1,0:T(8,128)(2,1)S(1)}, bf16[128,512]{1,0:T(8,128)(2,1)S(1)}, u32[]{:S(2)}, u32[]{:S(2)}) collective-permute-start(bf16[128,512]{1,0:T(8,128)(2,1)S(1)} %shard_map.129.refs_0_), channel_id=1, source_target_pairs={{0,4},{2,6},{4,0},{6,2},{1,5},{3,7},{5,1},{7,3},{8,12},{10,14},{12... | collective-permute-start | bytes 393224 | tf_op jit(solution)/shard_map/ppermute | solution.py:190
  78.1 1.0 %collective-permute-start.21 = (bf16[128,512]{1,0:T(8,128)(2,1)S(1)}, bf16[128,512]{1,0:T(8,128)(2,1)S(1)}, u32[]{:S(2)}, u32[]{:S(2)}) collective-permute-start(bf16[128,512]{1,0:T(8,128)(2,1)S(1)} %shard_map.129.refs_0_), channel_id=1, source_target_pairs={{0,2},{2,0},{4,6},{6,4},{1,3},{3,1},{5,7},{7,5},{8,10},{10,8},{12,... | collective-permute-start | bytes 393224 | tf_op jit(solution)/shard_map/ppermute | solution.py:190
  79.5 2.1 %collective-permute-done.23.refs_2_ = bf16[128,512]{1,0:T(8,128)(2,1)S(1)} collective-permute-done((bf16[128,512]{1,0:T(8,128)(2,1)S(1)}, bf16[128,512]{1,0:T(8,128)(2,1)S(1)}, u32[]{:S(2)}, u32[]{:S(2)}) %collective-permute-start.23) | collective-permute-done | bytes 131104 | tf_op jit(solution)/shard_map/ppermute | solution.py:190
  81.6 1.3 %collective-permute-done.22.refs_1_ = bf16[128,512]{1,0:T(8,128)(2,1)S(1)} collective-permute-done((bf16[128,512]{1,0:T(8,128)(2,1)S(1)}, bf16[128,512]{1,0:T(8,128)(2,1)S(1)}, u32[]{:S(2)}, u32[]{:S(2)}) %collective-permute-start.22) | collective-permute-done | bytes 131104 | tf_op jit(solution)/shard_map/ppermute | solution.py:190
  83.1 1.1 %shard_map.131.here_ref = f32[128,1152]{1,0:T(8,128)S(1)} custom-call(s32[1]{0:T(128)} %bitcast.place, bf16[128,512]{1,0:T(8,128)(2,1)S(1)} %collective-permute-done.21.refs_0_, bf16[128,512]{1,0:T(8,128)(2,1)S(1)} %collective-permute-done.22.refs_1_, bf16[128,512]{1,0:T(8,128)(2,1)S(1)} %collective-permute-done.23.refs_2_, bf16[2048,1152]{1,0:T(8,128)(2,1)S(1)} %bitcast.2, ...), custom_call_target="tpu_custom_call" | custom-call | flops 452984832 | bytes 3538944 | tf_op jit(solution)/shard_map/pallas_call | solution.py:206
  84.3 2.0 %collective-permute-done.24.there_ref = f32[128,1152]{1,0:T(8,128)S(1)} collective-permute-done((f32[128,1152]{1,0:T(8,128)S(1)}, f32[128,1152]{1,0:T(8,128)S(1)}, u32[]{:S(2)}, u32[]{:S(2)}) %collective-permute-start.24) | collective-permute-done | bytes 589856 | tf_op jit(solution)/shard_map/ppermute | solution.py:190
  86.4 1.2 %collective-permute-start.27 = (f32[8,128]{1,0:T(8,128)S(1)}, f32[8,128]{1,0:T(8,128)S(1)}, u32[]{:S(2)}, u32[]{:S(2)}) collective-permute-start(f32[8,128]{1,0:T(8,128)S(1)} %get-tuple-element.82.refs_0_), channel_id=1, source_target_pairs={{0,6},{2,4},{4,2},{6,0},{1,7},{3,5},{5,3},{7,1},{8,14},{10,12},{12... | collective-permute-start | bytes 12296 | tf_op jit(solution)/shard_map/ppermute | solution.py:190
  87.6 1.3 %collective-permute-start.26 = (f32[8,128]{1,0:T(8,128)S(1)}, f32[8,128]{1,0:T(8,128)S(1)}, u32[]{:S(2)}, u32[]{:S(2)}) collective-permute-start(f32[8,128]{1,0:T(8,128)S(1)} %get-tuple-element.82.refs_0_), channel_id=1, source_target_pairs={{0,4},{2,6},{4,0},{6,2},{1,5},{3,7},{5,1},{7,3},{8,12},{10,14},{12... | collective-permute-start | bytes 12296 | tf_op jit(solution)/shard_map/ppermute | solution.py:190
  88.9 1.0 %collective-permute-start.25 = (f32[8,128]{1,0:T(8,128)S(1)}, f32[8,128]{1,0:T(8,128)S(1)}, u32[]{:S(2)}, u32[]{:S(2)}) collective-permute-start(f32[8,128]{1,0:T(8,128)S(1)} %get-tuple-element.82.refs_0_), channel_id=1, source_target_pairs={{0,2},{2,0},{4,6},{6,4},{1,3},{3,1},{5,7},{7,5},{8,10},{10,8},{12,... | collective-permute-start | bytes 12296 | tf_op jit(solution)/shard_map/ppermute | solution.py:190
  89.9 1.0 %collective-permute-done.27.refs_3_ = f32[8,128]{1,0:T(8,128)S(1)} collective-permute-done((f32[8,128]{1,0:T(8,128)S(1)}, f32[8,128]{1,0:T(8,128)S(1)}, u32[]{:S(2)}, u32[]{:S(2)}) %collective-permute-start.27) | collective-permute-done | bytes 4128 | tf_op jit(solution)/shard_map/ppermute | solution.py:190
  91.2 1.3 %collective-permute-done.25.refs_1_ = f32[8,128]{1,0:T(8,128)S(1)} collective-permute-done((f32[8,128]{1,0:T(8,128)S(1)}, f32[8,128]{1,0:T(8,128)S(1)}, u32[]{:S(2)}, u32[]{:S(2)}) %collective-permute-start.25) | collective-permute-done | bytes 4128 | tf_op jit(solution)/shard_map/ppermute | solution.py:190
  92.5 1.0 %shard_map.133 = bf16[32,4,1152]{2,1,0:T(4,128)(2,1)} custom-call(s32[1]{0:T(128)} %bitcast.place, bf16[32,4,1152]{2,1,0:T(4,128)(2,1)S(1)} %copy-done.6, f32[128,1152]{1,0:T(8,128)S(1)} %get-tuple-element.81.attended_ref, f32[1152]{0:T(1024)S(1)} %copy-done.11, f32[8,128]{1,0:T(8,128)S(1)} %get-tuple-element.82.refs_0_, ...), custom_call_target="tpu_custom_call" | custom-call | flops 589824 | bytes 1179648 | tf_op jit(solution)/shard_map/pallas_call | solution.py:206
  (61 shorter events, 4.7 us)
Async XLA Ops:
  0.0 9.7 %copy-start.1 = (bf16[512,1024]{1,0:T(8,128)(2,1)S(1)}, bf16[512,1024]{1,0:T(8,128)(2,1)}, u32[]{:S(2)}) copy-start(bf16[512,1024]{1,0:T(8,128)(2,1)} %v_ref.13) | copy-start | bytes 3145732
  0.0 9.7 %copy-start = (bf16[512,1024]{1,0:T(8,128)(2,1)S(1)}, bf16[512,1024]{1,0:T(8,128)(2,1)}, u32[]{:S(2)}) copy-start(bf16[512,1024]{1,0:T(8,128)(2,1)} %k_ref.13) | copy-start | bytes 3145732
  0.0 15.2 %copy-start.12 = (s32[32]{0:T(128)S(1)}, s32[32]{0:T(128)}, u32[]{:S(2)}) copy-start(s32[32]{0:T(128)} %lengths.1) | copy-start | bytes 388
  5.2 10.5 %collective-permute-start = (bf16[144,512]{1,0:T(8,128)(2,1)}, bf16[144,512]{1,0:T(8,128)(2,1)S(1)}, u32[]{:S(2)}, u32[]{:S(2)}) collective-permute-start(bf16[144,512]{1,0:T(8,128)(2,1)} %get-tuple-element.45), channel_id=1, source_target_pairs={{0,2},{2,0},{4,6},{6,4},{1,3},{3,1},{5,7},{7,5},{8,10},{10,8},{12,... | collective-permute-start | bytes 442376 | tf_op jit(solution)/shard_map/ppermute | solution.py:190
  8.2 8.7 %collective-permute-start.1 = (bf16[144,512]{1,0:T(8,128)(2,1)}, bf16[144,512]{1,0:T(8,128)(2,1)S(1)}, u32[]{:S(2)}, u32[]{:S(2)}) collective-permute-start(bf16[144,512]{1,0:T(8,128)(2,1)} %get-tuple-element.46), channel_id=1, source_target_pairs={{0,4},{2,6},{4,0},{6,2},{1,5},{3,7},{5,1},{7,3},{8,12},{10,14},{12... | collective-permute-start | bytes 442376 | tf_op jit(solution)/shard_map/ppermute | solution.py:190
  9.7 7.9 %collective-permute-start.2 = (bf16[144,512]{1,0:T(8,128)(2,1)}, bf16[144,512]{1,0:T(8,128)(2,1)S(1)}, u32[]{:S(2)}, u32[]{:S(2)}) collective-permute-start(bf16[144,512]{1,0:T(8,128)(2,1)} %get-tuple-element.47), channel_id=1, source_target_pairs={{0,6},{2,4},{4,2},{6,0},{1,7},{3,5},{5,3},{7,1},{8,14},{10,12},{12... | collective-permute-start | bytes 442376 | tf_op jit(solution)/shard_map/ppermute | solution.py:190
  9.7 0.7 copy-start.9
  11.7 18.0 %collective-permute-start.9 = (bf16[512,256]{1,0:T(8,128)(2,1)}, bf16[512,256]{1,0:T(8,128)(2,1)S(1)}, u32[]{:S(2)}, u32[]{:S(2)}) collective-permute-start(bf16[512,256]{1,0:T(8,128)(2,1)} %get-tuple-element.58), channel_id=1, source_target_pairs={{0,2},{2,0},{4,6},{6,4},{1,3},{3,1},{5,7},{7,5},{8,10},{10,8},{12,... | collective-permute-start | bytes 786440 | tf_op jit(solution)/shard_map/ppermute | solution.py:190
  13.6 17.8 %collective-permute-start.10 = (bf16[512,256]{1,0:T(8,128)(2,1)}, bf16[512,256]{1,0:T(8,128)(2,1)S(1)}, u32[]{:S(2)}, u32[]{:S(2)}) collective-permute-start(bf16[512,256]{1,0:T(8,128)(2,1)} %get-tuple-element.59), channel_id=1, source_target_pairs={{0,4},{2,6},{4,0},{6,2},{1,5},{3,7},{5,1},{7,3},{8,12},{10,14},{12... | collective-permute-start | bytes 786440 | tf_op jit(solution)/shard_map/ppermute | solution.py:190
  15.7 17.0 %collective-permute-start.11 = (bf16[512,256]{1,0:T(8,128)(2,1)S(1)}, bf16[512,256]{1,0:T(8,128)(2,1)S(1)}, u32[]{:S(2)}, u32[]{:S(2)}) collective-permute-start(bf16[512,256]{1,0:T(8,128)(2,1)S(1)} %get-tuple-element.60), channel_id=1, source_target_pairs={{0,6},{2,4},{4,2},{6,0},{1,7},{3,5},{5,3},{7,1},{8,14},{10,12},{12... | collective-permute-start | bytes 786440 | tf_op jit(solution)/shard_map/ppermute | solution.py:190
  17.6 1.0 %copy-start.8 = (f32[128,512]{1,0:T(8,128)S(1)}, f32[128,512]{1,0:T(8,128)}, u32[]{:S(2)}) copy-start(f32[128,512]{1,0:T(8,128)} %get-tuple-element.44.own_ref) | copy-start | bytes 786436
  18.6 0.7 copy-start.10
  19.5 13.7 %collective-permute-start.8 = (bf16[512,128]{1,0:T(8,128)(2,1)S(1)}, bf16[512,128]{1,0:T(8,128)(2,1)S(1)}, u32[]{:S(2)}, u32[]{:S(2)}) collective-permute-start(bf16[512,128]{1,0:T(8,128)(2,1)S(1)} %get-tuple-element.49.refs_0_.q_ref), channel_id=1, source_target_pairs={{0,24},{8,16},{16,8},{24,0},{1,25},{9,17},{17,9},{25,1},{2,26},{10... | collective-permute-start | bytes 393224 | tf_op jit(solution)/shard_map/ppermute | solution.py:190
  23.1 11.6 %collective-permute-start.7 = (bf16[512,128]{1,0:T(8,128)(2,1)S(1)}, bf16[512,128]{1,0:T(8,128)(2,1)S(1)}, u32[]{:S(2)}, u32[]{:S(2)}) collective-permute-start(bf16[512,128]{1,0:T(8,128)(2,1)S(1)} %get-tuple-element.49.refs_0_.q_ref), channel_id=1, source_target_pairs={{0,16},{8,24},{16,0},{24,8},{1,17},{9,25},{17,1},{25,9},{2,18},{10... | collective-permute-start | bytes 393224 | tf_op jit(solution)/shard_map/ppermute | solution.py:190
  23.2 1.7 %copy-start.4 = (bf16[1152,1024]{1,0:T(8,128)(2,1)S(1)}, bf16[1152,1024]{1,0:T(8,128)(2,1)}, u32[]{:S(2)}) copy-start(bf16[1152,1024]{1,0:T(8,128)(2,1)} %k_ref.7) | copy-start | bytes 7077892
  24.8 1.7 %copy-start.5 = (bf16[1152,1024]{1,0:T(8,128)(2,1)S(1)}, bf16[1152,1024]{1,0:T(8,128)(2,1)}, u32[]{:S(2)}) copy-start(bf16[1152,1024]{1,0:T(8,128)(2,1)} %v_ref.7) | copy-start | bytes 7077892
  26.5 1.0 %copy-start.7 = (bf16[128,1152]{1,0:T(8,128)(2,1)S(1)}, bf16[128,1152]{1,0:T(8,128)(2,1)}, u32[]{:S(2)}) copy-start(bf16[128,1152]{1,0:T(8,128)(2,1)} %get-tuple-element.50.scaled_ref) | copy-start | bytes 884740
  27.4 24.6 %copy-start.3 = (bf16[8,256,1024]{2,1,0:T(8,128)(2,1)S(1)}, bf16[8,256,1024]{2,1,0:T(8,128)(2,1)}, u32[]{:S(2)}) copy-start(bf16[8,256,1024]{2,1,0:T(8,128)(2,1)} %refs_4_.3) | copy-start | bytes 12582916
  29.7 22.3 %copy-start.2 = (bf16[8,256,1024]{2,1,0:T(8,128)(2,1)S(1)}, bf16[8,256,1024]{2,1,0:T(8,128)(2,1)}, u32[]{:S(2)}) copy-start(bf16[8,256,1024]{2,1,0:T(8,128)(2,1)} %refs_3_.2) | copy-start | bytes 12582916
  29.7 7.2 %collective-permute-start.12 = (bf16[160,512]{1,0:T(8,128)(2,1)S(1)}, bf16[160,512]{1,0:T(8,128)(2,1)S(1)}, u32[]{:S(2)}, u32[]{:S(2)}) collective-permute-start(bf16[160,512]{1,0:T(8,128)(2,1)S(1)} %get-tuple-element.63), channel_id=1, source_target_pairs={{0,2},{2,0},{4,6},{6,4},{1,3},{3,1},{5,7},{7,5},{8,10},{10,8},{12,... | collective-permute-start | bytes 491528 | tf_op jit(solution)/shard_map/ppermute | solution.py:190
  31.4 5.0 %collective-permute-start.6 = (bf16[512,128]{1,0:T(8,128)(2,1)S(1)}, bf16[512,128]{1,0:T(8,128)(2,1)S(1)}, u32[]{:S(2)}, u32[]{:S(2)}) collective-permute-start(bf16[512,128]{1,0:T(8,128)(2,1)S(1)} %get-tuple-element.49.refs_0_.q_ref), channel_id=1, source_target_pairs={{0,8},{8,0},{16,24},{24,16},{1,9},{9,1},{17,25},{25,17},{2,10},{10... | collective-permute-start | bytes 393224 | tf_op jit(solution)/shard_map/ppermute | solution.py:190
  32.7 25.7 %collective-permute-start.3 = (bf16[512,256]{1,0:T(8,128)(2,1)S(1)}, bf16[512,256]{1,0:T(8,128)(2,1)S(1)}, u32[]{:S(2)}, u32[]{:S(2)}) collective-permute-start(bf16[512,256]{1,0:T(8,128)(2,1)S(1)} %get-tuple-element.55), channel_id=1, source_target_pairs={{0,2},{2,0},{4,6},{6,4},{1,3},{3,1},{5,7},{7,5},{8,10},{10,8},{12,... | collective-permute-start | bytes 786440 | tf_op jit(solution)/shard_map/ppermute | solution.py:190
  33.2 25.2 %collective-permute-start.4 = (bf16[512,256]{1,0:T(8,128)(2,1)S(1)}, bf16[512,256]{1,0:T(8,128)(2,1)S(1)}, u32[]{:S(2)}, u32[]{:S(2)}) collective-permute-start(bf16[512,256]{1,0:T(8,128)(2,1)S(1)} %get-tuple-element.56), channel_id=1, source_target_pairs={{0,4},{2,6},{4,0},{6,2},{1,5},{3,7},{5,1},{7,3},{8,12},{10,14},{12... | collective-permute-start | bytes 786440 | tf_op jit(solution)/shard_map/ppermute | solution.py:190
  34.8 23.6 %collective-permute-start.5 = (bf16[512,256]{1,0:T(8,128)(2,1)S(1)}, bf16[512,256]{1,0:T(8,128)(2,1)S(1)}, u32[]{:S(2)}, u32[]{:S(2)}) collective-permute-start(bf16[512,256]{1,0:T(8,128)(2,1)S(1)} %get-tuple-element.57), channel_id=1, source_target_pairs={{0,6},{2,4},{4,2},{6,0},{1,7},{3,5},{5,3},{7,1},{8,14},{10,12},{12... | collective-permute-start | bytes 786440 | tf_op jit(solution)/shard_map/ppermute | solution.py:190
  36.4 15.7 %collective-permute-start.13 = (bf16[160,512]{1,0:T(8,128)(2,1)S(1)}, bf16[160,512]{1,0:T(8,128)(2,1)S(1)}, u32[]{:S(2)}, u32[]{:S(2)}) collective-permute-start(bf16[160,512]{1,0:T(8,128)(2,1)S(1)} %get-tuple-element.64), channel_id=1, source_target_pairs={{0,4},{2,6},{4,0},{6,2},{1,5},{3,7},{5,1},{7,3},{8,12},{10,14},{12... | collective-permute-start | bytes 491528 | tf_op jit(solution)/shard_map/ppermute | solution.py:190
  36.9 15.2 %collective-permute-start.14 = (bf16[160,512]{1,0:T(8,128)(2,1)S(1)}, bf16[160,512]{1,0:T(8,128)(2,1)S(1)}, u32[]{:S(2)}, u32[]{:S(2)}) collective-permute-start(bf16[160,512]{1,0:T(8,128)(2,1)S(1)} %get-tuple-element.65), channel_id=1, source_target_pairs={{0,6},{2,4},{4,2},{6,0},{1,7},{3,5},{5,3},{7,1},{8,14},{10,12},{12... | collective-permute-start | bytes 491528 | tf_op jit(solution)/shard_map/ppermute | solution.py:190
  59.4 15.7 %collective-permute-start.15 = (bf16[528,128]{1,0:T(8,128)(2,1)S(1)}, bf16[528,128]{1,0:T(8,128)(2,1)S(1)}, u32[]{:S(2)}, u32[]{:S(2)}) collective-permute-start(bf16[528,128]{1,0:T(8,128)(2,1)S(1)} %shard_map.125.refs_12_), channel_id=1, source_target_pairs={{0,8},{8,0},{16,24},{24,16},{1,9},{9,1},{17,25},{25,17},{2,10},{10... | collective-permute-start | bytes 405512 | tf_op jit(solution)/shard_map/ppermute | solution.py:190
  59.7 19.4 %slice-start = ((s8[4718592]{0:T(1024)(128)(4,1)}), s8[4194304]{0:T(1024)(128)(4,1)S(1)}, s32[]{:S(2)}) async-start(s8[4718592]{0:T(1024)(128)(4,1)} %bitcast.1), calls=%async_computation | async-start | bytes 8388608
  60.7 14.4 %collective-permute-start.16 = (bf16[528,128]{1,0:T(8,128)(2,1)S(1)}, bf16[528,128]{1,0:T(8,128)(2,1)S(1)}, u32[]{:S(2)}, u32[]{:S(2)}) collective-permute-start(bf16[528,128]{1,0:T(8,128)(2,1)S(1)} %shard_map.126.refs_13_), channel_id=1, source_target_pairs={{0,16},{8,24},{16,0},{24,8},{1,17},{9,25},{17,1},{25,9},{2,18},{10... | collective-permute-start | bytes 405512 | tf_op jit(solution)/shard_map/ppermute | solution.py:190
  63.6 15.5 %slice-start.1 = ((s8[4718592]{0:T(1024)(128)(4,1)}), s8[524288]{0:T(1024)(128)(4,1)S(1)}, s32[]{:S(2)}) async-start(s8[4718592]{0:T(1024)(128)(4,1)} %bitcast.1), calls=%async_computation.1 | async-start | bytes 1048576
  64.6 10.5 %collective-permute-start.17 = (bf16[528,128]{1,0:T(8,128)(2,1)S(1)}, bf16[528,128]{1,0:T(8,128)(2,1)S(1)}, u32[]{:S(2)}, u32[]{:S(2)}) collective-permute-start(bf16[528,128]{1,0:T(8,128)(2,1)S(1)} %shard_map.127.refs_14_), channel_id=1, source_target_pairs={{0,24},{8,16},{16,8},{24,0},{1,25},{9,17},{17,9},{25,1},{2,26},{10... | collective-permute-start | bytes 405512 | tf_op jit(solution)/shard_map/ppermute | solution.py:190
  66.0 4.0 %collective-permute-start.18 = (bf16[144,128]{1,0:T(8,128)(2,1)S(1)}, bf16[144,128]{1,0:T(8,128)(2,1)S(1)}, u32[]{:S(2)}, u32[]{:S(2)}) collective-permute-start(bf16[144,128]{1,0:T(8,128)(2,1)S(1)} %get-tuple-element.78), channel_id=1, source_target_pairs={{0,2},{2,0},{4,6},{6,4},{1,3},{3,1},{5,7},{7,5},{8,10},{10,8},{12,... | collective-permute-start | bytes 110600 | tf_op jit(solution)/shard_map/ppermute | solution.py:190
  66.9 5.5 %collective-permute-start.19 = (bf16[144,128]{1,0:T(8,128)(2,1)S(1)}, bf16[144,128]{1,0:T(8,128)(2,1)S(1)}, u32[]{:S(2)}, u32[]{:S(2)}) collective-permute-start(bf16[144,128]{1,0:T(8,128)(2,1)S(1)} %get-tuple-element.79), channel_id=1, source_target_pairs={{0,4},{2,6},{4,0},{6,2},{1,5},{3,7},{5,1},{7,3},{8,12},{10,14},{12... | collective-permute-start | bytes 110600 | tf_op jit(solution)/shard_map/ppermute | solution.py:190
  69.9 5.2 %collective-permute-start.20 = (bf16[144,128]{1,0:T(8,128)(2,1)S(1)}, bf16[144,128]{1,0:T(8,128)(2,1)S(1)}, u32[]{:S(2)}, u32[]{:S(2)}) collective-permute-start(bf16[144,128]{1,0:T(8,128)(2,1)S(1)} %get-tuple-element.80), channel_id=1, source_target_pairs={{0,6},{2,4},{4,2},{6,0},{1,7},{3,5},{5,3},{7,1},{8,14},{10,12},{12... | collective-permute-start | bytes 110600 | tf_op jit(solution)/shard_map/ppermute | solution.py:190
  75.5 6.0 %collective-permute-start.23 = (bf16[128,512]{1,0:T(8,128)(2,1)S(1)}, bf16[128,512]{1,0:T(8,128)(2,1)S(1)}, u32[]{:S(2)}, u32[]{:S(2)}) collective-permute-start(bf16[128,512]{1,0:T(8,128)(2,1)S(1)} %shard_map.129.refs_0_), channel_id=1, source_target_pairs={{0,6},{2,4},{4,2},{6,0},{1,7},{3,5},{5,3},{7,1},{8,14},{10,12},{12... | collective-permute-start | bytes 393224 | tf_op jit(solution)/shard_map/ppermute | solution.py:190
  77.0 5.9 %collective-permute-start.22 = (bf16[128,512]{1,0:T(8,128)(2,1)S(1)}, bf16[128,512]{1,0:T(8,128)(2,1)S(1)}, u32[]{:S(2)}, u32[]{:S(2)}) collective-permute-start(bf16[128,512]{1,0:T(8,128)(2,1)S(1)} %shard_map.129.refs_0_), channel_id=1, source_target_pairs={{0,4},{2,6},{4,0},{6,2},{1,5},{3,7},{5,1},{7,3},{8,12},{10,14},{12... | collective-permute-start | bytes 393224 | tf_op jit(solution)/shard_map/ppermute | solution.py:190
  78.1 5.0 %collective-permute-start.21 = (bf16[128,512]{1,0:T(8,128)(2,1)S(1)}, bf16[128,512]{1,0:T(8,128)(2,1)S(1)}, u32[]{:S(2)}, u32[]{:S(2)}) collective-permute-start(bf16[128,512]{1,0:T(8,128)(2,1)S(1)} %shard_map.129.refs_0_), channel_id=1, source_target_pairs={{0,2},{2,0},{4,6},{6,4},{1,3},{3,1},{5,7},{7,5},{8,10},{10,8},{12,... | collective-permute-start | bytes 393224 | tf_op jit(solution)/shard_map/ppermute | solution.py:190
  79.5 13.0 %copy-start.6 = (bf16[32,4,1152]{2,1,0:T(4,128)(2,1)S(1)}, bf16[32,4,1152]{2,1,0:T(4,128)(2,1)}, u32[]{:S(2)}) copy-start(bf16[32,4,1152]{2,1,0:T(4,128)(2,1)} %x_ref.3) | copy-start | bytes 884740
  79.5 13.0 %copy-start.11 = (f32[1152]{0:T(1024)S(1)}, f32[1152]{0:T(1024)}, u32[]{:S(2)}) copy-start(f32[1152]{0:T(1024)} %gain_ref.3) | copy-start | bytes 13828
  84.2 2.1 %collective-permute-start.24 = (f32[128,1152]{1,0:T(8,128)S(1)}, f32[128,1152]{1,0:T(8,128)S(1)}, u32[]{:S(2)}, u32[]{:S(2)}) collective-permute-start(f32[128,1152]{1,0:T(8,128)S(1)} %shard_map.131.here_ref), channel_id=1, source_target_pairs={{0,1},{1,0},{2,3},{3,2},{4,5},{5,4},{6,7},{7,6},{8,9},{9,8},{10,11... | collective-permute-start | bytes 1769480 | tf_op jit(solution)/shard_map/ppermute | solution.py:190
  86.4 4.5 %collective-permute-start.27 = (f32[8,128]{1,0:T(8,128)S(1)}, f32[8,128]{1,0:T(8,128)S(1)}, u32[]{:S(2)}, u32[]{:S(2)}) collective-permute-start(f32[8,128]{1,0:T(8,128)S(1)} %get-tuple-element.82.refs_0_), channel_id=1, source_target_pairs={{0,6},{2,4},{4,2},{6,0},{1,7},{3,5},{5,3},{7,1},{8,14},{10,12},{12... | collective-permute-start | bytes 12296 | tf_op jit(solution)/shard_map/ppermute | solution.py:190
  87.6 3.6 %collective-permute-start.26 = (f32[8,128]{1,0:T(8,128)S(1)}, f32[8,128]{1,0:T(8,128)S(1)}, u32[]{:S(2)}, u32[]{:S(2)}) collective-permute-start(f32[8,128]{1,0:T(8,128)S(1)} %get-tuple-element.82.refs_0_), channel_id=1, source_target_pairs={{0,4},{2,6},{4,0},{6,2},{1,5},{3,7},{5,1},{7,3},{8,12},{10,14},{12... | collective-permute-start | bytes 12296 | tf_op jit(solution)/shard_map/ppermute | solution.py:190
  88.9 3.6 %collective-permute-start.25 = (f32[8,128]{1,0:T(8,128)S(1)}, f32[8,128]{1,0:T(8,128)S(1)}, u32[]{:S(2)}, u32[]{:S(2)}) collective-permute-start(f32[8,128]{1,0:T(8,128)S(1)} %get-tuple-element.82.refs_0_), channel_id=1, source_target_pairs={{0,2},{2,0},{4,6},{6,4},{1,3},{3,1},{5,7},{7,5},{8,10},{10,8},{12,... | collective-permute-start | bytes 12296 | tf_op jit(solution)/shard_map/ppermute | solution.py:190

commit v3 on v2

--- a/solution.py
+++ b/solution.py
@@ -14,10 +14,15 @@
 
 SOFTCAP = 50.0
 EPSILON = 1e-06
+SPREAD_AT = 2
 LOG2_E = 1.4426950408889634
 LANES = 128
-VMEM_LIMIT = 32 * 1024 * 1024
-LARGE_VMEM_LIMIT = 60 * 1024 * 1024
+VMEM_LIMIT = 24 * 1024 * 1024
+FIRST_LIMIT = 59 * 1024 * 1024
+ROPE_LIMIT = 59 * 1024 * 1024
+PAIR_LIMIT = 59 * 1024 * 1024
+SUFFIX_LIMIT = 24 * 1024 * 1024
+QUERY_SCALE = (MODEL_WIDTH // QUERY_HEADS) ** (-0.5)
 
 
 def apply_rotation(values, token_positions, heads):
@@ -277,139 +282,136 @@
     return values * cosine + pltpu.roll(values, HEAD_SIZE // 2, 1) * sine
 
 
-def flat_rows(ref):
-    members, steps, width = ref.shape
-    return ref[...].astype(jnp.float32).reshape(members * steps, width)
-
-
 def gain_row(ref):
     return ref[...].reshape(1, ref.shape[0])
 
 
-def query_projection_kernel(place, x_ref, gain_ref, w_ref, *refs):
-    *sent, own_ref, squares_ref, scaled_ref = refs
-    step = pl.program_id(0)
-    rows = scaled_ref.shape[0]
-
-    @pl.when(step == 0)
-    def _():
-        x = flat_rows(x_ref)
-        scaled_ref[...] = (x * gain_row(gain_ref)).astype(jnp.bfloat16)
-        total = jnp.sum(x * x, axis=1, keepdims=True)
-        across = jnp.broadcast_to(total, (rows, LANES)).T[:8]
-        squares_ref[...] = across
-        tail = split_rows(across)
-        for ref in sent:
-            ref[rows:, :] = jnp.zeros((16, ref.shape[1]), jnp.bfloat16)
-            ref[rows:, :rows] = tail
-
-    product = jnp.dot(scaled_ref[...], w_ref[...], preferred_element_type=jnp.float32)
-    for index, ref in enumerate(sent):
-
-        @pl.when(step == index)
-        def _():
-            ref[:rows, :] = product.astype(jnp.bfloat16)
-
-    @pl.when(step == len(sent))
-    def _():
-        own_ref[...] = product
-
-
-def query_projection(place, x, gain, weights, parts):
+def copy_in(source, target, semaphore):
+    copy = pltpu.make_async_copy(source, target, semaphore)
+    copy.start()
+    return copy
+
+
+def block_of(place, mask, width):
+    return pl.ds(pl.multiple_of((place[0] ^ mask) * width, width), width)
+
+
+def query_projection_kernel(parts, place, gain_ref, x_hbm, w_hbm, keys_hbm, values_hbm, *refs):
+    blocks, refs = refs[: parts - 1], refs[parts - 1 :]
+    *sent, own_ref, squares_ref, scaled_ref, x_ref, w_ref, block_ref, semaphores, block_semaphores = refs
+    rows, columns = own_ref.shape
+    masks = (*range(1, len(sent) + 1), 0)
+    x_copy = copy_in(x_hbm, x_ref, semaphores.at[len(masks)])
+    w_copies = [
+        copy_in(w_hbm.at[:, block_of(place, mask, columns)], w_ref.at[mask], semaphores.at[mask])
+        for mask in masks
+    ]
+    width = blocks[0].shape[1] // 2
+    block_copies = [
+        copy_in(
+            source.at[:, block_of(place, mask, width)],
+            block_ref.at[mask - 1, :, half * width : (half + 1) * width],
+            block_semaphores.at[mask - 1, half],
+        )
+        for mask in range(1, parts)
+        for half, source in enumerate((keys_hbm, values_hbm))
+    ]
+    x_copy.wait()
+    x = x_ref[...].astype(jnp.float32).reshape(rows, x_ref.shape[2])
+    scaled_ref[...] = (x * gain_row(gain_ref)).astype(jnp.bfloat16)
+    total = jnp.sum(x * x, axis=1, keepdims=True)
+    across = jnp.broadcast_to(total, (rows, LANES)).T[:8]
+    squares_ref[...] = across
+    tail = split_rows(across)
+    for ref in sent:
+        ref[rows:, :] = jnp.zeros((16, ref.shape[1]), jnp.bfloat16)
+        ref[rows:, :rows] = tail
+    for mask, copy, ref in zip(masks, w_copies, (*sent, own_ref)):
+        copy.wait()
+        if mask == SPREAD_AT:
+            for block_copy in block_copies:
+                block_copy.wait()
+            block_copies = [
+                copy_in(block_ref.at[index], target, block_semaphores.at[index, 0])
+                for index, target in enumerate(blocks)
+            ]
+        product = jnp.dot(scaled_ref[...], w_ref[mask], preferred_element_type=jnp.float32)
+        ref[:rows, :] = product.astype(ref.dtype)
+    for copy in block_copies:
+        copy.wait()
+
+
+def query_projection(place, x, gain, weights, keys, values, parts):
     members, steps, width = x.shape
     rows = members * steps
     columns = weights.shape[1] // parts
+    blocks = [shape((keys.shape[0], 2 * keys.shape[1] // parts), keys.dtype)] * (parts - 1)
     outs = [shape((rows + 16, columns), jnp.bfloat16)] * (parts - 1) + [
         shape((rows, columns), jnp.float32),
         shape((8, rows), jnp.float32),
         shape((rows, width), jnp.bfloat16),
     ]
+    far = pl.BlockSpec(memory_space=pl.ANY)
     return call(
-        query_projection_kernel,
+        functools.partial(query_projection_kernel, parts),
         (place,),
-        (x, gain, weights),
-        outs,
+        (gain, x, weights, keys, values),
+        blocks + outs,
+        [whole(gain), far, far, far, far],
+        [far] * (parts - 1) + [whole(a) for a in outs],
+        (1,),
         [
-            whole(x),
-            whole(gain),
-            pl.BlockSpec((width, columns), lambda i, p: (0, p[0] ^ ((i + 1) % parts))),
+            pltpu.VMEM(x.shape, x.dtype),
+            pltpu.VMEM((parts, width, columns), weights.dtype),
+            pltpu.VMEM((parts - 1, *blocks[0].shape), keys.dtype),
+            pltpu.SemaphoreType.DMA((parts + 1,)),
+            pltpu.SemaphoreType.DMA((parts - 1, 2)),
         ],
-        [whole(a) for a in outs],
-        (parts,),
-        [],
         2 * rows * width * weights.shape[1],
         2 * width * weights.shape[1],
-        LARGE_VMEM_LIMIT,
-    )
-
-
-def cache_columns_kernel(place, k_ref, v_ref, token_ref, *outs):
-    step = pl.program_id(0)
-    width = k_ref.shape[1]
-    for index, ref in enumerate(outs):
-
-        @pl.when(step == index)
-        def _():
-            ref[:, :width] = k_ref[...]
-            ref[:, width:] = v_ref[...]
-
-
-def cache_columns(place, keys, values, head, heads, parts, token):
-    tokens = keys.shape[0]
-    chosen = pl.BlockSpec(
-        (tokens, HEAD_SIZE), lambda i, p: (0, (p[0] ^ (i + 1)) * heads + head)
-    )
-    outs = [shape((tokens, 2 * HEAD_SIZE), jnp.bfloat16)] * (parts - 1)
-    return call(
-        cache_columns_kernel,
-        (place,),
-        (keys, values, token),
-        outs,
-        [chosen, chosen, corner(token)],
-        [whole(a) for a in outs],
-        (parts - 1,),
-        [],
-        0,
-        8 * (parts - 1) * tokens * HEAD_SIZE,
-    )
-
-
-def pair_projection_kernel(place, scaled_ref, k_ref, v_ref, *refs):
-    parts = len(refs) // 2 + 1
-    queries, (own_ref, *outs) = refs[: parts - 1], refs[parts - 1 :]
-    rows = scaled_ref.shape[0]
-    columns = k_ref.shape[1]
-    step = pl.program_id(0)
-    terms = [
-        jnp.dot(scaled_ref[...], w_ref[...], preferred_element_type=jnp.float32)
-        for w_ref in (k_ref, v_ref)
-    ]
-
-    def store(ref):
-        for index, term in enumerate(terms):
-            ref[:rows, index * columns : (index + 1) * columns] = term.astype(ref.dtype)
-
-    for index, (query_ref, ref) in enumerate(zip(queries, outs)):
-
-        @pl.when(step == index)
-        def _():
-            store(ref)
-            tall = ref.shape[0] - rows
-            for piece in range(query_ref.shape[0] // tall):
-                at = slice(piece * HEAD_SIZE, (piece + 1) * HEAD_SIZE)
-                ref[rows:, at] = query_ref[piece * tall : (piece + 1) * tall, :]
-
-    @pl.when(step == parts - 1)
-    def _():
-        store(own_ref)
+        FIRST_LIMIT,
+    )
+
+
+def pair_projection_kernel(place, scaled_ref, k_hbm, v_hbm, *refs):
+    parts = len(refs) // 2
+    queries, (own_ref, *outs), (w_ref, semaphores) = (
+        refs[: parts - 1],
+        refs[parts - 1 : 2 * parts - 1],
+        refs[2 * parts - 1 :],
+    )
+    rows, width = own_ref.shape
+    columns = width // 2
+    masks = (*range(1, parts), 0)
+    copies = {}
+    for mask in masks:
+        at = block_of(place, mask, columns)
+        copies[mask] = [
+            copy_in(
+                source.at[:, at],
+                w_ref.at[mask, :, half * columns : (half + 1) * columns],
+                semaphores.at[mask, half],
+            )
+            for half, source in enumerate((k_hbm, v_hbm))
+        ]
+    for ref, out_ref in zip(queries, outs):
+        tall = out_ref.shape[0] - rows
+        for piece in range(ref.shape[0] // tall):
+            out_ref[rows:, head_lanes(piece)] = ref[piece * tall : (piece + 1) * tall, :]
+    for mask in masks:
+        for copy in copies[mask]:
+            copy.wait()
+        term = jnp.dot(scaled_ref[...], w_ref[mask], preferred_element_type=jnp.float32)
+        target = outs[mask - 1] if mask else own_ref
+        target[:rows, :] = term.astype(target.dtype)
 
 
 def pair_projection(place, scaled, key_weights, value_weights, queries):
     parts = len(queries) + 1
     rows, width = scaled.shape
     columns = key_weights.shape[1] // parts
-    tall = queries[0].shape[0] * HEAD_SIZE // (2 * columns)
-    chosen = pl.BlockSpec((width, columns), lambda i, p: (0, p[0] ^ ((i + 1) % parts)))
+    far = pl.BlockSpec(memory_space=pl.ANY)
+    tall = queries[0].size // (2 * columns)
     outs = [shape((rows, 2 * columns), jnp.float32)] + [
         shape((rows + tall, 2 * columns), jnp.bfloat16)
     ] * (parts - 1)
@@ -418,18 +420,30 @@
         (place,),
         (scaled, key_weights, value_weights, *queries),
         outs,
-        [whole(scaled), chosen, chosen] + [whole(a) for a in queries],
+        [whole(scaled), far, far] + [whole(a) for a in queries],
         [whole(a) for a in outs],
-        (parts,),
-        [],
+        (1,),
+        [
+            pltpu.VMEM((parts, width, 2 * columns), key_weights.dtype),
+            pltpu.SemaphoreType.DMA((parts, 2)),
+        ],
         4 * rows * width * key_weights.shape[1],
         4 * width * key_weights.shape[1],
-    )
+        PAIR_LIMIT,
+    )
+
+
+def paired_heads(values, cosine, sine):
+    tiles = [
+        rotated(values[:, at : at + HEAD_SIZE], cosine, sine).reshape(-1, 8, HEAD_SIZE)
+        for at in (0, HEAD_SIZE)
+    ]
+    return jnp.stack(interleave(*tiles), axis=1).reshape(2 * values.shape[0], HEAD_SIZE)
 
 
 def query_rope_kernel(parts, place, own_ref, *refs):
-    received, (squares_ref, cos_ref, sin_ref, query_ref, *rest) = refs[: parts - 1], refs[parts - 1 :]
-    *suffix_refs, inverse_ref, held = rest
+    received, refs = refs[: parts - 1], refs[parts - 1 :]
+    squares_ref, cos_ref, sin_ref, query_ref, *suffix_refs, inverse_ref, held = refs
     rows, columns = own_ref.shape
     squares = squares_ref[0:1, :]
     total = own_ref[...]
@@ -438,28 +452,18 @@
         total = total + ref[:rows, :].astype(jnp.float32)
     inverse = lax.rsqrt(down_rows(squares) / MODEL_WIDTH + EPSILON)
     inverse_ref[...] = inverse
-    scale = (MODEL_WIDTH // QUERY_HEADS) ** (-0.5)
-    cosine = cos_ref[...] * inverse * scale
-    sine = sin_ref[...] * inverse * scale
+    cosine = cos_ref[...] * inverse * QUERY_SCALE
+    sine = sin_ref[...] * inverse * QUERY_SCALE
     pair = 2 * HEAD_SIZE
+    share = 2 * rows // parts
     for head in range(columns // pair):
-        tiles = []
-        for member in range(2):
-            at = head * pair + member * HEAD_SIZE
-            turned = rotated(total[:, at : at + HEAD_SIZE], cosine, sine)
-            tiles.append(turned.reshape(rows // 8, 8, HEAD_SIZE))
-        even, odd = interleave(*tiles)
-        held[head * 2 * rows : (head + 1) * 2 * rows, :] = jnp.stack([even, odd], axis=1).reshape(
-            2 * rows, HEAD_SIZE
-        )
-    query_ref[...] = held[...].astype(jnp.bfloat16)
-    share = 2 * rows // parts
-    for mask, ref in enumerate(suffix_refs):
-        for head in range(columns // pair):
-            first = pl.multiple_of(head * 2 * rows + (place[0] ^ mask) * share, share)
-            ref[head * share : (head + 1) * share, :] = held[pl.ds(first, share), :].astype(
-                jnp.bfloat16
-            )
+        at = slice(head * 2 * rows, (head + 1) * 2 * rows)
+        held[...] = paired_heads(total[:, head * pair : (head + 1) * pair], cosine, sine)
+        query_ref[at, :] = held[...].astype(jnp.bfloat16)
+        for mask, ref in enumerate(suffix_refs):
+            ref[head * share : (head + 1) * share, :] = held[
+                block_of(place, mask, share), :
+            ].astype(jnp.bfloat16)
 
 
 def query_rope(place, own, received, squares, cosine, sine, parts):
@@ -479,9 +483,10 @@
         [whole(a) for a in operands],
         [whole(a) for a in outs],
         (1,),
-        [pltpu.VMEM((count, HEAD_SIZE), jnp.float32)],
+        [pltpu.VMEM((2 * rows, HEAD_SIZE), jnp.float32)],
         10 * rows * columns,
         12 * rows * columns,
+        ROPE_LIMIT,
     )
 
 
@@ -497,108 +502,104 @@
     return result
 
 
-def cached_pairs(k_ref, v_ref, received):
-    return [(k_ref[...], v_ref[...])] + [
-        (ref[:, :HEAD_SIZE], ref[:, HEAD_SIZE:]) for ref in received
-    ]
-
-
 def total_rows(totals):
-    return [
-        totals[at : at + LANES].T[0:1] for at in range(0, totals.shape[0], LANES)
-    ]
+    return [totals[at : at + LANES].T[0:1] for at in range(0, totals.shape[0], LANES)]
+
+
+def head_lanes(head):
+    return slice(head * HEAD_SIZE, (head + 1) * HEAD_SIZE)
+
+
+def received_pair(ref, head, heads):
+    return ref[:, head_lanes(head)], ref[:, head_lanes(heads + head)]
 
 
 def prompt_first_kernel(chunks, place, *refs):
     queries, refs = refs[:chunks], refs[chunks:]
     k_ref, v_ref, *received = refs[: -2 * chunks]
     outs = refs[-2 * chunks :]
+    heads = k_ref.shape[1] // HEAD_SIZE
+    count = queries[0].shape[0] // heads
     for index, query_ref in enumerate(queries):
         sum_ref, total_ref = outs[2 * index : 2 * index + 2]
-        result = attend(query_ref[...], cached_pairs(k_ref, v_ref, received))
-        sum_ref[...] = result[:, :HEAD_SIZE].astype(sum_ref.dtype)
-        if index == 0:
-            total_ref[...] = result[:, HEAD_SIZE:]
-        else:
-            total_ref[...] = jnp.zeros(total_ref.shape, jnp.float32)
-            for row, values in enumerate(total_rows(result[:, HEAD_SIZE:])):
-                total_ref[row : row + 1, :] = values
-
-
-def prompt_first(place, queries, prompt_keys, prompt_values, received, heads):
-    count = queries[0].shape[0] // heads
+        for head in range(heads):
+            at = slice(head * count, (head + 1) * count)
+            pairs = [(k_ref[:, head_lanes(head)], v_ref[:, head_lanes(head)])]
+            pairs += [received_pair(ref, head, heads) for ref in received]
+            result = attend(query_ref[at, :], pairs)
+            sum_ref[at, :] = result[:, :HEAD_SIZE]
+            total_ref[at, :] = result[:, HEAD_SIZE:]
+
+
+def prompt_first(place, queries, prompt_keys, prompt_values, received, parts):
     tokens = prompt_keys.shape[0]
-    chosen = pl.BlockSpec((tokens, HEAD_SIZE), lambda i, p: (0, p[0] * heads))
-    outs = [shape((count, HEAD_SIZE), jnp.float32)] * 2 + [
-        shape((count, HEAD_SIZE), jnp.bfloat16),
-        shape((8, LANES), jnp.float32),
-    ] * (len(queries) - 1)
-    parts = len(received) + 1
+    chosen = pl.BlockSpec((tokens, prompt_keys.shape[1] // parts), lambda i, p: (0, p[0]))
+    outs = [shape(queries[0].shape, jnp.float32)] * (2 * len(queries))
     return call(
         functools.partial(prompt_first_kernel, len(queries)),
         (place,),
         (*queries, prompt_keys, prompt_values, *received),
         outs,
-        [pl.BlockSpec((count, HEAD_SIZE), lambda *_: (0, 0))] * len(queries)
-        + [chosen, chosen]
-        + [whole(a) for a in received],
+        [whole(a) for a in queries] + [chosen, chosen] + [whole(a) for a in received],
         [whole(a) for a in outs],
         (1,),
         [],
-        6 * len(queries) * count * parts * tokens * HEAD_SIZE,
+        6 * len(queries) * queries[0].size * (len(received) + 1) * tokens,
         4 * parts * tokens * HEAD_SIZE,
     )
 
 
-def prompt_second_kernel(place, q_ref, k_ref, v_ref, *refs):
-    *received, sum_ref, total_ref, token_ref, out_ref, held = refs
-    count = q_ref.shape[0]
-    result = attend(q_ref[...], cached_pairs(k_ref, v_ref, received))
-    out_ref[:count, :] = sum_ref[...]
-    out_ref[count : 2 * count, :] = result[:, :HEAD_SIZE].astype(jnp.bfloat16)
-    held[...] = total_ref[...]
-    for row, values in enumerate(total_rows(result[:, HEAD_SIZE:])):
-        at = count // LANES + row
-        held[at : at + 1, :] = values
-    out_ref[2 * count :, :] = split_rows(held[...])
-
-
-def prompt_second(place, queries, prompt_keys, prompt_values, received, first, heads, token):
-    count = queries.shape[0] // heads
-    tokens = prompt_keys.shape[0]
-    chosen = pl.BlockSpec((tokens, HEAD_SIZE), lambda i, p: (0, p[0] * heads + 1))
-    out = shape((heads * count + 16, HEAD_SIZE), jnp.bfloat16)
-    parts = len(received) + 1
+def prompt_last_kernel(place, q_ref, *refs):
+    *blocks, sum_ref, total_ref, out_ref, held = refs
+    heads = blocks[0].shape[1] // (2 * HEAD_SIZE)
+    count = q_ref.shape[0] // heads
+    held[...] = jnp.zeros(held.shape, jnp.float32)
+    for head in range(heads):
+        at = slice(head * count, (head + 1) * count)
+        result = attend(q_ref[at, :], [received_pair(ref, head, heads) for ref in blocks])
+        out_ref[at, :] = (sum_ref[at, :] + result[:, :HEAD_SIZE]).astype(jnp.bfloat16)
+        for row, values in enumerate(total_rows(total_ref[at, :] + result[:, HEAD_SIZE:])):
+            to = head * count // LANES + row
+            held[to : to + 1, :] = values
+    out_ref[heads * count :, :] = split_rows(held[...])
+
+
+def prompt_last(place, queries, blocks, first):
+    out = shape((queries.shape[0] + 16, HEAD_SIZE), jnp.bfloat16)
+    operands = (queries, *blocks, *first)
     return call(
-        prompt_second_kernel,
+        prompt_last_kernel,
         (place,),
-        (queries, prompt_keys, prompt_values, *received, *first, token),
+        operands,
         out,
-        [pl.BlockSpec((count, HEAD_SIZE), lambda *_: (1, 0)), chosen, chosen]
-        + [whole(a) for a in (*received, *first)]
-        + [corner(token)],
+        [whole(a) for a in operands],
         whole(out),
         (1,),
         [pltpu.VMEM((8, LANES), jnp.float32)],
-        6 * count * parts * tokens * HEAD_SIZE,
-        4 * parts * tokens * HEAD_SIZE,
+        6 * queries.size * len(blocks) * blocks[0].shape[0],
+        2 * len(blocks) * blocks[0].size,
     )
 
 
 def own_kernel(parts, place, q_ref, k_ref, v_ref, *refs):
+    blocks, refs = refs[: parts - 1], refs[parts - 1 :]
+    pair_ref, refs = refs[0], refs[1:]
     received, refs = refs[: parts - 1], refs[parts - 1 :]
-    first_sum, first_total, pair_ref, *refs = refs
-    terms, refs = refs[: parts - 1], refs[parts - 1 :]
-    inverse_ref, cos_ref, sin_ref, *_, sum_ref, total_ref = refs
-    count = first_sum.shape[0]
+    inverse_ref, cos_ref, sin_ref = refs[:3]
+    sum_ref, total_ref = refs[-2:]
+    heads = k_ref.shape[1] // HEAD_SIZE
+    count = q_ref.shape[0] // heads
     rows = inverse_ref.shape[0]
     inverse = inverse_ref[...]
     cosine = cos_ref[...] * inverse
     sine = sin_ref[...] * inverse
-    pair = pair_ref[...]
-    for ref in terms:
-        pair = pair + ref[:rows, :].astype(jnp.float32)
-    heads = pair.shape[1] // (2 * HEAD_SIZE)
+
+    def new_terms(index):
+        term = pair_ref[:, head_lanes(index)]
+        for ref in received:
+            term = term + ref[:rows, head_lanes(index)].astype(jnp.float32)
+        return term
+
     query_row = lax.broadcasted_iota(jnp.int32, (count, rows), 0)
     key_row = lax.broadcasted_iota(jnp.int32, (count, rows), 1)
     same = query_row // 8 == key_row // 4
@@ -607,9 +608,8 @@
     for head in range(heads):
         at = slice(head * count, (head + 1) * count)
         query = q_ref[at, :]
-        key = rotated(pair[:, head * HEAD_SIZE : (head + 1) * HEAD_SIZE], cosine, sine)
-        value_at = (heads + head) * HEAD_SIZE
-        value = pair[:, value_at : value_at + HEAD_SIZE] * inverse
+        key = rotated(new_terms(head), cosine, sine)
+        value = new_terms(heads + head) * inverse
         weight = capped_weight(dot_last(query, key.astype(jnp.bfloat16)))
         weight = jnp.where(valid, weight, 0.0).astype(jnp.bfloat16)
         result = jnp.dot(
@@ -617,24 +617,20 @@
             jnp.concatenate([value.astype(jnp.bfloat16), ones], axis=1),
             preferred_element_type=jnp.float32,
         )
-        if head == 0:
-            sum_ref[at, :] = first_sum[...] + result[:, :HEAD_SIZE]
-            total_ref[at, :] = first_total[...] + result[:, HEAD_SIZE:]
-        else:
-            result = result + attend(query, cached_pairs(k_ref, v_ref, received))
-            sum_ref[at, :] = result[:, :HEAD_SIZE]
-            total_ref[at, :] = result[:, HEAD_SIZE:]
-
-
-def own_attention_sums(
-    place, queries, prompt_keys, prompt_values, received, first, pair, terms, tables, tokens_after
+        pairs = [(k_ref[:, head_lanes(head)], v_ref[:, head_lanes(head)])]
+        pairs += [received_pair(ref, head, heads) for ref in blocks]
+        result = result + attend(query, pairs)
+        sum_ref[at, :] = result[:, :HEAD_SIZE]
+        total_ref[at, :] = result[:, HEAD_SIZE:]
+
+
+def own_sums(
+    place, queries, prompt_keys, prompt_values, blocks, pair, received, tables, tokens_after
 ):
-    count = first[0].shape[0]
-    heads = queries.shape[0] // count
+    parts = len(blocks) + 1
     tokens = prompt_keys.shape[0]
-    parts = len(received) + 1
-    chosen = pl.BlockSpec((tokens, HEAD_SIZE), lambda i, p: (0, p[0] * heads + 1))
-    operands = (*received, *first, pair, *terms, *tables)
+    chosen = pl.BlockSpec((tokens, prompt_keys.shape[1] // parts), lambda i, p: (0, p[0]))
+    operands = (*blocks, pair, *received, *tables)
     outs = [shape(queries.shape, jnp.float32)] * 2
     return call(
         functools.partial(own_kernel, parts),
@@ -647,98 +643,120 @@
         [whole(a) for a in outs],
         (1,),
         [],
-        6 * count * parts * tokens * HEAD_SIZE,
+        6 * queries.size * parts * tokens,
         4 * parts * tokens * HEAD_SIZE,
     )
 
 
 def suffix_kernel(parts, place, lengths, own_ref, *refs):
-    received, (k_ref, v_ref, _), refs = refs[: parts - 1], refs[parts - 1 : parts + 2], refs[parts + 2 :]
-    outs, (query_held, spread, result, sums, totals, packed) = refs[: parts + 1], refs[parts + 1 :]
-    member = pl.program_id(0)
-    members = pl.num_programs(0)
-    slots, columns = k_ref.shape[1:]
+    received, (k_hbm, v_hbm), refs = (
+        refs[: parts - 1],
+        refs[parts - 1 : parts + 1],
+        refs[-(parts + 8) :],
+    )
+    outs, refs = refs[: parts + 1], refs[parts + 1 :]
+    query_held, k_ref, v_ref, sums, totals, packed, semaphores = refs
+    members, slots, columns = k_ref.shape
     heads = columns // HEAD_SIZE
     near = heads // parts
     here = place[0]
-
-    @pl.when(member == 0)
-    def _():
-        spread[...] = jnp.zeros(spread.shape, jnp.float32)
-        packed[...] = jnp.zeros(packed.shape, jnp.float32)
-        query_held[0] = own_ref[...].astype(jnp.float32)
-        count = own_ref.shape[0]
-        for mask, ref in enumerate(received, start=1):
-            pieces = ref.shape[1] // HEAD_SIZE
-            tall = count // pieces
-            for piece in range(pieces):
-                at = slice(piece * HEAD_SIZE, (piece + 1) * HEAD_SIZE)
-                query_held[mask, piece * tall : (piece + 1) * tall, :] = ref[
-                    ref.shape[0] - tall :, at
+    copies = [
+        [
+            copy_in(source.at[member], ref.at[member], semaphores.at[member, half])
+            for half, (source, ref) in enumerate(((k_hbm, k_ref), (v_hbm, v_ref)))
+        ]
+        for member in range(members)
+    ]
+    packed[...] = jnp.zeros(packed.shape, jnp.float32)
+    count = members * 8
+    for mask, ref in enumerate((own_ref, *received)):
+        for head in range(near):
+            target = query_held.at[(here ^ mask) * near + head]
+            if mask == 0:
+                target[...] = ref[head * count : (head + 1) * count, :].astype(jnp.float32)
+                continue
+            tall = own_ref.shape[0] * HEAD_SIZE // ref.shape[1]
+            for half in range(count // tall):
+                target[half * tall : (half + 1) * tall, :] = ref[
+                    ref.shape[0] - tall :, head_lanes(head * count // tall + half)
                 ].astype(jnp.float32)
 
-    def places(mask, head):
-        owner = here ^ mask
-        row = pl.ds(pl.multiple_of((owner * near + head) * 8, 8), 8)
-        column = pl.ds(pl.multiple_of((owner * near + head) * HEAD_SIZE, HEAD_SIZE), HEAD_SIZE)
-        local = pl.ds(pl.multiple_of(head * members * 8 + member * 8, 8), 8)
-        return row, column, local
+    for member in range(members):
+        tile = slice(member * 8, (member + 1) * 8)
+        for copy in copies[member]:
+            copy.wait()
+        scores = jnp.concatenate(
+            [
+                dot_last(
+                    query_held[head, tile, :].astype(jnp.bfloat16),
+                    k_ref[member, :, head_lanes(head)],
+                )
+                for head in range(heads)
+            ],
+            axis=0,
+        )
+        valid = lax.broadcasted_iota(jnp.int32, scores.shape, 1) < lengths[here * members + member]
+        weight = jnp.where(valid, capped_weight(scores), 0.0)
+        total = jnp.broadcast_to(jnp.sum(weight, axis=1, keepdims=True), (heads * 8, LANES))
+        weight = weight.astype(jnp.bfloat16)
+        for head in range(heads):
+            rows = slice(head * 8, (head + 1) * 8)
+            sums[head, tile, :] = jnp.dot(
+                weight[rows],
+                v_ref[member, :, head_lanes(head)],
+                preferred_element_type=jnp.float32,
+            )
+            totals[head, tile, :] = total[rows]
 
     for mask in range(parts):
         for head in range(near):
-            row, column, local = places(mask, head)
-            spread[row, column] = query_held[mask, local, :]
-    weight = capped_weight(dot_last(k_ref[0], spread[...].astype(jnp.bfloat16)))
-    valid = lax.broadcasted_iota(jnp.int32, weight.shape, 0) < lengths[here * members + member]
-    weight = jnp.where(valid, weight, 0.0).astype(jnp.bfloat16)
-    result[:, :columns] = dot_first(weight, v_ref[0])
-    result[:, columns:] = dot_first(weight, jnp.ones((slots, LANES), jnp.bfloat16))
-    for mask in range(parts):
-        for head in range(near):
-            row, column, local = places(mask, head)
-            sums[mask, local, :] = result[row, column]
-            totals[mask, local, :] = result[row, columns:]
-
-    @pl.when(member == members - 1)
-    def _():
-        count = sums.shape[1]
-        outs[0][...] = sums[0]
-        outs[1][...] = totals[0]
-        for mask in range(1, parts):
-            ref = outs[mask + 1]
-            ref[:count, :] = sums[mask].astype(jnp.bfloat16)
-            packed[0:1, :] = totals[mask].T[0:1]
-            ref[count:, :] = split_rows(packed[...])
-
-
-def suffix_attention(place, lengths, own, received, cache_keys, cache_values, token):
+            at = slice(head * count, (head + 1) * count)
+            index = (here ^ mask) * near + head
+            if mask == 0:
+                outs[0][at, :] = sums[index]
+                outs[1][at, :] = totals[index]
+            else:
+                outs[mask + 1][at, :] = sums[index].astype(jnp.bfloat16)
+        if mask > 0:
+            both = jnp.concatenate(
+                [totals[(here ^ mask) * near + head] for head in range(near)], axis=0
+            )
+            packed[0:1, :] = both.T[0:1]
+            outs[mask + 1][near * count :, :] = split_rows(packed[...])
+
+
+def suffix_attention(place, lengths, own, received, cache_keys, cache_values, tokens_after):
     parts = len(received) + 1
     members, slots, columns = cache_keys.shape
-    count = own.shape[0]
-    spread_rows = 8 * columns // HEAD_SIZE
-    operands = (own, *received, cache_keys, cache_values, token)
+    heads = columns // HEAD_SIZE
+    count = heads // parts * members * 8
     outs = [shape((count, HEAD_SIZE), jnp.float32)] * 2 + [
         shape((count + 16, HEAD_SIZE), jnp.bfloat16)
     ] * (parts - 1)
-    cache = pl.BlockSpec((1, slots, columns), lambda i, p, n: (i, 0, 0))
+    far = pl.BlockSpec(memory_space=pl.ANY)
     return call(
         functools.partial(suffix_kernel, parts),
         (place, lengths),
-        operands,
+        (own, *received, cache_keys, cache_values, *tokens_after),
         outs,
-        [whole(own)] + [whole(a) for a in received] + [cache, cache, corner(token)],
+        [whole(own)]
+        + [whole(a) for a in received]
+        + [far, far]
+        + [corner(a) for a in tokens_after],
         [whole(a) for a in outs],
-        (members,),
+        (1,),
         [
-            pltpu.VMEM((parts, count, HEAD_SIZE), jnp.float32),
-            pltpu.VMEM((spread_rows, columns), jnp.float32),
-            pltpu.VMEM((spread_rows, columns + LANES), jnp.float32),
-            pltpu.VMEM((parts, count, HEAD_SIZE), jnp.float32),
-            pltpu.VMEM((parts, count, HEAD_SIZE), jnp.float32),
+            pltpu.VMEM((heads, members * 8, HEAD_SIZE), jnp.float32),
+            pltpu.VMEM(cache_keys.shape, cache_keys.dtype),
+            pltpu.VMEM(cache_values.shape, cache_values.dtype),
+            pltpu.VMEM((heads, members * 8, HEAD_SIZE), jnp.float32),
+            pltpu.VMEM((heads, members * 8, HEAD_SIZE), jnp.float32),
             pltpu.VMEM((8, LANES), jnp.float32),
+            pltpu.SemaphoreType.DMA((members, 2)),
         ],
-        4 * members * spread_rows * slots * columns,
+        4 * members * 8 * slots * columns,
         4 * members * slots * columns,
+        SUFFIX_LIMIT,
     )
 
 
@@ -766,7 +784,7 @@
         else:
             ref = suffix[mask - 1]
             near = ref[: count // parts, :].astype(jnp.float32)
-            near_weight = down_rows(joined_row(ref[count // parts :, :], 0))
+            near_weight = down_rows(joined_row(ref[count // parts : count // parts + 16, :], 0))
         for head in range(heads):
             first = pl.multiple_of(head * 2 * rows + (place[0] ^ mask) * share, share)
             at = pl.ds(first, share)
@@ -909,20 +927,21 @@
     rows = group_rows * steps
     parts = lax.axis_size("prefix")
     groups = lax.axis_size("prefill")
-    heads = prompt_keys.shape[1] // HEAD_SIZE // parts
     prompt_total = prompt_keys.shape[0] * groups * parts
     place = lax.axis_index("prefix").astype(jnp.int32).reshape(1)
     near = range(1, parts)
     far = range(1, groups)
 
     def swapped(arrays, axis):
-        return [paired(a, axis, m) for m, a in enumerate(arrays, start=1)]
-
-    *sent, own, squares, scaled = query_projection(place, hidden_in, pre_gain, w_query, parts)
-    received = swapped(sent, "prefix")
-    first_head = swapped(
-        cache_columns(place, prompt_keys, prompt_values, 0, heads, parts, squares), "prefix"
-    )
+        pairs = list(enumerate(arrays, start=1))
+        moved = {m: paired(a, axis, m) for m, a in pairs[-1:] + pairs[:-1]}
+        return [moved[m] for m, _ in pairs]
+
+    *sent, own, squares, scaled = query_projection(
+        place, hidden_in, pre_gain, w_query, prompt_keys, prompt_values, parts
+    )
+    received = swapped(sent[parts - 1 :], "prefix")
+    blocks = swapped(sent[: parts - 1], "prefix")
 
     positions = (
         (prompt_total + suffix_len[:, None] + jnp.arange(steps, dtype=jnp.int32)[None, :])
@@ -939,47 +958,38 @@
     queries, *split_queries, inverse = query_rope(
         place, own, received, squares, cosine, sine, parts
     )
-    far_queries = [paired(queries, "prefill", m) for m in far]
+    held_back = lax.optimization_barrier((queries, blocks[0]))[0]
+    far_queries = [paired(held_back if m == 1 else queries, "prefill", m) for m in far]
     pair, *sent = pair_projection(
         place, scaled, key_projection, value_projection, split_queries[1:]
     )
-    terms = swapped(sent, "prefix")
-    second_head = swapped(
-        cache_columns(place, prompt_keys, prompt_values, 1, heads, parts, pair), "prefix"
-    )
-
-    first = prompt_first(
-        place, [queries, *far_queries], prompt_keys, prompt_values, first_head, heads
-    )
-    near_sums, near_totals, *sent = suffix_attention(
-        place, suffix_len, split_queries[0], terms, suffix_key_cache, suffix_value_cache, first[1]
-    )
-    suffix = [near_sums, near_totals, *swapped(sent, "prefix")]
+    returned = swapped(sent, "prefix")
+    first = prompt_first(place, far_queries, prompt_keys, prompt_values, blocks[:1], parts)
     packed = [
-        prompt_second(
-            place,
-            far_queries[m - 1],
-            prompt_keys,
-            prompt_values,
-            second_head,
-            first[2 * m : 2 * m + 2],
-            heads,
-            near_totals,
-        )
-        for m in far
+        prompt_last(place, q, blocks[1:], first[2 * i : 2 * i + 2])
+        for i, q in enumerate(far_queries)
     ]
     prompt_results = swapped(packed, "prefill")
-    sums, totals = own_attention_sums(
+    near_sums, near_totals, *sent = suffix_attention(
+        place,
+        suffix_len,
+        split_queries[0],
+        returned,
+        suffix_key_cache,
+        suffix_value_cache,
+        packed,
+    )
+    suffix = [near_sums, near_totals, *swapped(sent, "prefix")]
+    sums, totals = own_sums(
         place,
         queries,
         prompt_keys,
         prompt_values,
-        second_head,
-        first[:2],
+        blocks,
         pair,
-        terms,
+        returned,
         (inverse, cosine, sine),
-        packed,
+        [near_totals],
     )
     mixed = mix(place, sums, totals, prompt_results, suffix, rows)
     others = [paired(mixed, "prefix", m) for m in near]

time: 93.8 us -> 81.6 us (0.87)
  waiting for transfers between devices: 25.5 us -> 15.6 us
  local copies, waits for them, and re-layouts: 6.73 us -> 0.57 us
  starting transfers between devices: 34.9 us -> 36.5 us
  Pallas kernels: 25.7 us -> 27.2 us
    ppermute x28 -> x25, waiting for transfers between devices: 25.5 us -> 15.6 us  [paired(): return lax.ppermute(values, axis, [(i, i ^ mask) for i in range(size)])]
    unnamed x30 -> x34, local copies, waits for them, and re-layouts: 6.62 us -> 0.47 us
    ppermute x28 -> x25, starting transfers between devices: 34.9 us -> 36.5 us  [paired(): return lax.ppermute(values, axis, [(i, i ^ mask) for i in range(size)])]
    pallas_call x16 -> x14, Pallas kernels: 25.7 us -> 27.2 us  [call(): pl.pallas_call(kernel, out_shape=out_shape, grid_spec=pltpu.PrefetchScala...]
  transfers between devices with their start and end apart: 28 -> 25, of which waited for: 13 -> 13; matrix products, arithmetic and copies ran while one was open for 1% -> 2% of each run, Pallas kernels for 18% -> 23%
where the time goes in v3:
time: 81.6 us; the launch traced here: 81.4 us
  starting transfers between devices  36.5 us (45%)
  Pallas kernels  27.2 us (33%)
  waiting for transfers between devices  15.6 us (19%)
  other arithmetic  1.16 us (1%)
    ppermute x25, starting transfers between devices, paired(): return lax.ppermute(values, axis, [(i, i ^ mask) for i in range(size)])  36.5 us
    pallas_call x14, Pallas kernels, call(): pl.pallas_call(kernel, out_shape=out_shape, grid_spec=pltpu.PrefetchScala...  27.2 us
    ppermute x25, waiting for transfers between devices, paired(): return lax.ppermute(values, axis, [(i, i ^ mask) for i in range(size)])  15.6 us
  transfers between devices with their start and end apart: 25, of which 13 were waited for; matrix products, arithmetic and copies ran while one was open for 2% of the time, Pallas kernels for 23%

profile of v3, /device:TPU:0, one launch (start us, length us, event | category | flops | bytes accessed | tf_op | source)
XLA Modules:
  0.0 81.4 jit_solution(10678171924477863736)
XLA Ops:
  0.0 5.8 %shard_map.118 = (bf16[512,512]{1,0:T(8,128)(2,1)}, bf16[512,512]{1,0:T(8,128)(2,1)}, bf16[512,512]{1,0:T(8,128)(2,1)}, bf16[144,512]{1,0:T(8,128)(2,1)}, bf16[1...) custom-call(s32[1]{0:T(128)} %bitcast.place, ...), custom_call_target="tpu_custom_call" | custom-call | flops 603979776 | bytes 4718592 | tf_op jit(solution)/shard_map/pallas_call | solution.py:211
  5.9 3.0 %collective-permute-start = (bf16[144,512]{1,0:T(8,128)(2,1)}, bf16[144,512]{1,0:T(8,128)(2,1)S(1)}, u32[]{:S(2)}, u32[]{:S(2)}) collective-permute-start(bf16[144,512]{1,0:T(8,128)(2,1)} %get-tuple-element.41), channel_id=1, source_target_pairs={{0,2},{2,0},{4,6},{6,4},{1,3},{3,1},{5,7},{7,5},{8,10},{10,8},{12,... | collective-permute-start | bytes 442376 | tf_op jit(solution)/shard_map/ppermute | solution.py:195
  8.9 1.5 %collective-permute-start.1 = (bf16[144,512]{1,0:T(8,128)(2,1)}, bf16[144,512]{1,0:T(8,128)(2,1)S(1)}, u32[]{:S(2)}, u32[]{:S(2)}) collective-permute-start(bf16[144,512]{1,0:T(8,128)(2,1)} %get-tuple-element.42), channel_id=1, source_target_pairs={{0,4},{2,6},{4,0},{6,2},{1,5},{3,7},{5,1},{7,3},{8,12},{10,14},{12... | collective-permute-start | bytes 442376 | tf_op jit(solution)/shard_map/ppermute | solution.py:195
  10.4 1.9 %collective-permute-start.3 = (bf16[512,512]{1,0:T(8,128)(2,1)}, bf16[512,512]{1,0:T(8,128)(2,1)S(1)}, u32[]{:S(2)}, u32[]{:S(2)}) collective-permute-start(bf16[512,512]{1,0:T(8,128)(2,1)} %get-tuple-element.46), channel_id=1, source_target_pairs={{0,2},{2,0},{4,6},{6,4},{1,3},{3,1},{5,7},{7,5},{8,10},{10,8},{12,... | collective-permute-start | bytes 1572872 | tf_op jit(solution)/shard_map/ppermute | solution.py:195
  12.4 1.5 %collective-permute-start.4 = (bf16[512,512]{1,0:T(8,128)(2,1)}, bf16[512,512]{1,0:T(8,128)(2,1)S(1)}, u32[]{:S(2)}, u32[]{:S(2)}) collective-permute-start(bf16[512,512]{1,0:T(8,128)(2,1)} %get-tuple-element.47), channel_id=1, source_target_pairs={{0,4},{2,6},{4,0},{6,2},{1,5},{3,7},{5,1},{7,3},{8,12},{10,14},{12... | collective-permute-start | bytes 1572872 | tf_op jit(solution)/shard_map/ppermute | solution.py:195
  14.1 2.7 %collective-permute-start.5 = (bf16[512,512]{1,0:T(8,128)(2,1)}, bf16[512,512]{1,0:T(8,128)(2,1)S(1)}, u32[]{:S(2)}, u32[]{:S(2)}) collective-permute-start(bf16[512,512]{1,0:T(8,128)(2,1)} %get-tuple-element.48), channel_id=1, source_target_pairs={{0,6},{2,4},{4,2},{6,0},{1,7},{3,5},{5,3},{7,1},{8,14},{10,12},{12... | collective-permute-start | bytes 1572872 | tf_op jit(solution)/shard_map/ppermute | solution.py:195
  16.8 0.3 fusion
  17.1 0.8 pad_maximum_fusion
  17.9 0.3 collective-permute-done.1.refs_1_
  18.2 0.3 collective-permute-done.2.refs_2_
  18.5 0.4 copy-done.14
  18.9 2.1 %shard_map.119 = (bf16[512,128]{1,0:T(8,128)(2,1)}, bf16[128,128]{1,0:T(8,128)(2,1)}, bf16[128,128]{1,0:T(8,128)(2,1)}, bf16[128,128]{1,0:T(8,128)(2,1)}, bf16[128,128]{1,0:T(8,128)(2,1)}, /*index=5*/f32[128,128]{1,0:T(8,128)}) custom-call(s32[1]{0:T(128)} %bitcast.place, f32[128,512]{1,0:T(8,128)} %get-tuple-element.40.own_ref, ...), custom_call_target="tpu_custom_call" | custom-call | flops 655360 | bytes 786432 | tf_op jit(solution)/shard_map/pallas_call | solution.py:211
  20.9 3.6 %collective-permute-start.11 = (bf16[512,128]{1,0:T(8,128)(2,1)}, bf16[512,128]{1,0:T(8,128)(2,1)S(1)}, u32[]{:S(2)}, u32[]{:S(2)}) collective-permute-start(bf16[512,128]{1,0:T(8,128)(2,1)} %get-tuple-element.59.q_ref), channel_id=1, source_target_pairs={{0,24},{8,16},{16,8},{24,0},{1,25},{9,17},{17,9},{25,1},{2,26},{10... | collective-permute-start | bytes 393224 | tf_op jit(solution)/shard_map/ppermute | solution.py:195
  24.5 4.1 %collective-permute-done.3.refs_5_.refs_0_ = bf16[512,512]{1,0:T(8,128)(2,1)S(1)} collective-permute-done((bf16[512,512]{1,0:T(8,128)(2,1)}, bf16[512,512]{1,0:T(8,128)(2,1)S(1)}, u32[]{:S(2)}, u32[]{:S(2)}) %collective-permute-start.3) | collective-permute-done | bytes 524320 | tf_op jit(solution)/shard_map/ppermute | solution.py:195
  28.6 1.6 %collective-permute-start.9 = (bf16[512,128]{1,0:T(8,128)(2,1)}, bf16[512,128]{1,0:T(8,128)(2,1)S(1)}, u32[]{:S(2)}, u32[]{:S(2)}) collective-permute-start(bf16[512,128]{1,0:T(8,128)(2,1)} %get-tuple-element.59.q_ref), channel_id=1, source_target_pairs={{0,8},{8,0},{16,24},{24,16},{1,9},{9,1},{17,25},{25,17},{2,10},{10... | collective-permute-start | bytes 393224 | tf_op jit(solution)/shard_map/ppermute | solution.py:195
  30.2 4.5 %shard_map.120 = (f32[128,512]{1,0:T(8,128)}, bf16[160,512]{1,0:T(8,128)(2,1)}, bf16[160,512]{1,0:T(8,128)(2,1)}, bf16[160,512]{1,0:T(8,128)(2,1)}) custom-call(s32[1]{0:T(128)} %bitcast.place, bf16[128,1152]{1,0:T(8,128)(2,1)} %get-tuple-element.49.scaled_ref, bf16[1152,1024]{1,0:T(8,128)(2,1)} %k_hbm.1, bf16[1152,1024]{1,0:T(8,128)(2,1)} %v_hbm.1, ...), custom_call_target="tpu_custom_call" | custom-call | flops 603979776 | bytes 4718592 | tf_op jit(solution)/shard_map/pallas_call | solution.py:211
  34.7 1.7 %collective-permute-start.6 = (bf16[160,512]{1,0:T(8,128)(2,1)}, bf16[160,512]{1,0:T(8,128)(2,1)S(1)}, u32[]{:S(2)}, u32[]{:S(2)}) collective-permute-start(bf16[160,512]{1,0:T(8,128)(2,1)} %get-tuple-element.54), channel_id=1, source_target_pairs={{0,2},{2,0},{4,6},{6,4},{1,3},{3,1},{5,7},{7,5},{8,10},{10,8},{12,... | collective-permute-start | bytes 491528 | tf_op jit(solution)/shard_map/ppermute | solution.py:195
  36.4 1.5 %collective-permute-start.7 = (bf16[160,512]{1,0:T(8,128)(2,1)}, bf16[160,512]{1,0:T(8,128)(2,1)S(1)}, u32[]{:S(2)}, u32[]{:S(2)}) collective-permute-start(bf16[160,512]{1,0:T(8,128)(2,1)} %get-tuple-element.55), channel_id=1, source_target_pairs={{0,4},{2,6},{4,0},{6,2},{1,5},{3,7},{5,1},{7,3},{8,12},{10,14},{12... | collective-permute-start | bytes 491528 | tf_op jit(solution)/shard_map/ppermute | solution.py:195
  37.9 0.4 collective-permute-start.8
  38.4 2.1 %shard_map.121 = (f32[512,128]{1,0:T(8,128)S(1)}, f32[512,128]{1,0:T(8,128)S(1)}, f32[512,128]{1,0:T(8,128)S(1)}, f32[512,128]{1,0:T(8,128)S(1)}, f32[512,128]{1,0:T(8,128)S(1)}, /*index=5*/f32[512,128]{1,0:T(8,128)S(1)}) custom-call(s32[1]{0:T(128)} %bitcast.place, bf16[512,128]{1,0:T(8,128)(2,1)S(1)} %collective-permute-done.9.refs_0_.q_ref, ...), custom_call_target="tpu_custom_call" | custom-call | flops 1207959552 | bytes 1048576 | tf_op jit(solution)/shard_map/pallas_call | solution.py:211
  40.6 0.3 collective-permute-done.5.refs_1_.refs_2_
  40.9 1.0 %shard_map.124.refs_7_ = bf16[528,128]{1,0:T(8,128)(2,1)S(1)} custom-call(s32[1]{0:T(128)} %bitcast.place, bf16[512,128]{1,0:T(8,128)(2,1)S(1)} %collective-permute-done.11.refs_2_.q_ref, bf16[512,512]{1,0:T(8,128)(2,1)S(1)} %collective-permute-done.4.refs_0_.refs_1_, bf16[512,512]{1,0:T(8,128)(2,1)S(1)} %collective-permute-done.5.refs_1_.refs_2_, ...), custom_call_target="tpu_custom_call" | custom-call | flops 402653184 | bytes 1048576 | tf_op jit(solution)/shard_map/pallas_call | solution.py:211
  41.9 3.6 %collective-permute-start.14 = (bf16[528,128]{1,0:T(8,128)(2,1)S(1)}, bf16[528,128]{1,0:T(8,128)(2,1)S(1)}, u32[]{:S(2)}, u32[]{:S(2)}) collective-permute-start(bf16[528,128]{1,0:T(8,128)(2,1)S(1)} %shard_map.124.refs_7_), channel_id=1, source_target_pairs={{0,24},{8,16},{16,8},{24,0},{1,25},{9,17},{17,9},{25,1},{2,26},{10... | collective-permute-start | bytes 405512 | tf_op jit(solution)/shard_map/ppermute | solution.py:195
  45.5 1.0 %shard_map.123.refs_6_ = bf16[528,128]{1,0:T(8,128)(2,1)S(1)} custom-call(s32[1]{0:T(128)} %bitcast.place, bf16[512,128]{1,0:T(8,128)(2,1)S(1)} %collective-permute-done.10.refs_1_.q_ref, bf16[512,512]{1,0:T(8,128)(2,1)S(1)} %collective-permute-done.4.refs_0_.refs_1_, bf16[512,512]{1,0:T(8,128)(2,1)S(1)} %collective-permute-done.5.refs_1_.refs_2_, ...), custom_call_target="tpu_custom_call" | custom-call | flops 402653184 | bytes 1048576 | tf_op jit(solution)/shard_map/pallas_call | solution.py:211
  46.6 1.0 %shard_map.122.refs_5_ = bf16[528,128]{1,0:T(8,128)(2,1)S(1)} custom-call(s32[1]{0:T(128)} %bitcast.place, bf16[512,128]{1,0:T(8,128)(2,1)S(1)} %collective-permute-done.9.refs_0_.q_ref, bf16[512,512]{1,0:T(8,128)(2,1)S(1)} %collective-permute-done.4.refs_0_.refs_1_, bf16[512,512]{1,0:T(8,128)(2,1)S(1)} %collective-permute-done.5.refs_1_.refs_2_, ...), custom_call_target="tpu_custom_call" | custom-call | flops 402653184 | bytes 1048576 | tf_op jit(solution)/shard_map/pallas_call | solution.py:211
  47.6 0.8 collective-permute-start.12
  48.5 4.6 %shard_map.125 = (f32[128,128]{1,0:T(8,128)S(1)}, f32[128,128]{1,0:T(8,128)S(1)}, bf16[144,128]{1,0:T(8,128)(2,1)S(1)}, bf16[144,128]{1,0:T(8,128)(2,1)S(1)}, bf16[144,128]{1,0:T(8,128)(2,1)S(1)}) custom-call(s32[1]{0:T(128)} %bitcast.place, s32[32]{0:T(128)S(1)} %copy-done.12, bf16[128,128]{1,0:T(8,128)(2,1)S(1)} %copy-done.10, ...), custom_call_target="tpu_custom_call" | custom-call | flops 67108864 | bytes 8388608 | tf_op jit(solution)/shard_map/pallas_call | solution.py:211
  53.2 1.7 %collective-permute-start.15 = (bf16[144,128]{1,0:T(8,128)(2,1)S(1)}, bf16[144,128]{1,0:T(8,128)(2,1)S(1)}, u32[]{:S(2)}, u32[]{:S(2)}) collective-permute-start(bf16[144,128]{1,0:T(8,128)(2,1)S(1)} %get-tuple-element.70), channel_id=1, source_target_pairs={{0,2},{2,0},{4,6},{6,4},{1,3},{3,1},{5,7},{7,5},{8,10},{10,8},{12,... | collective-permute-start | bytes 110600 | tf_op jit(solution)/shard_map/ppermute | solution.py:195
  54.8 1.1 %collective-permute-start.16 = (bf16[144,128]{1,0:T(8,128)(2,1)S(1)}, bf16[144,128]{1,0:T(8,128)(2,1)S(1)}, u32[]{:S(2)}, u32[]{:S(2)}) collective-permute-start(bf16[144,128]{1,0:T(8,128)(2,1)S(1)} %get-tuple-element.71), channel_id=1, source_target_pairs={{0,4},{2,6},{4,0},{6,2},{1,5},{3,7},{5,1},{7,3},{8,12},{10,14},{12... | collective-permute-start | bytes 110600 | tf_op jit(solution)/shard_map/ppermute | solution.py:195
  56.0 1.2 %collective-permute-done.15.refs_5_ = bf16[144,128]{1,0:T(8,128)(2,1)S(1)} collective-permute-done((bf16[144,128]{1,0:T(8,128)(2,1)S(1)}, bf16[144,128]{1,0:T(8,128)(2,1)S(1)}, u32[]{:S(2)}, u32[]{:S(2)}) %collective-permute-start.15) | collective-permute-done | bytes 36896 | tf_op jit(solution)/shard_map/ppermute | solution.py:195
  57.2 2.2 %collective-permute-start.17 = (bf16[144,128]{1,0:T(8,128)(2,1)S(1)}, bf16[144,128]{1,0:T(8,128)(2,1)S(1)}, u32[]{:S(2)}, u32[]{:S(2)}) collective-permute-start(bf16[144,128]{1,0:T(8,128)(2,1)S(1)} %get-tuple-element.72), channel_id=1, source_target_pairs={{0,6},{2,4},{4,2},{6,0},{1,7},{3,5},{5,3},{7,1},{8,14},{10,12},{12... | collective-permute-start | bytes 110600 | tf_op jit(solution)/shard_map/ppermute | solution.py:195
  59.4 2.0 %shard_map.126 = (f32[512,128]{1,0:T(8,128)S(1)}, f32[512,128]{1,0:T(8,128)S(1)}) custom-call(s32[1]{0:T(128)} %bitcast.place, bf16[512,128]{1,0:T(8,128)(2,1)S(1)} %copy-done.8, bf16[512,1024]{1,0:T(8,128)(2,1)S(1)} %copy-done, bf16[512,1024]{1,0:T(8,128)(2,1)S(1)} %copy-done.1, bf16[512,512]{1,0:T(8,128)(2,1)S(1)} %collective-permute-done.3.refs_5_.refs_0_, ...), custom_call_target="tpu_custom_call" | custom-call | flops 805306368 | bytes 1048576 | tf_op jit(solution)/shard_map/pallas_call | solution.py:211
  61.4 1.1 %collective-permute-done.17.refs_7_ = bf16[144,128]{1,0:T(8,128)(2,1)S(1)} collective-permute-done((bf16[144,128]{1,0:T(8,128)(2,1)S(1)}, bf16[144,128]{1,0:T(8,128)(2,1)S(1)}, u32[]{:S(2)}, u32[]{:S(2)}) %collective-permute-start.17) | collective-permute-done | bytes 36896 | tf_op jit(solution)/shard_map/ppermute | solution.py:195
  62.5 0.4 shard_map.127.refs_0_
  63.0 2.2 %collective-permute-start.20 = (bf16[128,512]{1,0:T(8,128)(2,1)S(1)}, bf16[128,512]{1,0:T(8,128)(2,1)S(1)}, u32[]{:S(2)}, u32[]{:S(2)}) collective-permute-start(bf16[128,512]{1,0:T(8,128)(2,1)S(1)} %shard_map.127.refs_0_), channel_id=1, source_target_pairs={{0,6},{2,4},{4,2},{6,0},{1,7},{3,5},{5,3},{7,1},{8,14},{10,12},{12... | collective-permute-start | bytes 393224 | tf_op jit(solution)/shard_map/ppermute | solution.py:195
  65.1 0.9 %collective-permute-start.19 = (bf16[128,512]{1,0:T(8,128)(2,1)S(1)}, bf16[128,512]{1,0:T(8,128)(2,1)S(1)}, u32[]{:S(2)}, u32[]{:S(2)}) collective-permute-start(bf16[128,512]{1,0:T(8,128)(2,1)S(1)} %shard_map.127.refs_0_), channel_id=1, source_target_pairs={{0,4},{2,6},{4,0},{6,2},{1,5},{3,7},{5,1},{7,3},{8,12},{10,14},{12... | collective-permute-start | bytes 393224 | tf_op jit(solution)/shard_map/ppermute | solution.py:195
  66.1 0.9 %collective-permute-start.18 = (bf16[128,512]{1,0:T(8,128)(2,1)S(1)}, bf16[128,512]{1,0:T(8,128)(2,1)S(1)}, u32[]{:S(2)}, u32[]{:S(2)}) collective-permute-start(bf16[128,512]{1,0:T(8,128)(2,1)S(1)} %shard_map.127.refs_0_), channel_id=1, source_target_pairs={{0,2},{2,0},{4,6},{6,4},{1,3},{3,1},{5,7},{7,5},{8,10},{10,8},{12,... | collective-permute-start | bytes 393224 | tf_op jit(solution)/shard_map/ppermute | solution.py:195
  67.0 0.3 shard_map.128.refs_4_
  67.4 1.5 %collective-permute-done.20.refs_2_ = bf16[128,512]{1,0:T(8,128)(2,1)S(1)} collective-permute-done((bf16[128,512]{1,0:T(8,128)(2,1)S(1)}, bf16[128,512]{1,0:T(8,128)(2,1)S(1)}, u32[]{:S(2)}, u32[]{:S(2)}) %collective-permute-start.20) | collective-permute-done | bytes 131104 | tf_op jit(solution)/shard_map/ppermute | solution.py:195
  68.9 1.4 %collective-permute-done.19.refs_1_ = bf16[128,512]{1,0:T(8,128)(2,1)S(1)} collective-permute-done((bf16[128,512]{1,0:T(8,128)(2,1)S(1)}, bf16[128,512]{1,0:T(8,128)(2,1)S(1)}, u32[]{:S(2)}, u32[]{:S(2)}) %collective-permute-start.19) | collective-permute-done | bytes 131104 | tf_op jit(solution)/shard_map/ppermute | solution.py:195
  70.3 1.1 %collective-permute-done.18.refs_0_ = bf16[128,512]{1,0:T(8,128)(2,1)S(1)} collective-permute-done((bf16[128,512]{1,0:T(8,128)(2,1)S(1)}, bf16[128,512]{1,0:T(8,128)(2,1)S(1)}, u32[]{:S(2)}, u32[]{:S(2)}) %collective-permute-start.18) | collective-permute-done | bytes 131104 | tf_op jit(solution)/shard_map/ppermute | solution.py:195
  71.4 1.1 %shard_map.129.here_ref = f32[128,1152]{1,0:T(8,128)S(1)} custom-call(s32[1]{0:T(128)} %bitcast.place, bf16[128,512]{1,0:T(8,128)(2,1)S(1)} %collective-permute-done.18.refs_0_, bf16[128,512]{1,0:T(8,128)(2,1)S(1)} %collective-permute-done.19.refs_1_, bf16[128,512]{1,0:T(8,128)(2,1)S(1)} %collective-permute-done.20.refs_2_, bf16[2048,1152]{1,0:T(8,128)(2,1)S(1)} %bitcast.2, ...), custom_call_target="tpu_custom_call" | custom-call | flops 452984832 | bytes 3538944 | tf_op jit(solution)/shard_map/pallas_call | solution.py:211
  72.6 2.0 %collective-permute-done.21.there_ref = f32[128,1152]{1,0:T(8,128)S(1)} collective-permute-done((f32[128,1152]{1,0:T(8,128)S(1)}, f32[128,1152]{1,0:T(8,128)S(1)}, u32[]{:S(2)}, u32[]{:S(2)}) %collective-permute-start.21) | collective-permute-done | bytes 589856 | tf_op jit(solution)/shard_map/ppermute | solution.py:195
  74.7 2.1 %collective-permute-start.24 = (f32[8,128]{1,0:T(8,128)S(1)}, f32[8,128]{1,0:T(8,128)S(1)}, u32[]{:S(2)}, u32[]{:S(2)}) collective-permute-start(f32[8,128]{1,0:T(8,128)S(1)} %get-tuple-element.74.refs_0_), channel_id=1, source_target_pairs={{0,6},{2,4},{4,2},{6,0},{1,7},{3,5},{5,3},{7,1},{8,14},{10,12},{12... | collective-permute-start | bytes 12296 | tf_op jit(solution)/shard_map/ppermute | solution.py:195
  76.8 1.4 %collective-permute-start.22 = (f32[8,128]{1,0:T(8,128)S(1)}, f32[8,128]{1,0:T(8,128)S(1)}, u32[]{:S(2)}, u32[]{:S(2)}) collective-permute-start(f32[8,128]{1,0:T(8,128)S(1)} %get-tuple-element.74.refs_0_), channel_id=1, source_target_pairs={{0,2},{2,0},{4,6},{6,4},{1,3},{3,1},{5,7},{7,5},{8,10},{10,8},{12,... | collective-permute-start | bytes 12296 | tf_op jit(solution)/shard_map/ppermute | solution.py:195
  78.2 1.0 %collective-permute-done.24.refs_3_ = f32[8,128]{1,0:T(8,128)S(1)} collective-permute-done((f32[8,128]{1,0:T(8,128)S(1)}, f32[8,128]{1,0:T(8,128)S(1)}, u32[]{:S(2)}, u32[]{:S(2)}) %collective-permute-start.24) | collective-permute-done | bytes 4128 | tf_op jit(solution)/shard_map/ppermute | solution.py:195
  79.2 1.1 %collective-permute-done.23.refs_2_ = f32[8,128]{1,0:T(8,128)S(1)} collective-permute-done((f32[8,128]{1,0:T(8,128)S(1)}, f32[8,128]{1,0:T(8,128)S(1)}, u32[]{:S(2)}, u32[]{:S(2)}) %collective-permute-start.23) | collective-permute-done | bytes 4128 | tf_op jit(solution)/shard_map/ppermute | solution.py:195
  80.4 1.0 %shard_map.131 = bf16[32,4,1152]{2,1,0:T(4,128)(2,1)} custom-call(s32[1]{0:T(128)} %bitcast.place, bf16[32,4,1152]{2,1,0:T(4,128)(2,1)S(1)} %copy-done.4, f32[128,1152]{1,0:T(8,128)S(1)} %get-tuple-element.73.attended_ref, f32[1152]{0:T(1024)S(1)} %copy-done.11, f32[8,128]{1,0:T(8,128)S(1)} %get-tuple-element.74.refs_0_, ...), custom_call_target="tpu_custom_call" | custom-call | flops 589824 | bytes 1179648 | tf_op jit(solution)/shard_map/pallas_call | solution.py:211
  (57 shorter events, 0.7 us)
Async XLA Ops:
  0.0 13.9 %copy-start.12 = (s32[32]{0:T(128)S(1)}, s32[32]{0:T(128)}, u32[]{:S(2)}) copy-start(s32[32]{0:T(128)} %lengths.1) | copy-start | bytes 388
  5.9 32.5 %copy-start = (bf16[512,1024]{1,0:T(8,128)(2,1)S(1)}, bf16[512,1024]{1,0:T(8,128)(2,1)}, u32[]{:S(2)}) copy-start(bf16[512,1024]{1,0:T(8,128)(2,1)} %k_ref.1) | copy-start | bytes 3145732
  5.9 32.5 %copy-start.1 = (bf16[512,1024]{1,0:T(8,128)(2,1)S(1)}, bf16[512,1024]{1,0:T(8,128)(2,1)}, u32[]{:S(2)}) copy-start(bf16[512,1024]{1,0:T(8,128)(2,1)} %v_ref.1) | copy-start | bytes 3145732
  5.9 8.2 %collective-permute-start = (bf16[144,512]{1,0:T(8,128)(2,1)}, bf16[144,512]{1,0:T(8,128)(2,1)S(1)}, u32[]{:S(2)}, u32[]{:S(2)}) collective-permute-start(bf16[144,512]{1,0:T(8,128)(2,1)} %get-tuple-element.41), channel_id=1, source_target_pairs={{0,2},{2,0},{4,6},{6,4},{1,3},{3,1},{5,7},{7,5},{8,10},{10,8},{12,... | collective-permute-start | bytes 442376 | tf_op jit(solution)/shard_map/ppermute | solution.py:195
  8.9 9.3 %collective-permute-start.1 = (bf16[144,512]{1,0:T(8,128)(2,1)}, bf16[144,512]{1,0:T(8,128)(2,1)S(1)}, u32[]{:S(2)}, u32[]{:S(2)}) collective-permute-start(bf16[144,512]{1,0:T(8,128)(2,1)} %get-tuple-element.42), channel_id=1, source_target_pairs={{0,4},{2,6},{4,0},{6,2},{1,5},{3,7},{5,1},{7,3},{8,12},{10,14},{12... | collective-permute-start | bytes 442376 | tf_op jit(solution)/shard_map/ppermute | solution.py:195
  10.4 8.0 %collective-permute-start.2 = (bf16[144,512]{1,0:T(8,128)(2,1)}, bf16[144,512]{1,0:T(8,128)(2,1)}, u32[]{:S(2)}, u32[]{:S(2)}) collective-permute-start(bf16[144,512]{1,0:T(8,128)(2,1)} %get-tuple-element.43), channel_id=1, source_target_pairs={{0,6},{2,4},{4,2},{6,0},{1,7},{3,5},{5,3},{7,1},{8,14},{10,12},{12... | collective-permute-start | bytes 442376 | tf_op jit(solution)/shard_map/ppermute | solution.py:195
  10.4 18.2 %collective-permute-start.3 = (bf16[512,512]{1,0:T(8,128)(2,1)}, bf16[512,512]{1,0:T(8,128)(2,1)S(1)}, u32[]{:S(2)}, u32[]{:S(2)}) collective-permute-start(bf16[512,512]{1,0:T(8,128)(2,1)} %get-tuple-element.46), channel_id=1, source_target_pairs={{0,2},{2,0},{4,6},{6,4},{1,3},{3,1},{5,7},{7,5},{8,10},{10,8},{12,... | collective-permute-start | bytes 1572872 | tf_op jit(solution)/shard_map/ppermute | solution.py:195
  12.4 28.2 %collective-permute-start.4 = (bf16[512,512]{1,0:T(8,128)(2,1)}, bf16[512,512]{1,0:T(8,128)(2,1)S(1)}, u32[]{:S(2)}, u32[]{:S(2)}) collective-permute-start(bf16[512,512]{1,0:T(8,128)(2,1)} %get-tuple-element.47), channel_id=1, source_target_pairs={{0,4},{2,6},{4,0},{6,2},{1,5},{3,7},{5,1},{7,3},{8,12},{10,14},{12... | collective-permute-start | bytes 1572872 | tf_op jit(solution)/shard_map/ppermute | solution.py:195
  14.1 4.3 %copy-start.13 = (bf16[144,512]{1,0:T(8,128)(2,1)}, bf16[144,512]{1,0:T(8,128)(2,1)S(1)}, u32[]{:S(2)}) copy-start(bf16[144,512]{1,0:T(8,128)(2,1)S(1)} %collective-permute-done.refs_0_) | copy-start | bytes 442372
  14.1 26.7 %collective-permute-start.5 = (bf16[512,512]{1,0:T(8,128)(2,1)}, bf16[512,512]{1,0:T(8,128)(2,1)S(1)}, u32[]{:S(2)}, u32[]{:S(2)}) collective-permute-start(bf16[512,512]{1,0:T(8,128)(2,1)} %get-tuple-element.48), channel_id=1, source_target_pairs={{0,6},{2,4},{4,2},{6,0},{1,7},{3,5},{5,3},{7,1},{8,14},{10,12},{12... | collective-permute-start | bytes 1572872 | tf_op jit(solution)/shard_map/ppermute | solution.py:195
  18.2 0.6 copy-start.14
  20.9 13.8 %collective-permute-start.11 = (bf16[512,128]{1,0:T(8,128)(2,1)}, bf16[512,128]{1,0:T(8,128)(2,1)S(1)}, u32[]{:S(2)}, u32[]{:S(2)}) collective-permute-start(bf16[512,128]{1,0:T(8,128)(2,1)} %get-tuple-element.59.q_ref), channel_id=1, source_target_pairs={{0,24},{8,16},{16,8},{24,0},{1,25},{9,17},{17,9},{25,1},{2,26},{10... | collective-permute-start | bytes 393224 | tf_op jit(solution)/shard_map/ppermute | solution.py:195
  24.5 11.9 %collective-permute-start.10 = (bf16[512,128]{1,0:T(8,128)(2,1)}, bf16[512,128]{1,0:T(8,128)(2,1)S(1)}, u32[]{:S(2)}, u32[]{:S(2)}) collective-permute-start(bf16[512,128]{1,0:T(8,128)(2,1)} %get-tuple-element.59.q_ref), channel_id=1, source_target_pairs={{0,16},{8,24},{16,0},{24,8},{1,17},{9,25},{17,1},{25,9},{2,18},{10... | collective-permute-start | bytes 393224 | tf_op jit(solution)/shard_map/ppermute | solution.py:195
  28.6 9.3 %collective-permute-start.9 = (bf16[512,128]{1,0:T(8,128)(2,1)}, bf16[512,128]{1,0:T(8,128)(2,1)S(1)}, u32[]{:S(2)}, u32[]{:S(2)}) collective-permute-start(bf16[512,128]{1,0:T(8,128)(2,1)} %get-tuple-element.59.q_ref), channel_id=1, source_target_pairs={{0,8},{8,0},{16,24},{24,16},{1,9},{9,1},{17,25},{25,17},{2,10},{10... | collective-permute-start | bytes 393224 | tf_op jit(solution)/shard_map/ppermute | solution.py:195
  34.7 12.9 %collective-permute-start.6 = (bf16[160,512]{1,0:T(8,128)(2,1)}, bf16[160,512]{1,0:T(8,128)(2,1)S(1)}, u32[]{:S(2)}, u32[]{:S(2)}) collective-permute-start(bf16[160,512]{1,0:T(8,128)(2,1)} %get-tuple-element.54), channel_id=1, source_target_pairs={{0,2},{2,0},{4,6},{6,4},{1,3},{3,1},{5,7},{7,5},{8,10},{10,8},{12,... | collective-permute-start | bytes 491528 | tf_op jit(solution)/shard_map/ppermute | solution.py:195
  36.4 12.0 %collective-permute-start.7 = (bf16[160,512]{1,0:T(8,128)(2,1)}, bf16[160,512]{1,0:T(8,128)(2,1)S(1)}, u32[]{:S(2)}, u32[]{:S(2)}) collective-permute-start(bf16[160,512]{1,0:T(8,128)(2,1)} %get-tuple-element.55), channel_id=1, source_target_pairs={{0,4},{2,6},{4,0},{6,2},{1,5},{3,7},{5,1},{7,3},{8,12},{10,14},{12... | collective-permute-start | bytes 491528 | tf_op jit(solution)/shard_map/ppermute | solution.py:195
  37.9 10.5 %copy-start.2 = (bf16[8,256,1024]{2,1,0:T(8,128)(2,1)S(1)}, bf16[8,256,1024]{2,1,0:T(8,128)(2,1)}, u32[]{:S(2)}) copy-start(bf16[8,256,1024]{2,1,0:T(8,128)(2,1)} %refs_3_.4) | copy-start | bytes 12582916
  37.9 10.5 %copy-start.3 = (bf16[8,256,1024]{2,1,0:T(8,128)(2,1)S(1)}, bf16[8,256,1024]{2,1,0:T(8,128)(2,1)}, u32[]{:S(2)}) copy-start(bf16[8,256,1024]{2,1,0:T(8,128)(2,1)} %refs_4_.3) | copy-start | bytes 12582916
  37.9 10.5 %copy-start.10 = (bf16[128,128]{1,0:T(8,128)(2,1)S(1)}, bf16[128,128]{1,0:T(8,128)(2,1)}, u32[]{:S(2)}) copy-start(bf16[128,128]{1,0:T(8,128)(2,1)} %get-tuple-element.58.own_ref) | copy-start | bytes 98308
  37.9 10.5 %collective-permute-start.8 = (bf16[160,512]{1,0:T(8,128)(2,1)}, bf16[160,512]{1,0:T(8,128)(2,1)S(1)}, u32[]{:S(2)}, u32[]{:S(2)}) collective-permute-start(bf16[160,512]{1,0:T(8,128)(2,1)} %get-tuple-element.56), channel_id=1, source_target_pairs={{0,6},{2,4},{4,2},{6,0},{1,7},{3,5},{5,3},{7,1},{8,14},{10,12},{12... | collective-permute-start | bytes 491528 | tf_op jit(solution)/shard_map/ppermute | solution.py:195
  41.9 20.6 %collective-permute-start.14 = (bf16[528,128]{1,0:T(8,128)(2,1)S(1)}, bf16[528,128]{1,0:T(8,128)(2,1)S(1)}, u32[]{:S(2)}, u32[]{:S(2)}) collective-permute-start(bf16[528,128]{1,0:T(8,128)(2,1)S(1)} %shard_map.124.refs_7_), channel_id=1, source_target_pairs={{0,24},{8,16},{16,8},{24,0},{1,25},{9,17},{17,9},{25,1},{2,26},{10... | collective-permute-start | bytes 405512 | tf_op jit(solution)/shard_map/ppermute | solution.py:195
  46.5 16.0 %collective-permute-start.13 = (bf16[528,128]{1,0:T(8,128)(2,1)S(1)}, bf16[528,128]{1,0:T(8,128)(2,1)S(1)}, u32[]{:S(2)}, u32[]{:S(2)}) collective-permute-start(bf16[528,128]{1,0:T(8,128)(2,1)S(1)} %shard_map.123.refs_6_), channel_id=1, source_target_pairs={{0,16},{8,24},{16,0},{24,8},{1,17},{9,25},{17,1},{25,9},{2,18},{10... | collective-permute-start | bytes 405512 | tf_op jit(solution)/shard_map/ppermute | solution.py:195
  47.6 14.9 %collective-permute-start.12 = (bf16[528,128]{1,0:T(8,128)(2,1)S(1)}, bf16[528,128]{1,0:T(8,128)(2,1)S(1)}, u32[]{:S(2)}, u32[]{:S(2)}) collective-permute-start(bf16[528,128]{1,0:T(8,128)(2,1)S(1)} %shard_map.122.refs_5_), channel_id=1, source_target_pairs={{0,8},{8,0},{16,24},{24,16},{1,9},{9,1},{17,25},{25,17},{2,10},{10... | collective-permute-start | bytes 405512 | tf_op jit(solution)/shard_map/ppermute | solution.py:195
  48.4 18.6 %slice-start = ((s8[4718592]{0:T(1024)(128)(4,1)}), s8[4194304]{0:T(1024)(128)(4,1)S(1)}, s32[]{:S(2)}) async-start(s8[4718592]{0:T(1024)(128)(4,1)} %bitcast.1), calls=%async_computation | async-start | bytes 8388608
  48.4 10.9 %copy-start.5 = (f32[128,128]{1,0:T(8,128)S(1)}, f32[128,128]{1,0:T(8,128)}, u32[]{:S(2)}) copy-start(f32[128,128]{1,0:T(8,128)} %get-tuple-element.78.refs_4_.refs_8_) | copy-start | bytes 196612
  48.5 10.9 %copy-start.6 = (f32[128,128]{1,0:T(8,128)S(1)}, f32[128,128]{1,0:T(8,128)}, u32[]{:S(2)}) copy-start(f32[128,128]{1,0:T(8,128)} %get-tuple-element.79.refs_5_.refs_9_) | copy-start | bytes 196612
  48.5 10.9 %copy-start.7 = (f32[128,512]{1,0:T(8,128)S(1)}, f32[128,512]{1,0:T(8,128)}, u32[]{:S(2)}) copy-start(f32[128,512]{1,0:T(8,128)} %get-tuple-element.53.refs_3_) | copy-start | bytes 786436
  48.5 10.9 %copy-start.8 = (bf16[512,128]{1,0:T(8,128)(2,1)S(1)}, bf16[512,128]{1,0:T(8,128)(2,1)}, u32[]{:S(2)}) copy-start(bf16[512,128]{1,0:T(8,128)(2,1)} %get-tuple-element.59.q_ref) | copy-start | bytes 393220
  48.5 10.9 %copy-start.9 = (f32[128,128]{1,0:T(8,128)S(1)}, f32[128,128]{1,0:T(8,128)}, u32[]{:S(2)}) copy-start(f32[128,128]{1,0:T(8,128)} %get-tuple-element.57.refs_7_) | copy-start | bytes 196612
  48.5 18.5 %slice-start.1 = ((s8[4718592]{0:T(1024)(128)(4,1)}), s8[524288]{0:T(1024)(128)(4,1)S(1)}, s32[]{:S(2)}) async-start(s8[4718592]{0:T(1024)(128)(4,1)} %bitcast.1), calls=%async_computation.1 | async-start | bytes 1048576
  53.2 4.0 %collective-permute-start.15 = (bf16[144,128]{1,0:T(8,128)(2,1)S(1)}, bf16[144,128]{1,0:T(8,128)(2,1)S(1)}, u32[]{:S(2)}, u32[]{:S(2)}) collective-permute-start(bf16[144,128]{1,0:T(8,128)(2,1)S(1)} %get-tuple-element.70), channel_id=1, source_target_pairs={{0,2},{2,0},{4,6},{6,4},{1,3},{3,1},{5,7},{7,5},{8,10},{10,8},{12,... | collective-permute-start | bytes 110600 | tf_op jit(solution)/shard_map/ppermute | solution.py:195
  54.8 6.6 %collective-permute-start.16 = (bf16[144,128]{1,0:T(8,128)(2,1)S(1)}, bf16[144,128]{1,0:T(8,128)(2,1)S(1)}, u32[]{:S(2)}, u32[]{:S(2)}) collective-permute-start(bf16[144,128]{1,0:T(8,128)(2,1)S(1)} %get-tuple-element.71), channel_id=1, source_target_pairs={{0,4},{2,6},{4,0},{6,2},{1,5},{3,7},{5,1},{7,3},{8,12},{10,14},{12... | collective-permute-start | bytes 110600 | tf_op jit(solution)/shard_map/ppermute | solution.py:195
  57.2 5.3 %collective-permute-start.17 = (bf16[144,128]{1,0:T(8,128)(2,1)S(1)}, bf16[144,128]{1,0:T(8,128)(2,1)S(1)}, u32[]{:S(2)}, u32[]{:S(2)}) collective-permute-start(bf16[144,128]{1,0:T(8,128)(2,1)S(1)} %get-tuple-element.72), channel_id=1, source_target_pairs={{0,6},{2,4},{4,2},{6,0},{1,7},{3,5},{5,3},{7,1},{8,14},{10,12},{12... | collective-permute-start | bytes 110600 | tf_op jit(solution)/shard_map/ppermute | solution.py:195
  63.0 6.0 %collective-permute-start.20 = (bf16[128,512]{1,0:T(8,128)(2,1)S(1)}, bf16[128,512]{1,0:T(8,128)(2,1)S(1)}, u32[]{:S(2)}, u32[]{:S(2)}) collective-permute-start(bf16[128,512]{1,0:T(8,128)(2,1)S(1)} %shard_map.127.refs_0_), channel_id=1, source_target_pairs={{0,6},{2,4},{4,2},{6,0},{1,7},{3,5},{5,3},{7,1},{8,14},{10,12},{12... | collective-permute-start | bytes 393224 | tf_op jit(solution)/shard_map/ppermute | solution.py:195
  65.1 5.2 %collective-permute-start.19 = (bf16[128,512]{1,0:T(8,128)(2,1)S(1)}, bf16[128,512]{1,0:T(8,128)(2,1)S(1)}, u32[]{:S(2)}, u32[]{:S(2)}) collective-permute-start(bf16[128,512]{1,0:T(8,128)(2,1)S(1)} %shard_map.127.refs_0_), channel_id=1, source_target_pairs={{0,4},{2,6},{4,0},{6,2},{1,5},{3,7},{5,1},{7,3},{8,12},{10,14},{12... | collective-permute-start | bytes 393224 | tf_op jit(solution)/shard_map/ppermute | solution.py:195
  66.1 5.3 %collective-permute-start.18 = (bf16[128,512]{1,0:T(8,128)(2,1)S(1)}, bf16[128,512]{1,0:T(8,128)(2,1)S(1)}, u32[]{:S(2)}, u32[]{:S(2)}) collective-permute-start(bf16[128,512]{1,0:T(8,128)(2,1)S(1)} %shard_map.127.refs_0_), channel_id=1, source_target_pairs={{0,2},{2,0},{4,6},{6,4},{1,3},{3,1},{5,7},{7,5},{8,10},{10,8},{12,... | collective-permute-start | bytes 393224 | tf_op jit(solution)/shard_map/ppermute | solution.py:195
  67.3 13.1 %copy-start.4 = (bf16[32,4,1152]{2,1,0:T(4,128)(2,1)S(1)}, bf16[32,4,1152]{2,1,0:T(4,128)(2,1)}, u32[]{:S(2)}) copy-start(bf16[32,4,1152]{2,1,0:T(4,128)(2,1)} %x_ref.1) | copy-start | bytes 884740
  67.4 13.0 %copy-start.11 = (f32[1152]{0:T(1024)S(1)}, f32[1152]{0:T(1024)}, u32[]{:S(2)}) copy-start(f32[1152]{0:T(1024)} %gain_ref.3) | copy-start | bytes 13828
  72.5 2.1 %collective-permute-start.21 = (f32[128,1152]{1,0:T(8,128)S(1)}, f32[128,1152]{1,0:T(8,128)S(1)}, u32[]{:S(2)}, u32[]{:S(2)}) collective-permute-start(f32[128,1152]{1,0:T(8,128)S(1)} %shard_map.129.here_ref), channel_id=1, source_target_pairs={{0,1},{1,0},{2,3},{3,2},{4,5},{5,4},{6,7},{7,6},{8,9},{9,8},{10,11... | collective-permute-start | bytes 1769480 | tf_op jit(solution)/shard_map/ppermute | solution.py:195
  74.7 4.5 %collective-permute-start.24 = (f32[8,128]{1,0:T(8,128)S(1)}, f32[8,128]{1,0:T(8,128)S(1)}, u32[]{:S(2)}, u32[]{:S(2)}) collective-permute-start(f32[8,128]{1,0:T(8,128)S(1)} %get-tuple-element.74.refs_0_), channel_id=1, source_target_pairs={{0,6},{2,4},{4,2},{6,0},{1,7},{3,5},{5,3},{7,1},{8,14},{10,12},{12... | collective-permute-start | bytes 12296 | tf_op jit(solution)/shard_map/ppermute | solution.py:195
  76.8 3.6 %collective-permute-start.23 = (f32[8,128]{1,0:T(8,128)S(1)}, f32[8,128]{1,0:T(8,128)S(1)}, u32[]{:S(2)}, u32[]{:S(2)}) collective-permute-start(f32[8,128]{1,0:T(8,128)S(1)} %get-tuple-element.74.refs_0_), channel_id=1, source_target_pairs={{0,4},{2,6},{4,0},{6,2},{1,5},{3,7},{5,1},{7,3},{8,12},{10,14},{12... | collective-permute-start | bytes 12296 | tf_op jit(solution)/shard_map/ppermute | solution.py:195
  76.8 3.6 %collective-permute-start.22 = (f32[8,128]{1,0:T(8,128)S(1)}, f32[8,128]{1,0:T(8,128)S(1)}, u32[]{:S(2)}, u32[]{:S(2)}) collective-permute-start(f32[8,128]{1,0:T(8,128)S(1)} %get-tuple-element.74.refs_0_), channel_id=1, source_target_pairs={{0,2},{2,0},{4,6},{6,4},{1,3},{3,1},{5,7},{7,5},{8,10},{10,8},{12,... | collective-permute-start | bytes 12296 | tf_op jit(solution)/shard_map/ppermute | solution.py:195

commit v4 on v3

--- a/solution.py
+++ b/solution.py
@@ -14,13 +14,12 @@
 
 SOFTCAP = 50.0
 EPSILON = 1e-06
-SPREAD_AT = 2
 LOG2_E = 1.4426950408889634
 LANES = 128
 VMEM_LIMIT = 24 * 1024 * 1024
 FIRST_LIMIT = 59 * 1024 * 1024
-ROPE_LIMIT = 59 * 1024 * 1024
-PAIR_LIMIT = 59 * 1024 * 1024
+ROPE_LIMIT = 24 * 1024 * 1024
+PAIR_LIMIT = 24 * 1024 * 1024
 SUFFIX_LIMIT = 24 * 1024 * 1024
 QUERY_SCALE = (MODEL_WIDTH // QUERY_HEADS) ** (-0.5)
 
@@ -296,80 +295,92 @@
     return pl.ds(pl.multiple_of((place[0] ^ mask) * width, width), width)
 
 
-def query_projection_kernel(parts, place, gain_ref, x_hbm, w_hbm, keys_hbm, values_hbm, *refs):
-    blocks, refs = refs[: parts - 1], refs[parts - 1 :]
-    *sent, own_ref, squares_ref, scaled_ref, x_ref, w_ref, block_ref, semaphores, block_semaphores = refs
-    rows, columns = own_ref.shape
+def query_projection_kernel(place, gain_ref, x_hbm, w_hbm, *refs):
+    *sent, own_ref, scaled_ref, x_ref, w_ref, semaphores = refs
+    rows, columns = scaled_ref.shape[0], own_ref.shape[1]
     masks = (*range(1, len(sent) + 1), 0)
     x_copy = copy_in(x_hbm, x_ref, semaphores.at[len(masks)])
     w_copies = [
         copy_in(w_hbm.at[:, block_of(place, mask, columns)], w_ref.at[mask], semaphores.at[mask])
         for mask in masks
     ]
-    width = blocks[0].shape[1] // 2
-    block_copies = [
-        copy_in(
-            source.at[:, block_of(place, mask, width)],
-            block_ref.at[mask - 1, :, half * width : (half + 1) * width],
-            block_semaphores.at[mask - 1, half],
-        )
-        for mask in range(1, parts)
-        for half, source in enumerate((keys_hbm, values_hbm))
-    ]
     x_copy.wait()
     x = x_ref[...].astype(jnp.float32).reshape(rows, x_ref.shape[2])
     scaled_ref[...] = (x * gain_row(gain_ref)).astype(jnp.bfloat16)
     total = jnp.sum(x * x, axis=1, keepdims=True)
     across = jnp.broadcast_to(total, (rows, LANES)).T[:8]
-    squares_ref[...] = across
+    own_ref[rows:, :] = jnp.zeros((8, columns), jnp.float32)
+    own_ref[rows:, :rows] = across
     tail = split_rows(across)
     for ref in sent:
         ref[rows:, :] = jnp.zeros((16, ref.shape[1]), jnp.bfloat16)
         ref[rows:, :rows] = tail
     for mask, copy, ref in zip(masks, w_copies, (*sent, own_ref)):
         copy.wait()
-        if mask == SPREAD_AT:
-            for block_copy in block_copies:
-                block_copy.wait()
-            block_copies = [
-                copy_in(block_ref.at[index], target, block_semaphores.at[index, 0])
-                for index, target in enumerate(blocks)
-            ]
         product = jnp.dot(scaled_ref[...], w_ref[mask], preferred_element_type=jnp.float32)
         ref[:rows, :] = product.astype(ref.dtype)
-    for copy in block_copies:
-        copy.wait()
-
-
-def query_projection(place, x, gain, weights, keys, values, parts):
+
+
+def query_projection(place, x, gain, weights, parts):
     members, steps, width = x.shape
     rows = members * steps
     columns = weights.shape[1] // parts
-    blocks = [shape((keys.shape[0], 2 * keys.shape[1] // parts), keys.dtype)] * (parts - 1)
     outs = [shape((rows + 16, columns), jnp.bfloat16)] * (parts - 1) + [
-        shape((rows, columns), jnp.float32),
-        shape((8, rows), jnp.float32),
+        shape((rows + 8, columns), jnp.float32),
         shape((rows, width), jnp.bfloat16),
     ]
     far = pl.BlockSpec(memory_space=pl.ANY)
     return call(
-        functools.partial(query_projection_kernel, parts),
+        query_projection_kernel,
         (place,),
-        (gain, x, weights, keys, values),
-        blocks + outs,
-        [whole(gain), far, far, far, far],
-        [far] * (parts - 1) + [whole(a) for a in outs],
+        (gain, x, weights),
+        outs,
+        [whole(gain), far, far],
+        [whole(a) for a in outs],
         (1,),
         [
             pltpu.VMEM(x.shape, x.dtype),
             pltpu.VMEM((parts, width, columns), weights.dtype),
-            pltpu.VMEM((parts - 1, *blocks[0].shape), keys.dtype),
             pltpu.SemaphoreType.DMA((parts + 1,)),
-            pltpu.SemaphoreType.DMA((parts - 1, 2)),
         ],
         2 * rows * width * weights.shape[1],
         2 * width * weights.shape[1],
         FIRST_LIMIT,
+    )
+
+
+def owner_columns_kernel(place, keys_hbm, values_hbm, *refs):
+    *outs, semaphores = refs
+    width = outs[0].shape[1] // 2
+    copies = [
+        copy_in(
+            source.at[:, block_of(place, mask, width)],
+            ref.at[:, half * width : (half + 1) * width],
+            semaphores.at[mask - 1, half],
+        )
+        for mask, ref in enumerate(outs, start=1)
+        for half, source in enumerate((keys_hbm, values_hbm))
+    ]
+    for copy in copies:
+        copy.wait()
+
+
+def owner_columns(place, keys, values, parts):
+    tokens = keys.shape[0]
+    columns = keys.shape[1] // parts
+    outs = [shape((tokens, 2 * columns), keys.dtype)] * (parts - 1)
+    far = pl.BlockSpec(memory_space=pl.ANY)
+    return call(
+        owner_columns_kernel,
+        (place,),
+        (keys, values),
+        outs,
+        [far, far],
+        [whole(a) for a in outs],
+        (1,),
+        [pltpu.SemaphoreType.DMA((parts - 1, 2))],
+        20000000000,
+        8 * (parts - 1) * tokens * columns,
     )
 
 
@@ -443,10 +454,10 @@
 
 def query_rope_kernel(parts, place, own_ref, *refs):
     received, refs = refs[: parts - 1], refs[parts - 1 :]
-    squares_ref, cos_ref, sin_ref, query_ref, *suffix_refs, inverse_ref, held = refs
-    rows, columns = own_ref.shape
-    squares = squares_ref[0:1, :]
-    total = own_ref[...]
+    cos_ref, sin_ref, query_ref, *suffix_refs, inverse_ref, held = refs
+    rows, columns = cos_ref.shape[0], own_ref.shape[1]
+    squares = own_ref[rows : rows + 1, :rows]
+    total = own_ref[:rows, :]
     for ref in received:
         squares = squares + joined_row(ref[rows:, :rows], 0)
         total = total + ref[:rows, :].astype(jnp.float32)
@@ -466,10 +477,10 @@
             ].astype(jnp.bfloat16)
 
 
-def query_rope(place, own, received, squares, cosine, sine, parts):
-    rows, columns = own.shape
+def query_rope(place, own, received, cosine, sine, parts):
+    rows, columns = cosine.shape[0], own.shape[1]
     count = rows * columns // HEAD_SIZE
-    operands = (own, *received, squares, cosine, sine)
+    operands = (own, *received, cosine, sine)
     outs = (
         [shape((count, HEAD_SIZE), jnp.bfloat16)]
         + [shape((count // parts, HEAD_SIZE), jnp.bfloat16)] * parts
@@ -484,7 +495,7 @@
         [whole(a) for a in outs],
         (1,),
         [pltpu.VMEM((2 * rows, HEAD_SIZE), jnp.float32)],
-        10 * rows * columns,
+        10000000000,
         12 * rows * columns,
         ROPE_LIMIT,
     )
@@ -648,25 +659,29 @@
     )
 
 
+def diagonal(first, second):
+    zero = jnp.zeros(first.shape, first.dtype)
+    return jnp.concatenate(
+        [
+            jnp.concatenate([first, zero], axis=1),
+            jnp.concatenate([zero, second], axis=1),
+        ],
+        axis=0,
+    )
+
+
 def suffix_kernel(parts, place, lengths, own_ref, *refs):
-    received, (k_hbm, v_hbm), refs = (
+    received, (k_ref, v_ref), refs = (
         refs[: parts - 1],
         refs[parts - 1 : parts + 1],
-        refs[-(parts + 8) :],
+        refs[-(parts + 5) :],
     )
     outs, refs = refs[: parts + 1], refs[parts + 1 :]
-    query_held, k_ref, v_ref, sums, totals, packed, semaphores = refs
+    query_held, sums, totals, packed = refs
     members, slots, columns = k_ref.shape
     heads = columns // HEAD_SIZE
     near = heads // parts
     here = place[0]
-    copies = [
-        [
-            copy_in(source.at[member], ref.at[member], semaphores.at[member, half])
-            for half, (source, ref) in enumerate(((k_hbm, k_ref), (v_hbm, v_ref)))
-        ]
-        for member in range(members)
-    ]
     packed[...] = jnp.zeros(packed.shape, jnp.float32)
     count = members * 8
     for mask, ref in enumerate((own_ref, *received)):
@@ -683,15 +698,16 @@
 
     for member in range(members):
         tile = slice(member * 8, (member + 1) * 8)
-        for copy in copies[member]:
-            copy.wait()
+        pairs = [slice(at, at + 2 * HEAD_SIZE) for at in range(0, columns, 2 * HEAD_SIZE)]
         scores = jnp.concatenate(
             [
                 dot_last(
-                    query_held[head, tile, :].astype(jnp.bfloat16),
-                    k_ref[member, :, head_lanes(head)],
+                    diagonal(
+                        query_held[2 * index, tile, :], query_held[2 * index + 1, tile, :]
+                    ).astype(jnp.bfloat16),
+                    k_ref[member, :, lanes],
                 )
-                for head in range(heads)
+                for index, lanes in enumerate(pairs)
             ],
             axis=0,
         )
@@ -699,14 +715,16 @@
         weight = jnp.where(valid, capped_weight(scores), 0.0)
         total = jnp.broadcast_to(jnp.sum(weight, axis=1, keepdims=True), (heads * 8, LANES))
         weight = weight.astype(jnp.bfloat16)
-        for head in range(heads):
-            rows = slice(head * 8, (head + 1) * 8)
-            sums[head, tile, :] = jnp.dot(
-                weight[rows],
-                v_ref[member, :, head_lanes(head)],
+        for index, lanes in enumerate(pairs):
+            result = jnp.dot(
+                weight[16 * index : 16 * (index + 1)],
+                v_ref[member, :, lanes],
                 preferred_element_type=jnp.float32,
             )
-            totals[head, tile, :] = total[rows]
+            sums[2 * index, tile, :] = result[:8, :HEAD_SIZE]
+            sums[2 * index + 1, tile, :] = result[8:, HEAD_SIZE:]
+        for head in range(heads):
+            totals[head, tile, :] = total[head * 8 : (head + 1) * 8]
 
     for mask in range(parts):
         for head in range(near):
@@ -733,7 +751,7 @@
     outs = [shape((count, HEAD_SIZE), jnp.float32)] * 2 + [
         shape((count + 16, HEAD_SIZE), jnp.bfloat16)
     ] * (parts - 1)
-    far = pl.BlockSpec(memory_space=pl.ANY)
+    far = pl.BlockSpec(memory_space=pltpu.VMEM)
     return call(
         functools.partial(suffix_kernel, parts),
         (place, lengths),
@@ -747,12 +765,9 @@
         (1,),
         [
             pltpu.VMEM((heads, members * 8, HEAD_SIZE), jnp.float32),
-            pltpu.VMEM(cache_keys.shape, cache_keys.dtype),
-            pltpu.VMEM(cache_values.shape, cache_values.dtype),
             pltpu.VMEM((heads, members * 8, HEAD_SIZE), jnp.float32),
             pltpu.VMEM((heads, members * 8, HEAD_SIZE), jnp.float32),
             pltpu.VMEM((8, LANES), jnp.float32),
-            pltpu.SemaphoreType.DMA((members, 2)),
         ],
         4 * members * 8 * slots * columns,
         4 * members * slots * columns,
@@ -857,7 +872,7 @@
 
 
 def attended_kernel(place, here_ref, there_ref, out_ref, squares_ref):
-    attended = here_ref[...] + there_ref[...]
+    attended = here_ref[...] + there_ref[...].astype(jnp.float32)
     out_ref[...] = attended
     total = jnp.sum(attended * attended, axis=1, keepdims=True)
     squares_ref[...] = jnp.broadcast_to(total, (total.shape[0], LANES)).T[:8]
@@ -937,11 +952,10 @@
         moved = {m: paired(a, axis, m) for m, a in pairs[-1:] + pairs[:-1]}
         return [moved[m] for m, _ in pairs]
 
-    *sent, own, squares, scaled = query_projection(
-        place, hidden_in, pre_gain, w_query, prompt_keys, prompt_values, parts
-    )
-    received = swapped(sent[parts - 1 :], "prefix")
-    blocks = swapped(sent[: parts - 1], "prefix")
+    *sent, own, scaled = query_projection(place, hidden_in, pre_gain, w_query, parts)
+    received = swapped(sent, "prefix")
+    keys, values, _ = lax.optimization_barrier((prompt_keys, prompt_values, own))
+    blocks = swapped(owner_columns(place, keys, values, parts), "prefix")
 
     positions = (
         (prompt_total + suffix_len[:, None] + jnp.arange(steps, dtype=jnp.int32)[None, :])
@@ -956,13 +970,13 @@
     sine = jnp.concatenate([-sine, sine], axis=1)
 
     queries, *split_queries, inverse = query_rope(
-        place, own, received, squares, cosine, sine, parts
-    )
-    held_back = lax.optimization_barrier((queries, blocks[0]))[0]
-    far_queries = [paired(held_back if m == 1 else queries, "prefill", m) for m in far]
+        place, own, received, cosine, sine, parts
+    )
     pair, *sent = pair_projection(
         place, scaled, key_projection, value_projection, split_queries[1:]
     )
+    held_back = lax.optimization_barrier((queries, blocks[0], pair))[0]
+    far_queries = [paired(held_back if m == 1 else queries, "prefill", m) for m in far]
     returned = swapped(sent, "prefix")
     first = prompt_first(place, far_queries, prompt_keys, prompt_values, blocks[:1], parts)
     packed = [
@@ -989,13 +1003,16 @@
         pair,
         returned,
         (inverse, cosine, sine),
-        [near_totals],
+        [near_totals, prompt_results[2]],
     )
     mixed = mix(place, sums, totals, prompt_results, suffix, rows)
     others = [paired(mixed, "prefix", m) for m in near]
     head_terms = output_projection(place, (0,), [mixed], w_out)
-    head_terms = output_projection(place, tuple(near), others, w_out, head_terms)
-    attended, squares = attended_squares(place, head_terms, paired(head_terms, "tensor", 1))
+    for mask, other in zip(near, others):
+        head_terms = output_projection(place, (mask,), [other], w_out, head_terms)
+    attended, squares = attended_squares(
+        place, head_terms, paired(head_terms.astype(jnp.bfloat16), "tensor", 1)
+    )
     squares = [squares] + [paired(squares, "prefix", m) for m in near]
     return finish(place, hidden_in, attended, post_gain, squares)
 

time: 81.6 us -> 75.4 us (0.924)
  Pallas kernels: 27.2 us -> 22.5 us
  starting transfers between devices: 36.5 us -> 32.6 us
  waiting for transfers between devices: 15.6 us -> 18.4 us
    pallas_call x14 -> x17, Pallas kernels: 27.2 us -> 22.5 us  [call(): pl.pallas_call(kernel, out_shape=out_shape, grid_spec=pltpu.PrefetchScala...]
    ppermute x25, starting transfers between devices: 36.5 us -> 32.6 us  [paired(): return lax.ppermute(values, axis, [(i, i ^ mask) for i in range(size)])]
    ppermute x25, waiting for transfers between devices: 15.6 us -> 18.4 us  [paired(): return lax.ppermute(values, axis, [(i, i ^ mask) for i in range(size)])]
  transfers between devices with their start and end apart: 25 -> 25, of which waited for: 13 -> 16; matrix products, arithmetic and copies ran while one was open for 2% -> 1% of each run, Pallas kernels for 23% -> 21%
where the time goes in v4:
time: 75.4 us; the launch traced here: 75.2 us
  starting transfers between devices  32.6 us (43%)
  Pallas kernels  22.5 us (30%)
  waiting for transfers between devices  18.4 us (24%)
  local copies, waits for them, and re-layouts  0.97 us (1%)
    ppermute x25, starting transfers between devices, paired(): return lax.ppermute(values, axis, [(i, i ^ mask) for i in range(size)])  32.6 us
    pallas_call x17, Pallas kernels, call(): pl.pallas_call(kernel, out_shape=out_shape, grid_spec=pltpu.PrefetchScala...  22.5 us
    ppermute x25, waiting for transfers between devices, paired(): return lax.ppermute(values, axis, [(i, i ^ mask) for i in range(size)])  18.4 us
  transfers between devices with their start and end apart: 25, of which 16 were waited for; matrix products, arithmetic and copies ran while one was open for 1% of the time, Pallas kernels for 21%

profile of v4, /device:TPU:0, one launch (start us, length us, event | category | flops | bytes accessed | tf_op | source)
XLA Modules:
  0.0 75.2 jit_solution(2424602831272724683)
XLA Ops:
  0.0 4.5 %shard_map.118 = (bf16[144,512]{1,0:T(8,128)(2,1)}, bf16[144,512]{1,0:T(8,128)(2,1)}, bf16[144,512]{1,0:T(8,128)(2,1)}, f32[136,512]{1,0:T(8,128)}, bf16[128,1152]{1,0:T(8,128)(2,1)}) custom-call(s32[1]{0:T(128)} %bitcast.place, f32[1152]{0:T(1024)} %gain_ref.2, bf16[32,4,1152]{2,1,0:T(4,128)(2,1)} %x_ref.1, bf16[1152,2048]{1,0:T(8,128)(2,1)} %w_hbm.1), custom_call_target="tpu_custom_call" | custom-call | flops 603979776 | bytes 4718592 | tf_op jit(solution)/shard_map/pallas_call | solution.py:210
  4.5 3.0 %collective-permute-start = (bf16[144,512]{1,0:T(8,128)(2,1)}, bf16[144,512]{1,0:T(8,128)(2,1)}, u32[]{:S(2)}, u32[]{:S(2)}) collective-permute-start(bf16[144,512]{1,0:T(8,128)(2,1)} %get-tuple-element.42), channel_id=1, source_target_pairs={{0,2},{2,0},{4,6},{6,4},{1,3},{3,1},{5,7},{7,5},{8,10},{10,8},{12,... | collective-permute-start | bytes 442376 | tf_op jit(solution)/shard_map/ppermute | solution.py:194
  7.5 1.5 %collective-permute-start.1 = (bf16[144,512]{1,0:T(8,128)(2,1)}, bf16[144,512]{1,0:T(8,128)(2,1)}, u32[]{:S(2)}, u32[]{:S(2)}) collective-permute-start(bf16[144,512]{1,0:T(8,128)(2,1)} %get-tuple-element.43), channel_id=1, source_target_pairs={{0,4},{2,6},{4,0},{6,2},{1,5},{3,7},{5,1},{7,3},{8,12},{10,14},{12... | collective-permute-start | bytes 442376 | tf_op jit(solution)/shard_map/ppermute | solution.py:194
  9.1 1.3 %shard_map.120 = (bf16[512,512]{1,0:T(8,128)(2,1)}, bf16[512,512]{1,0:T(8,128)(2,1)}, bf16[512,512]{1,0:T(8,128)(2,1)S(1)}) custom-call(s32[1]{0:T(128)} %bitcast.place, bf16[512,1024]{1,0:T(8,128)(2,1)S(1)} %copy-done.5, bf16[512,1024]{1,0:T(8,128)(2,1)S(1)} %copy-done.6), custom_call_target="tpu_custom_call" | custom-call | flops 20000000000 | bytes 3145728 | tf_op jit(solution)/shard_map/pallas_call | solution.py:210
  10.4 0.8 %copy-done.10 = bf16[512,512]{1,0:T(8,128)(2,1)} copy-done((bf16[512,512]{1,0:T(8,128)(2,1)}, bf16[512,512]{1,0:T(8,128)(2,1)S(1)}, u32[]{:S(2)}) %copy-start.10) | copy-done | bytes 524312
  11.2 1.9 %collective-permute-start.3 = (bf16[512,512]{1,0:T(8,128)(2,1)}, bf16[512,512]{1,0:T(8,128)(2,1)S(1)}, u32[]{:S(2)}, u32[]{:S(2)}) collective-permute-start(bf16[512,512]{1,0:T(8,128)(2,1)} %get-tuple-element.48), channel_id=1, source_target_pairs={{0,2},{2,0},{4,6},{6,4},{1,3},{3,1},{5,7},{7,5},{8,10},{10,8},{12,... | collective-permute-start | bytes 1572872 | tf_op jit(solution)/shard_map/ppermute | solution.py:194
  13.1 1.5 %collective-permute-start.4 = (bf16[512,512]{1,0:T(8,128)(2,1)}, bf16[512,512]{1,0:T(8,128)(2,1)S(1)}, u32[]{:S(2)}, u32[]{:S(2)}) collective-permute-start(bf16[512,512]{1,0:T(8,128)(2,1)} %get-tuple-element.49), channel_id=1, source_target_pairs={{0,4},{2,6},{4,0},{6,2},{1,5},{3,7},{5,1},{7,3},{8,12},{10,14},{12... | collective-permute-start | bytes 1572872 | tf_op jit(solution)/shard_map/ppermute | solution.py:194
  15.5 0.6 collective-permute-done.1.refs_1_
  16.1 0.9 %collective-permute-done.2.refs_2_ = bf16[144,512]{1,0:T(8,128)(2,1)} collective-permute-done((bf16[144,512]{1,0:T(8,128)(2,1)}, bf16[144,512]{1,0:T(8,128)(2,1)}, u32[]{:S(2)}, u32[]{:S(2)}) %collective-permute-start.2) | collective-permute-done | bytes 147488 | tf_op jit(solution)/shard_map/ppermute | solution.py:194
  17.1 1.4 %shard_map.119 = (bf16[512,128]{1,0:T(8,128)(2,1)S(1)}, bf16[128,128]{1,0:T(8,128)(2,1)S(1)}, bf16[128,128]{1,0:T(8,128)(2,1)S(1)}, bf16[128,128]{1,0:T(8,128)(2...) custom-call(s32[1]{0:T(128)} %bitcast.place, f32[136,512]{1,0:T(8,128)S(1)} %copy-done.11, ...), custom_call_target="tpu_custom_call" | custom-call | flops 10000000000 | bytes 786432 | tf_op jit(solution)/shard_map/pallas_call | solution.py:210
  18.5 3.7 %collective-permute-start.11 = (bf16[512,128]{1,0:T(8,128)(2,1)S(1)}, bf16[512,128]{1,0:T(8,128)(2,1)S(1)}, u32[]{:S(2)}, u32[]{:S(2)}) collective-permute-start(bf16[512,128]{1,0:T(8,128)(2,1)S(1)} %get-tuple-element.61.q_ref), channel_id=1, source_target_pairs={{0,24},{8,16},{16,8},{24,0},{1,25},{9,17},{17,9},{25,1},{2,26},{10... | collective-permute-start | bytes 393224 | tf_op jit(solution)/shard_map/ppermute | solution.py:194
  22.2 2.3 %shard_map.121 = (f32[128,512]{1,0:T(8,128)S(1)}, bf16[160,512]{1,0:T(8,128)(2,1)S(1)}, bf16[160,512]{1,0:T(8,128)(2,1)S(1)}, bf16[160,512]{1,0:T(8,128)(2,1)S(1)}) custom-call(s32[1]{0:T(128)} %bitcast.place, bf16[128,1152]{1,0:T(8,128)(2,1)S(1)} %copy-done.7, bf16[1152,1024]{1,0:T(8,128)(2,1)S(1)} %copy-done.2, bf16[1152,1024]{1,0:T(8,128)(2,1)S(1)} %copy-done.3, ...), custom_call_target="tpu_custom_call" | custom-call | flops 603979776 | bytes 4718592 | tf_op jit(solution)/shard_map/pallas_call | solution.py:210
  24.5 2.8 %collective-permute-done.3.refs_5_.refs_0_ = bf16[512,512]{1,0:T(8,128)(2,1)S(1)} collective-permute-done((bf16[512,512]{1,0:T(8,128)(2,1)}, bf16[512,512]{1,0:T(8,128)(2,1)S(1)}, u32[]{:S(2)}, u32[]{:S(2)}) %collective-permute-start.3) | collective-permute-done | bytes 524320 | tf_op jit(solution)/shard_map/ppermute | solution.py:194
  27.3 1.6 %collective-permute-start.9 = (bf16[512,128]{1,0:T(8,128)(2,1)S(1)}, bf16[512,128]{1,0:T(8,128)(2,1)S(1)}, u32[]{:S(2)}, u32[]{:S(2)}) collective-permute-start(bf16[512,128]{1,0:T(8,128)(2,1)S(1)} %get-tuple-element.61.q_ref), channel_id=1, source_target_pairs={{0,8},{8,0},{16,24},{24,16},{1,9},{9,1},{17,25},{25,17},{2,10},{10... | collective-permute-start | bytes 393224 | tf_op jit(solution)/shard_map/ppermute | solution.py:194
  28.8 1.6 %collective-permute-start.6 = (bf16[160,512]{1,0:T(8,128)(2,1)S(1)}, bf16[160,512]{1,0:T(8,128)(2,1)S(1)}, u32[]{:S(2)}, u32[]{:S(2)}) collective-permute-start(bf16[160,512]{1,0:T(8,128)(2,1)S(1)} %get-tuple-element.56), channel_id=1, source_target_pairs={{0,2},{2,0},{4,6},{6,4},{1,3},{3,1},{5,7},{7,5},{8,10},{10,8},{12,... | collective-permute-start | bytes 491528 | tf_op jit(solution)/shard_map/ppermute | solution.py:194
  30.4 1.2 %collective-permute-done.10.refs_1_.q_ref = bf16[512,128]{1,0:T(8,128)(2,1)S(1)} collective-permute-done((bf16[512,128]{1,0:T(8,128)(2,1)S(1)}, bf16[512,128]{1,0:T(8,128)(2,1)S(1)}, u32[]{:S(2)}, u32[]{:S(2)}) %collective-permute-start.10) | collective-permute-done | bytes 131104 | tf_op jit(solution)/shard_map/ppermute | solution.py:194
  31.6 0.5 collective-permute-start.7
  32.1 1.3 %collective-permute-done.9.refs_0_.q_ref = bf16[512,128]{1,0:T(8,128)(2,1)S(1)} collective-permute-done((bf16[512,128]{1,0:T(8,128)(2,1)S(1)}, bf16[512,128]{1,0:T(8,128)(2,1)S(1)}, u32[]{:S(2)}, u32[]{:S(2)}) %collective-permute-start.9) | collective-permute-done | bytes 131104 | tf_op jit(solution)/shard_map/ppermute | solution.py:194
  33.4 1.9 %collective-permute-start.8 = (bf16[160,512]{1,0:T(8,128)(2,1)S(1)}, bf16[160,512]{1,0:T(8,128)(2,1)S(1)}, u32[]{:S(2)}, u32[]{:S(2)}) collective-permute-start(bf16[160,512]{1,0:T(8,128)(2,1)S(1)} %get-tuple-element.58), channel_id=1, source_target_pairs={{0,6},{2,4},{4,2},{6,0},{1,7},{3,5},{5,3},{7,1},{8,14},{10,12},{12... | collective-permute-start | bytes 491528 | tf_op jit(solution)/shard_map/ppermute | solution.py:194
  35.2 2.1 %shard_map.122 = (f32[512,128]{1,0:T(8,128)S(1)}, f32[512,128]{1,0:T(8,128)S(1)}, f32[512,128]{1,0:T(8,128)S(1)}, f32[512,128]{1,0:T(8,128)S(1)}, f32[512,128]{1,0:T(8,128)S(1)}, /*index=5*/f32[512,128]{1,0:T(8,128)S(1)}) custom-call(s32[1]{0:T(128)} %bitcast.place, bf16[512,128]{1,0:T(8,128)(2,1)S(1)} %collective-permute-done.9.refs_0_.q_ref, ...), custom_call_target="tpu_custom_call" | custom-call | flops 1207959552 | bytes 1048576 | tf_op jit(solution)/shard_map/pallas_call | solution.py:210
  37.3 1.3 %collective-permute-done.4.refs_0_.refs_1_ = bf16[512,512]{1,0:T(8,128)(2,1)S(1)} collective-permute-done((bf16[512,512]{1,0:T(8,128)(2,1)}, bf16[512,512]{1,0:T(8,128)(2,1)S(1)}, u32[]{:S(2)}, u32[]{:S(2)}) %collective-permute-start.4) | collective-permute-done | bytes 524320 | tf_op jit(solution)/shard_map/ppermute | solution.py:194
  38.6 0.9 %collective-permute-done.5.refs_1_.refs_2_ = bf16[512,512]{1,0:T(8,128)(2,1)S(1)} collective-permute-done((bf16[512,512]{1,0:T(8,128)(2,1)}, bf16[512,512]{1,0:T(8,128)(2,1)S(1)}, u32[]{:S(2)}, u32[]{:S(2)}) %collective-permute-start.5) | collective-permute-done | bytes 524320 | tf_op jit(solution)/shard_map/ppermute | solution.py:194
  39.5 1.0 %shard_map.125.refs_7_ = bf16[528,128]{1,0:T(8,128)(2,1)S(1)} custom-call(s32[1]{0:T(128)} %bitcast.place, bf16[512,128]{1,0:T(8,128)(2,1)S(1)} %collective-permute-done.11.refs_2_.q_ref, bf16[512,512]{1,0:T(8,128)(2,1)S(1)} %collective-permute-done.4.refs_0_.refs_1_, bf16[512,512]{1,0:T(8,128)(2,1)S(1)} %collective-permute-done.5.refs_1_.refs_2_, ...), custom_call_target="tpu_custom_call" | custom-call | flops 402653184 | bytes 1048576 | tf_op jit(solution)/shard_map/pallas_call | solution.py:210
  40.5 3.6 %collective-permute-start.12 = (bf16[528,128]{1,0:T(8,128)(2,1)S(1)}, bf16[528,128]{1,0:T(8,128)(2,1)S(1)}, u32[]{:S(2)}, u32[]{:S(2)}) collective-permute-start(bf16[528,128]{1,0:T(8,128)(2,1)S(1)} %shard_map.125.refs_7_), channel_id=1, source_target_pairs={{0,24},{8,16},{16,8},{24,0},{1,25},{9,17},{17,9},{25,1},{2,26},{10... | collective-permute-start | bytes 405512 | tf_op jit(solution)/shard_map/ppermute | solution.py:194
  44.1 1.0 %shard_map.124.refs_6_ = bf16[528,128]{1,0:T(8,128)(2,1)S(1)} custom-call(s32[1]{0:T(128)} %bitcast.place, bf16[512,128]{1,0:T(8,128)(2,1)S(1)} %collective-permute-done.10.refs_1_.q_ref, bf16[512,512]{1,0:T(8,128)(2,1)S(1)} %collective-permute-done.4.refs_0_.refs_1_, bf16[512,512]{1,0:T(8,128)(2,1)S(1)} %collective-permute-done.5.refs_1_.refs_2_, ...), custom_call_target="tpu_custom_call" | custom-call | flops 402653184 | bytes 1048576 | tf_op jit(solution)/shard_map/pallas_call | solution.py:210
  45.2 1.0 %shard_map.123.refs_5_ = bf16[528,128]{1,0:T(8,128)(2,1)S(1)} custom-call(s32[1]{0:T(128)} %bitcast.place, bf16[512,128]{1,0:T(8,128)(2,1)S(1)} %collective-permute-done.9.refs_0_.q_ref, bf16[512,512]{1,0:T(8,128)(2,1)S(1)} %collective-permute-done.4.refs_0_.refs_1_, bf16[512,512]{1,0:T(8,128)(2,1)S(1)} %collective-permute-done.5.refs_1_.refs_2_, ...), custom_call_target="tpu_custom_call" | custom-call | flops 402653184 | bytes 1048576 | tf_op jit(solution)/shard_map/pallas_call | solution.py:210
  46.2 0.8 %collective-permute-start.13 = (bf16[528,128]{1,0:T(8,128)(2,1)S(1)}, bf16[528,128]{1,0:T(8,128)(2,1)S(1)}, u32[]{:S(2)}, u32[]{:S(2)}) collective-permute-start(bf16[528,128]{1,0:T(8,128)(2,1)S(1)} %shard_map.123.refs_5_), channel_id=1, source_target_pairs={{0,8},{8,0},{16,24},{24,16},{1,9},{9,1},{17,25},{25,17},{2,10},{10... | collective-permute-start | bytes 405512 | tf_op jit(solution)/shard_map/ppermute | solution.py:194
  47.1 2.9 %shard_map.126 = (f32[128,128]{1,0:T(8,128)S(1)}, f32[128,128]{1,0:T(8,128)S(1)}, bf16[144,128]{1,0:T(8,128)(2,1)S(1)}, bf16[144,128]{1,0:T(8,128)(2,1)S(1)}, bf16[144,128]{1,0:T(8,128)(2,1)S(1)}) custom-call(s32[1]{0:T(128)} %bitcast.place, s32[32]{0:T(128)S(1)} %copy-done.9, bf16[128,128]{1,0:T(8,128)(2,1)S(1)} %get-tuple-element.60.own_ref, ...), custom_call_target="tpu_custom_call" | custom-call | flops 67108864 | bytes 8388608 | tf_op jit(solution)/shard_map/pallas_call | solution.py:210
  49.9 1.7 %collective-permute-start.15 = (bf16[144,128]{1,0:T(8,128)(2,1)S(1)}, bf16[144,128]{1,0:T(8,128)(2,1)S(1)}, u32[]{:S(2)}, u32[]{:S(2)}) collective-permute-start(bf16[144,128]{1,0:T(8,128)(2,1)S(1)} %get-tuple-element.72), channel_id=1, source_target_pairs={{0,2},{2,0},{4,6},{6,4},{1,3},{3,1},{5,7},{7,5},{8,10},{10,8},{12,... | collective-permute-start | bytes 110600 | tf_op jit(solution)/shard_map/ppermute | solution.py:194
  51.6 0.5 collective-permute-start.16
  52.1 1.4 %collective-permute-start.17 = (bf16[144,128]{1,0:T(8,128)(2,1)S(1)}, bf16[144,128]{1,0:T(8,128)(2,1)S(1)}, u32[]{:S(2)}, u32[]{:S(2)}) collective-permute-start(bf16[144,128]{1,0:T(8,128)(2,1)S(1)} %get-tuple-element.74), channel_id=1, source_target_pairs={{0,6},{2,4},{4,2},{6,0},{1,7},{3,5},{5,3},{7,1},{8,14},{10,12},{12... | collective-permute-start | bytes 110600 | tf_op jit(solution)/shard_map/ppermute | solution.py:194
  53.5 2.0 %shard_map.127 = (f32[512,128]{1,0:T(8,128)S(1)}, f32[512,128]{1,0:T(8,128)S(1)}) custom-call(s32[1]{0:T(128)} %bitcast.place, bf16[512,128]{1,0:T(8,128)(2,1)S(1)} %get-tuple-element.61.q_ref, bf16[512,1024]{1,0:T(8,128)(2,1)S(1)} %copy-done.5, bf16[512,1024]{1,0:T(8,128)(2,1)S(1)} %copy-done.6, ...), custom_call_target="tpu_custom_call" | custom-call | flops 805306368 | bytes 1048576 | tf_op jit(solution)/shard_map/pallas_call | solution.py:210
  55.6 1.4 %collective-permute-done.17.refs_7_ = bf16[144,128]{1,0:T(8,128)(2,1)S(1)} collective-permute-done((bf16[144,128]{1,0:T(8,128)(2,1)S(1)}, bf16[144,128]{1,0:T(8,128)(2,1)S(1)}, u32[]{:S(2)}, u32[]{:S(2)}) %collective-permute-start.17) | collective-permute-done | bytes 36896 | tf_op jit(solution)/shard_map/ppermute | solution.py:194
  57.0 0.4 shard_map.128.refs_0_
  57.4 1.5 %collective-permute-start.20 = (bf16[128,512]{1,0:T(8,128)(2,1)S(1)}, bf16[128,512]{1,0:T(8,128)(2,1)S(1)}, u32[]{:S(2)}, u32[]{:S(2)}) collective-permute-start(bf16[128,512]{1,0:T(8,128)(2,1)S(1)} %shard_map.128.refs_0_), channel_id=1, source_target_pairs={{0,2},{2,0},{4,6},{6,4},{1,3},{3,1},{5,7},{7,5},{8,10},{10,8},{12,... | collective-permute-start | bytes 393224 | tf_op jit(solution)/shard_map/ppermute | solution.py:194
  58.9 0.5 collective-permute-start.19
  59.4 1.6 %collective-permute-start.18 = (bf16[128,512]{1,0:T(8,128)(2,1)S(1)}, bf16[128,512]{1,0:T(8,128)(2,1)S(1)}, u32[]{:S(2)}, u32[]{:S(2)}) collective-permute-start(bf16[128,512]{1,0:T(8,128)(2,1)S(1)} %shard_map.128.refs_0_), channel_id=1, source_target_pairs={{0,6},{2,4},{4,2},{6,0},{1,7},{3,5},{5,3},{7,1},{8,14},{10,12},{12... | collective-permute-start | bytes 393224 | tf_op jit(solution)/shard_map/ppermute | solution.py:194
  61.3 1.1 %collective-permute-done.20.refs_0_ = bf16[128,512]{1,0:T(8,128)(2,1)S(1)} collective-permute-done((bf16[128,512]{1,0:T(8,128)(2,1)S(1)}, bf16[128,512]{1,0:T(8,128)(2,1)S(1)}, u32[]{:S(2)}, u32[]{:S(2)}) %collective-permute-start.20) | collective-permute-done | bytes 131104 | tf_op jit(solution)/shard_map/ppermute | solution.py:194
  62.8 1.1 %collective-permute-done.19.refs_0_ = bf16[128,512]{1,0:T(8,128)(2,1)S(1)} collective-permute-done((bf16[128,512]{1,0:T(8,128)(2,1)S(1)}, bf16[128,512]{1,0:T(8,128)(2,1)S(1)}, u32[]{:S(2)}, u32[]{:S(2)}) %collective-permute-start.19) | collective-permute-done | bytes 131104 | tf_op jit(solution)/shard_map/ppermute | solution.py:194
  64.2 1.0 %collective-permute-done.18.refs_0_ = bf16[128,512]{1,0:T(8,128)(2,1)S(1)} collective-permute-done((bf16[128,512]{1,0:T(8,128)(2,1)S(1)}, bf16[128,512]{1,0:T(8,128)(2,1)S(1)}, u32[]{:S(2)}, u32[]{:S(2)}) %collective-permute-start.18) | collective-permute-done | bytes 131104 | tf_op jit(solution)/shard_map/ppermute | solution.py:194
  65.8 1.6 %collective-permute-done.21.there_ref = bf16[128,1152]{1,0:T(8,128)(2,1)S(1)} collective-permute-done((bf16[128,1152]{1,0:T(8,128)(2,1)S(1)}, bf16[128,1152]{1,0:T(8,128)(2,1)S(1)}, u32[]{:S(2)}, u32[]{:S(2)}) %collective-permute-start.21) | collective-permute-done | bytes 294944 | tf_op jit(solution)/shard_map/ppermute | solution.py:194
  67.5 1.6 %collective-permute-start.24 = (f32[8,128]{1,0:T(8,128)S(1)}, f32[8,128]{1,0:T(8,128)S(1)}, u32[]{:S(2)}, u32[]{:S(2)}) collective-permute-start(f32[8,128]{1,0:T(8,128)S(1)} %get-tuple-element.76.refs_0_), channel_id=1, source_target_pairs={{0,6},{2,4},{4,2},{6,0},{1,7},{3,5},{5,3},{7,1},{8,14},{10,12},{12... | collective-permute-start | bytes 12296 | tf_op jit(solution)/shard_map/ppermute | solution.py:194
  69.1 1.5 %collective-permute-start.23 = (f32[8,128]{1,0:T(8,128)S(1)}, f32[8,128]{1,0:T(8,128)S(1)}, u32[]{:S(2)}, u32[]{:S(2)}) collective-permute-start(f32[8,128]{1,0:T(8,128)S(1)} %get-tuple-element.76.refs_0_), channel_id=1, source_target_pairs={{0,4},{2,6},{4,0},{6,2},{1,5},{3,7},{5,1},{7,3},{8,12},{10,14},{12... | collective-permute-start | bytes 12296 | tf_op jit(solution)/shard_map/ppermute | solution.py:194
  70.6 0.4 collective-permute-start.22
  71.0 1.0 %collective-permute-done.24.refs_3_ = f32[8,128]{1,0:T(8,128)S(1)} collective-permute-done((f32[8,128]{1,0:T(8,128)S(1)}, f32[8,128]{1,0:T(8,128)S(1)}, u32[]{:S(2)}, u32[]{:S(2)}) %collective-permute-start.24) | collective-permute-done | bytes 4128 | tf_op jit(solution)/shard_map/ppermute | solution.py:194
  72.0 0.7 collective-permute-done.23.refs_2_
  72.7 1.5 %collective-permute-done.22.refs_1_ = f32[8,128]{1,0:T(8,128)S(1)} collective-permute-done((f32[8,128]{1,0:T(8,128)S(1)}, f32[8,128]{1,0:T(8,128)S(1)}, u32[]{:S(2)}, u32[]{:S(2)}) %collective-permute-start.22) | collective-permute-done | bytes 4128 | tf_op jit(solution)/shard_map/ppermute | solution.py:194
  74.2 1.0 %shard_map.134 = bf16[32,4,1152]{2,1,0:T(4,128)(2,1)} custom-call(s32[1]{0:T(128)} %bitcast.place, bf16[32,4,1152]{2,1,0:T(4,128)(2,1)S(1)} %copy-done.4, f32[128,1152]{1,0:T(8,128)S(1)} %get-tuple-element.75.attended_ref, f32[1152]{0:T(1024)S(1)} %copy-done.8, f32[8,128]{1,0:T(8,128)S(1)} %get-tuple-element.76.refs_0_, ...), custom_call_target="tpu_custom_call" | custom-call | flops 589824 | bytes 1179648 | tf_op jit(solution)/shard_map/pallas_call | solution.py:210
  (55 shorter events, 2.7 us)
Async XLA Ops:
  0.0 9.1 %copy-start.6 = (bf16[512,1024]{1,0:T(8,128)(2,1)S(1)}, bf16[512,1024]{1,0:T(8,128)(2,1)}, u32[]{:S(2)}) copy-start(bf16[512,1024]{1,0:T(8,128)(2,1)} %v_ref.1) | copy-start | bytes 3145732
  0.0 9.1 %copy-start.5 = (bf16[512,1024]{1,0:T(8,128)(2,1)S(1)}, bf16[512,1024]{1,0:T(8,128)(2,1)}, u32[]{:S(2)}) copy-start(bf16[512,1024]{1,0:T(8,128)(2,1)} %k_ref.1) | copy-start | bytes 3145732
  4.5 10.8 %collective-permute-start = (bf16[144,512]{1,0:T(8,128)(2,1)}, bf16[144,512]{1,0:T(8,128)(2,1)}, u32[]{:S(2)}, u32[]{:S(2)}) collective-permute-start(bf16[144,512]{1,0:T(8,128)(2,1)} %get-tuple-element.42), channel_id=1, source_target_pairs={{0,2},{2,0},{4,6},{6,4},{1,3},{3,1},{5,7},{7,5},{8,10},{10,8},{12,... | collective-permute-start | bytes 442376 | tf_op jit(solution)/shard_map/ppermute | solution.py:194
  7.5 8.6 %collective-permute-start.1 = (bf16[144,512]{1,0:T(8,128)(2,1)}, bf16[144,512]{1,0:T(8,128)(2,1)}, u32[]{:S(2)}, u32[]{:S(2)}) collective-permute-start(bf16[144,512]{1,0:T(8,128)(2,1)} %get-tuple-element.43), channel_id=1, source_target_pairs={{0,4},{2,6},{4,0},{6,2},{1,5},{3,7},{5,1},{7,3},{8,12},{10,14},{12... | collective-permute-start | bytes 442376 | tf_op jit(solution)/shard_map/ppermute | solution.py:194
  9.0 8.0 %collective-permute-start.2 = (bf16[144,512]{1,0:T(8,128)(2,1)}, bf16[144,512]{1,0:T(8,128)(2,1)}, u32[]{:S(2)}, u32[]{:S(2)}) collective-permute-start(bf16[144,512]{1,0:T(8,128)(2,1)} %get-tuple-element.44), channel_id=1, source_target_pairs={{0,6},{2,4},{4,2},{6,0},{1,7},{3,5},{5,3},{7,1},{8,14},{10,12},{12... | collective-permute-start | bytes 442376 | tf_op jit(solution)/shard_map/ppermute | solution.py:194
  9.1 5.6 %copy-start.9 = (s32[32]{0:T(128)S(1)}, s32[32]{0:T(128)}, u32[]{:S(2)}) copy-start(s32[32]{0:T(128)} %lengths.1) | copy-start | bytes 388
  9.1 8.0 %copy-start.11 = (f32[136,512]{1,0:T(8,128)S(1)}, f32[136,512]{1,0:T(8,128)}, u32[]{:S(2)}) copy-start(f32[136,512]{1,0:T(8,128)} %get-tuple-element.41.own_ref) | copy-start | bytes 835588
  10.4 0.8 %copy-start.10 = (bf16[512,512]{1,0:T(8,128)(2,1)}, bf16[512,512]{1,0:T(8,128)(2,1)S(1)}, u32[]{:S(2)}) copy-start(bf16[512,512]{1,0:T(8,128)(2,1)S(1)} %get-tuple-element.50) | copy-start | bytes 1572868
  11.2 16.1 %collective-permute-start.3 = (bf16[512,512]{1,0:T(8,128)(2,1)}, bf16[512,512]{1,0:T(8,128)(2,1)S(1)}, u32[]{:S(2)}, u32[]{:S(2)}) collective-permute-start(bf16[512,512]{1,0:T(8,128)(2,1)} %get-tuple-element.48), channel_id=1, source_target_pairs={{0,2},{2,0},{4,6},{6,4},{1,3},{3,1},{5,7},{7,5},{8,10},{10,8},{12,... | collective-permute-start | bytes 1572872 | tf_op jit(solution)/shard_map/ppermute | solution.py:194
  13.1 25.5 %collective-permute-start.4 = (bf16[512,512]{1,0:T(8,128)(2,1)}, bf16[512,512]{1,0:T(8,128)(2,1)S(1)}, u32[]{:S(2)}, u32[]{:S(2)}) collective-permute-start(bf16[512,512]{1,0:T(8,128)(2,1)} %get-tuple-element.49), channel_id=1, source_target_pairs={{0,4},{2,6},{4,0},{6,2},{1,5},{3,7},{5,1},{7,3},{8,12},{10,14},{12... | collective-permute-start | bytes 1572872 | tf_op jit(solution)/shard_map/ppermute | solution.py:194
  15.3 24.2 %collective-permute-start.5 = (bf16[512,512]{1,0:T(8,128)(2,1)}, bf16[512,512]{1,0:T(8,128)(2,1)S(1)}, u32[]{:S(2)}, u32[]{:S(2)}) collective-permute-start(bf16[512,512]{1,0:T(8,128)(2,1)} %copy-done.10), channel_id=1, source_target_pairs={{0,6},{2,4},{4,2},{6,0},{1,7},{3,5},{5,3},{7,1},{8,14},{10,12},{12... | collective-permute-start | bytes 1572872 | tf_op jit(solution)/shard_map/ppermute | solution.py:194
  17.1 5.1 %copy-start.2 = (bf16[1152,1024]{1,0:T(8,128)(2,1)S(1)}, bf16[1152,1024]{1,0:T(8,128)(2,1)}, u32[]{:S(2)}) copy-start(bf16[1152,1024]{1,0:T(8,128)(2,1)} %k_hbm.1) | copy-start | bytes 7077892
  17.1 5.1 %copy-start.3 = (bf16[1152,1024]{1,0:T(8,128)(2,1)S(1)}, bf16[1152,1024]{1,0:T(8,128)(2,1)}, u32[]{:S(2)}) copy-start(bf16[1152,1024]{1,0:T(8,128)(2,1)} %v_hbm.1) | copy-start | bytes 7077892
  17.1 5.1 %copy-start.7 = (bf16[128,1152]{1,0:T(8,128)(2,1)S(1)}, bf16[128,1152]{1,0:T(8,128)(2,1)}, u32[]{:S(2)}) copy-start(bf16[128,1152]{1,0:T(8,128)(2,1)} %get-tuple-element.51.scaled_ref) | copy-start | bytes 884740
  18.5 10.3 %collective-permute-start.11 = (bf16[512,128]{1,0:T(8,128)(2,1)S(1)}, bf16[512,128]{1,0:T(8,128)(2,1)S(1)}, u32[]{:S(2)}, u32[]{:S(2)}) collective-permute-start(bf16[512,128]{1,0:T(8,128)(2,1)S(1)} %get-tuple-element.61.q_ref), channel_id=1, source_target_pairs={{0,24},{8,16},{16,8},{24,0},{1,25},{9,17},{17,9},{25,1},{2,26},{10... | collective-permute-start | bytes 393224 | tf_op jit(solution)/shard_map/ppermute | solution.py:194
  22.2 9.5 %collective-permute-start.10 = (bf16[512,128]{1,0:T(8,128)(2,1)S(1)}, bf16[512,128]{1,0:T(8,128)(2,1)S(1)}, u32[]{:S(2)}, u32[]{:S(2)}) collective-permute-start(bf16[512,128]{1,0:T(8,128)(2,1)S(1)} %get-tuple-element.61.q_ref), channel_id=1, source_target_pairs={{0,16},{8,24},{16,0},{24,8},{1,17},{9,25},{17,1},{25,9},{2,18},{10... | collective-permute-start | bytes 393224 | tf_op jit(solution)/shard_map/ppermute | solution.py:194
  27.3 6.1 %collective-permute-start.9 = (bf16[512,128]{1,0:T(8,128)(2,1)S(1)}, bf16[512,128]{1,0:T(8,128)(2,1)S(1)}, u32[]{:S(2)}, u32[]{:S(2)}) collective-permute-start(bf16[512,128]{1,0:T(8,128)(2,1)S(1)} %get-tuple-element.61.q_ref), channel_id=1, source_target_pairs={{0,8},{8,0},{16,24},{24,16},{1,9},{9,1},{17,25},{25,17},{2,10},{10... | collective-permute-start | bytes 393224 | tf_op jit(solution)/shard_map/ppermute | solution.py:194
  28.8 17.4 %collective-permute-start.6 = (bf16[160,512]{1,0:T(8,128)(2,1)S(1)}, bf16[160,512]{1,0:T(8,128)(2,1)S(1)}, u32[]{:S(2)}, u32[]{:S(2)}) collective-permute-start(bf16[160,512]{1,0:T(8,128)(2,1)S(1)} %get-tuple-element.56), channel_id=1, source_target_pairs={{0,2},{2,0},{4,6},{6,4},{1,3},{3,1},{5,7},{7,5},{8,10},{10,8},{12,... | collective-permute-start | bytes 491528 | tf_op jit(solution)/shard_map/ppermute | solution.py:194
  31.6 15.4 %collective-permute-start.7 = (bf16[160,512]{1,0:T(8,128)(2,1)S(1)}, bf16[160,512]{1,0:T(8,128)(2,1)S(1)}, u32[]{:S(2)}, u32[]{:S(2)}) collective-permute-start(bf16[160,512]{1,0:T(8,128)(2,1)S(1)} %get-tuple-element.57), channel_id=1, source_target_pairs={{0,4},{2,6},{4,0},{6,2},{1,5},{3,7},{5,1},{7,3},{8,12},{10,14},{12... | collective-permute-start | bytes 491528 | tf_op jit(solution)/shard_map/ppermute | solution.py:194
  33.4 13.7 %copy-start = (bf16[8,256,1024]{2,1,0:T(8,128)(2,1)S(1)}, bf16[8,256,1024]{2,1,0:T(8,128)(2,1)}, u32[]{:S(2)}) copy-start(bf16[8,256,1024]{2,1,0:T(8,128)(2,1)} %refs_3_.3) | copy-start | bytes 12582916
  33.4 13.7 %copy-start.1 = (bf16[8,256,1024]{2,1,0:T(8,128)(2,1)S(1)}, bf16[8,256,1024]{2,1,0:T(8,128)(2,1)}, u32[]{:S(2)}) copy-start(bf16[8,256,1024]{2,1,0:T(8,128)(2,1)} %refs_4_.3) | copy-start | bytes 12582916
  33.4 13.7 %collective-permute-start.8 = (bf16[160,512]{1,0:T(8,128)(2,1)S(1)}, bf16[160,512]{1,0:T(8,128)(2,1)S(1)}, u32[]{:S(2)}, u32[]{:S(2)}) collective-permute-start(bf16[160,512]{1,0:T(8,128)(2,1)S(1)} %get-tuple-element.58), channel_id=1, source_target_pairs={{0,6},{2,4},{4,2},{6,0},{1,7},{3,5},{5,3},{7,1},{8,14},{10,12},{12... | collective-permute-start | bytes 491528 | tf_op jit(solution)/shard_map/ppermute | solution.py:194
  40.5 11.6 %collective-permute-start.12 = (bf16[528,128]{1,0:T(8,128)(2,1)S(1)}, bf16[528,128]{1,0:T(8,128)(2,1)S(1)}, u32[]{:S(2)}, u32[]{:S(2)}) collective-permute-start(bf16[528,128]{1,0:T(8,128)(2,1)S(1)} %shard_map.125.refs_7_), channel_id=1, source_target_pairs={{0,24},{8,16},{16,8},{24,0},{1,25},{9,17},{17,9},{25,1},{2,26},{10... | collective-permute-start | bytes 405512 | tf_op jit(solution)/shard_map/ppermute | solution.py:194
  45.1 11.8 %collective-permute-start.14 = (bf16[528,128]{1,0:T(8,128)(2,1)S(1)}, bf16[528,128]{1,0:T(8,128)(2,1)S(1)}, u32[]{:S(2)}, u32[]{:S(2)}) collective-permute-start(bf16[528,128]{1,0:T(8,128)(2,1)S(1)} %shard_map.124.refs_6_), channel_id=1, source_target_pairs={{0,16},{8,24},{16,0},{24,8},{1,17},{9,25},{17,1},{25,9},{2,18},{10... | collective-permute-start | bytes 405512 | tf_op jit(solution)/shard_map/ppermute | solution.py:194
  46.2 10.8 %collective-permute-start.13 = (bf16[528,128]{1,0:T(8,128)(2,1)S(1)}, bf16[528,128]{1,0:T(8,128)(2,1)S(1)}, u32[]{:S(2)}, u32[]{:S(2)}) collective-permute-start(bf16[528,128]{1,0:T(8,128)(2,1)S(1)} %shard_map.123.refs_5_), channel_id=1, source_target_pairs={{0,8},{8,0},{16,24},{24,16},{1,9},{9,1},{17,25},{25,17},{2,10},{10... | collective-permute-start | bytes 405512 | tf_op jit(solution)/shard_map/ppermute | solution.py:194
  47.0 13.9 %slice-start = ((s8[4718592]{0:T(1024)(128)(4,1)}), s8[4194304]{0:T(1024)(128)(4,1)S(1)}, s32[]{:S(2)}) async-start(s8[4718592]{0:T(1024)(128)(4,1)} %bitcast.1), calls=%async_computation | async-start | bytes 8388608
  47.1 13.9 %slice-start.1 = ((s8[4718592]{0:T(1024)(128)(4,1)}), s8[524288]{0:T(1024)(128)(4,1)S(1)}, s32[]{:S(2)}) async-start(s8[4718592]{0:T(1024)(128)(4,1)} %bitcast.1), calls=%async_computation.1 | async-start | bytes 1048576
  49.9 5.6 %collective-permute-start.15 = (bf16[144,128]{1,0:T(8,128)(2,1)S(1)}, bf16[144,128]{1,0:T(8,128)(2,1)S(1)}, u32[]{:S(2)}, u32[]{:S(2)}) collective-permute-start(bf16[144,128]{1,0:T(8,128)(2,1)S(1)} %get-tuple-element.72), channel_id=1, source_target_pairs={{0,2},{2,0},{4,6},{6,4},{1,3},{3,1},{5,7},{7,5},{8,10},{10,8},{12,... | collective-permute-start | bytes 110600 | tf_op jit(solution)/shard_map/ppermute | solution.py:194
  51.6 4.0 %collective-permute-start.16 = (bf16[144,128]{1,0:T(8,128)(2,1)S(1)}, bf16[144,128]{1,0:T(8,128)(2,1)S(1)}, u32[]{:S(2)}, u32[]{:S(2)}) collective-permute-start(bf16[144,128]{1,0:T(8,128)(2,1)S(1)} %get-tuple-element.73), channel_id=1, source_target_pairs={{0,4},{2,6},{4,0},{6,2},{1,5},{3,7},{5,1},{7,3},{8,12},{10,14},{12... | collective-permute-start | bytes 110600 | tf_op jit(solution)/shard_map/ppermute | solution.py:194
  52.1 4.9 %collective-permute-start.17 = (bf16[144,128]{1,0:T(8,128)(2,1)S(1)}, bf16[144,128]{1,0:T(8,128)(2,1)S(1)}, u32[]{:S(2)}, u32[]{:S(2)}) collective-permute-start(bf16[144,128]{1,0:T(8,128)(2,1)S(1)} %get-tuple-element.74), channel_id=1, source_target_pairs={{0,6},{2,4},{4,2},{6,0},{1,7},{3,5},{5,3},{7,1},{8,14},{10,12},{12... | collective-permute-start | bytes 110600 | tf_op jit(solution)/shard_map/ppermute | solution.py:194
  57.4 5.0 %collective-permute-start.20 = (bf16[128,512]{1,0:T(8,128)(2,1)S(1)}, bf16[128,512]{1,0:T(8,128)(2,1)S(1)}, u32[]{:S(2)}, u32[]{:S(2)}) collective-permute-start(bf16[128,512]{1,0:T(8,128)(2,1)S(1)} %shard_map.128.refs_0_), channel_id=1, source_target_pairs={{0,2},{2,0},{4,6},{6,4},{1,3},{3,1},{5,7},{7,5},{8,10},{10,8},{12,... | collective-permute-start | bytes 393224 | tf_op jit(solution)/shard_map/ppermute | solution.py:194
  58.9 5.0 %collective-permute-start.19 = (bf16[128,512]{1,0:T(8,128)(2,1)S(1)}, bf16[128,512]{1,0:T(8,128)(2,1)S(1)}, u32[]{:S(2)}, u32[]{:S(2)}) collective-permute-start(bf16[128,512]{1,0:T(8,128)(2,1)S(1)} %shard_map.128.refs_0_), channel_id=1, source_target_pairs={{0,4},{2,6},{4,0},{6,2},{1,5},{3,7},{5,1},{7,3},{8,12},{10,14},{12... | collective-permute-start | bytes 393224 | tf_op jit(solution)/shard_map/ppermute | solution.py:194
  59.4 5.9 %collective-permute-start.18 = (bf16[128,512]{1,0:T(8,128)(2,1)S(1)}, bf16[128,512]{1,0:T(8,128)(2,1)S(1)}, u32[]{:S(2)}, u32[]{:S(2)}) collective-permute-start(bf16[128,512]{1,0:T(8,128)(2,1)S(1)} %shard_map.128.refs_0_), channel_id=1, source_target_pairs={{0,6},{2,4},{4,2},{6,0},{1,7},{3,5},{5,3},{7,1},{8,14},{10,12},{12... | collective-permute-start | bytes 393224 | tf_op jit(solution)/shard_map/ppermute | solution.py:194
  64.2 10.0 %copy-start.4 = (bf16[32,4,1152]{2,1,0:T(4,128)(2,1)S(1)}, bf16[32,4,1152]{2,1,0:T(4,128)(2,1)}, u32[]{:S(2)}) copy-start(bf16[32,4,1152]{2,1,0:T(4,128)(2,1)} %x_ref.1) | copy-start | bytes 884740
  64.2 10.0 %copy-start.8 = (f32[1152]{0:T(1024)S(1)}, f32[1152]{0:T(1024)}, u32[]{:S(2)}) copy-start(f32[1152]{0:T(1024)} %gain_ref.3) | copy-start | bytes 13828
  65.7 1.6 %collective-permute-start.21 = (bf16[128,1152]{1,0:T(8,128)(2,1)S(1)}, bf16[128,1152]{1,0:T(8,128)(2,1)S(1)}, u32[]{:S(2)}, u32[]{:S(2)}) collective-permute-start(bf16[128,1152]{1,0:T(8,128)(2,1)S(1)} %convert_element_type.15), channel_id=1, source_target_pairs={{0,1},{1,0},{2,3},{3,2},{4,5},{5,4},{6,7},{7,6},{8,9},{9,8},{10,11... | collective-permute-start | bytes 884744 | tf_op jit(solution)/shard_map/ppermute | solution.py:194
  67.5 4.5 %collective-permute-start.24 = (f32[8,128]{1,0:T(8,128)S(1)}, f32[8,128]{1,0:T(8,128)S(1)}, u32[]{:S(2)}, u32[]{:S(2)}) collective-permute-start(f32[8,128]{1,0:T(8,128)S(1)} %get-tuple-element.76.refs_0_), channel_id=1, source_target_pairs={{0,6},{2,4},{4,2},{6,0},{1,7},{3,5},{5,3},{7,1},{8,14},{10,12},{12... | collective-permute-start | bytes 12296 | tf_op jit(solution)/shard_map/ppermute | solution.py:194
  69.1 3.6 %collective-permute-start.23 = (f32[8,128]{1,0:T(8,128)S(1)}, f32[8,128]{1,0:T(8,128)S(1)}, u32[]{:S(2)}, u32[]{:S(2)}) collective-permute-start(f32[8,128]{1,0:T(8,128)S(1)} %get-tuple-element.76.refs_0_), channel_id=1, source_target_pairs={{0,4},{2,6},{4,0},{6,2},{1,5},{3,7},{5,1},{7,3},{8,12},{10,14},{12... | collective-permute-start | bytes 12296 | tf_op jit(solution)/shard_map/ppermute | solution.py:194
  70.6 3.6 %collective-permute-start.22 = (f32[8,128]{1,0:T(8,128)S(1)}, f32[8,128]{1,0:T(8,128)S(1)}, u32[]{:S(2)}, u32[]{:S(2)}) collective-permute-start(f32[8,128]{1,0:T(8,128)S(1)} %get-tuple-element.76.refs_0_), channel_id=1, source_target_pairs={{0,2},{2,0},{4,6},{6,4},{1,3},{3,1},{5,7},{7,5},{8,10},{10,8},{12,... | collective-permute-start | bytes 12296 | tf_op jit(solution)/shard_map/ppermute | solution.py:194

commit v5 on v4

--- a/solution.py
+++ b/solution.py
@@ -313,19 +313,23 @@
     own_ref[rows:, :rows] = across
     tail = split_rows(across)
     for ref in sent:
-        ref[rows:, :] = jnp.zeros((16, ref.shape[1]), jnp.bfloat16)
-        ref[rows:, :rows] = tail
+        ref[ref.shape[0] - 16 :, :] = tail
     for mask, copy, ref in zip(masks, w_copies, (*sent, own_ref)):
         copy.wait()
         product = jnp.dot(scaled_ref[...], w_ref[mask], preferred_element_type=jnp.float32)
-        ref[:rows, :] = product.astype(ref.dtype)
+        if mask == 0:
+            own_ref[:rows, :] = product
+            continue
+        for head in range(columns // HEAD_SIZE):
+            at = slice(head * rows, (head + 1) * rows)
+            ref[at, :] = product[:, head_lanes(head)].astype(ref.dtype)
 
 
 def query_projection(place, x, gain, weights, parts):
     members, steps, width = x.shape
     rows = members * steps
     columns = weights.shape[1] // parts
-    outs = [shape((rows + 16, columns), jnp.bfloat16)] * (parts - 1) + [
+    outs = [shape((rows * columns // HEAD_SIZE + 16, HEAD_SIZE), jnp.bfloat16)] * (parts - 1) + [
         shape((rows + 8, columns), jnp.float32),
         shape((rows, width), jnp.bfloat16),
     ]
@@ -457,10 +461,8 @@
     cos_ref, sin_ref, query_ref, *suffix_refs, inverse_ref, held = refs
     rows, columns = cos_ref.shape[0], own_ref.shape[1]
     squares = own_ref[rows : rows + 1, :rows]
-    total = own_ref[:rows, :]
     for ref in received:
-        squares = squares + joined_row(ref[rows:, :rows], 0)
-        total = total + ref[:rows, :].astype(jnp.float32)
+        squares = squares + joined_row(ref[ref.shape[0] - 16 :, :], 0)
     inverse = lax.rsqrt(down_rows(squares) / MODEL_WIDTH + EPSILON)
     inverse_ref[...] = inverse
     cosine = cos_ref[...] * inverse * QUERY_SCALE
@@ -469,7 +471,13 @@
     share = 2 * rows // parts
     for head in range(columns // pair):
         at = slice(head * 2 * rows, (head + 1) * 2 * rows)
-        held[...] = paired_heads(total[:, head * pair : (head + 1) * pair], cosine, sine)
+        totals = []
+        for index in (2 * head, 2 * head + 1):
+            total = own_ref[:rows, head_lanes(index)]
+            for ref in received:
+                total = total + ref[index * rows : (index + 1) * rows, :].astype(jnp.float32)
+            totals.append(total)
+        held[...] = paired_heads(jnp.concatenate(totals, axis=1), cosine, sine)
         query_ref[at, :] = held[...].astype(jnp.bfloat16)
         for mask, ref in enumerate(suffix_refs):
             ref[head * share : (head + 1) * share, :] = held[
@@ -940,6 +948,21 @@
 ):
     group_rows, steps, _ = hidden_in.shape
     rows = group_rows * steps
+    if rows != LANES or steps != 4:
+        return per_device(
+            hidden_in,
+            pre_gain,
+            w_query,
+            key_projection,
+            value_projection,
+            w_out,
+            post_gain,
+            prompt_keys,
+            prompt_values,
+            suffix_key_cache,
+            suffix_value_cache,
+            suffix_len,
+        )
     parts = lax.axis_size("prefix")
     groups = lax.axis_size("prefill")
     prompt_total = prompt_keys.shape[0] * groups * parts

time: 75.4 us -> 74.8 us (level)
  waiting for transfers between devices: 18.4 us -> 16.3 us
  starting transfers between devices: 32.6 us -> 34.1 us
    ppermute x25, waiting for transfers between devices: 18.4 us -> 16.3 us  [paired(): return lax.ppermute(values, axis, [(i, i ^ mask) for i in range(size)])]
    ppermute x25, starting transfers between devices: 32.6 us -> 34.1 us  [paired(): return lax.ppermute(values, axis, [(i, i ^ mask) for i in range(size)])]
  transfers between devices with their start and end apart: 25 -> 25, of which waited for: 16 -> 13; matrix products, arithmetic and copies ran while one was open for 1% -> 1% of each run, Pallas kernels for 21% -> 21%
where the time goes in v5:
time: 74.8 us; the launch traced here: 74.6 us
  starting transfers between devices  34.1 us (46%)
  Pallas kernels  22.5 us (30%)
  waiting for transfers between devices  16.3 us (22%)
  local copies, waits for them, and re-layouts  0.97 us (1%)
    ppermute x25, starting transfers between devices, paired(): return lax.ppermute(values, axis, [(i, i ^ mask) for i in range(size)])  34.1 us
    pallas_call x17, Pallas kernels, call(): pl.pallas_call(kernel, out_shape=out_shape, grid_spec=pltpu.PrefetchScala...  22.5 us
    ppermute x25, waiting for transfers between devices, paired(): return lax.ppermute(values, axis, [(i, i ^ mask) for i in range(size)])  16.3 us
  transfers between devices with their start and end apart: 25, of which 13 were waited for; matrix products, arithmetic and copies ran while one was open for 1% of the time, Pallas kernels for 21%

profile of v5, /device:TPU:0, one launch (start us, length us, event | category | flops | bytes accessed | tf_op | source)
XLA Modules:
  0.0 74.6 jit_solution(15530622095462983173)
XLA Ops:
  0.0 4.5 %shard_map.118 = (bf16[528,128]{1,0:T(8,128)(2,1)}, bf16[528,128]{1,0:T(8,128)(2,1)}, bf16[528,128]{1,0:T(8,128)(2,1)}, f32[136,512]{1,0:T(8,128)}, bf16[128,1152]{1,0:T(8,128)(2,1)}) custom-call(s32[1]{0:T(128)} %bitcast.place, f32[1152]{0:T(1024)} %gain_ref.2, bf16[32,4,1152]{2,1,0:T(4,128)(2,1)} %x_ref.1, bf16[1152,2048]{1,0:T(8,128)(2,1)} %w_hbm.1), custom_call_target="tpu_custom_call" | custom-call | flops 603979776 | bytes 4718592 | tf_op jit(solution)/shard_map/pallas_call | solution.py:210
  4.5 3.0 %collective-permute-start = (bf16[528,128]{1,0:T(8,128)(2,1)}, bf16[528,128]{1,0:T(8,128)(2,1)}, u32[]{:S(2)}, u32[]{:S(2)}) collective-permute-start(bf16[528,128]{1,0:T(8,128)(2,1)} %get-tuple-element.42), channel_id=1, source_target_pairs={{0,2},{2,0},{4,6},{6,4},{1,3},{3,1},{5,7},{7,5},{8,10},{10,8},{12,... | collective-permute-start | bytes 405512 | tf_op jit(solution)/shard_map/ppermute | solution.py:194
  7.5 1.5 %collective-permute-start.1 = (bf16[528,128]{1,0:T(8,128)(2,1)}, bf16[528,128]{1,0:T(8,128)(2,1)}, u32[]{:S(2)}, u32[]{:S(2)}) collective-permute-start(bf16[528,128]{1,0:T(8,128)(2,1)} %get-tuple-element.43), channel_id=1, source_target_pairs={{0,4},{2,6},{4,0},{6,2},{1,5},{3,7},{5,1},{7,3},{8,12},{10,14},{12... | collective-permute-start | bytes 405512 | tf_op jit(solution)/shard_map/ppermute | solution.py:194
  9.1 1.3 %shard_map.120 = (bf16[512,512]{1,0:T(8,128)(2,1)}, bf16[512,512]{1,0:T(8,128)(2,1)}, bf16[512,512]{1,0:T(8,128)(2,1)S(1)}) custom-call(s32[1]{0:T(128)} %bitcast.place, bf16[512,1024]{1,0:T(8,128)(2,1)S(1)} %copy-done.5, bf16[512,1024]{1,0:T(8,128)(2,1)S(1)} %copy-done.6), custom_call_target="tpu_custom_call" | custom-call | flops 20000000000 | bytes 3145728 | tf_op jit(solution)/shard_map/pallas_call | solution.py:210
  10.4 0.8 %copy-done.10 = bf16[512,512]{1,0:T(8,128)(2,1)} copy-done((bf16[512,512]{1,0:T(8,128)(2,1)}, bf16[512,512]{1,0:T(8,128)(2,1)S(1)}, u32[]{:S(2)}) %copy-start.10) | copy-done | bytes 524312
  11.2 1.9 %collective-permute-start.3 = (bf16[512,512]{1,0:T(8,128)(2,1)}, bf16[512,512]{1,0:T(8,128)(2,1)S(1)}, u32[]{:S(2)}, u32[]{:S(2)}) collective-permute-start(bf16[512,512]{1,0:T(8,128)(2,1)} %get-tuple-element.48), channel_id=1, source_target_pairs={{0,2},{2,0},{4,6},{6,4},{1,3},{3,1},{5,7},{7,5},{8,10},{10,8},{12,... | collective-permute-start | bytes 1572872 | tf_op jit(solution)/shard_map/ppermute | solution.py:194
  13.1 1.5 %collective-permute-start.4 = (bf16[512,512]{1,0:T(8,128)(2,1)}, bf16[512,512]{1,0:T(8,128)(2,1)S(1)}, u32[]{:S(2)}, u32[]{:S(2)}) collective-permute-start(bf16[512,512]{1,0:T(8,128)(2,1)} %get-tuple-element.49), channel_id=1, source_target_pairs={{0,4},{2,6},{4,0},{6,2},{1,5},{3,7},{5,1},{7,3},{8,12},{10,14},{12... | collective-permute-start | bytes 1572872 | tf_op jit(solution)/shard_map/ppermute | solution.py:194
  15.4 1.2 %collective-permute-done.2.refs_2_ = bf16[528,128]{1,0:T(8,128)(2,1)} collective-permute-done((bf16[528,128]{1,0:T(8,128)(2,1)}, bf16[528,128]{1,0:T(8,128)(2,1)}, u32[]{:S(2)}, u32[]{:S(2)}) %collective-permute-start.2) | collective-permute-done | bytes 135200 | tf_op jit(solution)/shard_map/ppermute | solution.py:194
  16.7 1.4 %shard_map.119 = (bf16[512,128]{1,0:T(8,128)(2,1)S(1)}, bf16[128,128]{1,0:T(8,128)(2,1)S(1)}, bf16[128,128]{1,0:T(8,128)(2,1)S(1)}, bf16[128,128]{1,0:T(8,128)(2...) custom-call(s32[1]{0:T(128)} %bitcast.place, f32[136,512]{1,0:T(8,128)S(1)} %copy-done.11, ...), custom_call_target="tpu_custom_call" | custom-call | flops 10000000000 | bytes 786432 | tf_op jit(solution)/shard_map/pallas_call | solution.py:210
  18.1 3.7 %collective-permute-start.11 = (bf16[512,128]{1,0:T(8,128)(2,1)S(1)}, bf16[512,128]{1,0:T(8,128)(2,1)S(1)}, u32[]{:S(2)}, u32[]{:S(2)}) collective-permute-start(bf16[512,128]{1,0:T(8,128)(2,1)S(1)} %get-tuple-element.61.q_ref), channel_id=1, source_target_pairs={{0,24},{8,16},{16,8},{24,0},{1,25},{9,17},{17,9},{25,1},{2,26},{10... | collective-permute-start | bytes 393224 | tf_op jit(solution)/shard_map/ppermute | solution.py:194
  21.7 2.3 %shard_map.121 = (f32[128,512]{1,0:T(8,128)S(1)}, bf16[160,512]{1,0:T(8,128)(2,1)S(1)}, bf16[160,512]{1,0:T(8,128)(2,1)S(1)}, bf16[160,512]{1,0:T(8,128)(2,1)S(1)}) custom-call(s32[1]{0:T(128)} %bitcast.place, bf16[128,1152]{1,0:T(8,128)(2,1)S(1)} %copy-done.7, bf16[1152,1024]{1,0:T(8,128)(2,1)S(1)} %copy-done.2, bf16[1152,1024]{1,0:T(8,128)(2,1)S(1)} %copy-done.3, ...), custom_call_target="tpu_custom_call" | custom-call | flops 603979776 | bytes 4718592 | tf_op jit(solution)/shard_map/pallas_call | solution.py:210
  24.1 2.5 %collective-permute-done.3.refs_5_.refs_0_ = bf16[512,512]{1,0:T(8,128)(2,1)S(1)} collective-permute-done((bf16[512,512]{1,0:T(8,128)(2,1)}, bf16[512,512]{1,0:T(8,128)(2,1)S(1)}, u32[]{:S(2)}, u32[]{:S(2)}) %collective-permute-start.3) | collective-permute-done | bytes 524320 | tf_op jit(solution)/shard_map/ppermute | solution.py:194
  26.5 1.9 %collective-permute-start.9 = (bf16[512,128]{1,0:T(8,128)(2,1)S(1)}, bf16[512,128]{1,0:T(8,128)(2,1)S(1)}, u32[]{:S(2)}, u32[]{:S(2)}) collective-permute-start(bf16[512,128]{1,0:T(8,128)(2,1)S(1)} %get-tuple-element.61.q_ref), channel_id=1, source_target_pairs={{0,8},{8,0},{16,24},{24,16},{1,9},{9,1},{17,25},{25,17},{2,10},{10... | collective-permute-start | bytes 393224 | tf_op jit(solution)/shard_map/ppermute | solution.py:194
  28.4 1.4 %collective-permute-start.6 = (bf16[160,512]{1,0:T(8,128)(2,1)S(1)}, bf16[160,512]{1,0:T(8,128)(2,1)S(1)}, u32[]{:S(2)}, u32[]{:S(2)}) collective-permute-start(bf16[160,512]{1,0:T(8,128)(2,1)S(1)} %get-tuple-element.56), channel_id=1, source_target_pairs={{0,2},{2,0},{4,6},{6,4},{1,3},{3,1},{5,7},{7,5},{8,10},{10,8},{12,... | collective-permute-start | bytes 491528 | tf_op jit(solution)/shard_map/ppermute | solution.py:194
  29.8 1.0 %collective-permute-done.10.refs_1_.q_ref = bf16[512,128]{1,0:T(8,128)(2,1)S(1)} collective-permute-done((bf16[512,128]{1,0:T(8,128)(2,1)S(1)}, bf16[512,128]{1,0:T(8,128)(2,1)S(1)}, u32[]{:S(2)}, u32[]{:S(2)}) %collective-permute-start.10) | collective-permute-done | bytes 131104 | tf_op jit(solution)/shard_map/ppermute | solution.py:194
  30.8 1.1 %collective-permute-start.7 = (bf16[160,512]{1,0:T(8,128)(2,1)S(1)}, bf16[160,512]{1,0:T(8,128)(2,1)S(1)}, u32[]{:S(2)}, u32[]{:S(2)}) collective-permute-start(bf16[160,512]{1,0:T(8,128)(2,1)S(1)} %get-tuple-element.57), channel_id=1, source_target_pairs={{0,4},{2,6},{4,0},{6,2},{1,5},{3,7},{5,1},{7,3},{8,12},{10,14},{12... | collective-permute-start | bytes 491528 | tf_op jit(solution)/shard_map/ppermute | solution.py:194
  32.0 0.7 collective-permute-done.9.refs_0_.q_ref
  32.7 2.3 %collective-permute-start.8 = (bf16[160,512]{1,0:T(8,128)(2,1)S(1)}, bf16[160,512]{1,0:T(8,128)(2,1)S(1)}, u32[]{:S(2)}, u32[]{:S(2)}) collective-permute-start(bf16[160,512]{1,0:T(8,128)(2,1)S(1)} %get-tuple-element.58), channel_id=1, source_target_pairs={{0,6},{2,4},{4,2},{6,0},{1,7},{3,5},{5,3},{7,1},{8,14},{10,12},{12... | collective-permute-start | bytes 491528 | tf_op jit(solution)/shard_map/ppermute | solution.py:194
  35.0 2.1 %shard_map.122 = (f32[512,128]{1,0:T(8,128)S(1)}, f32[512,128]{1,0:T(8,128)S(1)}, f32[512,128]{1,0:T(8,128)S(1)}, f32[512,128]{1,0:T(8,128)S(1)}, f32[512,128]{1,0:T(8,128)S(1)}, /*index=5*/f32[512,128]{1,0:T(8,128)S(1)}) custom-call(s32[1]{0:T(128)} %bitcast.place, bf16[512,128]{1,0:T(8,128)(2,1)S(1)} %collective-permute-done.9.refs_0_.q_ref, ...), custom_call_target="tpu_custom_call" | custom-call | flops 1207959552 | bytes 1048576 | tf_op jit(solution)/shard_map/pallas_call | solution.py:210
  37.1 1.4 %collective-permute-done.4.refs_0_.refs_1_ = bf16[512,512]{1,0:T(8,128)(2,1)S(1)} collective-permute-done((bf16[512,512]{1,0:T(8,128)(2,1)}, bf16[512,512]{1,0:T(8,128)(2,1)S(1)}, u32[]{:S(2)}, u32[]{:S(2)}) %collective-permute-start.4) | collective-permute-done | bytes 524320 | tf_op jit(solution)/shard_map/ppermute | solution.py:194
  38.5 0.5 collective-permute-done.5.refs_1_.refs_2_
  39.1 1.0 %shard_map.125.refs_7_ = bf16[528,128]{1,0:T(8,128)(2,1)S(1)} custom-call(s32[1]{0:T(128)} %bitcast.place, bf16[512,128]{1,0:T(8,128)(2,1)S(1)} %collective-permute-done.11.refs_2_.q_ref, bf16[512,512]{1,0:T(8,128)(2,1)S(1)} %collective-permute-done.4.refs_0_.refs_1_, bf16[512,512]{1,0:T(8,128)(2,1)S(1)} %collective-permute-done.5.refs_1_.refs_2_, ...), custom_call_target="tpu_custom_call" | custom-call | flops 402653184 | bytes 1048576 | tf_op jit(solution)/shard_map/pallas_call | solution.py:210
  40.1 3.6 %collective-permute-start.12 = (bf16[528,128]{1,0:T(8,128)(2,1)S(1)}, bf16[528,128]{1,0:T(8,128)(2,1)S(1)}, u32[]{:S(2)}, u32[]{:S(2)}) collective-permute-start(bf16[528,128]{1,0:T(8,128)(2,1)S(1)} %shard_map.125.refs_7_), channel_id=1, source_target_pairs={{0,24},{8,16},{16,8},{24,0},{1,25},{9,17},{17,9},{25,1},{2,26},{10... | collective-permute-start | bytes 405512 | tf_op jit(solution)/shard_map/ppermute | solution.py:194
  43.7 1.0 %shard_map.124.refs_6_ = bf16[528,128]{1,0:T(8,128)(2,1)S(1)} custom-call(s32[1]{0:T(128)} %bitcast.place, bf16[512,128]{1,0:T(8,128)(2,1)S(1)} %collective-permute-done.10.refs_1_.q_ref, bf16[512,512]{1,0:T(8,128)(2,1)S(1)} %collective-permute-done.4.refs_0_.refs_1_, bf16[512,512]{1,0:T(8,128)(2,1)S(1)} %collective-permute-done.5.refs_1_.refs_2_, ...), custom_call_target="tpu_custom_call" | custom-call | flops 402653184 | bytes 1048576 | tf_op jit(solution)/shard_map/pallas_call | solution.py:210
  44.8 1.0 %shard_map.123.refs_5_ = bf16[528,128]{1,0:T(8,128)(2,1)S(1)} custom-call(s32[1]{0:T(128)} %bitcast.place, bf16[512,128]{1,0:T(8,128)(2,1)S(1)} %collective-permute-done.9.refs_0_.q_ref, bf16[512,512]{1,0:T(8,128)(2,1)S(1)} %collective-permute-done.4.refs_0_.refs_1_, bf16[512,512]{1,0:T(8,128)(2,1)S(1)} %collective-permute-done.5.refs_1_.refs_2_, ...), custom_call_target="tpu_custom_call" | custom-call | flops 402653184 | bytes 1048576 | tf_op jit(solution)/shard_map/pallas_call | solution.py:210
  45.8 0.8 %collective-permute-start.13 = (bf16[528,128]{1,0:T(8,128)(2,1)S(1)}, bf16[528,128]{1,0:T(8,128)(2,1)S(1)}, u32[]{:S(2)}, u32[]{:S(2)}) collective-permute-start(bf16[528,128]{1,0:T(8,128)(2,1)S(1)} %shard_map.123.refs_5_), channel_id=1, source_target_pairs={{0,8},{8,0},{16,24},{24,16},{1,9},{9,1},{17,25},{25,17},{2,10},{10... | collective-permute-start | bytes 405512 | tf_op jit(solution)/shard_map/ppermute | solution.py:194
  46.6 2.9 %shard_map.126 = (f32[128,128]{1,0:T(8,128)S(1)}, f32[128,128]{1,0:T(8,128)S(1)}, bf16[144,128]{1,0:T(8,128)(2,1)S(1)}, bf16[144,128]{1,0:T(8,128)(2,1)S(1)}, bf16[144,128]{1,0:T(8,128)(2,1)S(1)}) custom-call(s32[1]{0:T(128)} %bitcast.place, s32[32]{0:T(128)S(1)} %copy-done.9, bf16[128,128]{1,0:T(8,128)(2,1)S(1)} %get-tuple-element.60.own_ref, ...), custom_call_target="tpu_custom_call" | custom-call | flops 67108864 | bytes 8388608 | tf_op jit(solution)/shard_map/pallas_call | solution.py:210
  49.5 1.4 %collective-permute-start.15 = (bf16[144,128]{1,0:T(8,128)(2,1)S(1)}, bf16[144,128]{1,0:T(8,128)(2,1)S(1)}, u32[]{:S(2)}, u32[]{:S(2)}) collective-permute-start(bf16[144,128]{1,0:T(8,128)(2,1)S(1)} %get-tuple-element.72), channel_id=1, source_target_pairs={{0,2},{2,0},{4,6},{6,4},{1,3},{3,1},{5,7},{7,5},{8,10},{10,8},{12,... | collective-permute-start | bytes 110600 | tf_op jit(solution)/shard_map/ppermute | solution.py:194
  51.0 0.9 %collective-permute-start.16 = (bf16[144,128]{1,0:T(8,128)(2,1)S(1)}, bf16[144,128]{1,0:T(8,128)(2,1)S(1)}, u32[]{:S(2)}, u32[]{:S(2)}) collective-permute-start(bf16[144,128]{1,0:T(8,128)(2,1)S(1)} %get-tuple-element.73), channel_id=1, source_target_pairs={{0,4},{2,6},{4,0},{6,2},{1,5},{3,7},{5,1},{7,3},{8,12},{10,14},{12... | collective-permute-start | bytes 110600 | tf_op jit(solution)/shard_map/ppermute | solution.py:194
  51.8 1.4 %collective-permute-start.17 = (bf16[144,128]{1,0:T(8,128)(2,1)S(1)}, bf16[144,128]{1,0:T(8,128)(2,1)S(1)}, u32[]{:S(2)}, u32[]{:S(2)}) collective-permute-start(bf16[144,128]{1,0:T(8,128)(2,1)S(1)} %get-tuple-element.74), channel_id=1, source_target_pairs={{0,6},{2,4},{4,2},{6,0},{1,7},{3,5},{5,3},{7,1},{8,14},{10,12},{12... | collective-permute-start | bytes 110600 | tf_op jit(solution)/shard_map/ppermute | solution.py:194
  53.2 2.0 %shard_map.127 = (f32[512,128]{1,0:T(8,128)S(1)}, f32[512,128]{1,0:T(8,128)S(1)}) custom-call(s32[1]{0:T(128)} %bitcast.place, bf16[512,128]{1,0:T(8,128)(2,1)S(1)} %get-tuple-element.61.q_ref, bf16[512,1024]{1,0:T(8,128)(2,1)S(1)} %copy-done.5, bf16[512,1024]{1,0:T(8,128)(2,1)S(1)} %copy-done.6, ...), custom_call_target="tpu_custom_call" | custom-call | flops 805306368 | bytes 1048576 | tf_op jit(solution)/shard_map/pallas_call | solution.py:210
  55.2 1.6 %collective-permute-done.17.refs_7_ = bf16[144,128]{1,0:T(8,128)(2,1)S(1)} collective-permute-done((bf16[144,128]{1,0:T(8,128)(2,1)S(1)}, bf16[144,128]{1,0:T(8,128)(2,1)S(1)}, u32[]{:S(2)}, u32[]{:S(2)}) %collective-permute-start.17) | collective-permute-done | bytes 36896 | tf_op jit(solution)/shard_map/ppermute | solution.py:194
  56.8 0.4 shard_map.128.refs_0_
  57.3 2.3 %collective-permute-start.20 = (bf16[128,512]{1,0:T(8,128)(2,1)S(1)}, bf16[128,512]{1,0:T(8,128)(2,1)S(1)}, u32[]{:S(2)}, u32[]{:S(2)}) collective-permute-start(bf16[128,512]{1,0:T(8,128)(2,1)S(1)} %shard_map.128.refs_0_), channel_id=1, source_target_pairs={{0,2},{2,0},{4,6},{6,4},{1,3},{3,1},{5,7},{7,5},{8,10},{10,8},{12,... | collective-permute-start | bytes 393224 | tf_op jit(solution)/shard_map/ppermute | solution.py:194
  59.5 1.5 %collective-permute-start.18 = (bf16[128,512]{1,0:T(8,128)(2,1)S(1)}, bf16[128,512]{1,0:T(8,128)(2,1)S(1)}, u32[]{:S(2)}, u32[]{:S(2)}) collective-permute-start(bf16[128,512]{1,0:T(8,128)(2,1)S(1)} %shard_map.128.refs_0_), channel_id=1, source_target_pairs={{0,6},{2,4},{4,2},{6,0},{1,7},{3,5},{5,3},{7,1},{8,14},{10,12},{12... | collective-permute-start | bytes 393224 | tf_op jit(solution)/shard_map/ppermute | solution.py:194
  61.1 0.3 shard_map.129.refs_2_
  61.4 1.0 %collective-permute-done.20.refs_0_ = bf16[128,512]{1,0:T(8,128)(2,1)S(1)} collective-permute-done((bf16[128,512]{1,0:T(8,128)(2,1)S(1)}, bf16[128,512]{1,0:T(8,128)(2,1)S(1)}, u32[]{:S(2)}, u32[]{:S(2)}) %collective-permute-start.20) | collective-permute-done | bytes 131104 | tf_op jit(solution)/shard_map/ppermute | solution.py:194
  62.5 0.3 shard_map.130.refs_2_
  62.8 3.1 %collective-permute-done.19.refs_0_ = bf16[128,512]{1,0:T(8,128)(2,1)S(1)} collective-permute-done((bf16[128,512]{1,0:T(8,128)(2,1)S(1)}, bf16[128,512]{1,0:T(8,128)(2,1)S(1)}, u32[]{:S(2)}, u32[]{:S(2)}) %collective-permute-start.19) | collective-permute-done | bytes 131104 | tf_op jit(solution)/shard_map/ppermute | solution.py:194
  65.9 0.4 shard_map.131.refs_2_
  66.3 0.4 shard_map.132.here_ref
  66.8 1.6 %collective-permute-done.21.there_ref = bf16[128,1152]{1,0:T(8,128)(2,1)S(1)} collective-permute-done((bf16[128,1152]{1,0:T(8,128)(2,1)S(1)}, bf16[128,1152]{1,0:T(8,128)(2,1)S(1)}, u32[]{:S(2)}, u32[]{:S(2)}) %collective-permute-start.21) | collective-permute-done | bytes 294944 | tf_op jit(solution)/shard_map/ppermute | solution.py:194
  68.5 0.7 collective-permute-start.24
  69.2 0.8 %collective-permute-start.23 = (f32[8,128]{1,0:T(8,128)S(1)}, f32[8,128]{1,0:T(8,128)S(1)}, u32[]{:S(2)}, u32[]{:S(2)}) collective-permute-start(f32[8,128]{1,0:T(8,128)S(1)} %get-tuple-element.76.refs_0_), channel_id=1, source_target_pairs={{0,4},{2,6},{4,0},{6,2},{1,5},{3,7},{5,1},{7,3},{8,12},{10,14},{12... | collective-permute-start | bytes 12296 | tf_op jit(solution)/shard_map/ppermute | solution.py:194
  70.0 2.1 %collective-permute-start.22 = (f32[8,128]{1,0:T(8,128)S(1)}, f32[8,128]{1,0:T(8,128)S(1)}, u32[]{:S(2)}, u32[]{:S(2)}) collective-permute-start(f32[8,128]{1,0:T(8,128)S(1)} %get-tuple-element.76.refs_0_), channel_id=1, source_target_pairs={{0,2},{2,0},{4,6},{6,4},{1,3},{3,1},{5,7},{7,5},{8,10},{10,8},{12,... | collective-permute-start | bytes 12296 | tf_op jit(solution)/shard_map/ppermute | solution.py:194
  72.1 1.0 %collective-permute-done.24.refs_3_ = f32[8,128]{1,0:T(8,128)S(1)} collective-permute-done((f32[8,128]{1,0:T(8,128)S(1)}, f32[8,128]{1,0:T(8,128)S(1)}, u32[]{:S(2)}, u32[]{:S(2)}) %collective-permute-start.24) | collective-permute-done | bytes 4128 | tf_op jit(solution)/shard_map/ppermute | solution.py:194
  73.1 0.5 collective-permute-done.22.refs_1_
  73.6 1.0 %shard_map.134 = bf16[32,4,1152]{2,1,0:T(4,128)(2,1)} custom-call(s32[1]{0:T(128)} %bitcast.place, bf16[32,4,1152]{2,1,0:T(4,128)(2,1)S(1)} %copy-done.4, f32[128,1152]{1,0:T(8,128)S(1)} %get-tuple-element.75.attended_ref, f32[1152]{0:T(1024)S(1)} %copy-done.8, f32[8,128]{1,0:T(8,128)S(1)} %get-tuple-element.76.refs_0_, ...), custom_call_target="tpu_custom_call" | custom-call | flops 589824 | bytes 1179648 | tf_op jit(solution)/shard_map/pallas_call | solution.py:210
  (55 shorter events, 1.2 us)
Async XLA Ops:
  0.0 9.1 %copy-start.6 = (bf16[512,1024]{1,0:T(8,128)(2,1)S(1)}, bf16[512,1024]{1,0:T(8,128)(2,1)}, u32[]{:S(2)}) copy-start(bf16[512,1024]{1,0:T(8,128)(2,1)} %v_ref.1) | copy-start | bytes 3145732
  0.0 9.1 %copy-start.5 = (bf16[512,1024]{1,0:T(8,128)(2,1)S(1)}, bf16[512,1024]{1,0:T(8,128)(2,1)}, u32[]{:S(2)}) copy-start(bf16[512,1024]{1,0:T(8,128)(2,1)} %k_ref.1) | copy-start | bytes 3145732
  4.5 10.8 %collective-permute-start = (bf16[528,128]{1,0:T(8,128)(2,1)}, bf16[528,128]{1,0:T(8,128)(2,1)}, u32[]{:S(2)}, u32[]{:S(2)}) collective-permute-start(bf16[528,128]{1,0:T(8,128)(2,1)} %get-tuple-element.42), channel_id=1, source_target_pairs={{0,2},{2,0},{4,6},{6,4},{1,3},{3,1},{5,7},{7,5},{8,10},{10,8},{12,... | collective-permute-start | bytes 405512 | tf_op jit(solution)/shard_map/ppermute | solution.py:194
  7.5 7.9 %collective-permute-start.1 = (bf16[528,128]{1,0:T(8,128)(2,1)}, bf16[528,128]{1,0:T(8,128)(2,1)}, u32[]{:S(2)}, u32[]{:S(2)}) collective-permute-start(bf16[528,128]{1,0:T(8,128)(2,1)} %get-tuple-element.43), channel_id=1, source_target_pairs={{0,4},{2,6},{4,0},{6,2},{1,5},{3,7},{5,1},{7,3},{8,12},{10,14},{12... | collective-permute-start | bytes 405512 | tf_op jit(solution)/shard_map/ppermute | solution.py:194
  9.0 7.6 %collective-permute-start.2 = (bf16[528,128]{1,0:T(8,128)(2,1)}, bf16[528,128]{1,0:T(8,128)(2,1)}, u32[]{:S(2)}, u32[]{:S(2)}) collective-permute-start(bf16[528,128]{1,0:T(8,128)(2,1)} %get-tuple-element.44), channel_id=1, source_target_pairs={{0,6},{2,4},{4,2},{6,0},{1,7},{3,5},{5,3},{7,1},{8,14},{10,12},{12... | collective-permute-start | bytes 405512 | tf_op jit(solution)/shard_map/ppermute | solution.py:194
  9.1 5.6 %copy-start.9 = (s32[32]{0:T(128)S(1)}, s32[32]{0:T(128)}, u32[]{:S(2)}) copy-start(s32[32]{0:T(128)} %lengths.1) | copy-start | bytes 388
  9.1 7.6 %copy-start.11 = (f32[136,512]{1,0:T(8,128)S(1)}, f32[136,512]{1,0:T(8,128)}, u32[]{:S(2)}) copy-start(f32[136,512]{1,0:T(8,128)} %get-tuple-element.41.own_ref) | copy-start | bytes 835588
  10.4 0.8 %copy-start.10 = (bf16[512,512]{1,0:T(8,128)(2,1)}, bf16[512,512]{1,0:T(8,128)(2,1)S(1)}, u32[]{:S(2)}) copy-start(bf16[512,512]{1,0:T(8,128)(2,1)S(1)} %get-tuple-element.50) | copy-start | bytes 1572868
  11.2 15.3 %collective-permute-start.3 = (bf16[512,512]{1,0:T(8,128)(2,1)}, bf16[512,512]{1,0:T(8,128)(2,1)S(1)}, u32[]{:S(2)}, u32[]{:S(2)}) collective-permute-start(bf16[512,512]{1,0:T(8,128)(2,1)} %get-tuple-element.48), channel_id=1, source_target_pairs={{0,2},{2,0},{4,6},{6,4},{1,3},{3,1},{5,7},{7,5},{8,10},{10,8},{12,... | collective-permute-start | bytes 1572872 | tf_op jit(solution)/shard_map/ppermute | solution.py:194
  13.1 25.4 %collective-permute-start.4 = (bf16[512,512]{1,0:T(8,128)(2,1)}, bf16[512,512]{1,0:T(8,128)(2,1)S(1)}, u32[]{:S(2)}, u32[]{:S(2)}) collective-permute-start(bf16[512,512]{1,0:T(8,128)(2,1)} %get-tuple-element.49), channel_id=1, source_target_pairs={{0,4},{2,6},{4,0},{6,2},{1,5},{3,7},{5,1},{7,3},{8,12},{10,14},{12... | collective-permute-start | bytes 1572872 | tf_op jit(solution)/shard_map/ppermute | solution.py:194
  15.3 23.8 %collective-permute-start.5 = (bf16[512,512]{1,0:T(8,128)(2,1)}, bf16[512,512]{1,0:T(8,128)(2,1)S(1)}, u32[]{:S(2)}, u32[]{:S(2)}) collective-permute-start(bf16[512,512]{1,0:T(8,128)(2,1)} %copy-done.10), channel_id=1, source_target_pairs={{0,6},{2,4},{4,2},{6,0},{1,7},{3,5},{5,3},{7,1},{8,14},{10,12},{12... | collective-permute-start | bytes 1572872 | tf_op jit(solution)/shard_map/ppermute | solution.py:194
  16.7 5.1 %copy-start.2 = (bf16[1152,1024]{1,0:T(8,128)(2,1)S(1)}, bf16[1152,1024]{1,0:T(8,128)(2,1)}, u32[]{:S(2)}) copy-start(bf16[1152,1024]{1,0:T(8,128)(2,1)} %k_hbm.1) | copy-start | bytes 7077892
  16.7 5.1 %copy-start.3 = (bf16[1152,1024]{1,0:T(8,128)(2,1)S(1)}, bf16[1152,1024]{1,0:T(8,128)(2,1)}, u32[]{:S(2)}) copy-start(bf16[1152,1024]{1,0:T(8,128)(2,1)} %v_hbm.1) | copy-start | bytes 7077892
  16.7 5.1 %copy-start.7 = (bf16[128,1152]{1,0:T(8,128)(2,1)S(1)}, bf16[128,1152]{1,0:T(8,128)(2,1)}, u32[]{:S(2)}) copy-start(bf16[128,1152]{1,0:T(8,128)(2,1)} %get-tuple-element.51.scaled_ref) | copy-start | bytes 884740
  18.1 10.3 %collective-permute-start.11 = (bf16[512,128]{1,0:T(8,128)(2,1)S(1)}, bf16[512,128]{1,0:T(8,128)(2,1)S(1)}, u32[]{:S(2)}, u32[]{:S(2)}) collective-permute-start(bf16[512,128]{1,0:T(8,128)(2,1)S(1)} %get-tuple-element.61.q_ref), channel_id=1, source_target_pairs={{0,24},{8,16},{16,8},{24,0},{1,25},{9,17},{17,9},{25,1},{2,26},{10... | collective-permute-start | bytes 393224 | tf_op jit(solution)/shard_map/ppermute | solution.py:194
  21.7 9.1 %collective-permute-start.10 = (bf16[512,128]{1,0:T(8,128)(2,1)S(1)}, bf16[512,128]{1,0:T(8,128)(2,1)S(1)}, u32[]{:S(2)}, u32[]{:S(2)}) collective-permute-start(bf16[512,128]{1,0:T(8,128)(2,1)S(1)} %get-tuple-element.61.q_ref), channel_id=1, source_target_pairs={{0,16},{8,24},{16,0},{24,8},{1,17},{9,25},{17,1},{25,9},{2,18},{10... | collective-permute-start | bytes 393224 | tf_op jit(solution)/shard_map/ppermute | solution.py:194
  26.5 6.1 %collective-permute-start.9 = (bf16[512,128]{1,0:T(8,128)(2,1)S(1)}, bf16[512,128]{1,0:T(8,128)(2,1)S(1)}, u32[]{:S(2)}, u32[]{:S(2)}) collective-permute-start(bf16[512,128]{1,0:T(8,128)(2,1)S(1)} %get-tuple-element.61.q_ref), channel_id=1, source_target_pairs={{0,8},{8,0},{16,24},{24,16},{1,9},{9,1},{17,25},{25,17},{2,10},{10... | collective-permute-start | bytes 393224 | tf_op jit(solution)/shard_map/ppermute | solution.py:194
  28.4 17.4 %collective-permute-start.6 = (bf16[160,512]{1,0:T(8,128)(2,1)S(1)}, bf16[160,512]{1,0:T(8,128)(2,1)S(1)}, u32[]{:S(2)}, u32[]{:S(2)}) collective-permute-start(bf16[160,512]{1,0:T(8,128)(2,1)S(1)} %get-tuple-element.56), channel_id=1, source_target_pairs={{0,2},{2,0},{4,6},{6,4},{1,3},{3,1},{5,7},{7,5},{8,10},{10,8},{12,... | collective-permute-start | bytes 491528 | tf_op jit(solution)/shard_map/ppermute | solution.py:194
  30.8 15.8 %collective-permute-start.7 = (bf16[160,512]{1,0:T(8,128)(2,1)S(1)}, bf16[160,512]{1,0:T(8,128)(2,1)S(1)}, u32[]{:S(2)}, u32[]{:S(2)}) collective-permute-start(bf16[160,512]{1,0:T(8,128)(2,1)S(1)} %get-tuple-element.57), channel_id=1, source_target_pairs={{0,4},{2,6},{4,0},{6,2},{1,5},{3,7},{5,1},{7,3},{8,12},{10,14},{12... | collective-permute-start | bytes 491528 | tf_op jit(solution)/shard_map/ppermute | solution.py:194
  32.7 13.9 %copy-start = (bf16[8,256,1024]{2,1,0:T(8,128)(2,1)S(1)}, bf16[8,256,1024]{2,1,0:T(8,128)(2,1)}, u32[]{:S(2)}) copy-start(bf16[8,256,1024]{2,1,0:T(8,128)(2,1)} %refs_3_.3) | copy-start | bytes 12582916
  32.7 14.0 %copy-start.1 = (bf16[8,256,1024]{2,1,0:T(8,128)(2,1)S(1)}, bf16[8,256,1024]{2,1,0:T(8,128)(2,1)}, u32[]{:S(2)}) copy-start(bf16[8,256,1024]{2,1,0:T(8,128)(2,1)} %refs_4_.3) | copy-start | bytes 12582916
  32.7 13.9 %collective-permute-start.8 = (bf16[160,512]{1,0:T(8,128)(2,1)S(1)}, bf16[160,512]{1,0:T(8,128)(2,1)S(1)}, u32[]{:S(2)}, u32[]{:S(2)}) collective-permute-start(bf16[160,512]{1,0:T(8,128)(2,1)S(1)} %get-tuple-element.58), channel_id=1, source_target_pairs={{0,6},{2,4},{4,2},{6,0},{1,7},{3,5},{5,3},{7,1},{8,14},{10,12},{12... | collective-permute-start | bytes 491528 | tf_op jit(solution)/shard_map/ppermute | solution.py:194
  40.1 11.8 %collective-permute-start.12 = (bf16[528,128]{1,0:T(8,128)(2,1)S(1)}, bf16[528,128]{1,0:T(8,128)(2,1)S(1)}, u32[]{:S(2)}, u32[]{:S(2)}) collective-permute-start(bf16[528,128]{1,0:T(8,128)(2,1)S(1)} %shard_map.125.refs_7_), channel_id=1, source_target_pairs={{0,24},{8,16},{16,8},{24,0},{1,25},{9,17},{17,9},{25,1},{2,26},{10... | collective-permute-start | bytes 405512 | tf_op jit(solution)/shard_map/ppermute | solution.py:194
  44.7 12.1 %collective-permute-start.14 = (bf16[528,128]{1,0:T(8,128)(2,1)S(1)}, bf16[528,128]{1,0:T(8,128)(2,1)S(1)}, u32[]{:S(2)}, u32[]{:S(2)}) collective-permute-start(bf16[528,128]{1,0:T(8,128)(2,1)S(1)} %shard_map.124.refs_6_), channel_id=1, source_target_pairs={{0,16},{8,24},{16,0},{24,8},{1,17},{9,25},{17,1},{25,9},{2,18},{10... | collective-permute-start | bytes 405512 | tf_op jit(solution)/shard_map/ppermute | solution.py:194
  45.8 11.0 %collective-permute-start.13 = (bf16[528,128]{1,0:T(8,128)(2,1)S(1)}, bf16[528,128]{1,0:T(8,128)(2,1)S(1)}, u32[]{:S(2)}, u32[]{:S(2)}) collective-permute-start(bf16[528,128]{1,0:T(8,128)(2,1)S(1)} %shard_map.123.refs_5_), channel_id=1, source_target_pairs={{0,8},{8,0},{16,24},{24,16},{1,9},{9,1},{17,25},{25,17},{2,10},{10... | collective-permute-start | bytes 405512 | tf_op jit(solution)/shard_map/ppermute | solution.py:194
  46.6 14.5 %slice-start = ((s8[4718592]{0:T(1024)(128)(4,1)}), s8[4194304]{0:T(1024)(128)(4,1)S(1)}, s32[]{:S(2)}) async-start(s8[4718592]{0:T(1024)(128)(4,1)} %bitcast.1), calls=%async_computation | async-start | bytes 8388608
  46.6 14.5 %slice-start.1 = ((s8[4718592]{0:T(1024)(128)(4,1)}), s8[524288]{0:T(1024)(128)(4,1)S(1)}, s32[]{:S(2)}) async-start(s8[4718592]{0:T(1024)(128)(4,1)} %bitcast.1), calls=%async_computation.1 | async-start | bytes 1048576
  49.5 5.7 %collective-permute-start.15 = (bf16[144,128]{1,0:T(8,128)(2,1)S(1)}, bf16[144,128]{1,0:T(8,128)(2,1)S(1)}, u32[]{:S(2)}, u32[]{:S(2)}) collective-permute-start(bf16[144,128]{1,0:T(8,128)(2,1)S(1)} %get-tuple-element.72), channel_id=1, source_target_pairs={{0,2},{2,0},{4,6},{6,4},{1,3},{3,1},{5,7},{7,5},{8,10},{10,8},{12,... | collective-permute-start | bytes 110600 | tf_op jit(solution)/shard_map/ppermute | solution.py:194
  51.0 4.3 %collective-permute-start.16 = (bf16[144,128]{1,0:T(8,128)(2,1)S(1)}, bf16[144,128]{1,0:T(8,128)(2,1)S(1)}, u32[]{:S(2)}, u32[]{:S(2)}) collective-permute-start(bf16[144,128]{1,0:T(8,128)(2,1)S(1)} %get-tuple-element.73), channel_id=1, source_target_pairs={{0,4},{2,6},{4,0},{6,2},{1,5},{3,7},{5,1},{7,3},{8,12},{10,14},{12... | collective-permute-start | bytes 110600 | tf_op jit(solution)/shard_map/ppermute | solution.py:194
  51.8 5.0 %collective-permute-start.17 = (bf16[144,128]{1,0:T(8,128)(2,1)S(1)}, bf16[144,128]{1,0:T(8,128)(2,1)S(1)}, u32[]{:S(2)}, u32[]{:S(2)}) collective-permute-start(bf16[144,128]{1,0:T(8,128)(2,1)S(1)} %get-tuple-element.74), channel_id=1, source_target_pairs={{0,6},{2,4},{4,2},{6,0},{1,7},{3,5},{5,3},{7,1},{8,14},{10,12},{12... | collective-permute-start | bytes 110600 | tf_op jit(solution)/shard_map/ppermute | solution.py:194
  57.3 5.2 %collective-permute-start.20 = (bf16[128,512]{1,0:T(8,128)(2,1)S(1)}, bf16[128,512]{1,0:T(8,128)(2,1)S(1)}, u32[]{:S(2)}, u32[]{:S(2)}) collective-permute-start(bf16[128,512]{1,0:T(8,128)(2,1)S(1)} %shard_map.128.refs_0_), channel_id=1, source_target_pairs={{0,2},{2,0},{4,6},{6,4},{1,3},{3,1},{5,7},{7,5},{8,10},{10,8},{12,... | collective-permute-start | bytes 393224 | tf_op jit(solution)/shard_map/ppermute | solution.py:194
  59.5 6.4 %collective-permute-start.19 = (bf16[128,512]{1,0:T(8,128)(2,1)S(1)}, bf16[128,512]{1,0:T(8,128)(2,1)S(1)}, u32[]{:S(2)}, u32[]{:S(2)}) collective-permute-start(bf16[128,512]{1,0:T(8,128)(2,1)S(1)} %shard_map.128.refs_0_), channel_id=1, source_target_pairs={{0,4},{2,6},{4,0},{6,2},{1,5},{3,7},{5,1},{7,3},{8,12},{10,14},{12... | collective-permute-start | bytes 393224 | tf_op jit(solution)/shard_map/ppermute | solution.py:194
  59.5 6.8 %collective-permute-start.18 = (bf16[128,512]{1,0:T(8,128)(2,1)S(1)}, bf16[128,512]{1,0:T(8,128)(2,1)S(1)}, u32[]{:S(2)}, u32[]{:S(2)}) collective-permute-start(bf16[128,512]{1,0:T(8,128)(2,1)S(1)} %shard_map.128.refs_0_), channel_id=1, source_target_pairs={{0,6},{2,4},{4,2},{6,0},{1,7},{3,5},{5,3},{7,1},{8,14},{10,12},{12... | collective-permute-start | bytes 393224 | tf_op jit(solution)/shard_map/ppermute | solution.py:194
  66.3 7.4 %copy-start.4 = (bf16[32,4,1152]{2,1,0:T(4,128)(2,1)S(1)}, bf16[32,4,1152]{2,1,0:T(4,128)(2,1)}, u32[]{:S(2)}) copy-start(bf16[32,4,1152]{2,1,0:T(4,128)(2,1)} %x_ref.1) | copy-start | bytes 884740
  66.3 7.4 %copy-start.8 = (f32[1152]{0:T(1024)S(1)}, f32[1152]{0:T(1024)}, u32[]{:S(2)}) copy-start(f32[1152]{0:T(1024)} %gain_ref.3) | copy-start | bytes 13828
  66.7 1.6 %collective-permute-start.21 = (bf16[128,1152]{1,0:T(8,128)(2,1)S(1)}, bf16[128,1152]{1,0:T(8,128)(2,1)S(1)}, u32[]{:S(2)}, u32[]{:S(2)}) collective-permute-start(bf16[128,1152]{1,0:T(8,128)(2,1)S(1)} %convert_element_type.15), channel_id=1, source_target_pairs={{0,1},{1,0},{2,3},{3,2},{4,5},{5,4},{6,7},{7,6},{8,9},{9,8},{10,11... | collective-permute-start | bytes 884744 | tf_op jit(solution)/shard_map/ppermute | solution.py:194
  68.5 4.6 %collective-permute-start.24 = (f32[8,128]{1,0:T(8,128)S(1)}, f32[8,128]{1,0:T(8,128)S(1)}, u32[]{:S(2)}, u32[]{:S(2)}) collective-permute-start(f32[8,128]{1,0:T(8,128)S(1)} %get-tuple-element.76.refs_0_), channel_id=1, source_target_pairs={{0,6},{2,4},{4,2},{6,0},{1,7},{3,5},{5,3},{7,1},{8,14},{10,12},{12... | collective-permute-start | bytes 12296 | tf_op jit(solution)/shard_map/ppermute | solution.py:194
  69.2 3.9 %collective-permute-start.23 = (f32[8,128]{1,0:T(8,128)S(1)}, f32[8,128]{1,0:T(8,128)S(1)}, u32[]{:S(2)}, u32[]{:S(2)}) collective-permute-start(f32[8,128]{1,0:T(8,128)S(1)} %get-tuple-element.76.refs_0_), channel_id=1, source_target_pairs={{0,4},{2,6},{4,0},{6,2},{1,5},{3,7},{5,1},{7,3},{8,12},{10,14},{12... | collective-permute-start | bytes 12296 | tf_op jit(solution)/shard_map/ppermute | solution.py:194
  70.0 3.7 %collective-permute-start.22 = (f32[8,128]{1,0:T(8,128)S(1)}, f32[8,128]{1,0:T(8,128)S(1)}, u32[]{:S(2)}, u32[]{:S(2)}) collective-permute-start(f32[8,128]{1,0:T(8,128)S(1)} %get-tuple-element.76.refs_0_), channel_id=1, source_target_pairs={{0,2},{2,0},{4,6},{6,4},{1,3},{3,1},{5,7},{7,5},{8,10},{10,8},{12,... | collective-permute-start | bytes 12296 | tf_op jit(solution)/shard_map/ppermute | solution.py:194

commit v6 on v5

--- a/solution.py
+++ b/solution.py
@@ -704,35 +704,43 @@
                     ref.shape[0] - tall :, head_lanes(head * count // tall + half)
                 ].astype(jnp.float32)
 
-    for member in range(members):
-        tile = slice(member * 8, (member + 1) * 8)
-        pairs = [slice(at, at + 2 * HEAD_SIZE) for at in range(0, columns, 2 * HEAD_SIZE)]
-        scores = jnp.concatenate(
-            [
-                dot_last(
-                    diagonal(
-                        query_held[2 * index, tile, :], query_held[2 * index + 1, tile, :]
-                    ).astype(jnp.bfloat16),
-                    k_ref[member, :, lanes],
+    pairs = [slice(at, at + 2 * HEAD_SIZE) for at in range(0, columns, 2 * HEAD_SIZE)]
+    for start in range(0, members, 4):
+        together = range(start, min(start + 4, members))
+        tiles = [slice(member * 8, (member + 1) * 8) for member in together]
+        scores = [
+            jnp.concatenate(
+                [
+                    dot_last(
+                        diagonal(
+                            query_held[2 * index, tile, :], query_held[2 * index + 1, tile, :]
+                        ).astype(jnp.bfloat16),
+                        k_ref[member, :, lanes],
+                    )
+                    for index, lanes in enumerate(pairs)
+                ],
+                axis=0,
+            )
+            for member, tile in zip(together, tiles)
+        ]
+        weights = []
+        for member, tile, score in zip(together, tiles, scores):
+            length = lengths[here * members + member]
+            valid = lax.broadcasted_iota(jnp.int32, score.shape, 1) < length
+            weight = jnp.where(valid, capped_weight(score), 0.0)
+            total = jnp.broadcast_to(jnp.sum(weight, axis=1, keepdims=True), (heads * 8, LANES))
+            weights.append(weight.astype(jnp.bfloat16))
+            for head in range(heads):
+                totals[head, tile, :] = total[head * 8 : (head + 1) * 8]
+        for member, tile, weight in zip(together, tiles, weights):
+            for index, lanes in enumerate(pairs):
+                result = jnp.dot(
+                    weight[16 * index : 16 * (index + 1)],
+                    v_ref[member, :, lanes],
+                    preferred_element_type=jnp.float32,
                 )
-                for index, lanes in enumerate(pairs)
-            ],
-            axis=0,
-        )
-        valid = lax.broadcasted_iota(jnp.int32, scores.shape, 1) < lengths[here * members + member]
-        weight = jnp.where(valid, capped_weight(scores), 0.0)
-        total = jnp.broadcast_to(jnp.sum(weight, axis=1, keepdims=True), (heads * 8, LANES))
-        weight = weight.astype(jnp.bfloat16)
-        for index, lanes in enumerate(pairs):
-            result = jnp.dot(
-                weight[16 * index : 16 * (index + 1)],
-                v_ref[member, :, lanes],
-                preferred_element_type=jnp.float32,
-            )
-            sums[2 * index, tile, :] = result[:8, :HEAD_SIZE]
-            sums[2 * index + 1, tile, :] = result[8:, HEAD_SIZE:]
-        for head in range(heads):
-            totals[head, tile, :] = total[head * 8 : (head + 1) * 8]
+                sums[2 * index, tile, :] = result[:8, :HEAD_SIZE]
+                sums[2 * index + 1, tile, :] = result[8:, HEAD_SIZE:]
 
     for mask in range(parts):
         for head in range(near):

time: 74.8 us -> 74.3 us (level)
  no operation moved by 1% of the time
where the time goes in v6:
time: 74.3 us; the launch traced here: 74.1 us
  starting transfers between devices  34.1 us (46%)
  Pallas kernels  21.9 us (29%)
  waiting for transfers between devices  16.3 us (22%)
  local copies, waits for them, and re-layouts  0.97 us (1%)
    ppermute x25, starting transfers between devices, paired(): return lax.ppermute(values, axis, [(i, i ^ mask) for i in range(size)])  34.1 us
    pallas_call x17, Pallas kernels, call(): pl.pallas_call(kernel, out_shape=out_shape, grid_spec=pltpu.PrefetchScala...  21.9 us
    ppermute x25, waiting for transfers between devices, paired(): return lax.ppermute(values, axis, [(i, i ^ mask) for i in range(size)])  16.3 us
  transfers between devices with their start and end apart: 25, of which 13 were waited for; matrix products, arithmetic and copies ran while one was open for 1% of the time, Pallas kernels for 21%

profile of v6, /device:TPU:0, one launch (start us, length us, event | category | flops | bytes accessed | tf_op | source)
XLA Modules:
  0.0 74.1 jit_solution(8361885225199091836)
XLA Ops:
  0.0 4.5 %shard_map.118 = (bf16[528,128]{1,0:T(8,128)(2,1)}, bf16[528,128]{1,0:T(8,128)(2,1)}, bf16[528,128]{1,0:T(8,128)(2,1)}, f32[136,512]{1,0:T(8,128)}, bf16[128,1152]{1,0:T(8,128)(2,1)}) custom-call(s32[1]{0:T(128)} %bitcast.place, f32[1152]{0:T(1024)} %gain_ref.2, bf16[32,4,1152]{2,1,0:T(4,128)(2,1)} %x_ref.1, bf16[1152,2048]{1,0:T(8,128)(2,1)} %w_hbm.1), custom_call_target="tpu_custom_call" | custom-call | flops 603979776 | bytes 4718592 | tf_op jit(solution)/shard_map/pallas_call | solution.py:210
  4.5 3.0 %collective-permute-start = (bf16[528,128]{1,0:T(8,128)(2,1)}, bf16[528,128]{1,0:T(8,128)(2,1)}, u32[]{:S(2)}, u32[]{:S(2)}) collective-permute-start(bf16[528,128]{1,0:T(8,128)(2,1)} %get-tuple-element.42), channel_id=1, source_target_pairs={{0,2},{2,0},{4,6},{6,4},{1,3},{3,1},{5,7},{7,5},{8,10},{10,8},{12,... | collective-permute-start | bytes 405512 | tf_op jit(solution)/shard_map/ppermute | solution.py:194
  7.5 1.5 %collective-permute-start.1 = (bf16[528,128]{1,0:T(8,128)(2,1)}, bf16[528,128]{1,0:T(8,128)(2,1)}, u32[]{:S(2)}, u32[]{:S(2)}) collective-permute-start(bf16[528,128]{1,0:T(8,128)(2,1)} %get-tuple-element.43), channel_id=1, source_target_pairs={{0,4},{2,6},{4,0},{6,2},{1,5},{3,7},{5,1},{7,3},{8,12},{10,14},{12... | collective-permute-start | bytes 405512 | tf_op jit(solution)/shard_map/ppermute | solution.py:194
  9.1 1.3 %shard_map.120 = (bf16[512,512]{1,0:T(8,128)(2,1)}, bf16[512,512]{1,0:T(8,128)(2,1)}, bf16[512,512]{1,0:T(8,128)(2,1)S(1)}) custom-call(s32[1]{0:T(128)} %bitcast.place, bf16[512,1024]{1,0:T(8,128)(2,1)S(1)} %copy-done.5, bf16[512,1024]{1,0:T(8,128)(2,1)S(1)} %copy-done.6), custom_call_target="tpu_custom_call" | custom-call | flops 20000000000 | bytes 3145728 | tf_op jit(solution)/shard_map/pallas_call | solution.py:210
  10.4 0.8 %copy-done.10 = bf16[512,512]{1,0:T(8,128)(2,1)} copy-done((bf16[512,512]{1,0:T(8,128)(2,1)}, bf16[512,512]{1,0:T(8,128)(2,1)S(1)}, u32[]{:S(2)}) %copy-start.10) | copy-done | bytes 524312
  11.2 1.9 %collective-permute-start.3 = (bf16[512,512]{1,0:T(8,128)(2,1)}, bf16[512,512]{1,0:T(8,128)(2,1)S(1)}, u32[]{:S(2)}, u32[]{:S(2)}) collective-permute-start(bf16[512,512]{1,0:T(8,128)(2,1)} %get-tuple-element.48), channel_id=1, source_target_pairs={{0,2},{2,0},{4,6},{6,4},{1,3},{3,1},{5,7},{7,5},{8,10},{10,8},{12,... | collective-permute-start | bytes 1572872 | tf_op jit(solution)/shard_map/ppermute | solution.py:194
  13.1 1.5 %collective-permute-start.4 = (bf16[512,512]{1,0:T(8,128)(2,1)}, bf16[512,512]{1,0:T(8,128)(2,1)S(1)}, u32[]{:S(2)}, u32[]{:S(2)}) collective-permute-start(bf16[512,512]{1,0:T(8,128)(2,1)} %get-tuple-element.49), channel_id=1, source_target_pairs={{0,4},{2,6},{4,0},{6,2},{1,5},{3,7},{5,1},{7,3},{8,12},{10,14},{12... | collective-permute-start | bytes 1572872 | tf_op jit(solution)/shard_map/ppermute | solution.py:194
  15.4 1.2 %collective-permute-done.2.refs_2_ = bf16[528,128]{1,0:T(8,128)(2,1)} collective-permute-done((bf16[528,128]{1,0:T(8,128)(2,1)}, bf16[528,128]{1,0:T(8,128)(2,1)}, u32[]{:S(2)}, u32[]{:S(2)}) %collective-permute-start.2) | collective-permute-done | bytes 135200 | tf_op jit(solution)/shard_map/ppermute | solution.py:194
  16.7 1.4 %shard_map.119 = (bf16[512,128]{1,0:T(8,128)(2,1)S(1)}, bf16[128,128]{1,0:T(8,128)(2,1)S(1)}, bf16[128,128]{1,0:T(8,128)(2,1)S(1)}, bf16[128,128]{1,0:T(8,128)(2...) custom-call(s32[1]{0:T(128)} %bitcast.place, f32[136,512]{1,0:T(8,128)S(1)} %copy-done.11, ...), custom_call_target="tpu_custom_call" | custom-call | flops 10000000000 | bytes 786432 | tf_op jit(solution)/shard_map/pallas_call | solution.py:210
  18.1 3.7 %collective-permute-start.11 = (bf16[512,128]{1,0:T(8,128)(2,1)S(1)}, bf16[512,128]{1,0:T(8,128)(2,1)S(1)}, u32[]{:S(2)}, u32[]{:S(2)}) collective-permute-start(bf16[512,128]{1,0:T(8,128)(2,1)S(1)} %get-tuple-element.61.q_ref), channel_id=1, source_target_pairs={{0,24},{8,16},{16,8},{24,0},{1,25},{9,17},{17,9},{25,1},{2,26},{10... | collective-permute-start | bytes 393224 | tf_op jit(solution)/shard_map/ppermute | solution.py:194
  21.7 2.3 %shard_map.121 = (f32[128,512]{1,0:T(8,128)S(1)}, bf16[160,512]{1,0:T(8,128)(2,1)S(1)}, bf16[160,512]{1,0:T(8,128)(2,1)S(1)}, bf16[160,512]{1,0:T(8,128)(2,1)S(1)}) custom-call(s32[1]{0:T(128)} %bitcast.place, bf16[128,1152]{1,0:T(8,128)(2,1)S(1)} %copy-done.7, bf16[1152,1024]{1,0:T(8,128)(2,1)S(1)} %copy-done.2, bf16[1152,1024]{1,0:T(8,128)(2,1)S(1)} %copy-done.3, ...), custom_call_target="tpu_custom_call" | custom-call | flops 603979776 | bytes 4718592 | tf_op jit(solution)/shard_map/pallas_call | solution.py:210
  24.1 2.5 %collective-permute-done.3.refs_5_.refs_0_ = bf16[512,512]{1,0:T(8,128)(2,1)S(1)} collective-permute-done((bf16[512,512]{1,0:T(8,128)(2,1)}, bf16[512,512]{1,0:T(8,128)(2,1)S(1)}, u32[]{:S(2)}, u32[]{:S(2)}) %collective-permute-start.3) | collective-permute-done | bytes 524320 | tf_op jit(solution)/shard_map/ppermute | solution.py:194
  26.5 1.9 %collective-permute-start.9 = (bf16[512,128]{1,0:T(8,128)(2,1)S(1)}, bf16[512,128]{1,0:T(8,128)(2,1)S(1)}, u32[]{:S(2)}, u32[]{:S(2)}) collective-permute-start(bf16[512,128]{1,0:T(8,128)(2,1)S(1)} %get-tuple-element.61.q_ref), channel_id=1, source_target_pairs={{0,8},{8,0},{16,24},{24,16},{1,9},{9,1},{17,25},{25,17},{2,10},{10... | collective-permute-start | bytes 393224 | tf_op jit(solution)/shard_map/ppermute | solution.py:194
  28.4 1.4 %collective-permute-start.6 = (bf16[160,512]{1,0:T(8,128)(2,1)S(1)}, bf16[160,512]{1,0:T(8,128)(2,1)S(1)}, u32[]{:S(2)}, u32[]{:S(2)}) collective-permute-start(bf16[160,512]{1,0:T(8,128)(2,1)S(1)} %get-tuple-element.56), channel_id=1, source_target_pairs={{0,2},{2,0},{4,6},{6,4},{1,3},{3,1},{5,7},{7,5},{8,10},{10,8},{12,... | collective-permute-start | bytes 491528 | tf_op jit(solution)/shard_map/ppermute | solution.py:194
  29.8 1.0 %collective-permute-done.10.refs_1_.q_ref = bf16[512,128]{1,0:T(8,128)(2,1)S(1)} collective-permute-done((bf16[512,128]{1,0:T(8,128)(2,1)S(1)}, bf16[512,128]{1,0:T(8,128)(2,1)S(1)}, u32[]{:S(2)}, u32[]{:S(2)}) %collective-permute-start.10) | collective-permute-done | bytes 131104 | tf_op jit(solution)/shard_map/ppermute | solution.py:194
  30.8 1.1 %collective-permute-start.7 = (bf16[160,512]{1,0:T(8,128)(2,1)S(1)}, bf16[160,512]{1,0:T(8,128)(2,1)S(1)}, u32[]{:S(2)}, u32[]{:S(2)}) collective-permute-start(bf16[160,512]{1,0:T(8,128)(2,1)S(1)} %get-tuple-element.57), channel_id=1, source_target_pairs={{0,4},{2,6},{4,0},{6,2},{1,5},{3,7},{5,1},{7,3},{8,12},{10,14},{12... | collective-permute-start | bytes 491528 | tf_op jit(solution)/shard_map/ppermute | solution.py:194
  32.0 0.7 collective-permute-done.9.refs_0_.q_ref
  32.7 2.3 %collective-permute-start.8 = (bf16[160,512]{1,0:T(8,128)(2,1)S(1)}, bf16[160,512]{1,0:T(8,128)(2,1)S(1)}, u32[]{:S(2)}, u32[]{:S(2)}) collective-permute-start(bf16[160,512]{1,0:T(8,128)(2,1)S(1)} %get-tuple-element.58), channel_id=1, source_target_pairs={{0,6},{2,4},{4,2},{6,0},{1,7},{3,5},{5,3},{7,1},{8,14},{10,12},{12... | collective-permute-start | bytes 491528 | tf_op jit(solution)/shard_map/ppermute | solution.py:194
  35.0 2.1 %shard_map.122 = (f32[512,128]{1,0:T(8,128)S(1)}, f32[512,128]{1,0:T(8,128)S(1)}, f32[512,128]{1,0:T(8,128)S(1)}, f32[512,128]{1,0:T(8,128)S(1)}, f32[512,128]{1,0:T(8,128)S(1)}, /*index=5*/f32[512,128]{1,0:T(8,128)S(1)}) custom-call(s32[1]{0:T(128)} %bitcast.place, bf16[512,128]{1,0:T(8,128)(2,1)S(1)} %collective-permute-done.9.refs_0_.q_ref, ...), custom_call_target="tpu_custom_call" | custom-call | flops 1207959552 | bytes 1048576 | tf_op jit(solution)/shard_map/pallas_call | solution.py:210
  37.1 1.4 %collective-permute-done.4.refs_0_.refs_1_ = bf16[512,512]{1,0:T(8,128)(2,1)S(1)} collective-permute-done((bf16[512,512]{1,0:T(8,128)(2,1)}, bf16[512,512]{1,0:T(8,128)(2,1)S(1)}, u32[]{:S(2)}, u32[]{:S(2)}) %collective-permute-start.4) | collective-permute-done | bytes 524320 | tf_op jit(solution)/shard_map/ppermute | solution.py:194
  38.5 0.5 collective-permute-done.5.refs_1_.refs_2_
  39.1 1.0 %shard_map.125.refs_7_ = bf16[528,128]{1,0:T(8,128)(2,1)S(1)} custom-call(s32[1]{0:T(128)} %bitcast.place, bf16[512,128]{1,0:T(8,128)(2,1)S(1)} %collective-permute-done.11.refs_2_.q_ref, bf16[512,512]{1,0:T(8,128)(2,1)S(1)} %collective-permute-done.4.refs_0_.refs_1_, bf16[512,512]{1,0:T(8,128)(2,1)S(1)} %collective-permute-done.5.refs_1_.refs_2_, ...), custom_call_target="tpu_custom_call" | custom-call | flops 402653184 | bytes 1048576 | tf_op jit(solution)/shard_map/pallas_call | solution.py:210
  40.1 3.6 %collective-permute-start.12 = (bf16[528,128]{1,0:T(8,128)(2,1)S(1)}, bf16[528,128]{1,0:T(8,128)(2,1)S(1)}, u32[]{:S(2)}, u32[]{:S(2)}) collective-permute-start(bf16[528,128]{1,0:T(8,128)(2,1)S(1)} %shard_map.125.refs_7_), channel_id=1, source_target_pairs={{0,24},{8,16},{16,8},{24,0},{1,25},{9,17},{17,9},{25,1},{2,26},{10... | collective-permute-start | bytes 405512 | tf_op jit(solution)/shard_map/ppermute | solution.py:194
  43.7 1.0 %shard_map.124.refs_6_ = bf16[528,128]{1,0:T(8,128)(2,1)S(1)} custom-call(s32[1]{0:T(128)} %bitcast.place, bf16[512,128]{1,0:T(8,128)(2,1)S(1)} %collective-permute-done.10.refs_1_.q_ref, bf16[512,512]{1,0:T(8,128)(2,1)S(1)} %collective-permute-done.4.refs_0_.refs_1_, bf16[512,512]{1,0:T(8,128)(2,1)S(1)} %collective-permute-done.5.refs_1_.refs_2_, ...), custom_call_target="tpu_custom_call" | custom-call | flops 402653184 | bytes 1048576 | tf_op jit(solution)/shard_map/pallas_call | solution.py:210
  44.8 1.0 %shard_map.123.refs_5_ = bf16[528,128]{1,0:T(8,128)(2,1)S(1)} custom-call(s32[1]{0:T(128)} %bitcast.place, bf16[512,128]{1,0:T(8,128)(2,1)S(1)} %collective-permute-done.9.refs_0_.q_ref, bf16[512,512]{1,0:T(8,128)(2,1)S(1)} %collective-permute-done.4.refs_0_.refs_1_, bf16[512,512]{1,0:T(8,128)(2,1)S(1)} %collective-permute-done.5.refs_1_.refs_2_, ...), custom_call_target="tpu_custom_call" | custom-call | flops 402653184 | bytes 1048576 | tf_op jit(solution)/shard_map/pallas_call | solution.py:210
  45.8 0.8 %collective-permute-start.13 = (bf16[528,128]{1,0:T(8,128)(2,1)S(1)}, bf16[528,128]{1,0:T(8,128)(2,1)S(1)}, u32[]{:S(2)}, u32[]{:S(2)}) collective-permute-start(bf16[528,128]{1,0:T(8,128)(2,1)S(1)} %shard_map.123.refs_5_), channel_id=1, source_target_pairs={{0,8},{8,0},{16,24},{24,16},{1,9},{9,1},{17,25},{25,17},{2,10},{10... | collective-permute-start | bytes 405512 | tf_op jit(solution)/shard_map/ppermute | solution.py:194
  46.6 2.3 %shard_map.126 = (f32[128,128]{1,0:T(8,128)S(1)}, f32[128,128]{1,0:T(8,128)S(1)}, bf16[144,128]{1,0:T(8,128)(2,1)S(1)}, bf16[144,128]{1,0:T(8,128)(2,1)S(1)}, bf16[144,128]{1,0:T(8,128)(2,1)S(1)}) custom-call(s32[1]{0:T(128)} %bitcast.place, s32[32]{0:T(128)S(1)} %copy-done.9, bf16[128,128]{1,0:T(8,128)(2,1)S(1)} %get-tuple-element.60.own_ref, ...), custom_call_target="tpu_custom_call" | custom-call | flops 67108864 | bytes 8388608 | tf_op jit(solution)/shard_map/pallas_call | solution.py:210
  49.0 1.5 %collective-permute-start.15 = (bf16[144,128]{1,0:T(8,128)(2,1)S(1)}, bf16[144,128]{1,0:T(8,128)(2,1)S(1)}, u32[]{:S(2)}, u32[]{:S(2)}) collective-permute-start(bf16[144,128]{1,0:T(8,128)(2,1)S(1)} %get-tuple-element.72), channel_id=1, source_target_pairs={{0,2},{2,0},{4,6},{6,4},{1,3},{3,1},{5,7},{7,5},{8,10},{10,8},{12,... | collective-permute-start | bytes 110600 | tf_op jit(solution)/shard_map/ppermute | solution.py:194
  50.4 0.9 %collective-permute-start.16 = (bf16[144,128]{1,0:T(8,128)(2,1)S(1)}, bf16[144,128]{1,0:T(8,128)(2,1)S(1)}, u32[]{:S(2)}, u32[]{:S(2)}) collective-permute-start(bf16[144,128]{1,0:T(8,128)(2,1)S(1)} %get-tuple-element.73), channel_id=1, source_target_pairs={{0,4},{2,6},{4,0},{6,2},{1,5},{3,7},{5,1},{7,3},{8,12},{10,14},{12... | collective-permute-start | bytes 110600 | tf_op jit(solution)/shard_map/ppermute | solution.py:194
  51.3 1.4 %collective-permute-start.17 = (bf16[144,128]{1,0:T(8,128)(2,1)S(1)}, bf16[144,128]{1,0:T(8,128)(2,1)S(1)}, u32[]{:S(2)}, u32[]{:S(2)}) collective-permute-start(bf16[144,128]{1,0:T(8,128)(2,1)S(1)} %get-tuple-element.74), channel_id=1, source_target_pairs={{0,6},{2,4},{4,2},{6,0},{1,7},{3,5},{5,3},{7,1},{8,14},{10,12},{12... | collective-permute-start | bytes 110600 | tf_op jit(solution)/shard_map/ppermute | solution.py:194
  52.7 2.0 %shard_map.127 = (f32[512,128]{1,0:T(8,128)S(1)}, f32[512,128]{1,0:T(8,128)S(1)}) custom-call(s32[1]{0:T(128)} %bitcast.place, bf16[512,128]{1,0:T(8,128)(2,1)S(1)} %get-tuple-element.61.q_ref, bf16[512,1024]{1,0:T(8,128)(2,1)S(1)} %copy-done.5, bf16[512,1024]{1,0:T(8,128)(2,1)S(1)} %copy-done.6, ...), custom_call_target="tpu_custom_call" | custom-call | flops 805306368 | bytes 1048576 | tf_op jit(solution)/shard_map/pallas_call | solution.py:210
  54.7 1.6 %collective-permute-done.17.refs_7_ = bf16[144,128]{1,0:T(8,128)(2,1)S(1)} collective-permute-done((bf16[144,128]{1,0:T(8,128)(2,1)S(1)}, bf16[144,128]{1,0:T(8,128)(2,1)S(1)}, u32[]{:S(2)}, u32[]{:S(2)}) %collective-permute-start.17) | collective-permute-done | bytes 36896 | tf_op jit(solution)/shard_map/ppermute | solution.py:194
  56.3 0.4 shard_map.128.refs_0_
  56.7 2.3 %collective-permute-start.20 = (bf16[128,512]{1,0:T(8,128)(2,1)S(1)}, bf16[128,512]{1,0:T(8,128)(2,1)S(1)}, u32[]{:S(2)}, u32[]{:S(2)}) collective-permute-start(bf16[128,512]{1,0:T(8,128)(2,1)S(1)} %shard_map.128.refs_0_), channel_id=1, source_target_pairs={{0,2},{2,0},{4,6},{6,4},{1,3},{3,1},{5,7},{7,5},{8,10},{10,8},{12,... | collective-permute-start | bytes 393224 | tf_op jit(solution)/shard_map/ppermute | solution.py:194
  59.0 1.5 %collective-permute-start.18 = (bf16[128,512]{1,0:T(8,128)(2,1)S(1)}, bf16[128,512]{1,0:T(8,128)(2,1)S(1)}, u32[]{:S(2)}, u32[]{:S(2)}) collective-permute-start(bf16[128,512]{1,0:T(8,128)(2,1)S(1)} %shard_map.128.refs_0_), channel_id=1, source_target_pairs={{0,6},{2,4},{4,2},{6,0},{1,7},{3,5},{5,3},{7,1},{8,14},{10,12},{12... | collective-permute-start | bytes 393224 | tf_op jit(solution)/shard_map/ppermute | solution.py:194
  60.6 0.3 shard_map.129.refs_2_
  60.9 1.0 %collective-permute-done.20.refs_0_ = bf16[128,512]{1,0:T(8,128)(2,1)S(1)} collective-permute-done((bf16[128,512]{1,0:T(8,128)(2,1)S(1)}, bf16[128,512]{1,0:T(8,128)(2,1)S(1)}, u32[]{:S(2)}, u32[]{:S(2)}) %collective-permute-start.20) | collective-permute-done | bytes 131104 | tf_op jit(solution)/shard_map/ppermute | solution.py:194
  62.0 0.3 shard_map.130.refs_2_
  62.3 3.1 %collective-permute-done.19.refs_0_ = bf16[128,512]{1,0:T(8,128)(2,1)S(1)} collective-permute-done((bf16[128,512]{1,0:T(8,128)(2,1)S(1)}, bf16[128,512]{1,0:T(8,128)(2,1)S(1)}, u32[]{:S(2)}, u32[]{:S(2)}) %collective-permute-start.19) | collective-permute-done | bytes 131104 | tf_op jit(solution)/shard_map/ppermute | solution.py:194
  65.4 0.4 shard_map.131.refs_2_
  65.8 0.4 shard_map.132.here_ref
  66.3 1.6 %collective-permute-done.21.there_ref = bf16[128,1152]{1,0:T(8,128)(2,1)S(1)} collective-permute-done((bf16[128,1152]{1,0:T(8,128)(2,1)S(1)}, bf16[128,1152]{1,0:T(8,128)(2,1)S(1)}, u32[]{:S(2)}, u32[]{:S(2)}) %collective-permute-start.21) | collective-permute-done | bytes 294944 | tf_op jit(solution)/shard_map/ppermute | solution.py:194
  68.0 0.7 collective-permute-start.24
  68.7 0.8 %collective-permute-start.23 = (f32[8,128]{1,0:T(8,128)S(1)}, f32[8,128]{1,0:T(8,128)S(1)}, u32[]{:S(2)}, u32[]{:S(2)}) collective-permute-start(f32[8,128]{1,0:T(8,128)S(1)} %get-tuple-element.76.refs_0_), channel_id=1, source_target_pairs={{0,4},{2,6},{4,0},{6,2},{1,5},{3,7},{5,1},{7,3},{8,12},{10,14},{12... | collective-permute-start | bytes 12296 | tf_op jit(solution)/shard_map/ppermute | solution.py:194
  69.4 2.1 %collective-permute-start.22 = (f32[8,128]{1,0:T(8,128)S(1)}, f32[8,128]{1,0:T(8,128)S(1)}, u32[]{:S(2)}, u32[]{:S(2)}) collective-permute-start(f32[8,128]{1,0:T(8,128)S(1)} %get-tuple-element.76.refs_0_), channel_id=1, source_target_pairs={{0,2},{2,0},{4,6},{6,4},{1,3},{3,1},{5,7},{7,5},{8,10},{10,8},{12,... | collective-permute-start | bytes 12296 | tf_op jit(solution)/shard_map/ppermute | solution.py:194
  71.5 1.0 %collective-permute-done.24.refs_3_ = f32[8,128]{1,0:T(8,128)S(1)} collective-permute-done((f32[8,128]{1,0:T(8,128)S(1)}, f32[8,128]{1,0:T(8,128)S(1)}, u32[]{:S(2)}, u32[]{:S(2)}) %collective-permute-start.24) | collective-permute-done | bytes 4128 | tf_op jit(solution)/shard_map/ppermute | solution.py:194
  72.6 0.5 collective-permute-done.22.refs_1_
  73.1 1.0 %shard_map.134 = bf16[32,4,1152]{2,1,0:T(4,128)(2,1)} custom-call(s32[1]{0:T(128)} %bitcast.place, bf16[32,4,1152]{2,1,0:T(4,128)(2,1)S(1)} %copy-done.4, f32[128,1152]{1,0:T(8,128)S(1)} %get-tuple-element.75.attended_ref, f32[1152]{0:T(1024)S(1)} %copy-done.8, f32[8,128]{1,0:T(8,128)S(1)} %get-tuple-element.76.refs_0_, ...), custom_call_target="tpu_custom_call" | custom-call | flops 589824 | bytes 1179648 | tf_op jit(solution)/shard_map/pallas_call | solution.py:210
  (55 shorter events, 1.2 us)
Async XLA Ops:
  0.0 9.1 %copy-start.6 = (bf16[512,1024]{1,0:T(8,128)(2,1)S(1)}, bf16[512,1024]{1,0:T(8,128)(2,1)}, u32[]{:S(2)}) copy-start(bf16[512,1024]{1,0:T(8,128)(2,1)} %v_ref.1) | copy-start | bytes 3145732
  0.0 9.1 %copy-start.5 = (bf16[512,1024]{1,0:T(8,128)(2,1)S(1)}, bf16[512,1024]{1,0:T(8,128)(2,1)}, u32[]{:S(2)}) copy-start(bf16[512,1024]{1,0:T(8,128)(2,1)} %k_ref.1) | copy-start | bytes 3145732
  4.5 10.8 %collective-permute-start = (bf16[528,128]{1,0:T(8,128)(2,1)}, bf16[528,128]{1,0:T(8,128)(2,1)}, u32[]{:S(2)}, u32[]{:S(2)}) collective-permute-start(bf16[528,128]{1,0:T(8,128)(2,1)} %get-tuple-element.42), channel_id=1, source_target_pairs={{0,2},{2,0},{4,6},{6,4},{1,3},{3,1},{5,7},{7,5},{8,10},{10,8},{12,... | collective-permute-start | bytes 405512 | tf_op jit(solution)/shard_map/ppermute | solution.py:194
  7.5 7.9 %collective-permute-start.1 = (bf16[528,128]{1,0:T(8,128)(2,1)}, bf16[528,128]{1,0:T(8,128)(2,1)}, u32[]{:S(2)}, u32[]{:S(2)}) collective-permute-start(bf16[528,128]{1,0:T(8,128)(2,1)} %get-tuple-element.43), channel_id=1, source_target_pairs={{0,4},{2,6},{4,0},{6,2},{1,5},{3,7},{5,1},{7,3},{8,12},{10,14},{12... | collective-permute-start | bytes 405512 | tf_op jit(solution)/shard_map/ppermute | solution.py:194
  9.0 7.6 %collective-permute-start.2 = (bf16[528,128]{1,0:T(8,128)(2,1)}, bf16[528,128]{1,0:T(8,128)(2,1)}, u32[]{:S(2)}, u32[]{:S(2)}) collective-permute-start(bf16[528,128]{1,0:T(8,128)(2,1)} %get-tuple-element.44), channel_id=1, source_target_pairs={{0,6},{2,4},{4,2},{6,0},{1,7},{3,5},{5,3},{7,1},{8,14},{10,12},{12... | collective-permute-start | bytes 405512 | tf_op jit(solution)/shard_map/ppermute | solution.py:194
  9.1 5.6 %copy-start.9 = (s32[32]{0:T(128)S(1)}, s32[32]{0:T(128)}, u32[]{:S(2)}) copy-start(s32[32]{0:T(128)} %lengths.1) | copy-start | bytes 388
  9.1 7.6 %copy-start.11 = (f32[136,512]{1,0:T(8,128)S(1)}, f32[136,512]{1,0:T(8,128)}, u32[]{:S(2)}) copy-start(f32[136,512]{1,0:T(8,128)} %get-tuple-element.41.own_ref) | copy-start | bytes 835588
  10.4 0.8 %copy-start.10 = (bf16[512,512]{1,0:T(8,128)(2,1)}, bf16[512,512]{1,0:T(8,128)(2,1)S(1)}, u32[]{:S(2)}) copy-start(bf16[512,512]{1,0:T(8,128)(2,1)S(1)} %get-tuple-element.50) | copy-start | bytes 1572868
  11.2 15.3 %collective-permute-start.3 = (bf16[512,512]{1,0:T(8,128)(2,1)}, bf16[512,512]{1,0:T(8,128)(2,1)S(1)}, u32[]{:S(2)}, u32[]{:S(2)}) collective-permute-start(bf16[512,512]{1,0:T(8,128)(2,1)} %get-tuple-element.48), channel_id=1, source_target_pairs={{0,2},{2,0},{4,6},{6,4},{1,3},{3,1},{5,7},{7,5},{8,10},{10,8},{12,... | collective-permute-start | bytes 1572872 | tf_op jit(solution)/shard_map/ppermute | solution.py:194
  13.1 25.4 %collective-permute-start.4 = (bf16[512,512]{1,0:T(8,128)(2,1)}, bf16[512,512]{1,0:T(8,128)(2,1)S(1)}, u32[]{:S(2)}, u32[]{:S(2)}) collective-permute-start(bf16[512,512]{1,0:T(8,128)(2,1)} %get-tuple-element.49), channel_id=1, source_target_pairs={{0,4},{2,6},{4,0},{6,2},{1,5},{3,7},{5,1},{7,3},{8,12},{10,14},{12... | collective-permute-start | bytes 1572872 | tf_op jit(solution)/shard_map/ppermute | solution.py:194
  15.3 23.8 %collective-permute-start.5 = (bf16[512,512]{1,0:T(8,128)(2,1)}, bf16[512,512]{1,0:T(8,128)(2,1)S(1)}, u32[]{:S(2)}, u32[]{:S(2)}) collective-permute-start(bf16[512,512]{1,0:T(8,128)(2,1)} %copy-done.10), channel_id=1, source_target_pairs={{0,6},{2,4},{4,2},{6,0},{1,7},{3,5},{5,3},{7,1},{8,14},{10,12},{12... | collective-permute-start | bytes 1572872 | tf_op jit(solution)/shard_map/ppermute | solution.py:194
  16.7 5.1 %copy-start.2 = (bf16[1152,1024]{1,0:T(8,128)(2,1)S(1)}, bf16[1152,1024]{1,0:T(8,128)(2,1)}, u32[]{:S(2)}) copy-start(bf16[1152,1024]{1,0:T(8,128)(2,1)} %k_hbm.1) | copy-start | bytes 7077892
  16.7 5.1 %copy-start.3 = (bf16[1152,1024]{1,0:T(8,128)(2,1)S(1)}, bf16[1152,1024]{1,0:T(8,128)(2,1)}, u32[]{:S(2)}) copy-start(bf16[1152,1024]{1,0:T(8,128)(2,1)} %v_hbm.1) | copy-start | bytes 7077892
  16.7 5.1 %copy-start.7 = (bf16[128,1152]{1,0:T(8,128)(2,1)S(1)}, bf16[128,1152]{1,0:T(8,128)(2,1)}, u32[]{:S(2)}) copy-start(bf16[128,1152]{1,0:T(8,128)(2,1)} %get-tuple-element.51.scaled_ref) | copy-start | bytes 884740
  18.1 10.3 %collective-permute-start.11 = (bf16[512,128]{1,0:T(8,128)(2,1)S(1)}, bf16[512,128]{1,0:T(8,128)(2,1)S(1)}, u32[]{:S(2)}, u32[]{:S(2)}) collective-permute-start(bf16[512,128]{1,0:T(8,128)(2,1)S(1)} %get-tuple-element.61.q_ref), channel_id=1, source_target_pairs={{0,24},{8,16},{16,8},{24,0},{1,25},{9,17},{17,9},{25,1},{2,26},{10... | collective-permute-start | bytes 393224 | tf_op jit(solution)/shard_map/ppermute | solution.py:194
  21.7 9.1 %collective-permute-start.10 = (bf16[512,128]{1,0:T(8,128)(2,1)S(1)}, bf16[512,128]{1,0:T(8,128)(2,1)S(1)}, u32[]{:S(2)}, u32[]{:S(2)}) collective-permute-start(bf16[512,128]{1,0:T(8,128)(2,1)S(1)} %get-tuple-element.61.q_ref), channel_id=1, source_target_pairs={{0,16},{8,24},{16,0},{24,8},{1,17},{9,25},{17,1},{25,9},{2,18},{10... | collective-permute-start | bytes 393224 | tf_op jit(solution)/shard_map/ppermute | solution.py:194
  26.5 6.1 %collective-permute-start.9 = (bf16[512,128]{1,0:T(8,128)(2,1)S(1)}, bf16[512,128]{1,0:T(8,128)(2,1)S(1)}, u32[]{:S(2)}, u32[]{:S(2)}) collective-permute-start(bf16[512,128]{1,0:T(8,128)(2,1)S(1)} %get-tuple-element.61.q_ref), channel_id=1, source_target_pairs={{0,8},{8,0},{16,24},{24,16},{1,9},{9,1},{17,25},{25,17},{2,10},{10... | collective-permute-start | bytes 393224 | tf_op jit(solution)/shard_map/ppermute | solution.py:194
  28.4 17.4 %collective-permute-start.6 = (bf16[160,512]{1,0:T(8,128)(2,1)S(1)}, bf16[160,512]{1,0:T(8,128)(2,1)S(1)}, u32[]{:S(2)}, u32[]{:S(2)}) collective-permute-start(bf16[160,512]{1,0:T(8,128)(2,1)S(1)} %get-tuple-element.56), channel_id=1, source_target_pairs={{0,2},{2,0},{4,6},{6,4},{1,3},{3,1},{5,7},{7,5},{8,10},{10,8},{12,... | collective-permute-start | bytes 491528 | tf_op jit(solution)/shard_map/ppermute | solution.py:194
  30.8 15.8 %collective-permute-start.7 = (bf16[160,512]{1,0:T(8,128)(2,1)S(1)}, bf16[160,512]{1,0:T(8,128)(2,1)S(1)}, u32[]{:S(2)}, u32[]{:S(2)}) collective-permute-start(bf16[160,512]{1,0:T(8,128)(2,1)S(1)} %get-tuple-element.57), channel_id=1, source_target_pairs={{0,4},{2,6},{4,0},{6,2},{1,5},{3,7},{5,1},{7,3},{8,12},{10,14},{12... | collective-permute-start | bytes 491528 | tf_op jit(solution)/shard_map/ppermute | solution.py:194
  32.7 13.9 %copy-start = (bf16[8,256,1024]{2,1,0:T(8,128)(2,1)S(1)}, bf16[8,256,1024]{2,1,0:T(8,128)(2,1)}, u32[]{:S(2)}) copy-start(bf16[8,256,1024]{2,1,0:T(8,128)(2,1)} %refs_3_.3) | copy-start | bytes 12582916
  32.7 14.0 %copy-start.1 = (bf16[8,256,1024]{2,1,0:T(8,128)(2,1)S(1)}, bf16[8,256,1024]{2,1,0:T(8,128)(2,1)}, u32[]{:S(2)}) copy-start(bf16[8,256,1024]{2,1,0:T(8,128)(2,1)} %refs_4_.3) | copy-start | bytes 12582916
  32.7 13.9 %collective-permute-start.8 = (bf16[160,512]{1,0:T(8,128)(2,1)S(1)}, bf16[160,512]{1,0:T(8,128)(2,1)S(1)}, u32[]{:S(2)}, u32[]{:S(2)}) collective-permute-start(bf16[160,512]{1,0:T(8,128)(2,1)S(1)} %get-tuple-element.58), channel_id=1, source_target_pairs={{0,6},{2,4},{4,2},{6,0},{1,7},{3,5},{5,3},{7,1},{8,14},{10,12},{12... | collective-permute-start | bytes 491528 | tf_op jit(solution)/shard_map/ppermute | solution.py:194
  40.1 11.2 %collective-permute-start.12 = (bf16[528,128]{1,0:T(8,128)(2,1)S(1)}, bf16[528,128]{1,0:T(8,128)(2,1)S(1)}, u32[]{:S(2)}, u32[]{:S(2)}) collective-permute-start(bf16[528,128]{1,0:T(8,128)(2,1)S(1)} %shard_map.125.refs_7_), channel_id=1, source_target_pairs={{0,24},{8,16},{16,8},{24,0},{1,25},{9,17},{17,9},{25,1},{2,26},{10... | collective-permute-start | bytes 405512 | tf_op jit(solution)/shard_map/ppermute | solution.py:194
  44.7 11.6 %collective-permute-start.14 = (bf16[528,128]{1,0:T(8,128)(2,1)S(1)}, bf16[528,128]{1,0:T(8,128)(2,1)S(1)}, u32[]{:S(2)}, u32[]{:S(2)}) collective-permute-start(bf16[528,128]{1,0:T(8,128)(2,1)S(1)} %shard_map.124.refs_6_), channel_id=1, source_target_pairs={{0,16},{8,24},{16,0},{24,8},{1,17},{9,25},{17,1},{25,9},{2,18},{10... | collective-permute-start | bytes 405512 | tf_op jit(solution)/shard_map/ppermute | solution.py:194
  45.8 10.5 %collective-permute-start.13 = (bf16[528,128]{1,0:T(8,128)(2,1)S(1)}, bf16[528,128]{1,0:T(8,128)(2,1)S(1)}, u32[]{:S(2)}, u32[]{:S(2)}) collective-permute-start(bf16[528,128]{1,0:T(8,128)(2,1)S(1)} %shard_map.123.refs_5_), channel_id=1, source_target_pairs={{0,8},{8,0},{16,24},{24,16},{1,9},{9,1},{17,25},{25,17},{2,10},{10... | collective-permute-start | bytes 405512 | tf_op jit(solution)/shard_map/ppermute | solution.py:194
  46.6 14.0 %slice-start = ((s8[4718592]{0:T(1024)(128)(4,1)}), s8[4194304]{0:T(1024)(128)(4,1)S(1)}, s32[]{:S(2)}) async-start(s8[4718592]{0:T(1024)(128)(4,1)} %bitcast.1), calls=%async_computation | async-start | bytes 8388608
  46.6 13.9 %slice-start.1 = ((s8[4718592]{0:T(1024)(128)(4,1)}), s8[524288]{0:T(1024)(128)(4,1)S(1)}, s32[]{:S(2)}) async-start(s8[4718592]{0:T(1024)(128)(4,1)} %bitcast.1), calls=%async_computation.1 | async-start | bytes 1048576
  49.0 5.7 %collective-permute-start.15 = (bf16[144,128]{1,0:T(8,128)(2,1)S(1)}, bf16[144,128]{1,0:T(8,128)(2,1)S(1)}, u32[]{:S(2)}, u32[]{:S(2)}) collective-permute-start(bf16[144,128]{1,0:T(8,128)(2,1)S(1)} %get-tuple-element.72), channel_id=1, source_target_pairs={{0,2},{2,0},{4,6},{6,4},{1,3},{3,1},{5,7},{7,5},{8,10},{10,8},{12,... | collective-permute-start | bytes 110600 | tf_op jit(solution)/shard_map/ppermute | solution.py:194
  50.4 4.3 %collective-permute-start.16 = (bf16[144,128]{1,0:T(8,128)(2,1)S(1)}, bf16[144,128]{1,0:T(8,128)(2,1)S(1)}, u32[]{:S(2)}, u32[]{:S(2)}) collective-permute-start(bf16[144,128]{1,0:T(8,128)(2,1)S(1)} %get-tuple-element.73), channel_id=1, source_target_pairs={{0,4},{2,6},{4,0},{6,2},{1,5},{3,7},{5,1},{7,3},{8,12},{10,14},{12... | collective-permute-start | bytes 110600 | tf_op jit(solution)/shard_map/ppermute | solution.py:194
  51.3 5.0 %collective-permute-start.17 = (bf16[144,128]{1,0:T(8,128)(2,1)S(1)}, bf16[144,128]{1,0:T(8,128)(2,1)S(1)}, u32[]{:S(2)}, u32[]{:S(2)}) collective-permute-start(bf16[144,128]{1,0:T(8,128)(2,1)S(1)} %get-tuple-element.74), channel_id=1, source_target_pairs={{0,6},{2,4},{4,2},{6,0},{1,7},{3,5},{5,3},{7,1},{8,14},{10,12},{12... | collective-permute-start | bytes 110600 | tf_op jit(solution)/shard_map/ppermute | solution.py:194
  56.7 5.2 %collective-permute-start.20 = (bf16[128,512]{1,0:T(8,128)(2,1)S(1)}, bf16[128,512]{1,0:T(8,128)(2,1)S(1)}, u32[]{:S(2)}, u32[]{:S(2)}) collective-permute-start(bf16[128,512]{1,0:T(8,128)(2,1)S(1)} %shard_map.128.refs_0_), channel_id=1, source_target_pairs={{0,2},{2,0},{4,6},{6,4},{1,3},{3,1},{5,7},{7,5},{8,10},{10,8},{12,... | collective-permute-start | bytes 393224 | tf_op jit(solution)/shard_map/ppermute | solution.py:194
  59.0 6.4 %collective-permute-start.19 = (bf16[128,512]{1,0:T(8,128)(2,1)S(1)}, bf16[128,512]{1,0:T(8,128)(2,1)S(1)}, u32[]{:S(2)}, u32[]{:S(2)}) collective-permute-start(bf16[128,512]{1,0:T(8,128)(2,1)S(1)} %shard_map.128.refs_0_), channel_id=1, source_target_pairs={{0,4},{2,6},{4,0},{6,2},{1,5},{3,7},{5,1},{7,3},{8,12},{10,14},{12... | collective-permute-start | bytes 393224 | tf_op jit(solution)/shard_map/ppermute | solution.py:194
  59.0 6.8 %collective-permute-start.18 = (bf16[128,512]{1,0:T(8,128)(2,1)S(1)}, bf16[128,512]{1,0:T(8,128)(2,1)S(1)}, u32[]{:S(2)}, u32[]{:S(2)}) collective-permute-start(bf16[128,512]{1,0:T(8,128)(2,1)S(1)} %shard_map.128.refs_0_), channel_id=1, source_target_pairs={{0,6},{2,4},{4,2},{6,0},{1,7},{3,5},{5,3},{7,1},{8,14},{10,12},{12... | collective-permute-start | bytes 393224 | tf_op jit(solution)/shard_map/ppermute | solution.py:194
  65.7 7.4 %copy-start.4 = (bf16[32,4,1152]{2,1,0:T(4,128)(2,1)S(1)}, bf16[32,4,1152]{2,1,0:T(4,128)(2,1)}, u32[]{:S(2)}) copy-start(bf16[32,4,1152]{2,1,0:T(4,128)(2,1)} %x_ref.1) | copy-start | bytes 884740
  65.8 7.4 %copy-start.8 = (f32[1152]{0:T(1024)S(1)}, f32[1152]{0:T(1024)}, u32[]{:S(2)}) copy-start(f32[1152]{0:T(1024)} %gain_ref.3) | copy-start | bytes 13828
  66.2 1.6 %collective-permute-start.21 = (bf16[128,1152]{1,0:T(8,128)(2,1)S(1)}, bf16[128,1152]{1,0:T(8,128)(2,1)S(1)}, u32[]{:S(2)}, u32[]{:S(2)}) collective-permute-start(bf16[128,1152]{1,0:T(8,128)(2,1)S(1)} %convert_element_type.15), channel_id=1, source_target_pairs={{0,1},{1,0},{2,3},{3,2},{4,5},{5,4},{6,7},{7,6},{8,9},{9,8},{10,11... | collective-permute-start | bytes 884744 | tf_op jit(solution)/shard_map/ppermute | solution.py:194
  68.0 4.6 %collective-permute-start.24 = (f32[8,128]{1,0:T(8,128)S(1)}, f32[8,128]{1,0:T(8,128)S(1)}, u32[]{:S(2)}, u32[]{:S(2)}) collective-permute-start(f32[8,128]{1,0:T(8,128)S(1)} %get-tuple-element.76.refs_0_), channel_id=1, source_target_pairs={{0,6},{2,4},{4,2},{6,0},{1,7},{3,5},{5,3},{7,1},{8,14},{10,12},{12... | collective-permute-start | bytes 12296 | tf_op jit(solution)/shard_map/ppermute | solution.py:194
  68.7 3.9 %collective-permute-start.23 = (f32[8,128]{1,0:T(8,128)S(1)}, f32[8,128]{1,0:T(8,128)S(1)}, u32[]{:S(2)}, u32[]{:S(2)}) collective-permute-start(f32[8,128]{1,0:T(8,128)S(1)} %get-tuple-element.76.refs_0_), channel_id=1, source_target_pairs={{0,4},{2,6},{4,0},{6,2},{1,5},{3,7},{5,1},{7,3},{8,12},{10,14},{12... | collective-permute-start | bytes 12296 | tf_op jit(solution)/shard_map/ppermute | solution.py:194
  69.4 3.7 %collective-permute-start.22 = (f32[8,128]{1,0:T(8,128)S(1)}, f32[8,128]{1,0:T(8,128)S(1)}, u32[]{:S(2)}, u32[]{:S(2)}) collective-permute-start(f32[8,128]{1,0:T(8,128)S(1)} %get-tuple-element.76.refs_0_), channel_id=1, source_target_pairs={{0,2},{2,0},{4,6},{6,4},{1,3},{3,1},{5,7},{7,5},{8,10},{10,8},{12,... | collective-permute-start | bytes 12296 | tf_op jit(solution)/shard_map/ppermute | solution.py:194
